TPU v7x, 32 devices: a whole 2x2x4 slice. The times are simulated.
32 devices in a mesh: gx: 4 (over z), gy: 8 (over y, x, core).
Axes of the slice: x: 2, y: 2, z: 4, core: 2. Of those that a mesh axis runs over, the one named last changes fastest.
Arguments:
- positions: float32 [3, 65536], P(None, ('gx', 'gy')), may hold values from -1 to 1
- normals: float32 [3, 65536], P(None, ('gx', 'gy')), may hold values from -4 to 4
- emission: float32 [16, 65536], P(None, ('gx', 'gy')), may hold values from 0.05 to 2
- material: int32 [65536], P(('gx', 'gy')), may hold values from 0 to 7
- area_level: int32 [65536], P(('gx', 'gy')), may hold values from 0 to 7
- reflect_table: float32 [8, 16], replicated, may hold values from 0.1 to 0.9
- area_table: float32 [8], replicated, may hold values from 0.002 to 0.008
- pair_slots: int32 [32, 32, 2, 2], P(('gx', 'gy')), may hold values from -1 to 7, as said below
Outputs:
- radiosity: float32 [16, 65536], P(None, ('gx', 'gy'))
Inputs may be any that keep to these rules, and one draw needn't show every extreme that they name: `pair_slots`: in slot [q, p, c], a row entry is -1 exactly when its column entry is -1; the non-empty slots of one [q, p] come first, at most 2 of them, and the slot group [q, q] is always full. No unordered pair of blocks occurs twice, and a slot never names the same block twice.
All inputs are finite; a program needn't handle non-finite values.
Results may differ from a plain program's by a relative error of at most 0.0017.
Values may be sent and summed in bfloat16 or wider, within the bound.
No kernel may reach another device: no remote copies, remote signals or barrier semaphores. Data moves between devices by JAX's collectives and lax.ppermute only.
A program may use at most 64 MiB of HBM per device.

v0:
```python
import math

import jax
import jax.numpy as jnp
from jax import lax
from jax.sharding import PartitionSpec as P

BANDS = 16
BLK = 256
CAP = 2
ITERS = 2


def view_tile(row_geo, col_geo):
    delta = [col_geo[k][None, :] - row_geo[k][:, None] for k in range(3)]
    squared = delta[0] * delta[0] + delta[1] * delta[1] + delta[2] * delta[2]
    facing = jnp.maximum(
        row_geo[3][:, None] * delta[0]
        + row_geo[4][:, None] * delta[1]
        + row_geo[5][:, None] * delta[2],
        0.0,
    )
    seen = jnp.maximum(
        -(
            col_geo[3][None, :] * delta[0]
            + col_geo[4][None, :] * delta[1]
            + col_geo[5][None, :] * delta[2]
        ),
        0.0,
    )
    mean_area = 0.5 * (row_geo[6][:, None] + col_geo[6][None, :])
    return facing * seen / ((squared + mean_area) * (math.pi * squared + mean_area))


def move_flux(blocks):
    return lax.all_to_all(blocks, ("gx", "gy"), split_axis=0, concat_axis=0, tiled=True)


def move_back(blocks):
    return lax.all_to_all(
        blocks.astype(jnp.bfloat16), ("gx", "gy"), split_axis=0, concat_axis=0, tiled=True
    ).astype(blocks.dtype)


def per_device(
    positions, normals, emission, material, area_level, reflect_table, area_table, pair_slots
):
    patches = positions.shape[1]
    nblocks = patches // BLK
    level_hot = (
        area_level[None, :] == jnp.arange(area_table.shape[0], dtype=jnp.int32)[:, None]
    ).astype(jnp.float32)
    area = jnp.sum(level_hot * area_table[:, None], axis=0)
    kind_hot = (
        material[None, :] == jnp.arange(reflect_table.shape[0], dtype=jnp.int32)[:, None]
    ).astype(jnp.float32)
    reflect = jnp.dot(jnp.transpose(reflect_table), kind_hot, precision=lax.Precision.HIGHEST)
    geometry = jnp.concatenate([positions, normals, area[None, :]], axis=0)
    geo_blocks = jnp.transpose(geometry.reshape(7, nblocks, BLK), (1, 0, 2))
    slots_here = pair_slots[0]
    peers = slots_here.shape[0]
    width = peers * CAP
    row_local = slots_here[..., 0]
    col_local = slots_here[..., 1]
    usable = (row_local >= 0).astype(jnp.float32)
    row_block = jnp.maximum(row_local, 0)
    served = lax.all_to_all(col_local, ("gx", "gy"), split_axis=0, concat_axis=0, tiled=True)
    served_ok = (served >= 0).astype(jnp.float32)
    served_block = jnp.maximum(served, 0)
    local_geo = geo_blocks[row_block]
    requested_geo = geo_blocks[served_block]
    remote_geo = lax.all_to_all(
        requested_geo, ("gx", "gy"), split_axis=0, concat_axis=0, tiled=True
    )
    block_ids = jnp.arange(nblocks, dtype=jnp.int32)[:, None]
    row_hot = (row_block.reshape(width)[None, :] == block_ids).astype(jnp.float32) * usable.reshape(
        width
    )[None, :]
    served_hot = (served_block.reshape(width)[None, :] == block_ids).astype(
        jnp.float32
    ) * served_ok.reshape(width)[None, :]
    groups = width // 32
    local_geo_groups = local_geo.reshape(groups, 32, 7, BLK)
    remote_geo_groups = remote_geo.reshape(groups, 32, 7, BLK)
    mask_groups = usable.reshape(groups, 32)
    radiosity = emission
    for sweep in range(ITERS):
        flux = (area[None, :] * radiosity).astype(jnp.bfloat16)
        flux_blocks = jnp.transpose(flux.reshape(BANDS, nblocks, BLK), (1, 0, 2))
        leaving = flux_blocks[row_block]
        arriving = move_flux(flux_blocks[served_block])

        def one_group(carry, item):
            row_geo, col_geo, col_flux, row_flux, mask_here = item
            tiles = jax.vmap(view_tile)(row_geo, col_geo) * mask_here[:, None, None]
            tiles = tiles.astype(jnp.bfloat16)
            own = jnp.einsum("sbj,sij->sbi", col_flux, tiles, preferred_element_type=jnp.float32)
            back = jnp.einsum("sbi,sij->sbj", row_flux, tiles, preferred_element_type=jnp.float32)
            return (carry, (own, back))

        items = (
            local_geo_groups,
            remote_geo_groups,
            arriving.reshape(groups, 32, BANDS, BLK),
            leaving.reshape(groups, 32, BANDS, BLK),
            mask_groups,
        )
        unused, terms = lax.scan(one_group, jnp.zeros((), jnp.float32), items)
        own_terms, back_terms = terms
        returned = move_back(back_terms.reshape(peers, CAP, BANDS, BLK))
        local_sum = jnp.dot(
            row_hot, own_terms.reshape(width, BANDS * BLK), precision=lax.Precision.HIGHEST
        )
        returned_sum = jnp.dot(
            served_hot, returned.reshape(width, BANDS * BLK), precision=lax.Precision.HIGHEST
        )
        summed = (local_sum + returned_sum).reshape(nblocks, BANDS, BLK)
        irradiation = jnp.transpose(summed, (1, 0, 2)).reshape(BANDS, patches)
        radiosity = emission + reflect * irradiation
    return radiosity


def solution(mesh):
    placed = (
        P(None, ("gx", "gy")),
        P(None, ("gx", "gy")),
        P(None, ("gx", "gy")),
        P(("gx", "gy")),
        P(("gx", "gy")),
        P(),
        P(),
        P(("gx", "gy"), None, None, None),
    )
    return jax.shard_map(
        per_device, mesh=mesh, in_specs=placed, out_specs=P(None, ("gx", "gy")), check_vma=False
    )
```

profile of v0, /device:TPU:0, one launch (start us, length us, event | category | flops | bytes accessed | tf_op | source)
XLA Modules:
  0.0 239.0 jit_solution(6949766367384305630)
XLA Ops:
  0.0 0.8 fusion.81
  0.8 0.7 copy.61
  1.5 7.3 %all-to-all-start = ((s32[32,1,2]{2,1,0:T(1,128)}), s32[32,1,2]{2,1,0:T(1,128)S(1)}, u32[]{:S(2)}, u32[]{:S(2)}) async-start(s32[32,1,2]{2,1,0:T(1,128)} %copy.61), calls=%async_computation | async-start | bytes 32768 | tf_op jit(solution)/shard_map/all_to_all | solution.py:67
  8.8 0.8 select_reduce_fusion
  9.6 0.8 maximum_bitcast_fusion
  10.4 5.5 %all-to-all-done = s32[32,1,2]{2,1,0:T(1,128)S(1)} async-done(((s32[32,1,2]{2,1,0:T(1,128)}), s32[32,1,2]{2,1,0:T(1,128)S(1)}, u32[]{:S(2)}, u32[]{:S(2)}) %all-to-all-start) | async-done | bytes 288 | tf_op jit(solution)/shard_map/all_to_all | solution.py:67
  16.0 0.4 copy-done.9
  16.4 0.6 gather_fusion.2
  17.1 1.0 copy.63
  18.1 2.6 %all-to-all-start.2 = ((f32[32,2,7,256]{3,1,2,0:T(2,128)}), f32[32,2,7,256]{3,1,2,0:T(2,128)S(1)}, u32[]{:S(2)}, u32[]{:S(2)}) async-start(f32[32,2,7,256]{3,1,2,0:T(2,128)} %copy.63), calls=%async_computation.2 | async-start | bytes 917504 | tf_op jit(solution)/shard_map/all_to_all | solution.py:72
  20.8 1.4 gather_fusion
  22.2 12.9 %all-to-all-done.2 = f32[32,2,7,256]{3,1,2,0:T(2,128)S(1)} async-done(((f32[32,2,7,256]{3,1,2,0:T(2,128)}), f32[32,2,7,256]{3,1,2,0:T(2,128)S(1)}, u32[]{:S(2)}, u32[]{:S(2)}) %all-to-all-start.2) | async-done | bytes 458784 | tf_op jit(solution)/shard_map/all_to_all | solution.py:72
  35.1 2.8 %all-to-all-start.1 = ((bf16[32,2,16,256]{3,2,1,0:T(8,128)(2,1)}), bf16[32,2,16,256]{3,2,1,0:T(8,128)(2,1)S(1)}, u32[]{:S(2)}, u32[]{:S(2)}) async-start(bf16[32,2,16,256]{3,2,1,0:T(8,128)(2,1)} %bitcast.46), calls=%async_computation.1 | async-start | bytes 1048576 | tf_op jit(solution)/shard_map/all_to_all | solution.py:36
  38.1 0.6 gather_fusion.3
  38.7 0.6 gather_fusion.1
  39.5 0.8 fusion.80
  40.4 1.9 copy.92
  42.5 0.3 reshape.137
  42.9 10.5 %all-to-all-done.1 = bf16[32,2,16,256]{3,2,1,0:T(8,128)(2,1)S(1)} async-done(((bf16[32,2,16,256]{3,2,1,0:T(8,128)(2,1)}), bf16[32,2,16,256]{3,2,1,0:T(8,128)(2,1)S(1)}, u32[]{:S(2)}, u32[]{:S(2)}) %all-to-all-start.1) | async-done | bytes 524320 | tf_op jit(solution)/shard_map/all_to_all | solution.py:36
  53.5 62.3 %while.24 = (s32[]{:T(128)}, f32[2,32,16,256]{3,2,1,0:T(8,128)S(1)}, bf16[2,32,16,256]{3,2,1,0:T(8,128)(2,1)}, bf16[2,32,16,256]{3,2,1,0:T(8,128)(2,1)S(1)}, f32...) while((s32[]{:T(128)}, ...), condition=%wide.region_2.3_spmd, body=%wide.region_1.2_spmd.sunk | while | flops 264241152 | bytes 4328813 | solution.py:108
  53.6 16.0 %fusion.107 = bf16[2,32,16,256]{3,2,1,0:T(8,128)(2,1)} fusion(bf16[2,32,16,256]{3,2,1,0:T(8,128)(2,1)} %get-tuple-element.402, s32[]{:T(128)S(6)} %copy.93, bf16[2,32,16,256]{3,2,1,0:T(8,128)(2,1)S(1)} %get-tuple-element.416, f32[32]{0:T(128)S(1)} %fusion.105, f32[32,256]{1,0:T(8,128)S(1)} %get-tuple-element.352, ...), kind=kOutput, calls=%fused_computation.33.clone.1 | convolution fusion | flops 132120576 | bytes 1246720 | tf_op jit(solution)/shard_map/while/body/eval_jaxpr/sbi,sij->sbj/dot_general | solution.py:98
  69.6 15.1 %fusion.106 = f32[2,32,16,256]{3,2,1,0:T(8,128)S(1)} fusion(f32[2,32,16,256]{3,2,1,0:T(8,128)S(1)} %get-tuple-element.401, s32[]{:T(128)S(6)} %copy.93, bf16[2,32,16,256]{3,2,1,0:T(8,128)(2,1)S(1)} %get-tuple-element.412, f32[32]{0:T(128)S(1)} %fusion.105, f32[32,256]{1,0:T(8,128)S(1)} %get-tuple-element.352, f32[32,256]{1,0:T(8,128)S(1)} %get-tuple-element.354, ...), kind=kOutput, calls=%fused_computation.35.clone.1 | convolution fusion | flops 132120576 | bytes 1246720 | tf_op jit(solution)/shard_map/while/body/eval_jaxpr/sbj,sij->sbi/dot_general | solution.py:97
  84.8 15.9 %fusion.107 = bf16[2,32,16,256]{3,2,1,0:T(8,128)(2,1)} fusion(bf16[2,32,16,256]{3,2,1,0:T(8,128)(2,1)} %get-tuple-element.402, s32[]{:T(128)S(6)} %copy.93, bf16[2,32,16,256]{3,2,1,0:T(8,128)(2,1)S(1)} %get-tuple-element.416, f32[32]{0:T(128)S(1)} %fusion.105, f32[32,256]{1,0:T(8,128)S(1)} %get-tuple-element.352, ...), kind=kOutput, calls=%fused_computation.33.clone.1 | convolution fusion | flops 132120576 | bytes 1246720 | tf_op jit(solution)/shard_map/while/body/eval_jaxpr/sbi,sij->sbj/dot_general | solution.py:98
  100.7 15.1 %fusion.106 = f32[2,32,16,256]{3,2,1,0:T(8,128)S(1)} fusion(f32[2,32,16,256]{3,2,1,0:T(8,128)S(1)} %get-tuple-element.401, s32[]{:T(128)S(6)} %copy.93, bf16[2,32,16,256]{3,2,1,0:T(8,128)(2,1)S(1)} %get-tuple-element.412, f32[32]{0:T(128)S(1)} %fusion.105, f32[32,256]{1,0:T(8,128)S(1)} %get-tuple-element.352, f32[32,256]{1,0:T(8,128)S(1)} %get-tuple-element.354, ...), kind=kOutput, calls=%fused_computation.35.clone.1 | convolution fusion | flops 132120576 | bytes 1246720 | tf_op jit(solution)/shard_map/while/body/eval_jaxpr/sbj,sij->sbi/dot_general | solution.py:97
  115.8 3.1 %all-to-all-start.3 = ((bf16[32,2,16,256]{3,2,1,0:T(8,128)(2,1)}), bf16[32,2,16,256]{3,2,1,0:T(8,128)(2,1)S(1)}, u32[]{:S(2)}, u32[]{:S(2)}) async-start(bf16[32,2,16,256]{3,2,1,0:T(8,128)(2,1)} %bitcast.56), calls=%async_computation.3 | async-start | bytes 1048576 | tf_op jit(solution)/shard_map/all_to_all | solution.py:40
  119.2 0.6 copy.76
  119.8 0.6 fusion.62
  120.4 14.0 %all-to-all-done.3 = bf16[32,2,16,256]{3,2,1,0:T(8,128)(2,1)S(1)} async-done(((bf16[32,2,16,256]{3,2,1,0:T(8,128)(2,1)}), bf16[32,2,16,256]{3,2,1,0:T(8,128)(2,1)S(1)}, u32[]{:S(2)}, u32[]{:S(2)}) %all-to-all-start.3) | async-done | bytes 524320 | tf_op jit(solution)/shard_map/all_to_all | solution.py:40
  134.4 0.2 copy.77
  134.6 0.3 convolution_add_fusion.1
  135.0 0.3 copy-done.2
  135.3 0.9 multiply_convert_fusion
  136.3 1.4 gather_fusion.4
  137.7 3.1 %all-to-all-start.4 = ((bf16[32,2,16,256]{3,2,1,0:T(8,128)(2,1)}), bf16[32,2,16,256]{3,2,1,0:T(8,128)(2,1)S(1)}, u32[]{:S(2)}, u32[]{:S(2)}) async-start(bf16[32,2,16,256]{3,2,1,0:T(8,128)(2,1)} %bitcast.60), calls=%async_computation.4 | async-start | bytes 1048576 | tf_op jit(solution)/shard_map/all_to_all | solution.py:36
  140.8 0.6 gather_fusion.5
  141.4 14.9 %all-to-all-done.4 = bf16[32,2,16,256]{3,2,1,0:T(8,128)(2,1)S(1)} async-done(((bf16[32,2,16,256]{3,2,1,0:T(8,128)(2,1)}), bf16[32,2,16,256]{3,2,1,0:T(8,128)(2,1)S(1)}, u32[]{:S(2)}, u32[]{:S(2)}) %all-to-all-start.4) | async-done | bytes 524320 | tf_op jit(solution)/shard_map/all_to_all | solution.py:36
  156.4 62.3 %while.25 = (s32[]{:T(128)}, f32[2,32,16,256]{3,2,1,0:T(8,128)S(1)}, bf16[2,32,16,256]{3,2,1,0:T(8,128)(2,1)}, bf16[2,32,16,256]{3,2,1,0:T(8,128)(2,1)S(1)}, f32...) while((s32[]{:T(128)}, ...), condition=%wide.region_4.5_spmd, body=%wide.region_3.4_spmd.sunk | while | flops 264241152 | bytes 4328813 | solution.py:108
  156.5 16.0 %fusion.114 = bf16[2,32,16,256]{3,2,1,0:T(8,128)(2,1)} fusion(bf16[2,32,16,256]{3,2,1,0:T(8,128)(2,1)} %get-tuple-element.429, s32[]{:T(128)S(6)} %copy.102, bf16[2,32,16,256]{3,2,1,0:T(8,128)(2,1)S(1)} %get-tuple-element.443, f32[32]{0:T(128)S(1)} %fusion.112, f32[32,256]{1,0:T(8,128)S(1)} %get-tuple-element.376, ...), kind=kOutput, calls=%fused_computation.87.clone.1 | convolution fusion | flops 132120576 | bytes 1246720 | tf_op jit(solution)/shard_map/while/body/eval_jaxpr/sbi,sij->sbj/dot_general | solution.py:98
  172.5 15.1 %fusion.113 = f32[2,32,16,256]{3,2,1,0:T(8,128)S(1)} fusion(f32[2,32,16,256]{3,2,1,0:T(8,128)S(1)} %get-tuple-element.428, s32[]{:T(128)S(6)} %copy.102, bf16[2,32,16,256]{3,2,1,0:T(8,128)(2,1)S(1)} %get-tuple-element.439, f32[32]{0:T(128)S(1)} %fusion.112, f32[32,256]{1,0:T(8,128)S(1)} %get-tuple-element.376, ...), kind=kOutput, calls=%fused_computation.89.clone.1 | convolution fusion | flops 132120576 | bytes 1246720 | tf_op jit(solution)/shard_map/while/body/eval_jaxpr/sbj,sij->sbi/dot_general | solution.py:97
  187.7 16.0 %fusion.114 = bf16[2,32,16,256]{3,2,1,0:T(8,128)(2,1)} fusion(bf16[2,32,16,256]{3,2,1,0:T(8,128)(2,1)} %get-tuple-element.429, s32[]{:T(128)S(6)} %copy.102, bf16[2,32,16,256]{3,2,1,0:T(8,128)(2,1)S(1)} %get-tuple-element.443, f32[32]{0:T(128)S(1)} %fusion.112, f32[32,256]{1,0:T(8,128)S(1)} %get-tuple-element.376, ...), kind=kOutput, calls=%fused_computation.87.clone.1 | convolution fusion | flops 132120576 | bytes 1246720 | tf_op jit(solution)/shard_map/while/body/eval_jaxpr/sbi,sij->sbj/dot_general | solution.py:98
  203.6 15.1 %fusion.113 = f32[2,32,16,256]{3,2,1,0:T(8,128)S(1)} fusion(f32[2,32,16,256]{3,2,1,0:T(8,128)S(1)} %get-tuple-element.428, s32[]{:T(128)S(6)} %copy.102, bf16[2,32,16,256]{3,2,1,0:T(8,128)(2,1)S(1)} %get-tuple-element.439, f32[32]{0:T(128)S(1)} %fusion.112, f32[32,256]{1,0:T(8,128)S(1)} %get-tuple-element.376, ...), kind=kOutput, calls=%fused_computation.89.clone.1 | convolution fusion | flops 132120576 | bytes 1246720 | tf_op jit(solution)/shard_map/while/body/eval_jaxpr/sbj,sij->sbi/dot_general | solution.py:97
  218.7 3.1 %all-to-all-start.5 = ((bf16[32,2,16,256]{3,2,1,0:T(8,128)(2,1)}), bf16[32,2,16,256]{3,2,1,0:T(8,128)(2,1)S(1)}, u32[]{:S(2)}, u32[]{:S(2)}) async-start(bf16[32,2,16,256]{3,2,1,0:T(8,128)(2,1)} %bitcast.64), calls=%async_computation.5 | async-start | bytes 1048576 | tf_op jit(solution)/shard_map/all_to_all | solution.py:40
  221.8 0.6 copy.79
  222.4 0.6 fusion.60
  223.0 14.3 %all-to-all-done.5 = bf16[32,2,16,256]{3,2,1,0:T(8,128)(2,1)S(1)} async-done(((bf16[32,2,16,256]{3,2,1,0:T(8,128)(2,1)}), bf16[32,2,16,256]{3,2,1,0:T(8,128)(2,1)S(1)}, u32[]{:S(2)}, u32[]{:S(2)}) %all-to-all-start.5) | async-done | bytes 524320 | tf_op jit(solution)/shard_map/all_to_all | solution.py:40
  237.5 0.3 convolution_add_fusion
  237.9 0.3 copy-done.3
  238.3 0.7 multiply_add_fusion
  (89 shorter events, 2.1 us)
Async XLA Ops:
  0.0 135.0 %copy-start = (f32[8,16]{1,0:T(8,128)S(1)}, f32[8,16]{1,0:T(8,128)}, u32[]{:S(2)}) copy-start(f32[8,16]{1,0:T(8,128)} %param.17) | copy-start | bytes 1540
  1.5 14.4 %all-to-all-start = ((s32[32,1,2]{2,1,0:T(1,128)}), s32[32,1,2]{2,1,0:T(1,128)S(1)}, u32[]{:S(2)}, u32[]{:S(2)}) async-start(s32[32,1,2]{2,1,0:T(1,128)} %copy.61), calls=%async_computation | async-start | bytes 32768 | tf_op jit(solution)/shard_map/all_to_all | solution.py:67
  9.6 11.1 %copy-start.13 = (f32[2048]{0:T(1024)}, f32[2048]{0:T(1024)S(1)}, u32[]{:S(2)}) copy-start(f32[2048]{0:T(1024)S(1)} %select_reduce_fusion) | copy-start | bytes 24580
  15.8 0.6 copy-start.9
  16.4 1.7 copy-start.15
  16.4 4.3 %copy-start.4 = (s32[1024]{0:T(1024)}, s32[1024]{0:T(1024)S(1)}, u32[]{:S(2)}) copy-start(s32[1024]{0:T(1024)S(1)} %pad_clamp_fusion.1) | copy-start | bytes 12292
  17.1 3.6 %copy-start.1 = (f32[16,2048]{1,0:T(8,128)S(1)}, f32[16,2048]{1,0:T(8,128)}, u32[]{:S(2)}) copy-start(f32[16,2048]{1,0:T(8,128)} %param.14) | copy-start | bytes 393220
  18.1 17.0 %all-to-all-start.2 = ((f32[32,2,7,256]{3,1,2,0:T(2,128)}), f32[32,2,7,256]{3,1,2,0:T(2,128)S(1)}, u32[]{:S(2)}, u32[]{:S(2)}) async-start(f32[32,2,7,256]{3,1,2,0:T(2,128)} %copy.63), calls=%async_computation.2 | async-start | bytes 917504 | tf_op jit(solution)/shard_map/all_to_all | solution.py:72
  35.1 18.3 %all-to-all-start.1 = ((bf16[32,2,16,256]{3,2,1,0:T(8,128)(2,1)}), bf16[32,2,16,256]{3,2,1,0:T(8,128)(2,1)S(1)}, u32[]{:S(2)}, u32[]{:S(2)}) async-start(bf16[32,2,16,256]{3,2,1,0:T(8,128)(2,1)} %bitcast.46), calls=%async_computation.1 | async-start | bytes 1048576 | tf_op jit(solution)/shard_map/all_to_all | solution.py:36
  38.0 1.3 copy-start.18
  38.1 1.3 copy-start.6
  39.4 2.9 %copy-start.11 = (f32[32,2,1]{1,0,2:T(8,128)}, f32[32,2,1]{1,0,2:T(8,128)S(1)}, u32[]{:S(2)}) copy-start(f32[32,2,1]{1,0,2:T(8,128)S(1)} %copy.59) | copy-start | bytes 772
  115.8 3.1 %copy-start.12 = (f32[32,2,1]{1,0,2:T(8,128)S(1)}, f32[32,2,1]{1,0,2:T(8,128)}, u32[]{:S(2)}) copy-start(f32[32,2,1]{1,0,2:T(8,128)} %copy-done.11) | copy-start | bytes 772
  115.8 3.2 %copy-start.10 = (s32[32,1,2]{2,1,0:T(1,128)S(1)}, s32[32,1,2]{2,1,0:T(1,128)}, u32[]{:S(2)}) copy-start(s32[32,1,2]{2,1,0:T(1,128)} %copy-done.9) | copy-start | bytes 772
  115.8 18.6 %all-to-all-start.3 = ((bf16[32,2,16,256]{3,2,1,0:T(8,128)(2,1)}), bf16[32,2,16,256]{3,2,1,0:T(8,128)(2,1)S(1)}, u32[]{:S(2)}, u32[]{:S(2)}) async-start(bf16[32,2,16,256]{3,2,1,0:T(8,128)(2,1)} %bitcast.56), calls=%async_computation.3 | async-start | bytes 1048576 | tf_op jit(solution)/shard_map/all_to_all | solution.py:40
  119.0 0.8 copy-start.24
  119.2 15.5 %copy-start.22 = (f32[64]{0:T(128)}, f32[64]{0:T(128)S(1)}, u32[]{:S(2)}) copy-start(f32[64]{0:T(128)S(1)} %reshape.152) | copy-start | bytes 772
  119.2 0.6 copy-start.19
  119.8 14.8 %copy-start.16 = (s32[64]{0:T(128)S(1)}, s32[64]{0:T(128)}, u32[]{:S(2)}) copy-start(s32[64]{0:T(128)} %copy-done.15) | copy-start | bytes 772
  134.4 0.9 copy-start.2
  134.4 0.9 copy-start.14
  134.4 0.9 copy-start.21
  134.6 1.6 copy-start.5
  136.2 4.5 %copy-start.7 = (s32[1024]{0:T(1024)S(1)}, s32[1024]{0:T(1024)}, u32[]{:S(2)}) copy-start(s32[1024]{0:T(1024)} %copy-done.6) | copy-start | bytes 12292
  137.7 18.6 %all-to-all-start.4 = ((bf16[32,2,16,256]{3,2,1,0:T(8,128)(2,1)}), bf16[32,2,16,256]{3,2,1,0:T(8,128)(2,1)S(1)}, u32[]{:S(2)}, u32[]{:S(2)}) async-start(bf16[32,2,16,256]{3,2,1,0:T(8,128)(2,1)} %bitcast.60), calls=%async_computation.4 | async-start | bytes 1048576 | tf_op jit(solution)/shard_map/all_to_all | solution.py:36
  218.7 18.6 %all-to-all-start.5 = ((bf16[32,2,16,256]{3,2,1,0:T(8,128)(2,1)}), bf16[32,2,16,256]{3,2,1,0:T(8,128)(2,1)S(1)}, u32[]{:S(2)}, u32[]{:S(2)}) async-start(bf16[32,2,16,256]{3,2,1,0:T(8,128)(2,1)} %bitcast.64), calls=%async_computation.5 | async-start | bytes 1048576 | tf_op jit(solution)/shard_map/all_to_all | solution.py:40
  221.8 0.6 copy-start.20
  221.8 0.6 copy-start.25
  222.4 15.1 %copy-start.17 = (s32[64]{0:T(128)S(1)}, s32[64]{0:T(128)}, u32[]{:S(2)}) copy-start(s32[64]{0:T(128)} %copy-done.15) | copy-start | bytes 772
  222.4 15.1 %copy-start.23 = (f32[64]{0:T(128)S(1)}, f32[64]{0:T(128)}, u32[]{:S(2)}) copy-start(f32[64]{0:T(128)} %copy-done.22) | copy-start | bytes 772
  237.3 0.9 copy-start.3
  237.3 1.0 copy-start.8
where the time goes:
time: 240 us; the launch traced here: 239 us
  matrix products  127 us (53%)
  waiting for transfers between devices  72 us (30%)
  starting transfers between devices  21.9 us (9%)
  local copies, waits for them, and re-layouts  14.4 us (6%)
  other arithmetic  3.25 us (1%)
    dot_general x4, matrix products, one_group(): jnp.einsum('sbi,sij->sbj', row_flux, tiles, preferred_element_type=jnp.fl...  63.8 us
    dot_general x4, matrix products, one_group(): jnp.einsum('sbj,sij->sbi', col_flux, tiles, preferred_element_type=jnp.fl...  60.2 us
    all_to_all x2, waiting for transfers between devices, move_back(): lax.all_to_all(blocks.astype(jnp.bfloat16), ('gx', 'gy'), split_axis=0, c...  28.2 us
    all_to_all x2, waiting for transfers between devices, move_flux(): lax.all_to_all(blocks, ('gx', 'gy'), split_axis=0, concat_axis=0, tiled=T...  25.4 us
    all_to_all x1, waiting for transfers between devices, per_device(): lax.all_to_all(requested_geo, ('gx', 'gy'), split_axis=0, concat_axis=0,...  12.9 us
    all_to_all x1, starting transfers between devices, per_device(): lax.all_to_all(col_local, ('gx', 'gy'), split_axis=0, concat_axis=0, tile...  7.3 us
    all_to_all x2, starting transfers between devices, move_back(): lax.all_to_all(blocks.astype(jnp.bfloat16), ('gx', 'gy'), split_axis=0, c...  6.17 us
    all_to_all x2, starting transfers between devices, move_flux(): lax.all_to_all(blocks, ('gx', 'gy'), split_axis=0, concat_axis=0, tiled=T...  5.83 us
  transfers between devices with their start and end apart: 6, of which 6 were waited for; matrix products, arithmetic and copies ran while one was open for 5% of the time, Pallas kernels for 0%

commit v1 on v0

v1 whole, which is shorter than its diff:
```python
import functools
import math

import jax
import jax.numpy as jnp
from jax import lax
from jax.experimental import pallas as pl
from jax.experimental.pallas import tpu as pltpu
from jax.sharding import PartitionSpec as P

BANDS = 16
BLK = 256
CAP = 2
GEO = 16
KDIM = 48
KEEP_BYTES = 24 * 2**20
BF16 = jnp.bfloat16
F32 = jnp.float32

VMEM = functools.partial(pl.BlockSpec, memory_space=pltpu.VMEM)
SMEM = functools.partial(pl.BlockSpec, memory_space=pltpu.SMEM)


def split(value, terms):
    out = []
    for _ in range(terms):
        part = value.astype(BF16).astype(F32)
        out.append(part)
        value = value - part
    return out


def pack_kernel(pos_ref, nrm_ref, emi_ref, level_ref, table_ref, slot_ref, pay_ref, geo_ref, area_ref, rows):
    level = level_ref[...]
    area = jnp.zeros(level.shape, F32)
    for k in range(table_ref.shape[0]):
        area = jnp.where(level == k, table_ref[k], area)
    area_ref[...] = area
    p1, p2 = split(pos_ref[...], 2)
    n1, n2 = split(nrm_ref[...], 2)
    a1, a2 = split(area, 2)
    rows[0:3, :] = p1
    rows[3:6, :] = p2
    rows[6:9, :] = n1
    rows[9:12, :] = n2
    rows[12:13, :] = a1
    rows[13:14, :] = a2
    rows[14:15, :] = slot_ref[...]
    rows[15:16, :] = jnp.zeros_like(area)
    geo = rows[...].astype(BF16)
    geo_ref[...] = geo
    pay_ref[0:GEO, :] = geo
    pay_ref[GEO:, :] = (area * emi_ref[...]).astype(BF16)


def constants(g):
    p = g[0:3] + g[3:6]
    n = g[6:9] + g[9:12]
    half = 0.5 * (g[12:13] + g[13:14])
    pp = p[0:1] * p[0:1] + p[1:2] * p[1:2] + p[2:3] * p[2:3]
    np_ = n[0:1] * p[0:1] + n[1:2] * p[1:2] + n[2:3] * p[2:3]
    return p, split(pp + half, 3), split(math.pi * pp + half, 3), split(-np_, 3)


def column_features(g, feat):
    _, q, r, c = constants(g)
    one = jnp.ones_like(q[0])
    feat[0:12, :] = g[0:12]
    feat[12:24, :] = g[0:12]
    feat[24:30, :] = g[0:6]
    for t in range(3):
        feat[30 + t : 31 + t, :] = q[t]
        feat[33 + t : 34 + t, :] = r[t]
        feat[36 + t : 37 + t, :] = c[t]
        feat[39 + t : 40 + t, :] = one
    feat[42:48, :] = jnp.zeros((6,) + one.shape[1:], F32)


def row_features(g, feat, variant):
    p, q, r, c = constants(g)
    one = jnp.ones_like(q[0])
    feat[...] = jnp.zeros(feat.shape, F32)
    if variant == 0:
        feat[0:3, :] = g[6:9]
        feat[3:6, :] = g[6:9]
        feat[12:15, :] = g[9:12]
        feat[15:18, :] = g[9:12]
        last = c
    elif variant == 1:
        feat[6:9, :] = g[0:3]
        feat[9:12, :] = g[0:3]
        feat[18:21, :] = g[3:6]
        feat[21:24, :] = g[3:6]
        for t in range(3):
            feat[36 + t : 37 + t, :] = one
        last = None
    elif variant == 2:
        u1, u2 = -2.0 * g[0:3], -2.0 * g[3:6]
        feat[0:3, :] = u1
        feat[3:6, :] = u1
        feat[12:15, :] = u2
        feat[15:18, :] = u2
        for t in range(3):
            feat[30 + t : 31 + t, :] = one
        last = q
    else:
        u1, u2, u3 = split((-2.0 * math.pi) * p, 3)
        feat[0:3, :] = u1
        feat[3:6, :] = u1
        feat[12:15, :] = u2
        feat[15:18, :] = u2
        feat[24:27, :] = u3
        feat[27:30, :] = u3
        for t in range(3):
            feat[33 + t : 34 + t, :] = one
        last = r
    if last is not None:
        for t in range(3):
            feat[39 + t : 40 + t, :] = last[t]


def list_pairs(nz, ny, nb, place_ref, slots, pairs):
    z, k = place_ref[0], place_ref[1]
    most = nz * ny * 2 * CAP

    def peer(e, count):
        s = e // ny
        m = e % ny
        zs = lax.rem(z - s + nz, nz)
        own = (z * ny + jnp.bitwise_xor(k, m)) * (2 * CAP)
        served = (zs * ny + k) * (2 * CAP)
        for t in range(CAP):
            row, col = slots[s, own + 2 * t], slots[s, own + 2 * t + 1]
            pairs[count] = (s * nb + row) * 4096 + m * nb + col
            count = count + (row >= 0).astype(jnp.int32)
            col, row = slots[nz + m, served + 2 * t], slots[nz + m, served + 2 * t + 1]
            pairs[count] = (s * nb + row) * 4096 + m * nb + col
            count = count + (row >= 0).astype(jnp.int32)
        return count

    pairs[most + 1] = lax.fori_loop(0, nz * ny, peer, jnp.int32(0))


def put_out(nz, nb, acc, out_refs):
    for s in range(nz):
        for b in range(nb):
            out_refs[s][:, b * BLK : (b + 1) * BLK] = acc[s * nb + b].astype(out_refs[s].dtype)


def form_kernel(nz, ny, nb, keep, fresh, place_ref, *refs):
    geos, refs = refs[:nz], refs[nz:]
    pays, refs = refs[:ny], refs[ny:]
    if fresh:
        fluxes, refs = refs[:ny], refs[ny:]
    outs, refs = refs[:nz], refs[nz:]
    if keep:
        tiles_ref, pairs, refs = refs[0], refs[1], refs[2:]
    feat, row_feat, col_feat, flux, acc, slots_v, slots, sem, *more = refs
    if not keep:
        pairs = more[0]
    most = nz * ny * 2 * CAP
    width = slots.shape[1]
    for s in range(nz):
        g = geos[s][...].astype(F32)
        slots_v[s : s + 1, :] = g[14:15, :width].astype(jnp.int32)
    for m in range(ny):
        g = pays[m][0:GEO, :].astype(F32)
        slots_v[nz + m : nz + m + 1, :] = g[14:15, :width].astype(jnp.int32)
    copy = pltpu.make_async_copy(slots_v, slots, sem)
    copy.start()
    for s in range(nz):
        g = geos[s][...].astype(F32)
        for v in range(4):
            row_features(g, feat, v)
            for b in range(nb):
                row_feat[s * nb + b, v] = feat[:, b * BLK : (b + 1) * BLK].astype(BF16)
    for m in range(ny):
        g = pays[m][0:GEO, :].astype(F32)
        column_features(g, feat)
        for b in range(nb):
            col_feat[m * nb + b] = jnp.transpose(feat[:, b * BLK : (b + 1) * BLK]).astype(BF16)
            here = slice(b * BLK, (b + 1) * BLK)
            flux[m * nb + b] = fluxes[m][:, here] if fresh else pays[m][GEO:, here]
    acc[...] = jnp.zeros(acc.shape, F32)
    copy.wait()
    list_pairs(nz, ny, nb, place_ref, slots, pairs)

    def one(t, carry):
        code = pairs[t]
        rb = code // 4096
        cb = code % 4096
        parts = []
        for j in range(0, BLK, 64):
            left = col_feat[cb, j : j + 64, :]
            f, s, q, r = (
                jnp.dot(left, row_feat[rb, v], preferred_element_type=F32) for v in range(4)
            )
            top = jnp.maximum(f, 0.0) * jnp.maximum(s, 0.0)
            parts.append((top * pl.reciprocal(q * r, approx=True)).astype(BF16))
        tile = jnp.concatenate(parts, axis=0)
        if keep:
            tiles_ref[t] = tile
        acc[rb] += jnp.dot(flux[cb], tile, preferred_element_type=F32)
        return carry

    lax.fori_loop(0, pairs[most + 1], one, 0)
    put_out(nz, nb, acc, outs)


def apply_kernel(nz, ny, nb, pairs, tiles_ref, *refs):
    fluxes, refs = refs[:ny], refs[ny:]
    outs, refs = refs[:nz], refs[nz:]
    flux, acc = refs
    most = nz * ny * 2 * CAP
    for m in range(ny):
        for b in range(nb):
            flux[m * nb + b] = fluxes[m][:, b * BLK : (b + 1) * BLK]
    acc[...] = jnp.zeros(acc.shape, F32)

    def one(t, carry):
        code = pairs[t]
        rb = code // 4096
        cb = code % 4096
        acc[rb] += jnp.dot(flux[cb], tiles_ref[t], preferred_element_type=F32)
        return carry

    lax.fori_loop(0, pairs[most + 1], one, 0)
    put_out(nz, nb, acc, outs)


def per_device(nz, ny, positions, normals, emission, material, area_level, reflect_table, area_table, pair_slots):
    patches = positions.shape[1]
    nb = patches // BLK
    most = nz * ny * 2 * CAP
    width = most if nz * ny * 2 * CAP == pair_slots.size else pair_slots.size
    keep = most * BLK * BLK * 2 <= KEEP_BYTES
    params = pltpu.CompilerParams(vmem_limit_bytes=(30 if keep else 56) * 2**20)
    place = jnp.stack([lax.axis_index("gx"), lax.axis_index("gy")]).astype(jnp.int32)
    slot_row = pair_slots.reshape(1, -1).astype(F32)
    slot_row = jnp.pad(slot_row, ((0, 0), (0, patches - slot_row.shape[1])))
    payload, geo, area = pl.pallas_call(
        pack_kernel,
        out_shape=(
            jax.ShapeDtypeStruct((GEO + BANDS, patches), BF16),
            jax.ShapeDtypeStruct((GEO, patches), BF16),
            jax.ShapeDtypeStruct((1, patches), F32),
        ),
        in_specs=[VMEM()] * 4 + [SMEM(), VMEM()],
        out_specs=(VMEM(),) * 3,
        scratch_shapes=[pltpu.VMEM((GEO, patches), F32)],
        name="pack",
    )(positions, normals, emission, area_level.reshape(1, patches), area_table, slot_row)

    def along(x):
        return [lax.ppermute(x, "gx", [(i, (i + s) % nz) for i in range(nz)]) for s in range(1, nz)]

    def plane(x):
        got = {0: x}
        for m in range(2, ny, 2):
            got[m] = lax.ppermute(x, "gy", [(i, i ^ m) for i in range(ny)])
        for m in range(0, ny, 2):
            got[m + 1] = lax.ppermute(got[m], "gy", [(i, i ^ 1) for i in range(ny)])
        return [got[m] for m in range(ny)]

    def home(parts):
        total = parts[0]
        for s in range(1, nz):
            back = lax.ppermute(parts[s], "gx", [(i, (i - s) % nz) for i in range(nz)])
            total = total + back.astype(F32)
        return total

    rows = [geo] + along(geo)
    cols = plane(payload)
    out_parts = [jax.ShapeDtypeStruct((BANDS, patches), F32)] + [
        jax.ShapeDtypeStruct((BANDS, patches), BF16)
    ] * (nz - 1)

    def form(fluxes):
        fresh = fluxes is not None
        outs = list(out_parts)
        specs = [VMEM()] * nz
        if keep:
            outs += [
                pltpu.VMEM((most, BLK, BLK), BF16),
                jax.ShapeDtypeStruct((most + 8,), jnp.int32),
            ]
            specs += [VMEM(), SMEM()]
        scratch = [
            pltpu.VMEM((KDIM, patches), F32),
            pltpu.VMEM((nz * nb, 4, KDIM, BLK), BF16),
            pltpu.VMEM((ny * nb, BLK, KDIM), BF16),
            pltpu.VMEM((ny * nb, BANDS, BLK), BF16),
            pltpu.VMEM((nz * nb, BANDS, BLK), F32),
            pltpu.VMEM((-(-(nz + ny) // 8) * 8, width), jnp.int32),
            pltpu.SMEM((-(-(nz + ny) // 8) * 8, width), jnp.int32),
            pltpu.SemaphoreType.DMA,
        ]
        if not keep:
            scratch += [pltpu.SMEM((most + 8,), jnp.int32)]
        return pl.pallas_call(
            functools.partial(form_kernel, nz, ny, nb, keep, fresh),
            out_shape=tuple(outs),
            in_specs=[SMEM()] + [VMEM()] * (nz + ny + (ny if fresh else 0)),
            out_specs=tuple(specs),
            scratch_shapes=scratch,
            compiler_params=params,
            name="form",
        )(place, *rows, *cols, *(fluxes or []))

    def apply(pairs, tiles, fluxes):
        return pl.pallas_call(
            functools.partial(apply_kernel, nz, ny, nb),
            out_shape=tuple(out_parts),
            in_specs=[SMEM()] + [VMEM()] * (1 + ny),
            out_specs=(VMEM(),) * nz,
            scratch_shapes=[
                pltpu.VMEM((ny * nb, BANDS, BLK), BF16),
                pltpu.VMEM((nz * nb, BANDS, BLK), F32),
            ],
            compiler_params=params,
            name="apply",
        )(pairs, tiles, *fluxes)

    kind_hot = (
        material[None, :] == jnp.arange(reflect_table.shape[0], dtype=jnp.int32)[:, None]
    ).astype(F32)
    reflect = jnp.dot(jnp.transpose(reflect_table), kind_hot, precision=lax.Precision.HIGHEST)

    first = form(None)
    radiosity = emission + reflect * home(first[:nz])
    fluxes = plane((area * radiosity).astype(BF16))
    second = apply(first[nz + 1], first[nz], fluxes) if keep else form(fluxes)
    return emission + reflect * home(second[:nz])


def solution(mesh):
    nz, ny = mesh.shape["gx"], mesh.shape["gy"]
    both = ("gx", "gy")
    placed = (
        P(None, both),
        P(None, both),
        P(None, both),
        P(both),
        P(both),
        P(),
        P(),
        P(both, None, None, None),
    )
    return jax.shard_map(
        functools.partial(per_device, nz, ny),
        mesh=mesh,
        in_specs=placed,
        out_specs=P(None, both),
        check_vma=False,
    )
```

time: 240 us -> 110 us (0.46)
  matrix products: 127 us -> 0.95 us
  waiting for transfers between devices: 72 us -> 20.9 us
  Pallas kernels: 0 us -> 45.9 us
  starting transfers between devices: 21.9 us -> 24.6 us
    dot_general x12 -> x0, matrix products: 126 us -> none  [the longest x4 63.8 us: one_group(): jnp.einsum('sbi,sij->sbj', row_flux, tiles, preferred_element_type=jnp.fl...]
    all_to_all x6 -> x0, waiting for transfers between devices: 72 us -> none  [the longest x2 28.2 us: move_back(): lax.all_to_all(blocks.astype(jnp.bfloat16), ('gx', 'gy'), split_axis=0, c...]
    pallas_call x0 -> x3, Pallas kernels: none -> 45.9 us  [the longest x1 33.8 us: form(): pl.pallas_call(functools.partial(form_kernel, nz, ny, nb, keep, fresh), o...]
    ppermute x0 -> x23, starting transfers between devices: none -> 24.6 us  [the longest x6 8.37 us: home(): back = lax.ppermute(parts[s], 'gx', [(i, (i - s) % nz) for i in range(nz)])]
    all_to_all x6 -> x0, starting transfers between devices: 21.9 us -> none  [the longest x1 7.3 us: per_device(): lax.all_to_all(col_local, ('gx', 'gy'), split_axis=0, concat_axis=0, tile...]
    ppermute x0 -> x23, waiting for transfers between devices: none -> 20.9 us  [the longest x6 10.7 us: home(): back = lax.ppermute(parts[s], 'gx', [(i, (i - s) % nz) for i in range(nz)])]
    unnamed x59 -> x12, local copies, waits for them, and re-layouts: 4.76 us -> 13.2 us
    gather x7 -> x0, local copies, waits for them, and re-layouts: 6.27 us -> none  [the longest x2 2.82 us: per_device(): arriving = move_flux(flux_blocks[served_block])]
  transfers between devices with their start and end apart: 6 -> 23, of which waited for: 6 -> 11; matrix products, arithmetic and copies ran while one was open for 5% -> 1% of each run, Pallas kernels for 0% -> 0%
where the time goes in v1:
time: 110 us; the launch traced here: 109 us
  Pallas kernels  45.9 us (42%)
  starting transfers between devices  24.6 us (22%)
  waiting for transfers between devices  20.9 us (19%)
  local copies, waits for them, and re-layouts  14.1 us (13%)
  other arithmetic  2.45 us (2%)
    pallas_call x1, Pallas kernels, form(): pl.pallas_call(functools.partial(form_kernel, nz, ny, nb, keep, fresh), o...  33.8 us
    unnamed x12, local copies, waits for them, and re-layouts  13.2 us
    ppermute x6, waiting for transfers between devices, home(): back = lax.ppermute(parts[s], 'gx', [(i, (i - s) % nz) for i in range(nz)])  10.7 us
    pallas_call x1, Pallas kernels, apply(): pl.pallas_call(functools.partial(apply_kernel, nz, ny, nb), out_shape=tup...  10.4 us
    ppermute x6, starting transfers between devices, home(): back = lax.ppermute(parts[s], 'gx', [(i, (i - s) % nz) for i in range(nz)])  8.37 us
    ppermute x6, starting transfers between devices, plane(): got[m] = lax.ppermute(x, 'gy', [(i, i ^ m) for i in range(ny)])  8.01 us
    ppermute x3, starting transfers between devices, along(): lax.ppermute(x, 'gx', [(i, (i + s) % nz) for i in range(nz)])  7.23 us
    ppermute x6, waiting for transfers between devices, plane(): got[m] = lax.ppermute(x, 'gy', [(i, i ^ m) for i in range(ny)])  4.49 us
  transfers between devices with their start and end apart: 23, of which 11 were waited for; matrix products, arithmetic and copies ran while one was open for 1% of the time, Pallas kernels for 0%

profile of v1, /device:TPU:0, one launch (start us, length us, event | category | flops | bytes accessed | tf_op | source)
XLA Modules:
  0.0 109.0 jit_solution(13369932393857565687)
XLA Ops:
  0.0 0.7 convert_element_type.38
  0.7 0.1 copy.10
  0.8 0.1 convert_element_type.39
  1.0 0.6 pad.4.slot_ref
  1.6 1.7 %pack.1 = (bf16[32,2048]{1,0:T(8,128)(2,1)}, bf16[16,2048]{1,0:T(8,128)(2,1)}, f32[1,2048]{1,0:T(1,128)}) custom-call(f32[3,2048]{1,0:T(4,128)} %pos_ref.1, f32[3,2048]{1,0:T(4,128)} %nrm_ref.1, f32[16,2048]{1,0:T(8,128)} %emi_ref.1, s32[1,2048]{1,0:T(1,128)} %bitcast.7, f32[8]{0:T(128)} %table_ref.1, f32[1,2048]{1,0:T(1,128)} %pad.4.slot_ref), custom_call_target="tpu_custom_call" | custom-call | tf_op jit(solution)/shard_map/pack/pallas_call | solution.py:241
  3.3 2.9 %collective-permute-start.4 = (bf16[32,2048]{1,0:T(8,128)(2,1)}, bf16[32,2048]{1,0:T(8,128)(2,1)S(1)}, u32[]{:S(2)}, u32[]{:S(2)}) collective-permute-start(bf16[32,2048]{1,0:T(8,128)(2,1)} %get-tuple-element.19.refs_4_), channel_id=1, source_target_pairs={{0,2},{1,3},{2,0},{3,1},{4,6},{5,7},{6,4},{7,5},{8,10},{9,11},{10,... | collective-permute-start | bytes 393224 | tf_op jit(solution)/shard_map/ppermute | solution.py:260
  6.3 1.5 %collective-permute-start.6 = (bf16[32,2048]{1,0:T(8,128)(2,1)}, bf16[32,2048]{1,0:T(8,128)(2,1)S(1)}, u32[]{:S(2)}, u32[]{:S(2)}) collective-permute-start(bf16[32,2048]{1,0:T(8,128)(2,1)} %get-tuple-element.19.refs_4_), channel_id=1, source_target_pairs={{0,4},{1,5},{2,6},{3,7},{4,0},{5,1},{6,2},{7,3},{8,12},{9,13},{10,... | collective-permute-start | bytes 393224 | tf_op jit(solution)/shard_map/ppermute | solution.py:260
  7.8 0.0 collective-permute-start.8
  7.8 2.1 %collective-permute-start = (bf16[16,2048]{1,0:T(8,128)(2,1)}, bf16[16,2048]{1,0:T(8,128)(2,1)S(1)}, u32[]{:S(2)}, u32[]{:S(2)}) collective-permute-start(bf16[16,2048]{1,0:T(8,128)(2,1)} %get-tuple-element.18.refs_0_), channel_id=1, source_target_pairs={{0,8},{8,16},{16,24},{24,0},{1,9},{9,17},{17,25},{25,1},{2,10},{10... | collective-permute-start | bytes 196616 | tf_op jit(solution)/shard_map/ppermute | solution.py:255
  9.8 2.6 %collective-permute-start.1 = (bf16[16,2048]{1,0:T(8,128)(2,1)}, bf16[16,2048]{1,0:T(8,128)(2,1)S(1)}, u32[]{:S(2)}, u32[]{:S(2)}) collective-permute-start(bf16[16,2048]{1,0:T(8,128)(2,1)} %get-tuple-element.18.refs_0_), channel_id=1, source_target_pairs={{0,16},{8,24},{16,0},{24,8},{1,17},{9,25},{17,1},{25,9},{2,18},{10... | collective-permute-start | bytes 196616 | tf_op jit(solution)/shard_map/ppermute | solution.py:255
  12.4 2.3 %collective-permute-done.refs_1_ = bf16[16,2048]{1,0:T(8,128)(2,1)S(1)} collective-permute-done((bf16[16,2048]{1,0:T(8,128)(2,1)}, bf16[16,2048]{1,0:T(8,128)(2,1)S(1)}, u32[]{:S(2)}, u32[]{:S(2)}) %collective-permute-start) | collective-permute-done | bytes 65568 | tf_op jit(solution)/shard_map/ppermute | solution.py:255
  14.8 0.5 collective-permute-start.5
  15.3 0.1 collective-permute-start.7
  15.3 0.4 collective-permute-start.9
  15.8 2.6 %collective-permute-start.2 = (bf16[16,2048]{1,0:T(8,128)(2,1)}, bf16[16,2048]{1,0:T(8,128)(2,1)S(1)}, u32[]{:S(2)}, u32[]{:S(2)}) collective-permute-start(bf16[16,2048]{1,0:T(8,128)(2,1)} %get-tuple-element.18.refs_0_), channel_id=1, source_target_pairs={{0,24},{8,0},{16,8},{24,16},{1,25},{9,1},{17,9},{25,17},{2,26},{10... | collective-permute-start | bytes 196616 | tf_op jit(solution)/shard_map/ppermute | solution.py:255
  18.4 0.1 pad_add_fusion.place_ref
  18.4 2.1 %collective-permute-done.2.refs_3_ = bf16[16,2048]{1,0:T(8,128)(2,1)S(1)} collective-permute-done((bf16[16,2048]{1,0:T(8,128)(2,1)}, bf16[16,2048]{1,0:T(8,128)(2,1)S(1)}, u32[]{:S(2)}, u32[]{:S(2)}) %collective-permute-start.2) | collective-permute-done | bytes 65568 | tf_op jit(solution)/shard_map/ppermute | solution.py:255
  20.6 0.0 collective-permute-done.3.refs_5_
  20.6 0.0 collective-permute-done.5.refs_7_
  20.6 0.0 collective-permute-done.7.refs_9_
  20.6 0.0 copy-start.3
  20.6 0.9 copy-done.3
  21.5 0.8 copy-done.4
  22.4 33.8 %form.1 = (f32[16,2048]{1,0:T(8,128)S(1)}, bf16[16,2048]{1,0:T(8,128)(2,1)S(1)}, bf16[16,2048]{1,0:T(8,128)(2,1)S(1)}, bf16[16,2048]{1,0:T(8,128)(2,1)S(1)}, bf1...) custom-call(s32[2]{0:T(128)S(1)} %pad_add_fusion.place_ref, bf16[16,2048]{1,0:T(8,128)(2,1)S(1)} %copy-done.4, ...), custom_call_target="tpu_custom_call" | custom-call | tf_op jit(solution)/shard_map/form/pallas_call | solution.py:300
  56.2 5.7 %copy-done.1 = bf16[128,256,256]{2,1,0:T(8,128)(2,1)} copy-done((bf16[128,256,256]{2,1,0:T(8,128)(2,1)}, bf16[128,256,256]{2,1,0:T(8,128)(2,1)S(1)}, u32[]{:S(2)}) %copy-start.1) | copy-done | bytes 16777240
  61.9 1.6 %collective-permute-start.10 = (bf16[16,2048]{1,0:T(8,128)(2,1)S(1)}, bf16[16,2048]{1,0:T(8,128)(2,1)S(1)}, u32[]{:S(2)}, u32[]{:S(2)}) collective-permute-start(bf16[16,2048]{1,0:T(8,128)(2,1)S(1)} %get-tuple-element.24), channel_id=1, source_target_pairs={{0,24},{8,0},{16,8},{24,16},{1,25},{9,1},{17,9},{25,17},{2,26},{10... | collective-permute-start | bytes 196616 | tf_op jit(solution)/shard_map/ppermute | solution.py:268
  63.5 3.0 %collective-permute-start.11 = (bf16[16,2048]{1,0:T(8,128)(2,1)S(1)}, bf16[16,2048]{1,0:T(8,128)(2,1)S(1)}, u32[]{:S(2)}, u32[]{:S(2)}) collective-permute-start(bf16[16,2048]{1,0:T(8,128)(2,1)S(1)} %get-tuple-element.25), channel_id=1, source_target_pairs={{0,16},{8,24},{16,0},{24,8},{1,17},{9,25},{17,1},{25,9},{2,18},{10... | collective-permute-start | bytes 196616 | tf_op jit(solution)/shard_map/ppermute | solution.py:268
  66.5 0.9 convolution_bitcast_fusion
  67.4 0.2 collective-permute-done.10
  67.6 4.2 %collective-permute-done.11 = bf16[16,2048]{1,0:T(8,128)(2,1)S(1)} collective-permute-done((bf16[16,2048]{1,0:T(8,128)(2,1)S(1)}, bf16[16,2048]{1,0:T(8,128)(2,1)S(1)}, u32[]{:S(2)}, u32[]{:S(2)}) %collective-permute-start.11) | collective-permute-done | bytes 65568 | tf_op jit(solution)/shard_map/ppermute | solution.py:268
  71.9 0.8 collective-permute-done.12
  72.6 1.0 multiply_convert_fusion.refs_0_
  73.6 2.0 %collective-permute-start.14 = (bf16[16,2048]{1,0:T(8,128)(2,1)S(1)}, bf16[16,2048]{1,0:T(8,128)(2,1)S(1)}, u32[]{:S(2)}, u32[]{:S(2)}) collective-permute-start(bf16[16,2048]{1,0:T(8,128)(2,1)S(1)} %multiply_convert_fusion.refs_0_), channel_id=1, source_target_pairs={{0,2},{1,3},{2,0},{3,1},{4,6},{5,7},{6,4},{7,5},{8,10},{9,11},{10,... | collective-permute-start | bytes 196616 | tf_op jit(solution)/shard_map/ppermute | solution.py:260
  75.6 0.9 collective-permute-start.16
  76.5 0.7 collective-permute-start.18
  77.2 0.0 collective-permute-start.13
  77.2 0.8 collective-permute-done.14.refs_2_
  78.0 2.2 %collective-permute-done.16.refs_4_ = bf16[16,2048]{1,0:T(8,128)(2,1)S(1)} collective-permute-done((bf16[16,2048]{1,0:T(8,128)(2,1)S(1)}, bf16[16,2048]{1,0:T(8,128)(2,1)S(1)}, u32[]{:S(2)}, u32[]{:S(2)}) %collective-permute-start.16) | collective-permute-done | bytes 65568 | tf_op jit(solution)/shard_map/ppermute | solution.py:260
  80.2 1.4 %collective-permute-done.18.refs_6_ = bf16[16,2048]{1,0:T(8,128)(2,1)S(1)} collective-permute-done((bf16[16,2048]{1,0:T(8,128)(2,1)S(1)}, bf16[16,2048]{1,0:T(8,128)(2,1)S(1)}, u32[]{:S(2)}, u32[]{:S(2)}) %collective-permute-start.18) | collective-permute-done | bytes 65568 | tf_op jit(solution)/shard_map/ppermute | solution.py:260
  81.7 1.2 %collective-permute-done.19.refs_7_ = bf16[16,2048]{1,0:T(8,128)(2,1)S(1)} collective-permute-done((bf16[16,2048]{1,0:T(8,128)(2,1)S(1)}, bf16[16,2048]{1,0:T(8,128)(2,1)S(1)}, u32[]{:S(2)}, u32[]{:S(2)}) %collective-permute-start.19) | collective-permute-done | bytes 65568 | tf_op jit(solution)/shard_map/ppermute | solution.py:262
  82.9 5.8 %copy-done.2 = bf16[128,256,256]{2,1,0:T(8,128)(2,1)S(1)} copy-done((bf16[128,256,256]{2,1,0:T(8,128)(2,1)S(1)}, bf16[128,256,256]{2,1,0:T(8,128)(2,1)}, u32[]{:S(2)}) %copy-start.2) | copy-done | bytes 16777240
  88.7 10.4 %apply.1 = (f32[16,2048]{1,0:T(8,128)S(1)}, bf16[16,2048]{1,0:T(8,128)(2,1)S(1)}, bf16[16,2048]{1,0:T(8,128)(2,1)S(1)}, bf16[16,2048]{1,0:T(8,128)(2,1)S(1)}) custom-call(s32[136]{0:T(256)S(1)} %get-tuple-element.20.pairs, bf16[128,256,256]{2,1,0:T(8,128)(2,1)S(1)} %copy-done.2, bf16[16,2048]{1,0:T(8,128)(2,1)S(1)} %multiply_convert_fusion.refs_0_, ...), custom_call_target="tpu_custom_call" | custom-call | tf_op jit(solution)/shard_map/apply/pallas_call | solution.py:311
  99.1 0.3 collective-permute-start.20
  99.5 2.0 %collective-permute-start.21 = (bf16[16,2048]{1,0:T(8,128)(2,1)S(1)}, bf16[16,2048]{1,0:T(8,128)(2,1)S(1)}, u32[]{:S(2)}, u32[]{:S(2)}) collective-permute-start(bf16[16,2048]{1,0:T(8,128)(2,1)S(1)} %get-tuple-element.29), channel_id=1, source_target_pairs={{0,16},{8,24},{16,0},{24,8},{1,17},{9,25},{17,1},{25,9},{2,18},{10... | collective-permute-start | bytes 196616 | tf_op jit(solution)/shard_map/ppermute | solution.py:268
  101.4 1.5 %collective-permute-start.22 = (bf16[16,2048]{1,0:T(8,128)(2,1)S(1)}, bf16[16,2048]{1,0:T(8,128)(2,1)S(1)}, u32[]{:S(2)}, u32[]{:S(2)}) collective-permute-start(bf16[16,2048]{1,0:T(8,128)(2,1)S(1)} %get-tuple-element.30), channel_id=1, source_target_pairs={{0,8},{8,16},{16,24},{24,0},{1,9},{9,17},{17,25},{25,1},{2,10},{10... | collective-permute-start | bytes 196616 | tf_op jit(solution)/shard_map/ppermute | solution.py:268
  102.9 0.9 collective-permute-done.20
  103.8 4.5 %collective-permute-done.21 = bf16[16,2048]{1,0:T(8,128)(2,1)S(1)} collective-permute-done((bf16[16,2048]{1,0:T(8,128)(2,1)S(1)}, bf16[16,2048]{1,0:T(8,128)(2,1)S(1)}, u32[]{:S(2)}, u32[]{:S(2)}) %collective-permute-start.21) | collective-permute-done | bytes 65568 | tf_op jit(solution)/shard_map/ppermute | solution.py:268
  108.3 0.7 multiply_add_fusion
  (21 shorter events, 0.0 us)
Async XLA Ops:
  0.0 66.5 %copy-start = (f32[8,16]{1,0:T(8,128)S(1)}, f32[8,16]{1,0:T(8,128)}, u32[]{:S(2)}) copy-start(f32[8,16]{1,0:T(8,128)} %param.13) | copy-start | bytes 1540
  0.0 108.3 %copy-start.5 = (f32[16,2048]{1,0:T(8,128)S(1)}, f32[16,2048]{1,0:T(8,128)}, u32[]{:S(2)}) copy-start(f32[16,2048]{1,0:T(8,128)} %emi_ref.1) | copy-start | bytes 393220
  3.3 11.4 %collective-permute-start.4 = (bf16[32,2048]{1,0:T(8,128)(2,1)}, bf16[32,2048]{1,0:T(8,128)(2,1)S(1)}, u32[]{:S(2)}, u32[]{:S(2)}) collective-permute-start(bf16[32,2048]{1,0:T(8,128)(2,1)} %get-tuple-element.19.refs_4_), channel_id=1, source_target_pairs={{0,2},{1,3},{2,0},{3,1},{4,6},{5,7},{6,4},{7,5},{8,10},{9,11},{10,... | collective-permute-start | bytes 393224 | tf_op jit(solution)/shard_map/ppermute | solution.py:260
  6.3 9.0 %collective-permute-start.6 = (bf16[32,2048]{1,0:T(8,128)(2,1)}, bf16[32,2048]{1,0:T(8,128)(2,1)S(1)}, u32[]{:S(2)}, u32[]{:S(2)}) collective-permute-start(bf16[32,2048]{1,0:T(8,128)(2,1)} %get-tuple-element.19.refs_4_), channel_id=1, source_target_pairs={{0,4},{1,5},{2,6},{3,7},{4,0},{5,1},{6,2},{7,3},{8,12},{9,13},{10,... | collective-permute-start | bytes 393224 | tf_op jit(solution)/shard_map/ppermute | solution.py:260
  7.8 7.6 %collective-permute-start.8 = (bf16[32,2048]{1,0:T(8,128)(2,1)}, bf16[32,2048]{1,0:T(8,128)(2,1)S(1)}, u32[]{:S(2)}, u32[]{:S(2)}) collective-permute-start(bf16[32,2048]{1,0:T(8,128)(2,1)} %get-tuple-element.19.refs_4_), channel_id=1, source_target_pairs={{0,6},{1,7},{2,4},{3,5},{4,2},{5,3},{6,0},{7,1},{8,14},{9,15},{10,... | collective-permute-start | bytes 393224 | tf_op jit(solution)/shard_map/ppermute | solution.py:260
  7.8 7.0 %collective-permute-start = (bf16[16,2048]{1,0:T(8,128)(2,1)}, bf16[16,2048]{1,0:T(8,128)(2,1)S(1)}, u32[]{:S(2)}, u32[]{:S(2)}) collective-permute-start(bf16[16,2048]{1,0:T(8,128)(2,1)} %get-tuple-element.18.refs_0_), channel_id=1, source_target_pairs={{0,8},{8,16},{16,24},{24,0},{1,9},{9,17},{17,25},{25,1},{2,10},{10... | collective-permute-start | bytes 196616 | tf_op jit(solution)/shard_map/ppermute | solution.py:255
  9.8 5.9 %collective-permute-start.1 = (bf16[16,2048]{1,0:T(8,128)(2,1)}, bf16[16,2048]{1,0:T(8,128)(2,1)S(1)}, u32[]{:S(2)}, u32[]{:S(2)}) collective-permute-start(bf16[16,2048]{1,0:T(8,128)(2,1)} %get-tuple-element.18.refs_0_), channel_id=1, source_target_pairs={{0,16},{8,24},{16,0},{24,8},{1,17},{9,25},{17,1},{25,9},{2,18},{10... | collective-permute-start | bytes 196616 | tf_op jit(solution)/shard_map/ppermute | solution.py:255
  14.7 5.8 %collective-permute-start.3 = (bf16[32,2048]{1,0:T(8,128)(2,1)}, bf16[32,2048]{1,0:T(8,128)(2,1)S(1)}, u32[]{:S(2)}, u32[]{:S(2)}) collective-permute-start(bf16[32,2048]{1,0:T(8,128)(2,1)} %get-tuple-element.19.refs_4_), channel_id=1, source_target_pairs={{0,1},{1,0},{2,3},{3,2},{4,5},{5,4},{6,7},{7,6},{8,9},{9,8},{10,11... | collective-permute-start | bytes 393224 | tf_op jit(solution)/shard_map/ppermute | solution.py:262
  14.8 5.8 %collective-permute-start.5 = (bf16[32,2048]{1,0:T(8,128)(2,1)S(1)}, bf16[32,2048]{1,0:T(8,128)(2,1)S(1)}, u32[]{:S(2)}, u32[]{:S(2)}) collective-permute-start(bf16[32,2048]{1,0:T(8,128)(2,1)S(1)} %collective-permute-done.4.refs_6_), channel_id=1, source_target_pairs={{0,1},{1,0},{2,3},{3,2},{4,5},{5,4},{6,7},{7,6},{8,9},{9,8},{10,11... | collective-permute-start | bytes 393224 | tf_op jit(solution)/shard_map/ppermute | solution.py:262
  15.3 5.3 %collective-permute-start.7 = (bf16[32,2048]{1,0:T(8,128)(2,1)S(1)}, bf16[32,2048]{1,0:T(8,128)(2,1)S(1)}, u32[]{:S(2)}, u32[]{:S(2)}) collective-permute-start(bf16[32,2048]{1,0:T(8,128)(2,1)S(1)} %collective-permute-done.6.refs_8_), channel_id=1, source_target_pairs={{0,1},{1,0},{2,3},{3,2},{4,5},{5,4},{6,7},{7,6},{8,9},{9,8},{10,11... | collective-permute-start | bytes 393224 | tf_op jit(solution)/shard_map/ppermute | solution.py:262
  15.3 5.3 %collective-permute-start.9 = (bf16[32,2048]{1,0:T(8,128)(2,1)S(1)}, bf16[32,2048]{1,0:T(8,128)(2,1)S(1)}, u32[]{:S(2)}, u32[]{:S(2)}) collective-permute-start(bf16[32,2048]{1,0:T(8,128)(2,1)S(1)} %collective-permute-done.8.refs_10_), channel_id=1, source_target_pairs={{0,1},{1,0},{2,3},{3,2},{4,5},{5,4},{6,7},{7,6},{8,9},{9,8},{10,11... | collective-permute-start | bytes 393224 | tf_op jit(solution)/shard_map/ppermute | solution.py:262
  15.8 4.8 %collective-permute-start.2 = (bf16[16,2048]{1,0:T(8,128)(2,1)}, bf16[16,2048]{1,0:T(8,128)(2,1)S(1)}, u32[]{:S(2)}, u32[]{:S(2)}) collective-permute-start(bf16[16,2048]{1,0:T(8,128)(2,1)} %get-tuple-element.18.refs_0_), channel_id=1, source_target_pairs={{0,24},{8,0},{16,8},{24,16},{1,25},{9,1},{17,9},{25,17},{2,26},{10... | collective-permute-start | bytes 196616 | tf_op jit(solution)/shard_map/ppermute | solution.py:255
  20.6 0.9 copy-start.3
  21.5 0.8 copy-start.4
  56.1 5.7 %copy-start.1 = (bf16[128,256,256]{2,1,0:T(8,128)(2,1)}, bf16[128,256,256]{2,1,0:T(8,128)(2,1)S(1)}, u32[]{:S(2)}) copy-start(bf16[128,256,256]{2,1,0:T(8,128)(2,1)S(1)} %get-tuple-element.21.tiles_ref) | copy-start | bytes 50331652
  61.9 5.8 %collective-permute-start.10 = (bf16[16,2048]{1,0:T(8,128)(2,1)S(1)}, bf16[16,2048]{1,0:T(8,128)(2,1)S(1)}, u32[]{:S(2)}, u32[]{:S(2)}) collective-permute-start(bf16[16,2048]{1,0:T(8,128)(2,1)S(1)} %get-tuple-element.24), channel_id=1, source_target_pairs={{0,24},{8,0},{16,8},{24,16},{1,25},{9,1},{17,9},{25,17},{2,26},{10... | collective-permute-start | bytes 196616 | tf_op jit(solution)/shard_map/ppermute | solution.py:268
  63.5 8.4 %collective-permute-start.11 = (bf16[16,2048]{1,0:T(8,128)(2,1)S(1)}, bf16[16,2048]{1,0:T(8,128)(2,1)S(1)}, u32[]{:S(2)}, u32[]{:S(2)}) collective-permute-start(bf16[16,2048]{1,0:T(8,128)(2,1)S(1)} %get-tuple-element.25), channel_id=1, source_target_pairs={{0,16},{8,24},{16,0},{24,8},{1,17},{9,25},{17,1},{25,9},{2,18},{10... | collective-permute-start | bytes 196616 | tf_op jit(solution)/shard_map/ppermute | solution.py:268
  66.5 6.2 %collective-permute-start.12 = (bf16[16,2048]{1,0:T(8,128)(2,1)S(1)}, bf16[16,2048]{1,0:T(8,128)(2,1)S(1)}, u32[]{:S(2)}, u32[]{:S(2)}) collective-permute-start(bf16[16,2048]{1,0:T(8,128)(2,1)S(1)} %get-tuple-element.26), channel_id=1, source_target_pairs={{0,8},{8,16},{16,24},{24,0},{1,9},{9,17},{17,25},{25,1},{2,10},{10... | collective-permute-start | bytes 196616 | tf_op jit(solution)/shard_map/ppermute | solution.py:268
  73.6 4.4 %collective-permute-start.14 = (bf16[16,2048]{1,0:T(8,128)(2,1)S(1)}, bf16[16,2048]{1,0:T(8,128)(2,1)S(1)}, u32[]{:S(2)}, u32[]{:S(2)}) collective-permute-start(bf16[16,2048]{1,0:T(8,128)(2,1)S(1)} %multiply_convert_fusion.refs_0_), channel_id=1, source_target_pairs={{0,2},{1,3},{2,0},{3,1},{4,6},{5,7},{6,4},{7,5},{8,10},{9,11},{10,... | collective-permute-start | bytes 196616 | tf_op jit(solution)/shard_map/ppermute | solution.py:260
  75.6 4.6 %collective-permute-start.16 = (bf16[16,2048]{1,0:T(8,128)(2,1)S(1)}, bf16[16,2048]{1,0:T(8,128)(2,1)S(1)}, u32[]{:S(2)}, u32[]{:S(2)}) collective-permute-start(bf16[16,2048]{1,0:T(8,128)(2,1)S(1)} %multiply_convert_fusion.refs_0_), channel_id=1, source_target_pairs={{0,4},{1,5},{2,6},{3,7},{4,0},{5,1},{6,2},{7,3},{8,12},{9,13},{10,... | collective-permute-start | bytes 196616 | tf_op jit(solution)/shard_map/ppermute | solution.py:260
  76.5 5.2 %collective-permute-start.18 = (bf16[16,2048]{1,0:T(8,128)(2,1)S(1)}, bf16[16,2048]{1,0:T(8,128)(2,1)S(1)}, u32[]{:S(2)}, u32[]{:S(2)}) collective-permute-start(bf16[16,2048]{1,0:T(8,128)(2,1)S(1)} %multiply_convert_fusion.refs_0_), channel_id=1, source_target_pairs={{0,6},{1,7},{2,4},{3,5},{4,2},{5,3},{6,0},{7,1},{8,14},{9,15},{10,... | collective-permute-start | bytes 196616 | tf_op jit(solution)/shard_map/ppermute | solution.py:260
  77.2 4.5 %collective-permute-start.13 = (bf16[16,2048]{1,0:T(8,128)(2,1)S(1)}, bf16[16,2048]{1,0:T(8,128)(2,1)S(1)}, u32[]{:S(2)}, u32[]{:S(2)}) collective-permute-start(bf16[16,2048]{1,0:T(8,128)(2,1)S(1)} %multiply_convert_fusion.refs_0_), channel_id=1, source_target_pairs={{0,1},{1,0},{2,3},{3,2},{4,5},{5,4},{6,7},{7,6},{8,9},{9,8},{10,11... | collective-permute-start | bytes 196616 | tf_op jit(solution)/shard_map/ppermute | solution.py:262
  78.0 3.7 %collective-permute-start.15 = (bf16[16,2048]{1,0:T(8,128)(2,1)S(1)}, bf16[16,2048]{1,0:T(8,128)(2,1)S(1)}, u32[]{:S(2)}, u32[]{:S(2)}) collective-permute-start(bf16[16,2048]{1,0:T(8,128)(2,1)S(1)} %collective-permute-done.14.refs_2_), channel_id=1, source_target_pairs={{0,1},{1,0},{2,3},{3,2},{4,5},{5,4},{6,7},{7,6},{8,9},{9,8},{10,11... | collective-permute-start | bytes 196616 | tf_op jit(solution)/shard_map/ppermute | solution.py:262
  80.2 1.5 %collective-permute-start.17 = (bf16[16,2048]{1,0:T(8,128)(2,1)S(1)}, bf16[16,2048]{1,0:T(8,128)(2,1)S(1)}, u32[]{:S(2)}, u32[]{:S(2)}) collective-permute-start(bf16[16,2048]{1,0:T(8,128)(2,1)S(1)} %collective-permute-done.16.refs_4_), channel_id=1, source_target_pairs={{0,1},{1,0},{2,3},{3,2},{4,5},{5,4},{6,7},{7,6},{8,9},{9,8},{10,11... | collective-permute-start | bytes 196616 | tf_op jit(solution)/shard_map/ppermute | solution.py:262
  81.7 1.3 %collective-permute-start.19 = (bf16[16,2048]{1,0:T(8,128)(2,1)S(1)}, bf16[16,2048]{1,0:T(8,128)(2,1)S(1)}, u32[]{:S(2)}, u32[]{:S(2)}) collective-permute-start(bf16[16,2048]{1,0:T(8,128)(2,1)S(1)} %collective-permute-done.18.refs_6_), channel_id=1, source_target_pairs={{0,1},{1,0},{2,3},{3,2},{4,5},{5,4},{6,7},{7,6},{8,9},{9,8},{10,11... | collective-permute-start | bytes 196616 | tf_op jit(solution)/shard_map/ppermute | solution.py:262
  82.9 5.8 %copy-start.2 = (bf16[128,256,256]{2,1,0:T(8,128)(2,1)S(1)}, bf16[128,256,256]{2,1,0:T(8,128)(2,1)}, u32[]{:S(2)}) copy-start(bf16[128,256,256]{2,1,0:T(8,128)(2,1)} %copy-done.1) | copy-start | bytes 50331652
  99.1 4.7 %collective-permute-start.20 = (bf16[16,2048]{1,0:T(8,128)(2,1)S(1)}, bf16[16,2048]{1,0:T(8,128)(2,1)S(1)}, u32[]{:S(2)}, u32[]{:S(2)}) collective-permute-start(bf16[16,2048]{1,0:T(8,128)(2,1)S(1)} %get-tuple-element.28), channel_id=1, source_target_pairs={{0,24},{8,0},{16,8},{24,16},{1,25},{9,1},{17,9},{25,17},{2,26},{10... | collective-permute-start | bytes 196616 | tf_op jit(solution)/shard_map/ppermute | solution.py:268
  99.5 8.9 %collective-permute-start.21 = (bf16[16,2048]{1,0:T(8,128)(2,1)S(1)}, bf16[16,2048]{1,0:T(8,128)(2,1)S(1)}, u32[]{:S(2)}, u32[]{:S(2)}) collective-permute-start(bf16[16,2048]{1,0:T(8,128)(2,1)S(1)} %get-tuple-element.29), channel_id=1, source_target_pairs={{0,16},{8,24},{16,0},{24,8},{1,17},{9,25},{17,1},{25,9},{2,18},{10... | collective-permute-start | bytes 196616 | tf_op jit(solution)/shard_map/ppermute | solution.py:268
  101.4 6.9 %collective-permute-start.22 = (bf16[16,2048]{1,0:T(8,128)(2,1)S(1)}, bf16[16,2048]{1,0:T(8,128)(2,1)S(1)}, u32[]{:S(2)}, u32[]{:S(2)}) collective-permute-start(bf16[16,2048]{1,0:T(8,128)(2,1)S(1)} %get-tuple-element.30), channel_id=1, source_target_pairs={{0,8},{8,16},{16,24},{24,0},{1,9},{9,17},{17,25},{25,1},{2,10},{10... | collective-permute-start | bytes 196616 | tf_op jit(solution)/shard_map/ppermute | solution.py:268

commit v2 on v1

--- a/solution.py
+++ b/solution.py
@@ -12,7 +12,11 @@
 BLK = 256
 CAP = 2
 GEO = 16
+LANES = 128
 KDIM = 48
+FORM_UNROLL = 4
+APPLY_UNROLL = 8
+SPARE = 8
 KEEP_BYTES = 24 * 2**20
 BF16 = jnp.bfloat16
 F32 = jnp.float32
@@ -45,8 +49,10 @@
     rows[9:12, :] = n2
     rows[12:13, :] = a1
     rows[13:14, :] = a2
-    rows[14:15, :] = slot_ref[...]
-    rows[15:16, :] = jnp.zeros_like(area)
+    rows[14:16, :] = jnp.zeros((2, area.shape[1]), F32)
+    peers = slot_ref.shape[-1]
+    for t in range(2 * CAP):
+        rows[14:15, t * LANES : t * LANES + peers] = slot_ref[t // 2, t % 2 : t % 2 + 1, :].astype(F32)
     geo = rows[...].astype(BF16)
     geo_ref[...] = geo
     pay_ref[0:GEO, :] = geo
@@ -127,18 +133,21 @@
         s = e // ny
         m = e % ny
         zs = lax.rem(z - s + nz, nz)
-        own = (z * ny + jnp.bitwise_xor(k, m)) * (2 * CAP)
-        served = (zs * ny + k) * (2 * CAP)
+        own = z * ny + jnp.bitwise_xor(k, m)
+        served = zs * ny + k
         for t in range(CAP):
-            row, col = slots[s, own + 2 * t], slots[s, own + 2 * t + 1]
+            row, col = slots[s, 2 * t * LANES + own], slots[s, (2 * t + 1) * LANES + own]
             pairs[count] = (s * nb + row) * 4096 + m * nb + col
             count = count + (row >= 0).astype(jnp.int32)
-            col, row = slots[nz + m, served + 2 * t], slots[nz + m, served + 2 * t + 1]
+            col, row = slots[nz + m, 2 * t * LANES + served], slots[nz + m, (2 * t + 1) * LANES + served]
             pairs[count] = (s * nb + row) * 4096 + m * nb + col
             count = count + (row >= 0).astype(jnp.int32)
         return count
 
-    pairs[most + 1] = lax.fori_loop(0, nz * ny, peer, jnp.int32(0))
+    count = lax.fori_loop(0, nz * ny, peer, jnp.int32(0))
+    for t in range(SPARE):
+        pairs[count + t] = nz * nb * 4096
+    pairs[most + SPARE] = count
 
 
 def put_out(nz, nb, acc, out_refs):
@@ -185,26 +194,50 @@
     copy.wait()
     list_pairs(nz, ny, nb, place_ref, slots, pairs)
 
-    def one(t, carry):
+    count = pairs[most + SPARE]
+
+    def tile_of(t):
         code = pairs[t]
-        rb = code // 4096
-        cb = code % 4096
-        parts = []
-        for j in range(0, BLK, 64):
-            left = col_feat[cb, j : j + 64, :]
-            f, s, q, r = (
-                jnp.dot(left, row_feat[rb, v], preferred_element_type=F32) for v in range(4)
-            )
-            top = jnp.maximum(f, 0.0) * jnp.maximum(s, 0.0)
-            parts.append((top * pl.reciprocal(q * r, approx=True)).astype(BF16))
-        tile = jnp.concatenate(parts, axis=0)
-        if keep:
-            tiles_ref[t] = tile
-        acc[rb] += jnp.dot(flux[cb], tile, preferred_element_type=F32)
+        rb = jnp.minimum(code // 4096, nz * nb - 1)
+        left = col_feat[code % 4096]
+        f, s, q, r = (
+            jnp.dot(left, row_feat[rb, v], preferred_element_type=F32) for v in range(4)
+        )
+        top = jnp.maximum(f, 0.0) * jnp.maximum(s, 0.0)
+        return (top * pltpu.reciprocal(q * r, approx=True)).astype(BF16)
+
+    if keep:
+
+        def some(t, carry):
+            for u in range(FORM_UNROLL):
+                tiles_ref[t * FORM_UNROLL + u] = tile_of(t * FORM_UNROLL + u)
+            return carry
+
+        lax.fori_loop(0, (count + FORM_UNROLL - 1) // FORM_UNROLL, some, 0)
+        apply_tiles(count, pairs, tiles_ref, flux, acc)
+    else:
+
+        def one(t, carry):
+            code = pairs[t]
+            acc[code // 4096] += jnp.dot(flux[code % 4096], tile_of(t), preferred_element_type=F32)
+            return carry
+
+        lax.fori_loop(0, count, one, 0)
+    put_out(nz, nb, acc, outs)
+
+
+def apply_tiles(count, pairs, tiles_ref, flux, acc):
+    def some(t, carry):
+        sums = []
+        for u in range(APPLY_UNROLL):
+            code = pairs[t * APPLY_UNROLL + u]
+            tile = tiles_ref[t * APPLY_UNROLL + u]
+            sums.append((code // 4096, jnp.dot(flux[code % 4096], tile, preferred_element_type=F32)))
+        for rb, total in sums:
+            acc[rb] += total
         return carry
 
-    lax.fori_loop(0, pairs[most + 1], one, 0)
-    put_out(nz, nb, acc, outs)
+    lax.fori_loop(0, (count + APPLY_UNROLL - 1) // APPLY_UNROLL, some, 0)
 
 
 def apply_kernel(nz, ny, nb, pairs, tiles_ref, *refs):
@@ -216,15 +249,7 @@
         for b in range(nb):
             flux[m * nb + b] = fluxes[m][:, b * BLK : (b + 1) * BLK]
     acc[...] = jnp.zeros(acc.shape, F32)
-
-    def one(t, carry):
-        code = pairs[t]
-        rb = code // 4096
-        cb = code % 4096
-        acc[rb] += jnp.dot(flux[cb], tiles_ref[t], preferred_element_type=F32)
-        return carry
-
-    lax.fori_loop(0, pairs[most + 1], one, 0)
+    apply_tiles(pairs[most + SPARE], pairs, tiles_ref, flux, acc)
     put_out(nz, nb, acc, outs)
 
 
@@ -232,24 +257,23 @@
     patches = positions.shape[1]
     nb = patches // BLK
     most = nz * ny * 2 * CAP
-    width = most if nz * ny * 2 * CAP == pair_slots.size else pair_slots.size
-    keep = most * BLK * BLK * 2 <= KEEP_BYTES
-    params = pltpu.CompilerParams(vmem_limit_bytes=(30 if keep else 56) * 2**20)
+    width = 2 * CAP * LANES
+    keep = (most + SPARE) * BLK * BLK * 2 <= KEEP_BYTES
+    params = [pltpu.CompilerParams(vmem_limit_bytes=n * 2**20) for n in ((14, 4) if keep else (56, 4))]
     place = jnp.stack([lax.axis_index("gx"), lax.axis_index("gy")]).astype(jnp.int32)
-    slot_row = pair_slots.reshape(1, -1).astype(F32)
-    slot_row = jnp.pad(slot_row, ((0, 0), (0, patches - slot_row.shape[1])))
+    slot_rows = jnp.transpose(pair_slots[0], (1, 2, 0))
     payload, geo, area = pl.pallas_call(
         pack_kernel,
         out_shape=(
-            jax.ShapeDtypeStruct((GEO + BANDS, patches), BF16),
-            jax.ShapeDtypeStruct((GEO, patches), BF16),
+            pltpu.VMEM((GEO + BANDS, patches), BF16),
+            pltpu.VMEM((GEO, patches), BF16),
             jax.ShapeDtypeStruct((1, patches), F32),
         ),
         in_specs=[VMEM()] * 4 + [SMEM(), VMEM()],
         out_specs=(VMEM(),) * 3,
         scratch_shapes=[pltpu.VMEM((GEO, patches), F32)],
         name="pack",
-    )(positions, normals, emission, area_level.reshape(1, patches), area_table, slot_row)
+    )(positions, normals, emission, area_level.reshape(1, patches), area_table, slot_rows)
 
     def along(x):
         return [lax.ppermute(x, "gx", [(i, (i + s) % nz) for i in range(nz)]) for s in range(1, nz)]
@@ -281,8 +305,8 @@
         specs = [VMEM()] * nz
         if keep:
             outs += [
-                pltpu.VMEM((most, BLK, BLK), BF16),
-                jax.ShapeDtypeStruct((most + 8,), jnp.int32),
+                pltpu.VMEM((most + SPARE, BLK, BLK), BF16),
+                jax.ShapeDtypeStruct((most + SPARE + 1,), jnp.int32),
             ]
             specs += [VMEM(), SMEM()]
         scratch = [
@@ -290,20 +314,20 @@
             pltpu.VMEM((nz * nb, 4, KDIM, BLK), BF16),
             pltpu.VMEM((ny * nb, BLK, KDIM), BF16),
             pltpu.VMEM((ny * nb, BANDS, BLK), BF16),
-            pltpu.VMEM((nz * nb, BANDS, BLK), F32),
+            pltpu.VMEM((nz * nb + 1, BANDS, BLK), F32),
             pltpu.VMEM((-(-(nz + ny) // 8) * 8, width), jnp.int32),
             pltpu.SMEM((-(-(nz + ny) // 8) * 8, width), jnp.int32),
             pltpu.SemaphoreType.DMA,
         ]
         if not keep:
-            scratch += [pltpu.SMEM((most + 8,), jnp.int32)]
+            scratch += [pltpu.SMEM((most + SPARE + 1,), jnp.int32)]
         return pl.pallas_call(
             functools.partial(form_kernel, nz, ny, nb, keep, fresh),
             out_shape=tuple(outs),
             in_specs=[SMEM()] + [VMEM()] * (nz + ny + (ny if fresh else 0)),
             out_specs=tuple(specs),
             scratch_shapes=scratch,
-            compiler_params=params,
+            compiler_params=params[0],
             name="form",
         )(place, *rows, *cols, *(fluxes or []))
 
@@ -315,9 +339,9 @@
             out_specs=(VMEM(),) * nz,
             scratch_shapes=[
                 pltpu.VMEM((ny * nb, BANDS, BLK), BF16),
-                pltpu.VMEM((nz * nb, BANDS, BLK), F32),
+                pltpu.VMEM((nz * nb + 1, BANDS, BLK), F32),
             ],
-            compiler_params=params,
+            compiler_params=params[1],
             name="apply",
         )(pairs, tiles, *fluxes)
 

time: 110 us -> 73.6 us (0.67)
  Pallas kernels: 45.9 us -> 23.3 us
  local copies, waits for them, and re-layouts: 14.1 us -> 0.01 us
  starting transfers between devices: 24.6 us -> 27.7 us
  waiting for transfers between devices: 20.9 us -> 19.4 us
    pallas_call x1, Pallas kernels: 33.8 us -> 19.3 us  [form(): pl.pallas_call(functools.partial(form_kernel, nz, ny, nb, keep, fresh), o...]
    unnamed x12 -> x4, local copies, waits for them, and re-layouts: 13.2 us -> 0.01 us
    pallas_call x1, Pallas kernels: 10.4 us -> 2.43 us  [apply(): pl.pallas_call(functools.partial(apply_kernel, nz, ny, nb), out_shape=tup...]
    ppermute x6, starting transfers between devices: 8.01 us -> 10.4 us  [plane(): got[m] = lax.ppermute(x, 'gy', [(i, i ^ m) for i in range(ny)])]
  transfers between devices with their start and end apart: 23 -> 23, of which waited for: 11 -> 10; matrix products, arithmetic and copies ran while one was open for 1% -> 1% of each run, Pallas kernels for 0% -> 0%
where the time goes in v2:
time: 73.6 us; the launch traced here: 73.1 us
  starting transfers between devices  27.7 us (38%)
  Pallas kernels  23.3 us (32%)
  waiting for transfers between devices  19.4 us (26%)
  other arithmetic  1.73 us (2%)
  matrix products  0.95 us (1%)
    pallas_call x1, Pallas kernels, form(): pl.pallas_call(functools.partial(form_kernel, nz, ny, nb, keep, fresh), o...  19.3 us
    ppermute x6, waiting for transfers between devices, home(): back = lax.ppermute(parts[s], 'gx', [(i, (i - s) % nz) for i in range(nz)])  10.5 us
    ppermute x6, starting transfers between devices, plane(): got[m] = lax.ppermute(x, 'gy', [(i, i ^ m) for i in range(ny)])  10.4 us
    ppermute x6, starting transfers between devices, home(): back = lax.ppermute(parts[s], 'gx', [(i, (i - s) % nz) for i in range(nz)])  8.93 us
    ppermute x3, starting transfers between devices, along(): lax.ppermute(x, 'gx', [(i, (i + s) % nz) for i in range(nz)])  7.23 us
    ppermute x3, waiting for transfers between devices, along(): lax.ppermute(x, 'gx', [(i, (i + s) % nz) for i in range(nz)])  3.94 us
    ppermute x6, waiting for transfers between devices, plane(): got[m] = lax.ppermute(x, 'gy', [(i, i ^ m) for i in range(ny)])  3.64 us
    pallas_call x1, Pallas kernels, apply(): pl.pallas_call(functools.partial(apply_kernel, nz, ny, nb), out_shape=tup...  2.43 us
  transfers between devices with their start and end apart: 23, of which 10 were waited for; matrix products, arithmetic and copies ran while one was open for 1% of the time, Pallas kernels for 0%

profile of v2, /device:TPU:0, one launch (start us, length us, event | category | flops | bytes accessed | tf_op | source)
XLA Modules:
  0.0 73.1 jit_solution(2562716211870489147)
XLA Ops:
  0.0 1.6 %pack.1 = (bf16[32,2048]{1,0:T(8,128)(2,1)S(1)}, bf16[16,2048]{1,0:T(8,128)(2,1)S(1)}, f32[1,2048]{1,0:T(1,128)}) custom-call(f32[3,2048]{1,0:T(4,128)} %pos_ref.1, f32[3,2048]{1,0:T(4,128)} %nrm_ref.1, f32[16,2048]{1,0:T(8,128)} %emi_ref.1, s32[1,2048]{1,0:T(1,128)} %bitcast.10, f32[8]{0:T(128)} %table_ref.1, s32[2,2,32]{2,1,0:T(2,128)} %bitcast.12), custom_call_target="tpu_custom_call" | custom-call | tf_op jit(solution)/shard_map/pack/pallas_call | solution.py:265
  1.6 2.9 %collective-permute-start.4 = (bf16[32,2048]{1,0:T(8,128)(2,1)S(1)}, bf16[32,2048]{1,0:T(8,128)(2,1)S(1)}, u32[]{:S(2)}, u32[]{:S(2)}) collective-permute-start(bf16[32,2048]{1,0:T(8,128)(2,1)S(1)} %get-tuple-element.19.refs_4_), channel_id=1, source_target_pairs={{0,2},{1,3},{2,0},{3,1},{4,6},{5,7},{6,4},{7,5},{8,10},{9,11},{10,... | collective-permute-start | bytes 393224 | tf_op jit(solution)/shard_map/ppermute | solution.py:284
  4.6 1.5 %collective-permute-start.6 = (bf16[32,2048]{1,0:T(8,128)(2,1)S(1)}, bf16[32,2048]{1,0:T(8,128)(2,1)S(1)}, u32[]{:S(2)}, u32[]{:S(2)}) collective-permute-start(bf16[32,2048]{1,0:T(8,128)(2,1)S(1)} %get-tuple-element.19.refs_4_), channel_id=1, source_target_pairs={{0,4},{1,5},{2,6},{3,7},{4,0},{5,1},{6,2},{7,3},{8,12},{9,13},{10,... | collective-permute-start | bytes 393224 | tf_op jit(solution)/shard_map/ppermute | solution.py:284
  6.1 0.0 collective-permute-start.8
  6.1 2.1 %collective-permute-start = (bf16[16,2048]{1,0:T(8,128)(2,1)S(1)}, bf16[16,2048]{1,0:T(8,128)(2,1)S(1)}, u32[]{:S(2)}, u32[]{:S(2)}) collective-permute-start(bf16[16,2048]{1,0:T(8,128)(2,1)S(1)} %get-tuple-element.18.refs_0_), channel_id=1, source_target_pairs={{0,8},{8,16},{16,24},{24,0},{1,9},{9,17},{17,25},{25,1},{2,10},{10... | collective-permute-start | bytes 196616 | tf_op jit(solution)/shard_map/ppermute | solution.py:279
  8.1 2.6 %collective-permute-start.1 = (bf16[16,2048]{1,0:T(8,128)(2,1)S(1)}, bf16[16,2048]{1,0:T(8,128)(2,1)S(1)}, u32[]{:S(2)}, u32[]{:S(2)}) collective-permute-start(bf16[16,2048]{1,0:T(8,128)(2,1)S(1)} %get-tuple-element.18.refs_0_), channel_id=1, source_target_pairs={{0,16},{8,24},{16,0},{24,8},{1,17},{9,25},{17,1},{25,9},{2,18},{10... | collective-permute-start | bytes 196616 | tf_op jit(solution)/shard_map/ppermute | solution.py:279
  10.7 2.1 %collective-permute-done.refs_1_ = bf16[16,2048]{1,0:T(8,128)(2,1)S(1)} collective-permute-done((bf16[16,2048]{1,0:T(8,128)(2,1)S(1)}, bf16[16,2048]{1,0:T(8,128)(2,1)S(1)}, u32[]{:S(2)}, u32[]{:S(2)}) %collective-permute-start) | collective-permute-done | bytes 65568 | tf_op jit(solution)/shard_map/ppermute | solution.py:279
  12.8 0.0 collective-permute-start.3
  12.8 0.0 collective-permute-done.4.refs_6_
  12.8 0.5 collective-permute-start.5
  13.4 0.0 collective-permute-done.6.refs_8_
  13.4 0.1 collective-permute-start.7
  13.4 0.0 collective-permute-done.8.refs_10_
  13.4 0.4 collective-permute-start.9
  13.9 0.0 collective-permute-done.1.refs_2_
  13.9 2.6 %collective-permute-start.2 = (bf16[16,2048]{1,0:T(8,128)(2,1)S(1)}, bf16[16,2048]{1,0:T(8,128)(2,1)S(1)}, u32[]{:S(2)}, u32[]{:S(2)}) collective-permute-start(bf16[16,2048]{1,0:T(8,128)(2,1)S(1)} %get-tuple-element.18.refs_0_), channel_id=1, source_target_pairs={{0,24},{8,0},{16,8},{24,16},{1,25},{9,1},{17,9},{25,17},{2,26},{10... | collective-permute-start | bytes 196616 | tf_op jit(solution)/shard_map/ppermute | solution.py:279
  16.5 0.1 pad_add_fusion.place_ref
  16.5 1.8 %collective-permute-done.2.refs_3_ = bf16[16,2048]{1,0:T(8,128)(2,1)S(1)} collective-permute-done((bf16[16,2048]{1,0:T(8,128)(2,1)S(1)}, bf16[16,2048]{1,0:T(8,128)(2,1)S(1)}, u32[]{:S(2)}, u32[]{:S(2)}) %collective-permute-start.2) | collective-permute-done | bytes 65568 | tf_op jit(solution)/shard_map/ppermute | solution.py:279
  18.4 0.0 collective-permute-done.3.refs_5_
  18.4 0.0 collective-permute-done.5.refs_7_
  18.4 0.0 collective-permute-done.9.refs_11_
  18.4 19.3 %form.1 = (f32[16,2048]{1,0:T(8,128)S(1)}, bf16[16,2048]{1,0:T(8,128)(2,1)S(1)}, bf16[16,2048]{1,0:T(8,128)(2,1)S(1)}, bf16[16,2048]{1,0:T(8,128)(2,1)S(1)}, bf1...) custom-call(s32[2]{0:T(128)S(1)} %pad_add_fusion.place_ref, bf16[16,2048]{1,0:T(8,128)(2,1)S(1)} %get-tuple-element.18.refs_0_, ...), custom_call_target="tpu_custom_call" | custom-call | tf_op jit(solution)/shard_map/form/pallas_call | solution.py:324
  37.7 5.1 %collective-permute-start.10 = (bf16[16,2048]{1,0:T(8,128)(2,1)S(1)}, bf16[16,2048]{1,0:T(8,128)(2,1)S(1)}, u32[]{:S(2)}, u32[]{:S(2)}) collective-permute-start(bf16[16,2048]{1,0:T(8,128)(2,1)S(1)} %get-tuple-element.24), channel_id=1, source_target_pairs={{0,24},{8,0},{16,8},{24,16},{1,25},{9,1},{17,9},{25,17},{2,26},{10... | collective-permute-start | bytes 196616 | tf_op jit(solution)/shard_map/ppermute | solution.py:292
  42.7 0.0 collective-permute-start.11
  42.7 0.6 collective-permute-start.12
  43.4 0.9 %convolution_bitcast_fusion = f32[16,2048]{1,0:T(8,128)S(1)} fusion(f32[8,16]{1,0:T(8,128)S(1)} %copy-done, s32[2048]{0:T(1024)} %param.11), kind=kOutput, calls=%fused_computation | convolution fusion | flops 3162112 | bytes 139776 | tf_op jit(solution)/shard_map/dot_general | solution.py:351
  44.3 0.9 %collective-permute-done.10 = bf16[16,2048]{1,0:T(8,128)(2,1)S(1)} collective-permute-done((bf16[16,2048]{1,0:T(8,128)(2,1)S(1)}, bf16[16,2048]{1,0:T(8,128)(2,1)S(1)}, u32[]{:S(2)}, u32[]{:S(2)}) %collective-permute-start.10) | collective-permute-done | bytes 65568 | tf_op jit(solution)/shard_map/ppermute | solution.py:292
  45.2 3.9 %collective-permute-done.11 = bf16[16,2048]{1,0:T(8,128)(2,1)S(1)} collective-permute-done((bf16[16,2048]{1,0:T(8,128)(2,1)S(1)}, bf16[16,2048]{1,0:T(8,128)(2,1)S(1)}, u32[]{:S(2)}, u32[]{:S(2)}) %collective-permute-start.11) | collective-permute-done | bytes 65568 | tf_op jit(solution)/shard_map/ppermute | solution.py:292
  49.2 1.0 %multiply_convert_fusion.refs_0_ = bf16[16,2048]{1,0:T(8,128)(2,1)S(1)} fusion(f32[16,2048]{1,0:T(8,128)} %emi_ref.1, f32[16,2048]{1,0:T(8,128)S(1)} %convolution_bitcast_fusion, bf16[16,2048]{1,0:T(8,128)(2,1)S(1)} %collective-permute-done.12, bf16[16,2048]{1,0:T(8,128)(2,1)S(1)} %collective-permute-done.11, f32[16,2048]{1,0:T(8,128)S(1)} %get-tuple-element.23, ...), kind=kLoop, calls=%fused_computation.2 | loop fusion | flops 327680 | bytes 663552 | tf_op jit(solution)/shard_map/convert_element_type | solution.py:355
  50.1 4.1 %collective-permute-start.14 = (bf16[16,2048]{1,0:T(8,128)(2,1)S(1)}, bf16[16,2048]{1,0:T(8,128)(2,1)S(1)}, u32[]{:S(2)}, u32[]{:S(2)}) collective-permute-start(bf16[16,2048]{1,0:T(8,128)(2,1)S(1)} %multiply_convert_fusion.refs_0_), channel_id=1, source_target_pairs={{0,2},{1,3},{2,0},{3,1},{4,6},{5,7},{6,4},{7,5},{8,10},{9,11},{10,... | collective-permute-start | bytes 196616 | tf_op jit(solution)/shard_map/ppermute | solution.py:284
  54.2 0.5 collective-permute-start.16
  54.7 1.4 %collective-permute-start.18 = (bf16[16,2048]{1,0:T(8,128)(2,1)S(1)}, bf16[16,2048]{1,0:T(8,128)(2,1)S(1)}, u32[]{:S(2)}, u32[]{:S(2)}) collective-permute-start(bf16[16,2048]{1,0:T(8,128)(2,1)S(1)} %multiply_convert_fusion.refs_0_), channel_id=1, source_target_pairs={{0,6},{1,7},{2,4},{3,5},{4,2},{5,3},{6,0},{7,1},{8,14},{9,15},{10,... | collective-permute-start | bytes 196616 | tf_op jit(solution)/shard_map/ppermute | solution.py:284
  56.1 0.0 collective-permute-start.13
  56.1 0.4 collective-permute-done.14.refs_2_
  56.4 0.1 collective-permute-start.15
  56.6 1.9 %collective-permute-done.16.refs_4_ = bf16[16,2048]{1,0:T(8,128)(2,1)S(1)} collective-permute-done((bf16[16,2048]{1,0:T(8,128)(2,1)S(1)}, bf16[16,2048]{1,0:T(8,128)(2,1)S(1)}, u32[]{:S(2)}, u32[]{:S(2)}) %collective-permute-start.16) | collective-permute-done | bytes 65568 | tf_op jit(solution)/shard_map/ppermute | solution.py:284
  58.5 0.0 collective-permute-start.17
  58.5 1.4 %collective-permute-done.18.refs_6_ = bf16[16,2048]{1,0:T(8,128)(2,1)S(1)} collective-permute-done((bf16[16,2048]{1,0:T(8,128)(2,1)S(1)}, bf16[16,2048]{1,0:T(8,128)(2,1)S(1)}, u32[]{:S(2)}, u32[]{:S(2)}) %collective-permute-start.18) | collective-permute-done | bytes 65568 | tf_op jit(solution)/shard_map/ppermute | solution.py:284
  59.8 0.0 collective-permute-start.19
  59.9 1.2 %collective-permute-done.19.refs_7_ = bf16[16,2048]{1,0:T(8,128)(2,1)S(1)} collective-permute-done((bf16[16,2048]{1,0:T(8,128)(2,1)S(1)}, bf16[16,2048]{1,0:T(8,128)(2,1)S(1)}, u32[]{:S(2)}, u32[]{:S(2)}) %collective-permute-start.19) | collective-permute-done | bytes 65568 | tf_op jit(solution)/shard_map/ppermute | solution.py:286
  61.1 2.4 %apply.1 = (f32[16,2048]{1,0:T(8,128)S(1)}, bf16[16,2048]{1,0:T(8,128)(2,1)S(1)}, bf16[16,2048]{1,0:T(8,128)(2,1)S(1)}, bf16[16,2048]{1,0:T(8,128)(2,1)S(1)}) custom-call(s32[137]{0:T(256)S(1)} %get-tuple-element.20.pairs, bf16[136,256,256]{2,1,0:T(8,128)(2,1)S(1)} %get-tuple-element.21.tiles_ref, bf16[16,2048]{1,0:T(8,128)(2,1)S(1)} %multiply_convert_fusion.refs_0_, ...), custom_call_target="tpu_custom_call" | custom-call | tf_op jit(solution)/shard_map/apply/pallas_call | solution.py:335
  63.5 1.0 %collective-permute-start.20 = (bf16[16,2048]{1,0:T(8,128)(2,1)S(1)}, bf16[16,2048]{1,0:T(8,128)(2,1)S(1)}, u32[]{:S(2)}, u32[]{:S(2)}) collective-permute-start(bf16[16,2048]{1,0:T(8,128)(2,1)S(1)} %get-tuple-element.28), channel_id=1, source_target_pairs={{0,24},{8,0},{16,8},{24,16},{1,25},{9,1},{17,9},{25,17},{2,26},{10... | collective-permute-start | bytes 196616 | tf_op jit(solution)/shard_map/ppermute | solution.py:292
  64.5 0.6 collective-permute-start.21
  65.2 1.6 %collective-permute-start.22 = (bf16[16,2048]{1,0:T(8,128)(2,1)S(1)}, bf16[16,2048]{1,0:T(8,128)(2,1)S(1)}, u32[]{:S(2)}, u32[]{:S(2)}) collective-permute-start(bf16[16,2048]{1,0:T(8,128)(2,1)S(1)} %get-tuple-element.30), channel_id=1, source_target_pairs={{0,8},{8,16},{16,24},{24,0},{1,9},{9,17},{17,25},{25,1},{2,10},{10... | collective-permute-start | bytes 196616 | tf_op jit(solution)/shard_map/ppermute | solution.py:292
  66.8 2.2 %collective-permute-done.20 = bf16[16,2048]{1,0:T(8,128)(2,1)S(1)} collective-permute-done((bf16[16,2048]{1,0:T(8,128)(2,1)S(1)}, bf16[16,2048]{1,0:T(8,128)(2,1)S(1)}, u32[]{:S(2)}, u32[]{:S(2)}) %collective-permute-start.20) | collective-permute-done | bytes 65568 | tf_op jit(solution)/shard_map/ppermute | solution.py:292
  69.0 3.5 %collective-permute-done.21 = bf16[16,2048]{1,0:T(8,128)(2,1)S(1)} collective-permute-done((bf16[16,2048]{1,0:T(8,128)(2,1)S(1)}, bf16[16,2048]{1,0:T(8,128)(2,1)S(1)}, u32[]{:S(2)}, u32[]{:S(2)}) %collective-permute-start.21) | collective-permute-done | bytes 65568 | tf_op jit(solution)/shard_map/ppermute | solution.py:292
  72.4 0.0 collective-permute-done.22
  72.4 0.7 multiply_add_fusion
  (9 shorter events, 0.0 us)
Async XLA Ops:
  0.0 43.4 %copy-start = (f32[8,16]{1,0:T(8,128)S(1)}, f32[8,16]{1,0:T(8,128)}, u32[]{:S(2)}) copy-start(f32[8,16]{1,0:T(8,128)} %param.13) | copy-start | bytes 1540
  0.0 72.4 %copy-start.1 = (f32[16,2048]{1,0:T(8,128)S(1)}, f32[16,2048]{1,0:T(8,128)}, u32[]{:S(2)}) copy-start(f32[16,2048]{1,0:T(8,128)} %emi_ref.1) | copy-start | bytes 393220
  1.6 11.2 %collective-permute-start.4 = (bf16[32,2048]{1,0:T(8,128)(2,1)S(1)}, bf16[32,2048]{1,0:T(8,128)(2,1)S(1)}, u32[]{:S(2)}, u32[]{:S(2)}) collective-permute-start(bf16[32,2048]{1,0:T(8,128)(2,1)S(1)} %get-tuple-element.19.refs_4_), channel_id=1, source_target_pairs={{0,2},{1,3},{2,0},{3,1},{4,6},{5,7},{6,4},{7,5},{8,10},{9,11},{10,... | collective-permute-start | bytes 393224 | tf_op jit(solution)/shard_map/ppermute | solution.py:284
  4.6 8.8 %collective-permute-start.6 = (bf16[32,2048]{1,0:T(8,128)(2,1)S(1)}, bf16[32,2048]{1,0:T(8,128)(2,1)S(1)}, u32[]{:S(2)}, u32[]{:S(2)}) collective-permute-start(bf16[32,2048]{1,0:T(8,128)(2,1)S(1)} %get-tuple-element.19.refs_4_), channel_id=1, source_target_pairs={{0,4},{1,5},{2,6},{3,7},{4,0},{5,1},{6,2},{7,3},{8,12},{9,13},{10,... | collective-permute-start | bytes 393224 | tf_op jit(solution)/shard_map/ppermute | solution.py:284
  6.1 7.3 %collective-permute-start.8 = (bf16[32,2048]{1,0:T(8,128)(2,1)S(1)}, bf16[32,2048]{1,0:T(8,128)(2,1)S(1)}, u32[]{:S(2)}, u32[]{:S(2)}) collective-permute-start(bf16[32,2048]{1,0:T(8,128)(2,1)S(1)} %get-tuple-element.19.refs_4_), channel_id=1, source_target_pairs={{0,6},{1,7},{2,4},{3,5},{4,2},{5,3},{6,0},{7,1},{8,14},{9,15},{10,... | collective-permute-start | bytes 393224 | tf_op jit(solution)/shard_map/ppermute | solution.py:284
  6.1 6.8 %collective-permute-start = (bf16[16,2048]{1,0:T(8,128)(2,1)S(1)}, bf16[16,2048]{1,0:T(8,128)(2,1)S(1)}, u32[]{:S(2)}, u32[]{:S(2)}) collective-permute-start(bf16[16,2048]{1,0:T(8,128)(2,1)S(1)} %get-tuple-element.18.refs_0_), channel_id=1, source_target_pairs={{0,8},{8,16},{16,24},{24,0},{1,9},{9,17},{17,25},{25,1},{2,10},{10... | collective-permute-start | bytes 196616 | tf_op jit(solution)/shard_map/ppermute | solution.py:279
  8.1 5.7 %collective-permute-start.1 = (bf16[16,2048]{1,0:T(8,128)(2,1)S(1)}, bf16[16,2048]{1,0:T(8,128)(2,1)S(1)}, u32[]{:S(2)}, u32[]{:S(2)}) collective-permute-start(bf16[16,2048]{1,0:T(8,128)(2,1)S(1)} %get-tuple-element.18.refs_0_), channel_id=1, source_target_pairs={{0,16},{8,24},{16,0},{24,8},{1,17},{9,25},{17,1},{25,9},{2,18},{10... | collective-permute-start | bytes 196616 | tf_op jit(solution)/shard_map/ppermute | solution.py:279
  12.8 5.5 %collective-permute-start.3 = (bf16[32,2048]{1,0:T(8,128)(2,1)S(1)}, bf16[32,2048]{1,0:T(8,128)(2,1)S(1)}, u32[]{:S(2)}, u32[]{:S(2)}) collective-permute-start(bf16[32,2048]{1,0:T(8,128)(2,1)S(1)} %get-tuple-element.19.refs_4_), channel_id=1, source_target_pairs={{0,1},{1,0},{2,3},{3,2},{4,5},{5,4},{6,7},{7,6},{8,9},{9,8},{10,11... | collective-permute-start | bytes 393224 | tf_op jit(solution)/shard_map/ppermute | solution.py:286
  12.8 5.5 %collective-permute-start.5 = (bf16[32,2048]{1,0:T(8,128)(2,1)S(1)}, bf16[32,2048]{1,0:T(8,128)(2,1)S(1)}, u32[]{:S(2)}, u32[]{:S(2)}) collective-permute-start(bf16[32,2048]{1,0:T(8,128)(2,1)S(1)} %collective-permute-done.4.refs_6_), channel_id=1, source_target_pairs={{0,1},{1,0},{2,3},{3,2},{4,5},{5,4},{6,7},{7,6},{8,9},{9,8},{10,11... | collective-permute-start | bytes 393224 | tf_op jit(solution)/shard_map/ppermute | solution.py:286
  13.4 5.0 %collective-permute-start.7 = (bf16[32,2048]{1,0:T(8,128)(2,1)S(1)}, bf16[32,2048]{1,0:T(8,128)(2,1)S(1)}, u32[]{:S(2)}, u32[]{:S(2)}) collective-permute-start(bf16[32,2048]{1,0:T(8,128)(2,1)S(1)} %collective-permute-done.6.refs_8_), channel_id=1, source_target_pairs={{0,1},{1,0},{2,3},{3,2},{4,5},{5,4},{6,7},{7,6},{8,9},{9,8},{10,11... | collective-permute-start | bytes 393224 | tf_op jit(solution)/shard_map/ppermute | solution.py:286
  13.4 5.0 %collective-permute-start.9 = (bf16[32,2048]{1,0:T(8,128)(2,1)S(1)}, bf16[32,2048]{1,0:T(8,128)(2,1)S(1)}, u32[]{:S(2)}, u32[]{:S(2)}) collective-permute-start(bf16[32,2048]{1,0:T(8,128)(2,1)S(1)} %collective-permute-done.8.refs_10_), channel_id=1, source_target_pairs={{0,1},{1,0},{2,3},{3,2},{4,5},{5,4},{6,7},{7,6},{8,9},{9,8},{10,11... | collective-permute-start | bytes 393224 | tf_op jit(solution)/shard_map/ppermute | solution.py:286
  13.9 4.5 %collective-permute-start.2 = (bf16[16,2048]{1,0:T(8,128)(2,1)S(1)}, bf16[16,2048]{1,0:T(8,128)(2,1)S(1)}, u32[]{:S(2)}, u32[]{:S(2)}) collective-permute-start(bf16[16,2048]{1,0:T(8,128)(2,1)S(1)} %get-tuple-element.18.refs_0_), channel_id=1, source_target_pairs={{0,24},{8,0},{16,8},{24,16},{1,25},{9,1},{17,9},{25,17},{2,26},{10... | collective-permute-start | bytes 196616 | tf_op jit(solution)/shard_map/ppermute | solution.py:279
  37.7 7.6 %collective-permute-start.10 = (bf16[16,2048]{1,0:T(8,128)(2,1)S(1)}, bf16[16,2048]{1,0:T(8,128)(2,1)S(1)}, u32[]{:S(2)}, u32[]{:S(2)}) collective-permute-start(bf16[16,2048]{1,0:T(8,128)(2,1)S(1)} %get-tuple-element.24), channel_id=1, source_target_pairs={{0,24},{8,0},{16,8},{24,16},{1,25},{9,1},{17,9},{25,17},{2,26},{10... | collective-permute-start | bytes 196616 | tf_op jit(solution)/shard_map/ppermute | solution.py:292
  42.7 6.5 %collective-permute-start.11 = (bf16[16,2048]{1,0:T(8,128)(2,1)S(1)}, bf16[16,2048]{1,0:T(8,128)(2,1)S(1)}, u32[]{:S(2)}, u32[]{:S(2)}) collective-permute-start(bf16[16,2048]{1,0:T(8,128)(2,1)S(1)} %get-tuple-element.25), channel_id=1, source_target_pairs={{0,16},{8,24},{16,0},{24,8},{1,17},{9,25},{17,1},{25,9},{2,18},{10... | collective-permute-start | bytes 196616 | tf_op jit(solution)/shard_map/ppermute | solution.py:292
  42.7 6.5 %collective-permute-start.12 = (bf16[16,2048]{1,0:T(8,128)(2,1)S(1)}, bf16[16,2048]{1,0:T(8,128)(2,1)S(1)}, u32[]{:S(2)}, u32[]{:S(2)}) collective-permute-start(bf16[16,2048]{1,0:T(8,128)(2,1)S(1)} %get-tuple-element.26), channel_id=1, source_target_pairs={{0,8},{8,16},{16,24},{24,0},{1,9},{9,17},{17,25},{25,1},{2,10},{10... | collective-permute-start | bytes 196616 | tf_op jit(solution)/shard_map/ppermute | solution.py:292
  50.1 6.3 %collective-permute-start.14 = (bf16[16,2048]{1,0:T(8,128)(2,1)S(1)}, bf16[16,2048]{1,0:T(8,128)(2,1)S(1)}, u32[]{:S(2)}, u32[]{:S(2)}) collective-permute-start(bf16[16,2048]{1,0:T(8,128)(2,1)S(1)} %multiply_convert_fusion.refs_0_), channel_id=1, source_target_pairs={{0,2},{1,3},{2,0},{3,1},{4,6},{5,7},{6,4},{7,5},{8,10},{9,11},{10,... | collective-permute-start | bytes 196616 | tf_op jit(solution)/shard_map/ppermute | solution.py:284
  54.2 4.3 %collective-permute-start.16 = (bf16[16,2048]{1,0:T(8,128)(2,1)S(1)}, bf16[16,2048]{1,0:T(8,128)(2,1)S(1)}, u32[]{:S(2)}, u32[]{:S(2)}) collective-permute-start(bf16[16,2048]{1,0:T(8,128)(2,1)S(1)} %multiply_convert_fusion.refs_0_), channel_id=1, source_target_pairs={{0,4},{1,5},{2,6},{3,7},{4,0},{5,1},{6,2},{7,3},{8,12},{9,13},{10,... | collective-permute-start | bytes 196616 | tf_op jit(solution)/shard_map/ppermute | solution.py:284
  54.7 5.2 %collective-permute-start.18 = (bf16[16,2048]{1,0:T(8,128)(2,1)S(1)}, bf16[16,2048]{1,0:T(8,128)(2,1)S(1)}, u32[]{:S(2)}, u32[]{:S(2)}) collective-permute-start(bf16[16,2048]{1,0:T(8,128)(2,1)S(1)} %multiply_convert_fusion.refs_0_), channel_id=1, source_target_pairs={{0,6},{1,7},{2,4},{3,5},{4,2},{5,3},{6,0},{7,1},{8,14},{9,15},{10,... | collective-permute-start | bytes 196616 | tf_op jit(solution)/shard_map/ppermute | solution.py:284
  56.1 3.8 %collective-permute-start.13 = (bf16[16,2048]{1,0:T(8,128)(2,1)S(1)}, bf16[16,2048]{1,0:T(8,128)(2,1)S(1)}, u32[]{:S(2)}, u32[]{:S(2)}) collective-permute-start(bf16[16,2048]{1,0:T(8,128)(2,1)S(1)} %multiply_convert_fusion.refs_0_), channel_id=1, source_target_pairs={{0,1},{1,0},{2,3},{3,2},{4,5},{5,4},{6,7},{7,6},{8,9},{9,8},{10,11... | collective-permute-start | bytes 196616 | tf_op jit(solution)/shard_map/ppermute | solution.py:286
  56.4 3.4 %collective-permute-start.15 = (bf16[16,2048]{1,0:T(8,128)(2,1)S(1)}, bf16[16,2048]{1,0:T(8,128)(2,1)S(1)}, u32[]{:S(2)}, u32[]{:S(2)}) collective-permute-start(bf16[16,2048]{1,0:T(8,128)(2,1)S(1)} %collective-permute-done.14.refs_2_), channel_id=1, source_target_pairs={{0,1},{1,0},{2,3},{3,2},{4,5},{5,4},{6,7},{7,6},{8,9},{9,8},{10,11... | collective-permute-start | bytes 196616 | tf_op jit(solution)/shard_map/ppermute | solution.py:286
  58.5 1.4 %collective-permute-start.17 = (bf16[16,2048]{1,0:T(8,128)(2,1)S(1)}, bf16[16,2048]{1,0:T(8,128)(2,1)S(1)}, u32[]{:S(2)}, u32[]{:S(2)}) collective-permute-start(bf16[16,2048]{1,0:T(8,128)(2,1)S(1)} %collective-permute-done.16.refs_4_), channel_id=1, source_target_pairs={{0,1},{1,0},{2,3},{3,2},{4,5},{5,4},{6,7},{7,6},{8,9},{9,8},{10,11... | collective-permute-start | bytes 196616 | tf_op jit(solution)/shard_map/ppermute | solution.py:286
  59.8 1.3 %collective-permute-start.19 = (bf16[16,2048]{1,0:T(8,128)(2,1)S(1)}, bf16[16,2048]{1,0:T(8,128)(2,1)S(1)}, u32[]{:S(2)}, u32[]{:S(2)}) collective-permute-start(bf16[16,2048]{1,0:T(8,128)(2,1)S(1)} %collective-permute-done.18.refs_6_), channel_id=1, source_target_pairs={{0,1},{1,0},{2,3},{3,2},{4,5},{5,4},{6,7},{7,6},{8,9},{9,8},{10,11... | collective-permute-start | bytes 196616 | tf_op jit(solution)/shard_map/ppermute | solution.py:286
  63.5 5.4 %collective-permute-start.20 = (bf16[16,2048]{1,0:T(8,128)(2,1)S(1)}, bf16[16,2048]{1,0:T(8,128)(2,1)S(1)}, u32[]{:S(2)}, u32[]{:S(2)}) collective-permute-start(bf16[16,2048]{1,0:T(8,128)(2,1)S(1)} %get-tuple-element.28), channel_id=1, source_target_pairs={{0,24},{8,0},{16,8},{24,16},{1,25},{9,1},{17,9},{25,17},{2,26},{10... | collective-permute-start | bytes 196616 | tf_op jit(solution)/shard_map/ppermute | solution.py:292
  64.5 7.9 %collective-permute-start.21 = (bf16[16,2048]{1,0:T(8,128)(2,1)S(1)}, bf16[16,2048]{1,0:T(8,128)(2,1)S(1)}, u32[]{:S(2)}, u32[]{:S(2)}) collective-permute-start(bf16[16,2048]{1,0:T(8,128)(2,1)S(1)} %get-tuple-element.29), channel_id=1, source_target_pairs={{0,16},{8,24},{16,0},{24,8},{1,17},{9,25},{17,1},{25,9},{2,18},{10... | collective-permute-start | bytes 196616 | tf_op jit(solution)/shard_map/ppermute | solution.py:292
  65.2 7.3 %collective-permute-start.22 = (bf16[16,2048]{1,0:T(8,128)(2,1)S(1)}, bf16[16,2048]{1,0:T(8,128)(2,1)S(1)}, u32[]{:S(2)}, u32[]{:S(2)}) collective-permute-start(bf16[16,2048]{1,0:T(8,128)(2,1)S(1)} %get-tuple-element.30), channel_id=1, source_target_pairs={{0,8},{8,16},{16,24},{24,0},{1,9},{9,17},{17,25},{25,1},{2,10},{10... | collective-permute-start | bytes 196616 | tf_op jit(solution)/shard_map/ppermute | solution.py:292

commit v3 on v2

--- a/solution.py
+++ b/solution.py
@@ -14,7 +14,7 @@
 GEO = 16
 LANES = 128
 KDIM = 48
-FORM_UNROLL = 4
+FORM_UNROLL = 8
 APPLY_UNROLL = 8
 SPARE = 8
 KEEP_BYTES = 24 * 2**20
@@ -45,10 +45,10 @@
     a1, a2 = split(area, 2)
     rows[0:3, :] = p1
     rows[3:6, :] = p2
-    rows[6:9, :] = n1
-    rows[9:12, :] = n2
-    rows[12:13, :] = a1
-    rows[13:14, :] = a2
+    rows[6:7, :] = a1
+    rows[7:8, :] = a2
+    rows[8:11, :] = n1
+    rows[11:14, :] = n2
     rows[14:16, :] = jnp.zeros((2, area.shape[1]), F32)
     peers = slot_ref.shape[-1]
     for t in range(2 * CAP):
@@ -59,70 +59,56 @@
     pay_ref[GEO:, :] = (area * emi_ref[...]).astype(BF16)
 
 
-def constants(g):
-    p = g[0:3] + g[3:6]
-    n = g[6:9] + g[9:12]
-    half = 0.5 * (g[12:13] + g[13:14])
-    pp = p[0:1] * p[0:1] + p[1:2] * p[1:2] + p[2:3] * p[2:3]
-    np_ = n[0:1] * p[0:1] + n[1:2] * p[1:2] + n[2:3] * p[2:3]
-    return p, split(pp + half, 3), split(math.pi * pp + half, 3), split(-np_, 3)
-
-
-def column_features(g, feat):
-    _, q, r, c = constants(g)
-    one = jnp.ones_like(q[0])
-    feat[0:12, :] = g[0:12]
-    feat[12:24, :] = g[0:12]
-    feat[24:30, :] = g[0:6]
-    for t in range(3):
-        feat[30 + t : 31 + t, :] = q[t]
-        feat[33 + t : 34 + t, :] = r[t]
-        feat[36 + t : 37 + t, :] = c[t]
-        feat[39 + t : 40 + t, :] = one
-    feat[42:48, :] = jnp.zeros((6,) + one.shape[1:], F32)
-
-
-def row_features(g, feat, variant):
-    p, q, r, c = constants(g)
-    one = jnp.ones_like(q[0])
-    feat[...] = jnp.zeros(feat.shape, F32)
-    if variant == 0:
-        feat[0:3, :] = g[6:9]
-        feat[3:6, :] = g[6:9]
-        feat[12:15, :] = g[9:12]
-        feat[15:18, :] = g[9:12]
-        last = c
-    elif variant == 1:
-        feat[6:9, :] = g[0:3]
-        feat[9:12, :] = g[0:3]
-        feat[18:21, :] = g[3:6]
-        feat[21:24, :] = g[3:6]
-        for t in range(3):
-            feat[36 + t : 37 + t, :] = one
-        last = None
-    elif variant == 2:
-        u1, u2 = -2.0 * g[0:3], -2.0 * g[3:6]
-        feat[0:3, :] = u1
-        feat[3:6, :] = u1
-        feat[12:15, :] = u2
-        feat[15:18, :] = u2
-        for t in range(3):
-            feat[30 + t : 31 + t, :] = one
-        last = q
-    else:
-        u1, u2, u3 = split((-2.0 * math.pi) * p, 3)
-        feat[0:3, :] = u1
-        feat[3:6, :] = u1
-        feat[12:15, :] = u2
-        feat[15:18, :] = u2
-        feat[24:27, :] = u3
-        feat[27:30, :] = u3
-        for t in range(3):
-            feat[33 + t : 34 + t, :] = one
-        last = r
-    if last is not None:
-        for t in range(3):
-            feat[39 + t : 40 + t, :] = last[t]
+def terms_of(g):
+    pos, nrm = g[0:8], g[8:16]
+    row = lax.broadcasted_iota(jnp.int32, pos.shape, 0)
+    p = pos + pltpu.roll(pos, 5, 0)
+    n = nrm + pltpu.roll(nrm, 5, 0)
+    half = 0.5 * (pos[6:7] + pos[7:8])
+    pp = jnp.sum(jnp.where(row < 3, p * p, 0.0), axis=0, keepdims=True)
+    dot = jnp.sum(jnp.where(row < 3, n * p, 0.0), axis=0, keepdims=True)
+    return pos, nrm, row, split(pp + half, 3), split(-dot, 3), (math.pi - 1.0) * half
+
+
+def column_features(g):
+    pos, nrm, row, q, c, h = terms_of(g)
+    zero = jnp.zeros(pos.shape, F32)
+    one = jnp.where(row == 6, 1.0, zero)
+    pos = jnp.where(row < 6, pos, one)
+    nrm = jnp.where(row < 6, nrm, one)
+    consts, areas = zero, zero
+    for t, value in enumerate(q + c):
+        consts = jnp.where(row == t, value, consts)
+    for t, value in enumerate(split(h, 3)):
+        areas = jnp.where(row == t, value, areas)
+    return jnp.concatenate([pos, nrm, pos, nrm, consts, areas], axis=0)
+
+
+def row_features(g):
+    pos, nrm, row, q, c, h = terms_of(g)
+    zero = jnp.zeros(pos.shape, F32)
+
+    def both(x):
+        high = jnp.where(row < 3, x, pltpu.roll(x, 3, 0))
+        low = jnp.where(row < 3, pltpu.roll(x, 5, 0), x)
+        return jnp.where(row < 6, high, 0.0), jnp.where(row < 6, low, 0.0)
+
+    def with_last(x, value):
+        return jnp.where(row == 6, value, x)
+
+    p_hi, p_lo = both(pos)
+    n_hi, n_lo = both(nrm)
+    facing = [with_last(n_hi, c[0]), with_last(zero, c[1]), with_last(n_lo, c[2]), zero, zero, zero]
+    seen = [zero, p_hi, zero, p_lo, jnp.where((row >= 3) & (row < 6), 1.0, zero), zero]
+    near = [
+        with_last(-2.0 * p_hi, q[0]),
+        with_last(zero, q[1]),
+        with_last(-2.0 * p_lo, q[2]),
+        zero,
+        jnp.where(row < 3, 1.0, zero),
+        zero,
+    ]
+    return [jnp.concatenate(parts, axis=0).astype(BF16) for parts in (facing, seen, near)], h
 
 
 def list_pairs(nz, ny, nb, place_ref, slots, pairs):
@@ -144,10 +130,30 @@
             count = count + (row >= 0).astype(jnp.int32)
         return count
 
-    count = lax.fori_loop(0, nz * ny, peer, jnp.int32(0))
+    count = jnp.int32(0)
+    if nz * ny <= 32:
+        for e in range(nz * ny):
+            count = peer(e, count)
+    else:
+        count = lax.fori_loop(0, nz * ny, peer, count)
     for t in range(SPARE):
         pairs[count + t] = nz * nb * 4096
     pairs[most + SPARE] = count
+
+
+def form_scratch(nz, ny, nb, patches):
+    devices = -(-(nz + ny) // 8) * 8
+    return [
+        pltpu.VMEM((nz * nb, 3, KDIM, BLK), BF16),
+        pltpu.VMEM((nz * nb, 1, BLK), F32),
+        pltpu.VMEM((ny * nb, BLK, KDIM), BF16),
+        pltpu.VMEM((ny * nb, BLK, LANES), F32),
+        pltpu.VMEM((ny * nb, BANDS, BLK), BF16),
+        pltpu.VMEM((nz * nb + 1, BANDS, BLK), F32),
+        pltpu.VMEM((devices, 2 * CAP * LANES), jnp.int32),
+        pltpu.SMEM((devices, 2 * CAP * LANES), jnp.int32),
+        pltpu.SemaphoreType.DMA,
+    ]
 
 
 def put_out(nz, nb, acc, out_refs):
@@ -164,7 +170,7 @@
     outs, refs = refs[:nz], refs[nz:]
     if keep:
         tiles_ref, pairs, refs = refs[0], refs[1], refs[2:]
-    feat, row_feat, col_feat, flux, acc, slots_v, slots, sem, *more = refs
+    row_feat, row_area, col_feat, col_area, flux, acc, slots_v, slots, sem, *more = refs
     if not keep:
         pairs = more[0]
     most = nz * ny * 2 * CAP
@@ -178,33 +184,38 @@
     copy = pltpu.make_async_copy(slots_v, slots, sem)
     copy.start()
     for s in range(nz):
-        g = geos[s][...].astype(F32)
-        for v in range(4):
-            row_features(g, feat, v)
-            for b in range(nb):
-                row_feat[s * nb + b, v] = feat[:, b * BLK : (b + 1) * BLK].astype(BF16)
-    for m in range(ny):
-        g = pays[m][0:GEO, :].astype(F32)
-        column_features(g, feat)
+        forms, h = row_features(geos[s][...].astype(F32))
         for b in range(nb):
-            col_feat[m * nb + b] = jnp.transpose(feat[:, b * BLK : (b + 1) * BLK]).astype(BF16)
             here = slice(b * BLK, (b + 1) * BLK)
-            flux[m * nb + b] = fluxes[m][:, here] if fresh else pays[m][GEO:, here]
+            row_area[s * nb + b] = h[:, here]
+            for v in range(3):
+                row_feat[s * nb + b, v] = forms[v][:, here]
     acc[...] = jnp.zeros(acc.shape, F32)
     copy.wait()
     list_pairs(nz, ny, nb, place_ref, slots, pairs)
-
+    depth = lax.broadcasted_iota(jnp.int32, (KDIM, LANES), 0)
+    pick = jnp.where((depth >= 40) & (depth < 43), 1.0, 0.0).astype(BF16)
+    for m in range(ny):
+        feat = column_features(pays[m][0:GEO, :].astype(F32)).astype(BF16)
+        for b in range(nb):
+            here = slice(b * BLK, (b + 1) * BLK)
+            turned = jnp.transpose(feat[:, here])
+            col_feat[m * nb + b] = turned
+            col_area[m * nb + b] = jnp.dot(turned, pick, preferred_element_type=F32)
+            flux[m * nb + b] = fluxes[m][:, here] if fresh else pays[m][GEO:, here]
     count = pairs[most + SPARE]
 
     def tile_of(t):
         code = pairs[t]
         rb = jnp.minimum(code // 4096, nz * nb - 1)
         left = col_feat[code % 4096]
-        f, s, q, r = (
-            jnp.dot(left, row_feat[rb, v], preferred_element_type=F32) for v in range(4)
+        f, s, q = (
+            jnp.dot(left, row_feat[rb, v], preferred_element_type=F32) for v in range(3)
         )
+        area = col_area[code % 4096]
+        area = jnp.concatenate([area] * (BLK // LANES), axis=1) + row_area[rb]
         top = jnp.maximum(f, 0.0) * jnp.maximum(s, 0.0)
-        return (top * pltpu.reciprocal(q * r, approx=True)).astype(BF16)
+        return (top * pltpu.reciprocal(q * (math.pi * q - area), approx=True)).astype(BF16)
 
     if keep:
 
@@ -259,7 +270,7 @@
     most = nz * ny * 2 * CAP
     width = 2 * CAP * LANES
     keep = (most + SPARE) * BLK * BLK * 2 <= KEEP_BYTES
-    params = [pltpu.CompilerParams(vmem_limit_bytes=n * 2**20) for n in ((14, 4) if keep else (56, 4))]
+    params = [pltpu.CompilerParams(vmem_limit_bytes=n * 2**20) for n in ((30, 4) if keep else (60, 4))]
     place = jnp.stack([lax.axis_index("gx"), lax.axis_index("gy")]).astype(jnp.int32)
     slot_rows = jnp.transpose(pair_slots[0], (1, 2, 0))
     payload, geo, area = pl.pallas_call(
@@ -309,16 +320,7 @@
                 jax.ShapeDtypeStruct((most + SPARE + 1,), jnp.int32),
             ]
             specs += [VMEM(), SMEM()]
-        scratch = [
-            pltpu.VMEM((KDIM, patches), F32),
-            pltpu.VMEM((nz * nb, 4, KDIM, BLK), BF16),
-            pltpu.VMEM((ny * nb, BLK, KDIM), BF16),
-            pltpu.VMEM((ny * nb, BANDS, BLK), BF16),
-            pltpu.VMEM((nz * nb + 1, BANDS, BLK), F32),
-            pltpu.VMEM((-(-(nz + ny) // 8) * 8, width), jnp.int32),
-            pltpu.SMEM((-(-(nz + ny) // 8) * 8, width), jnp.int32),
-            pltpu.SemaphoreType.DMA,
-        ]
+        scratch = form_scratch(nz, ny, nb, patches)
         if not keep:
             scratch += [pltpu.SMEM((most + SPARE + 1,), jnp.int32)]
         return pl.pallas_call(

time: 73.6 us -> 67.2 us (0.913)
  starting transfers between devices: 27.7 us -> 24.5 us
  Pallas kernels: 23.3 us -> 20.2 us
    pallas_call x1, Pallas kernels: 19.3 us -> 15.6 us  [form(): pl.pallas_call(functools.partial(form_kernel, nz, ny, nb, keep, fresh), o...]
    ppermute x6, starting transfers between devices: 8.93 us -> 7.09 us  [home(): back = lax.ppermute(parts[s], 'gx', [(i, (i - s) % nz) for i in range(nz)])]
    ppermute x6, starting transfers between devices: 10.4 us -> 9.02 us  [plane(): got[m] = lax.ppermute(x, 'gy', [(i, i ^ m) for i in range(ny)])]
    ppermute x6, waiting for transfers between devices: 10.5 us -> 9.42 us  [home(): back = lax.ppermute(parts[s], 'gx', [(i, (i - s) % nz) for i in range(nz)])]
  transfers between devices with their start and end apart: 23 -> 23, of which waited for: 10 -> 9; matrix products, arithmetic and copies ran while one was open for 1% -> 2% of each run, Pallas kernels for 0% -> 0%
where the time goes in v3:
time: 67.2 us; the launch traced here: 66.4 us
  starting transfers between devices  24.5 us (36%)
  Pallas kernels  20.2 us (30%)
  waiting for transfers between devices  19 us (28%)
  other arithmetic  1.73 us (3%)
  matrix products  0.95 us (1%)
    pallas_call x1, Pallas kernels, form(): pl.pallas_call(functools.partial(form_kernel, nz, ny, nb, keep, fresh), o...  15.6 us
    ppermute x6, waiting for transfers between devices, home(): back = lax.ppermute(parts[s], 'gx', [(i, (i - s) % nz) for i in range(nz)])  9.42 us
    ppermute x6, starting transfers between devices, plane(): got[m] = lax.ppermute(x, 'gy', [(i, i ^ m) for i in range(ny)])  9.02 us
    ppermute x3, starting transfers between devices, along(): lax.ppermute(x, 'gx', [(i, (i + s) % nz) for i in range(nz)])  7.23 us
    ppermute x6, starting transfers between devices, home(): back = lax.ppermute(parts[s], 'gx', [(i, (i - s) % nz) for i in range(nz)])  7.09 us
    ppermute x6, waiting for transfers between devices, plane(): got[m] = lax.ppermute(x, 'gy', [(i, i ^ m) for i in range(ny)])  4.35 us
    ppermute x3, waiting for transfers between devices, along(): lax.ppermute(x, 'gx', [(i, (i + s) % nz) for i in range(nz)])  3.94 us
    pallas_call x1, Pallas kernels, apply(): pl.pallas_call(functools.partial(apply_kernel, nz, ny, nb), out_shape=tup...  2.95 us
  transfers between devices with their start and end apart: 23, of which 9 were waited for; matrix products, arithmetic and copies ran while one was open for 2% of the time, Pallas kernels for 0%

profile of v3, /device:TPU:0, one launch (start us, length us, event | category | flops | bytes accessed | tf_op | source)
XLA Modules:
  0.0 66.4 jit_solution(6312536685128102990)
XLA Ops:
  0.0 1.6 %pack.1 = (bf16[32,2048]{1,0:T(8,128)(2,1)S(1)}, bf16[16,2048]{1,0:T(8,128)(2,1)S(1)}, f32[1,2048]{1,0:T(1,128)}) custom-call(f32[3,2048]{1,0:T(4,128)} %pos_ref.1, f32[3,2048]{1,0:T(4,128)} %nrm_ref.1, f32[16,2048]{1,0:T(8,128)} %emi_ref.1, s32[1,2048]{1,0:T(1,128)} %bitcast.10, f32[8]{0:T(128)} %table_ref.1, s32[2,2,32]{2,1,0:T(2,128)} %bitcast.12), custom_call_target="tpu_custom_call" | custom-call | tf_op jit(solution)/shard_map/pack/pallas_call | solution.py:276
  1.6 2.9 %collective-permute-start.4 = (bf16[32,2048]{1,0:T(8,128)(2,1)S(1)}, bf16[32,2048]{1,0:T(8,128)(2,1)S(1)}, u32[]{:S(2)}, u32[]{:S(2)}) collective-permute-start(bf16[32,2048]{1,0:T(8,128)(2,1)S(1)} %get-tuple-element.19.refs_4_), channel_id=1, source_target_pairs={{0,2},{1,3},{2,0},{3,1},{4,6},{5,7},{6,4},{7,5},{8,10},{9,11},{10,... | collective-permute-start | bytes 393224 | tf_op jit(solution)/shard_map/ppermute | solution.py:295
  4.6 1.5 %collective-permute-start.6 = (bf16[32,2048]{1,0:T(8,128)(2,1)S(1)}, bf16[32,2048]{1,0:T(8,128)(2,1)S(1)}, u32[]{:S(2)}, u32[]{:S(2)}) collective-permute-start(bf16[32,2048]{1,0:T(8,128)(2,1)S(1)} %get-tuple-element.19.refs_4_), channel_id=1, source_target_pairs={{0,4},{1,5},{2,6},{3,7},{4,0},{5,1},{6,2},{7,3},{8,12},{9,13},{10,... | collective-permute-start | bytes 393224 | tf_op jit(solution)/shard_map/ppermute | solution.py:295
  6.1 0.0 collective-permute-start.8
  6.1 2.1 %collective-permute-start = (bf16[16,2048]{1,0:T(8,128)(2,1)S(1)}, bf16[16,2048]{1,0:T(8,128)(2,1)S(1)}, u32[]{:S(2)}, u32[]{:S(2)}) collective-permute-start(bf16[16,2048]{1,0:T(8,128)(2,1)S(1)} %get-tuple-element.18.refs_0_), channel_id=1, source_target_pairs={{0,8},{8,16},{16,24},{24,0},{1,9},{9,17},{17,25},{25,1},{2,10},{10... | collective-permute-start | bytes 196616 | tf_op jit(solution)/shard_map/ppermute | solution.py:290
  8.1 2.6 %collective-permute-start.1 = (bf16[16,2048]{1,0:T(8,128)(2,1)S(1)}, bf16[16,2048]{1,0:T(8,128)(2,1)S(1)}, u32[]{:S(2)}, u32[]{:S(2)}) collective-permute-start(bf16[16,2048]{1,0:T(8,128)(2,1)S(1)} %get-tuple-element.18.refs_0_), channel_id=1, source_target_pairs={{0,16},{8,24},{16,0},{24,8},{1,17},{9,25},{17,1},{25,9},{2,18},{10... | collective-permute-start | bytes 196616 | tf_op jit(solution)/shard_map/ppermute | solution.py:290
  10.7 2.1 %collective-permute-done.refs_1_ = bf16[16,2048]{1,0:T(8,128)(2,1)S(1)} collective-permute-done((bf16[16,2048]{1,0:T(8,128)(2,1)S(1)}, bf16[16,2048]{1,0:T(8,128)(2,1)S(1)}, u32[]{:S(2)}, u32[]{:S(2)}) %collective-permute-start) | collective-permute-done | bytes 65568 | tf_op jit(solution)/shard_map/ppermute | solution.py:290
  12.8 0.0 collective-permute-start.3
  12.8 0.5 collective-permute-start.5
  13.4 0.1 collective-permute-start.7
  13.4 0.0 collective-permute-done.8.refs_10_
  13.4 0.4 collective-permute-start.9
  13.9 2.6 %collective-permute-start.2 = (bf16[16,2048]{1,0:T(8,128)(2,1)S(1)}, bf16[16,2048]{1,0:T(8,128)(2,1)S(1)}, u32[]{:S(2)}, u32[]{:S(2)}) collective-permute-start(bf16[16,2048]{1,0:T(8,128)(2,1)S(1)} %get-tuple-element.18.refs_0_), channel_id=1, source_target_pairs={{0,24},{8,0},{16,8},{24,16},{1,25},{9,1},{17,9},{25,17},{2,26},{10... | collective-permute-start | bytes 196616 | tf_op jit(solution)/shard_map/ppermute | solution.py:290
  16.5 0.1 pad_add_fusion.place_ref
  16.5 1.8 %collective-permute-done.2.refs_3_ = bf16[16,2048]{1,0:T(8,128)(2,1)S(1)} collective-permute-done((bf16[16,2048]{1,0:T(8,128)(2,1)S(1)}, bf16[16,2048]{1,0:T(8,128)(2,1)S(1)}, u32[]{:S(2)}, u32[]{:S(2)}) %collective-permute-start.2) | collective-permute-done | bytes 65568 | tf_op jit(solution)/shard_map/ppermute | solution.py:290
  18.4 0.0 collective-permute-done.3.refs_5_
  18.4 0.0 collective-permute-done.5.refs_7_
  18.4 0.0 collective-permute-done.9.refs_11_
  18.4 15.6 %form.1 = (f32[16,2048]{1,0:T(8,128)S(1)}, bf16[16,2048]{1,0:T(8,128)(2,1)S(1)}, bf16[16,2048]{1,0:T(8,128)(2,1)S(1)}, bf16[16,2048]{1,0:T(8,128)(2,1)S(1)}, bf1...) custom-call(s32[2]{0:T(128)S(1)} %pad_add_fusion.place_ref, bf16[16,2048]{1,0:T(8,128)(2,1)S(1)} %get-tuple-element.18.refs_0_, ...), custom_call_target="tpu_custom_call" | custom-call | tf_op jit(solution)/shard_map/form/pallas_call | solution.py:326
  34.0 1.7 %collective-permute-start.10 = (bf16[16,2048]{1,0:T(8,128)(2,1)S(1)}, bf16[16,2048]{1,0:T(8,128)(2,1)S(1)}, u32[]{:S(2)}, u32[]{:S(2)}) collective-permute-start(bf16[16,2048]{1,0:T(8,128)(2,1)S(1)} %get-tuple-element.24), channel_id=1, source_target_pairs={{0,24},{8,0},{16,8},{24,16},{1,25},{9,1},{17,9},{25,17},{2,26},{10... | collective-permute-start | bytes 196616 | tf_op jit(solution)/shard_map/ppermute | solution.py:303
  35.8 0.2 collective-permute-start.11
  36.0 1.9 %collective-permute-start.12 = (bf16[16,2048]{1,0:T(8,128)(2,1)S(1)}, bf16[16,2048]{1,0:T(8,128)(2,1)S(1)}, u32[]{:S(2)}, u32[]{:S(2)}) collective-permute-start(bf16[16,2048]{1,0:T(8,128)(2,1)S(1)} %get-tuple-element.26), channel_id=1, source_target_pairs={{0,8},{8,16},{16,24},{24,0},{1,9},{9,17},{17,25},{25,1},{2,10},{10... | collective-permute-start | bytes 196616 | tf_op jit(solution)/shard_map/ppermute | solution.py:303
  37.9 0.9 %convolution_bitcast_fusion = f32[16,2048]{1,0:T(8,128)S(1)} fusion(f32[8,16]{1,0:T(8,128)S(1)} %copy-done, s32[2048]{0:T(1024)} %param.11), kind=kOutput, calls=%fused_computation | convolution fusion | flops 3162112 | bytes 139776 | tf_op jit(solution)/shard_map/dot_general | solution.py:353
  38.9 0.0 collective-permute-done.10
  38.9 3.9 %collective-permute-done.11 = bf16[16,2048]{1,0:T(8,128)(2,1)S(1)} collective-permute-done((bf16[16,2048]{1,0:T(8,128)(2,1)S(1)}, bf16[16,2048]{1,0:T(8,128)(2,1)S(1)}, u32[]{:S(2)}, u32[]{:S(2)}) %collective-permute-start.11) | collective-permute-done | bytes 65568 | tf_op jit(solution)/shard_map/ppermute | solution.py:303
  42.8 0.0 collective-permute-done.12
  42.8 1.0 %multiply_convert_fusion.refs_0_ = bf16[16,2048]{1,0:T(8,128)(2,1)S(1)} fusion(f32[16,2048]{1,0:T(8,128)} %emi_ref.1, f32[16,2048]{1,0:T(8,128)S(1)} %convolution_bitcast_fusion, bf16[16,2048]{1,0:T(8,128)(2,1)S(1)} %collective-permute-done.12, bf16[16,2048]{1,0:T(8,128)(2,1)S(1)} %collective-permute-done.11, f32[16,2048]{1,0:T(8,128)S(1)} %get-tuple-element.23, ...), kind=kLoop, calls=%fused_computation.2 | loop fusion | flops 327680 | bytes 663552 | tf_op jit(solution)/shard_map/convert_element_type | solution.py:357
  43.8 2.6 %collective-permute-start.14 = (bf16[16,2048]{1,0:T(8,128)(2,1)S(1)}, bf16[16,2048]{1,0:T(8,128)(2,1)S(1)}, u32[]{:S(2)}, u32[]{:S(2)}) collective-permute-start(bf16[16,2048]{1,0:T(8,128)(2,1)S(1)} %multiply_convert_fusion.refs_0_), channel_id=1, source_target_pairs={{0,2},{1,3},{2,0},{3,1},{4,6},{5,7},{6,4},{7,5},{8,10},{9,11},{10,... | collective-permute-start | bytes 196616 | tf_op jit(solution)/shard_map/ppermute | solution.py:295
  46.4 1.2 %collective-permute-start.16 = (bf16[16,2048]{1,0:T(8,128)(2,1)S(1)}, bf16[16,2048]{1,0:T(8,128)(2,1)S(1)}, u32[]{:S(2)}, u32[]{:S(2)}) collective-permute-start(bf16[16,2048]{1,0:T(8,128)(2,1)S(1)} %multiply_convert_fusion.refs_0_), channel_id=1, source_target_pairs={{0,4},{1,5},{2,6},{3,7},{4,0},{5,1},{6,2},{7,3},{8,12},{9,13},{10,... | collective-permute-start | bytes 196616 | tf_op jit(solution)/shard_map/ppermute | solution.py:295
  47.6 0.7 %collective-permute-start.18 = (bf16[16,2048]{1,0:T(8,128)(2,1)S(1)}, bf16[16,2048]{1,0:T(8,128)(2,1)S(1)}, u32[]{:S(2)}, u32[]{:S(2)}) collective-permute-start(bf16[16,2048]{1,0:T(8,128)(2,1)S(1)} %multiply_convert_fusion.refs_0_), channel_id=1, source_target_pairs={{0,6},{1,7},{2,4},{3,5},{4,2},{5,3},{6,0},{7,1},{8,14},{9,15},{10,... | collective-permute-start | bytes 196616 | tf_op jit(solution)/shard_map/ppermute | solution.py:295
  48.3 0.0 collective-permute-start.13
  48.3 0.4 collective-permute-done.14.refs_2_
  48.8 0.1 collective-permute-start.15
  48.9 2.3 %collective-permute-done.16.refs_4_ = bf16[16,2048]{1,0:T(8,128)(2,1)S(1)} collective-permute-done((bf16[16,2048]{1,0:T(8,128)(2,1)S(1)}, bf16[16,2048]{1,0:T(8,128)(2,1)S(1)}, u32[]{:S(2)}, u32[]{:S(2)}) %collective-permute-start.16) | collective-permute-done | bytes 65568 | tf_op jit(solution)/shard_map/ppermute | solution.py:295
  51.2 0.0 collective-permute-start.17
  51.2 1.6 %collective-permute-done.18.refs_6_ = bf16[16,2048]{1,0:T(8,128)(2,1)S(1)} collective-permute-done((bf16[16,2048]{1,0:T(8,128)(2,1)S(1)}, bf16[16,2048]{1,0:T(8,128)(2,1)S(1)}, u32[]{:S(2)}, u32[]{:S(2)}) %collective-permute-start.18) | collective-permute-done | bytes 65568 | tf_op jit(solution)/shard_map/ppermute | solution.py:295
  52.8 0.0 collective-permute-done.13.refs_1_
  52.8 0.0 collective-permute-done.15.refs_3_
  52.8 0.0 collective-permute-done.17.refs_5_
  52.8 1.2 %collective-permute-done.19.refs_7_ = bf16[16,2048]{1,0:T(8,128)(2,1)S(1)} collective-permute-done((bf16[16,2048]{1,0:T(8,128)(2,1)S(1)}, bf16[16,2048]{1,0:T(8,128)(2,1)S(1)}, u32[]{:S(2)}, u32[]{:S(2)}) %collective-permute-start.19) | collective-permute-done | bytes 65568 | tf_op jit(solution)/shard_map/ppermute | solution.py:297
  54.1 3.0 %apply.1 = (f32[16,2048]{1,0:T(8,128)S(1)}, bf16[16,2048]{1,0:T(8,128)(2,1)S(1)}, bf16[16,2048]{1,0:T(8,128)(2,1)S(1)}, bf16[16,2048]{1,0:T(8,128)(2,1)S(1)}) custom-call(s32[137]{0:T(256)S(1)} %get-tuple-element.20.pairs, bf16[136,256,256]{2,1,0:T(8,128)(2,1)S(1)} %get-tuple-element.21.tiles_ref, bf16[16,2048]{1,0:T(8,128)(2,1)S(1)} %multiply_convert_fusion.refs_0_, ...), custom_call_target="tpu_custom_call" | custom-call | tf_op jit(solution)/shard_map/apply/pallas_call | solution.py:337
  57.0 0.8 %collective-permute-start.20 = (bf16[16,2048]{1,0:T(8,128)(2,1)S(1)}, bf16[16,2048]{1,0:T(8,128)(2,1)S(1)}, u32[]{:S(2)}, u32[]{:S(2)}) collective-permute-start(bf16[16,2048]{1,0:T(8,128)(2,1)S(1)} %get-tuple-element.28), channel_id=1, source_target_pairs={{0,24},{8,0},{16,8},{24,16},{1,25},{9,1},{17,9},{25,17},{2,26},{10... | collective-permute-start | bytes 196616 | tf_op jit(solution)/shard_map/ppermute | solution.py:303
  57.8 0.4 collective-permute-start.21
  58.3 1.9 %collective-permute-start.22 = (bf16[16,2048]{1,0:T(8,128)(2,1)S(1)}, bf16[16,2048]{1,0:T(8,128)(2,1)S(1)}, u32[]{:S(2)}, u32[]{:S(2)}) collective-permute-start(bf16[16,2048]{1,0:T(8,128)(2,1)S(1)} %get-tuple-element.30), channel_id=1, source_target_pairs={{0,8},{8,16},{16,24},{24,0},{1,9},{9,17},{17,25},{25,1},{2,10},{10... | collective-permute-start | bytes 196616 | tf_op jit(solution)/shard_map/ppermute | solution.py:303
  60.2 1.1 %collective-permute-done.20 = bf16[16,2048]{1,0:T(8,128)(2,1)S(1)} collective-permute-done((bf16[16,2048]{1,0:T(8,128)(2,1)S(1)}, bf16[16,2048]{1,0:T(8,128)(2,1)S(1)}, u32[]{:S(2)}, u32[]{:S(2)}) %collective-permute-start.20) | collective-permute-done | bytes 65568 | tf_op jit(solution)/shard_map/ppermute | solution.py:303
  61.3 4.4 %collective-permute-done.21 = bf16[16,2048]{1,0:T(8,128)(2,1)S(1)} collective-permute-done((bf16[16,2048]{1,0:T(8,128)(2,1)S(1)}, bf16[16,2048]{1,0:T(8,128)(2,1)S(1)}, u32[]{:S(2)}, u32[]{:S(2)}) %collective-permute-start.21) | collective-permute-done | bytes 65568 | tf_op jit(solution)/shard_map/ppermute | solution.py:303
  65.7 0.0 collective-permute-done.22
  65.7 0.7 %multiply_add_fusion = f32[16,2048]{1,0:T(8,128)} fusion(f32[16,2048]{1,0:T(8,128)S(1)} %copy-done.1, f32[16,2048]{1,0:T(8,128)S(1)} %convolution_bitcast_fusion, bf16[16,2048]{1,0:T(8,128)(2,1)S(1)} %collective-permute-done.22, bf16[16,2048]{1,0:T(8,128)(2,1)S(1)} %collective-permute-done.21, f32[16,2048]{1,0:T(8,128)S(1)} %get-tuple-element.27, ...), kind=kLoop, calls=%fused_computation.1 | loop fusion | flops 262144 | bytes 720896 | tf_op jit(solution)/shard_map/add | solution.py:359
  (9 shorter events, 0.0 us)
Async XLA Ops:
  0.0 37.9 %copy-start = (f32[8,16]{1,0:T(8,128)S(1)}, f32[8,16]{1,0:T(8,128)}, u32[]{:S(2)}) copy-start(f32[8,16]{1,0:T(8,128)} %param.13) | copy-start | bytes 1540
  0.0 65.7 %copy-start.1 = (f32[16,2048]{1,0:T(8,128)S(1)}, f32[16,2048]{1,0:T(8,128)}, u32[]{:S(2)}) copy-start(f32[16,2048]{1,0:T(8,128)} %emi_ref.1) | copy-start | bytes 393220
  1.6 11.2 %collective-permute-start.4 = (bf16[32,2048]{1,0:T(8,128)(2,1)S(1)}, bf16[32,2048]{1,0:T(8,128)(2,1)S(1)}, u32[]{:S(2)}, u32[]{:S(2)}) collective-permute-start(bf16[32,2048]{1,0:T(8,128)(2,1)S(1)} %get-tuple-element.19.refs_4_), channel_id=1, source_target_pairs={{0,2},{1,3},{2,0},{3,1},{4,6},{5,7},{6,4},{7,5},{8,10},{9,11},{10,... | collective-permute-start | bytes 393224 | tf_op jit(solution)/shard_map/ppermute | solution.py:295
  4.6 8.8 %collective-permute-start.6 = (bf16[32,2048]{1,0:T(8,128)(2,1)S(1)}, bf16[32,2048]{1,0:T(8,128)(2,1)S(1)}, u32[]{:S(2)}, u32[]{:S(2)}) collective-permute-start(bf16[32,2048]{1,0:T(8,128)(2,1)S(1)} %get-tuple-element.19.refs_4_), channel_id=1, source_target_pairs={{0,4},{1,5},{2,6},{3,7},{4,0},{5,1},{6,2},{7,3},{8,12},{9,13},{10,... | collective-permute-start | bytes 393224 | tf_op jit(solution)/shard_map/ppermute | solution.py:295
  6.1 7.3 %collective-permute-start.8 = (bf16[32,2048]{1,0:T(8,128)(2,1)S(1)}, bf16[32,2048]{1,0:T(8,128)(2,1)S(1)}, u32[]{:S(2)}, u32[]{:S(2)}) collective-permute-start(bf16[32,2048]{1,0:T(8,128)(2,1)S(1)} %get-tuple-element.19.refs_4_), channel_id=1, source_target_pairs={{0,6},{1,7},{2,4},{3,5},{4,2},{5,3},{6,0},{7,1},{8,14},{9,15},{10,... | collective-permute-start | bytes 393224 | tf_op jit(solution)/shard_map/ppermute | solution.py:295
  6.1 6.8 %collective-permute-start = (bf16[16,2048]{1,0:T(8,128)(2,1)S(1)}, bf16[16,2048]{1,0:T(8,128)(2,1)S(1)}, u32[]{:S(2)}, u32[]{:S(2)}) collective-permute-start(bf16[16,2048]{1,0:T(8,128)(2,1)S(1)} %get-tuple-element.18.refs_0_), channel_id=1, source_target_pairs={{0,8},{8,16},{16,24},{24,0},{1,9},{9,17},{17,25},{25,1},{2,10},{10... | collective-permute-start | bytes 196616 | tf_op jit(solution)/shard_map/ppermute | solution.py:290
  8.1 5.7 %collective-permute-start.1 = (bf16[16,2048]{1,0:T(8,128)(2,1)S(1)}, bf16[16,2048]{1,0:T(8,128)(2,1)S(1)}, u32[]{:S(2)}, u32[]{:S(2)}) collective-permute-start(bf16[16,2048]{1,0:T(8,128)(2,1)S(1)} %get-tuple-element.18.refs_0_), channel_id=1, source_target_pairs={{0,16},{8,24},{16,0},{24,8},{1,17},{9,25},{17,1},{25,9},{2,18},{10... | collective-permute-start | bytes 196616 | tf_op jit(solution)/shard_map/ppermute | solution.py:290
  12.8 5.5 %collective-permute-start.3 = (bf16[32,2048]{1,0:T(8,128)(2,1)S(1)}, bf16[32,2048]{1,0:T(8,128)(2,1)S(1)}, u32[]{:S(2)}, u32[]{:S(2)}) collective-permute-start(bf16[32,2048]{1,0:T(8,128)(2,1)S(1)} %get-tuple-element.19.refs_4_), channel_id=1, source_target_pairs={{0,1},{1,0},{2,3},{3,2},{4,5},{5,4},{6,7},{7,6},{8,9},{9,8},{10,11... | collective-permute-start | bytes 393224 | tf_op jit(solution)/shard_map/ppermute | solution.py:297
  12.8 5.5 %collective-permute-start.5 = (bf16[32,2048]{1,0:T(8,128)(2,1)S(1)}, bf16[32,2048]{1,0:T(8,128)(2,1)S(1)}, u32[]{:S(2)}, u32[]{:S(2)}) collective-permute-start(bf16[32,2048]{1,0:T(8,128)(2,1)S(1)} %collective-permute-done.4.refs_6_), channel_id=1, source_target_pairs={{0,1},{1,0},{2,3},{3,2},{4,5},{5,4},{6,7},{7,6},{8,9},{9,8},{10,11... | collective-permute-start | bytes 393224 | tf_op jit(solution)/shard_map/ppermute | solution.py:297
  13.4 5.0 %collective-permute-start.7 = (bf16[32,2048]{1,0:T(8,128)(2,1)S(1)}, bf16[32,2048]{1,0:T(8,128)(2,1)S(1)}, u32[]{:S(2)}, u32[]{:S(2)}) collective-permute-start(bf16[32,2048]{1,0:T(8,128)(2,1)S(1)} %collective-permute-done.6.refs_8_), channel_id=1, source_target_pairs={{0,1},{1,0},{2,3},{3,2},{4,5},{5,4},{6,7},{7,6},{8,9},{9,8},{10,11... | collective-permute-start | bytes 393224 | tf_op jit(solution)/shard_map/ppermute | solution.py:297
  13.4 5.0 %collective-permute-start.9 = (bf16[32,2048]{1,0:T(8,128)(2,1)S(1)}, bf16[32,2048]{1,0:T(8,128)(2,1)S(1)}, u32[]{:S(2)}, u32[]{:S(2)}) collective-permute-start(bf16[32,2048]{1,0:T(8,128)(2,1)S(1)} %collective-permute-done.8.refs_10_), channel_id=1, source_target_pairs={{0,1},{1,0},{2,3},{3,2},{4,5},{5,4},{6,7},{7,6},{8,9},{9,8},{10,11... | collective-permute-start | bytes 393224 | tf_op jit(solution)/shard_map/ppermute | solution.py:297
  13.9 4.5 %collective-permute-start.2 = (bf16[16,2048]{1,0:T(8,128)(2,1)S(1)}, bf16[16,2048]{1,0:T(8,128)(2,1)S(1)}, u32[]{:S(2)}, u32[]{:S(2)}) collective-permute-start(bf16[16,2048]{1,0:T(8,128)(2,1)S(1)} %get-tuple-element.18.refs_0_), channel_id=1, source_target_pairs={{0,24},{8,0},{16,8},{24,16},{1,25},{9,1},{17,9},{25,17},{2,26},{10... | collective-permute-start | bytes 196616 | tf_op jit(solution)/shard_map/ppermute | solution.py:290
  34.0 4.8 %collective-permute-start.10 = (bf16[16,2048]{1,0:T(8,128)(2,1)S(1)}, bf16[16,2048]{1,0:T(8,128)(2,1)S(1)}, u32[]{:S(2)}, u32[]{:S(2)}) collective-permute-start(bf16[16,2048]{1,0:T(8,128)(2,1)S(1)} %get-tuple-element.24), channel_id=1, source_target_pairs={{0,24},{8,0},{16,8},{24,16},{1,25},{9,1},{17,9},{25,17},{2,26},{10... | collective-permute-start | bytes 196616 | tf_op jit(solution)/shard_map/ppermute | solution.py:303
  35.8 7.1 %collective-permute-start.11 = (bf16[16,2048]{1,0:T(8,128)(2,1)S(1)}, bf16[16,2048]{1,0:T(8,128)(2,1)S(1)}, u32[]{:S(2)}, u32[]{:S(2)}) collective-permute-start(bf16[16,2048]{1,0:T(8,128)(2,1)S(1)} %get-tuple-element.25), channel_id=1, source_target_pairs={{0,16},{8,24},{16,0},{24,8},{1,17},{9,25},{17,1},{25,9},{2,18},{10... | collective-permute-start | bytes 196616 | tf_op jit(solution)/shard_map/ppermute | solution.py:303
  36.0 6.9 %collective-permute-start.12 = (bf16[16,2048]{1,0:T(8,128)(2,1)S(1)}, bf16[16,2048]{1,0:T(8,128)(2,1)S(1)}, u32[]{:S(2)}, u32[]{:S(2)}) collective-permute-start(bf16[16,2048]{1,0:T(8,128)(2,1)S(1)} %get-tuple-element.26), channel_id=1, source_target_pairs={{0,8},{8,16},{16,24},{24,0},{1,9},{9,17},{17,25},{25,1},{2,10},{10... | collective-permute-start | bytes 196616 | tf_op jit(solution)/shard_map/ppermute | solution.py:303
  43.8 5.0 %collective-permute-start.14 = (bf16[16,2048]{1,0:T(8,128)(2,1)S(1)}, bf16[16,2048]{1,0:T(8,128)(2,1)S(1)}, u32[]{:S(2)}, u32[]{:S(2)}) collective-permute-start(bf16[16,2048]{1,0:T(8,128)(2,1)S(1)} %multiply_convert_fusion.refs_0_), channel_id=1, source_target_pairs={{0,2},{1,3},{2,0},{3,1},{4,6},{5,7},{6,4},{7,5},{8,10},{9,11},{10,... | collective-permute-start | bytes 196616 | tf_op jit(solution)/shard_map/ppermute | solution.py:295
  46.4 4.8 %collective-permute-start.16 = (bf16[16,2048]{1,0:T(8,128)(2,1)S(1)}, bf16[16,2048]{1,0:T(8,128)(2,1)S(1)}, u32[]{:S(2)}, u32[]{:S(2)}) collective-permute-start(bf16[16,2048]{1,0:T(8,128)(2,1)S(1)} %multiply_convert_fusion.refs_0_), channel_id=1, source_target_pairs={{0,4},{1,5},{2,6},{3,7},{4,0},{5,1},{6,2},{7,3},{8,12},{9,13},{10,... | collective-permute-start | bytes 196616 | tf_op jit(solution)/shard_map/ppermute | solution.py:295
  47.6 5.2 %collective-permute-start.18 = (bf16[16,2048]{1,0:T(8,128)(2,1)S(1)}, bf16[16,2048]{1,0:T(8,128)(2,1)S(1)}, u32[]{:S(2)}, u32[]{:S(2)}) collective-permute-start(bf16[16,2048]{1,0:T(8,128)(2,1)S(1)} %multiply_convert_fusion.refs_0_), channel_id=1, source_target_pairs={{0,6},{1,7},{2,4},{3,5},{4,2},{5,3},{6,0},{7,1},{8,14},{9,15},{10,... | collective-permute-start | bytes 196616 | tf_op jit(solution)/shard_map/ppermute | solution.py:295
  48.3 4.5 %collective-permute-start.13 = (bf16[16,2048]{1,0:T(8,128)(2,1)S(1)}, bf16[16,2048]{1,0:T(8,128)(2,1)S(1)}, u32[]{:S(2)}, u32[]{:S(2)}) collective-permute-start(bf16[16,2048]{1,0:T(8,128)(2,1)S(1)} %multiply_convert_fusion.refs_0_), channel_id=1, source_target_pairs={{0,1},{1,0},{2,3},{3,2},{4,5},{5,4},{6,7},{7,6},{8,9},{9,8},{10,11... | collective-permute-start | bytes 196616 | tf_op jit(solution)/shard_map/ppermute | solution.py:297
  48.8 4.1 %collective-permute-start.15 = (bf16[16,2048]{1,0:T(8,128)(2,1)S(1)}, bf16[16,2048]{1,0:T(8,128)(2,1)S(1)}, u32[]{:S(2)}, u32[]{:S(2)}) collective-permute-start(bf16[16,2048]{1,0:T(8,128)(2,1)S(1)} %collective-permute-done.14.refs_2_), channel_id=1, source_target_pairs={{0,1},{1,0},{2,3},{3,2},{4,5},{5,4},{6,7},{7,6},{8,9},{9,8},{10,11... | collective-permute-start | bytes 196616 | tf_op jit(solution)/shard_map/ppermute | solution.py:297
  51.2 1.7 %collective-permute-start.17 = (bf16[16,2048]{1,0:T(8,128)(2,1)S(1)}, bf16[16,2048]{1,0:T(8,128)(2,1)S(1)}, u32[]{:S(2)}, u32[]{:S(2)}) collective-permute-start(bf16[16,2048]{1,0:T(8,128)(2,1)S(1)} %collective-permute-done.16.refs_4_), channel_id=1, source_target_pairs={{0,1},{1,0},{2,3},{3,2},{4,5},{5,4},{6,7},{7,6},{8,9},{9,8},{10,11... | collective-permute-start | bytes 196616 | tf_op jit(solution)/shard_map/ppermute | solution.py:297
  52.8 1.3 %collective-permute-start.19 = (bf16[16,2048]{1,0:T(8,128)(2,1)S(1)}, bf16[16,2048]{1,0:T(8,128)(2,1)S(1)}, u32[]{:S(2)}, u32[]{:S(2)}) collective-permute-start(bf16[16,2048]{1,0:T(8,128)(2,1)S(1)} %collective-permute-done.18.refs_6_), channel_id=1, source_target_pairs={{0,1},{1,0},{2,3},{3,2},{4,5},{5,4},{6,7},{7,6},{8,9},{9,8},{10,11... | collective-permute-start | bytes 196616 | tf_op jit(solution)/shard_map/ppermute | solution.py:297
  57.0 4.3 %collective-permute-start.20 = (bf16[16,2048]{1,0:T(8,128)(2,1)S(1)}, bf16[16,2048]{1,0:T(8,128)(2,1)S(1)}, u32[]{:S(2)}, u32[]{:S(2)}) collective-permute-start(bf16[16,2048]{1,0:T(8,128)(2,1)S(1)} %get-tuple-element.28), channel_id=1, source_target_pairs={{0,24},{8,0},{16,8},{24,16},{1,25},{9,1},{17,9},{25,17},{2,26},{10... | collective-permute-start | bytes 196616 | tf_op jit(solution)/shard_map/ppermute | solution.py:303
  57.8 7.9 %collective-permute-start.21 = (bf16[16,2048]{1,0:T(8,128)(2,1)S(1)}, bf16[16,2048]{1,0:T(8,128)(2,1)S(1)}, u32[]{:S(2)}, u32[]{:S(2)}) collective-permute-start(bf16[16,2048]{1,0:T(8,128)(2,1)S(1)} %get-tuple-element.29), channel_id=1, source_target_pairs={{0,16},{8,24},{16,0},{24,8},{1,17},{9,25},{17,1},{25,9},{2,18},{10... | collective-permute-start | bytes 196616 | tf_op jit(solution)/shard_map/ppermute | solution.py:303
  58.3 7.4 %collective-permute-start.22 = (bf16[16,2048]{1,0:T(8,128)(2,1)S(1)}, bf16[16,2048]{1,0:T(8,128)(2,1)S(1)}, u32[]{:S(2)}, u32[]{:S(2)}) collective-permute-start(bf16[16,2048]{1,0:T(8,128)(2,1)S(1)} %get-tuple-element.30), channel_id=1, source_target_pairs={{0,8},{8,16},{16,24},{24,0},{1,9},{9,17},{17,25},{25,1},{2,10},{10... | collective-permute-start | bytes 196616 | tf_op jit(solution)/shard_map/ppermute | solution.py:303

commit v4 on v3

v4 whole, which is shorter than its diff:
```python
import functools
import math

import jax
import jax.numpy as jnp
from jax import lax
from jax.experimental import pallas as pl
from jax.experimental.pallas import tpu as pltpu
from jax.sharding import PartitionSpec as P

BANDS = 16
BLK = 256
CAP = 2
GEO = 16
LANES = 128
KDIM = 48
APPLY_UNROLL = 8
SPARE = 8
KEEP_BYTES = 24 * 2**20
BF16 = jnp.bfloat16
F32 = jnp.float32

VMEM = functools.partial(pl.BlockSpec, memory_space=pltpu.VMEM)
SMEM = functools.partial(pl.BlockSpec, memory_space=pltpu.SMEM)


def split(value, terms):
    out = []
    for _ in range(terms):
        part = value.astype(BF16).astype(F32)
        out.append(part)
        value = value - part
    return out


def pack_kernel(pos_ref, nrm_ref, emi_ref, level_ref, table_ref, slot_ref, pay_ref, geo_ref, area_ref, rows):
    level = level_ref[...]
    area = jnp.zeros(level.shape, F32)
    for k in range(table_ref.shape[0]):
        area = jnp.where(level == k, table_ref[k], area)
    area_ref[...] = area
    p1, p2 = split(pos_ref[...], 2)
    n1, n2 = split(nrm_ref[...], 2)
    a1, a2 = split(area, 2)
    rows[0:3, :] = p1
    rows[3:6, :] = p2
    rows[6:7, :] = a1
    rows[7:8, :] = a2
    rows[8:11, :] = n1
    rows[11:14, :] = n2
    rows[14:16, :] = jnp.zeros((2, area.shape[1]), F32)
    peers = slot_ref.shape[-1]
    for t in range(2 * CAP):
        rows[14:15, t * LANES : t * LANES + peers] = slot_ref[t // 2, t % 2 : t % 2 + 1, :].astype(F32)
    geo = rows[...].astype(BF16)
    geo_ref[...] = geo
    pay_ref[0:GEO, :] = geo
    pay_ref[GEO:, :] = (area * emi_ref[...]).astype(BF16)


def terms_of(g):
    pos, nrm = g[0:8], g[8:16]
    row = lax.broadcasted_iota(jnp.int32, pos.shape, 0)
    p = pos + pltpu.roll(pos, 5, 0)
    n = nrm + pltpu.roll(nrm, 5, 0)
    half = 0.5 * (pos[6:7] + pos[7:8])
    pp = jnp.sum(jnp.where(row < 3, p * p, 0.0), axis=0, keepdims=True)
    dot = jnp.sum(jnp.where(row < 3, n * p, 0.0), axis=0, keepdims=True)
    return pos, nrm, row, split(pp + half, 3), split(-dot, 3), (math.pi - 1.0) * half


def column_features(g):
    pos, nrm, row, q, c, h = terms_of(g)
    zero = jnp.zeros(pos.shape, F32)
    one = jnp.where(row == 6, 1.0, zero)
    pos = jnp.where(row < 6, pos, one)
    nrm = jnp.where(row < 6, nrm, one)
    consts, areas = zero, zero
    for t, value in enumerate(q + c):
        consts = jnp.where(row == t, value, consts)
    for t, value in enumerate(split(h, 3)):
        areas = jnp.where(row == t, value, areas)
    return jnp.concatenate([pos, nrm, pos, nrm, consts, areas], axis=0)


def row_features(g):
    pos, nrm, row, q, c, h = terms_of(g)
    zero = jnp.zeros(pos.shape, F32)

    def both(x):
        high = jnp.where(row < 3, x, pltpu.roll(x, 3, 0))
        low = jnp.where(row < 3, pltpu.roll(x, 5, 0), x)
        return jnp.where(row < 6, high, 0.0), jnp.where(row < 6, low, 0.0)

    def with_last(x, value):
        return jnp.where(row == 6, value, x)

    p_hi, p_lo = both(pos)
    n_hi, n_lo = both(nrm)
    facing = [with_last(n_hi, c[0]), with_last(zero, c[1]), with_last(n_lo, c[2]), zero, zero, zero]
    seen = [zero, p_hi, zero, p_lo, jnp.where((row >= 3) & (row < 6), 1.0, zero), zero]
    near = [
        with_last(-2.0 * p_hi, q[0]),
        with_last(zero, q[1]),
        with_last(-2.0 * p_lo, q[2]),
        zero,
        jnp.where(row < 3, 1.0, zero),
        zero,
    ]
    return [jnp.concatenate(parts, axis=0).astype(BF16) for parts in (facing, seen, near)], h


def sections(nz, ny):
    one = ny * 2 * CAP
    second = (nz - 1) * one + SPARE
    return second, second + one + SPARE


def list_pairs(nz, ny, nb, place_ref, slots, pairs):
    z, k = place_ref[0], place_ref[1]
    second, numbers = sections(nz, ny)

    def peer(s, m, count):
        zs = lax.rem(z - s + nz, nz)
        own = z * ny + jnp.bitwise_xor(k, m)
        served = zs * ny + k
        for t in range(CAP):
            row, col = slots[s, 2 * t * LANES + own], slots[s, (2 * t + 1) * LANES + own]
            pairs[count] = (s * nb + row) * 4096 + m * nb + col
            count = count + (row >= 0).astype(jnp.int32)
            col, row = slots[nz + m, 2 * t * LANES + served], slots[nz + m, (2 * t + 1) * LANES + served]
            pairs[count] = (s * nb + row) * 4096 + m * nb + col
            count = count + (row >= 0).astype(jnp.int32)
        return count

    for section, (start, lines) in enumerate(((0, range(1, nz)), (second, range(1)))):
        count = jnp.int32(start)
        for s in lines:
            if ny <= 8:
                for m in range(ny):
                    count = peer(s, m, count)
            else:
                count = lax.fori_loop(0, ny, functools.partial(peer, s), count)
        for t in range(SPARE):
            pairs[count + t] = nz * nb * 4096
        pairs[numbers + section] = count - start


def feature_scratch(nz, ny, nb):
    return [
        pltpu.VMEM((nz * nb, 3, KDIM, BLK), BF16),
        pltpu.VMEM((nz * nb, 1, BLK), F32),
        pltpu.VMEM((ny * nb, BLK, KDIM), BF16),
        pltpu.VMEM((ny * nb, BLK, LANES), F32),
        pltpu.VMEM((ny * nb, BANDS, BLK), BF16),
    ]


def own_scratch(nz, ny, nb):
    devices = -(-(nz + ny) // 8) * 8
    return [
        pltpu.VMEM((nz * nb + 1, BANDS, BLK), F32),
        pltpu.VMEM((devices, 2 * CAP * LANES), jnp.int32),
        pltpu.SMEM((devices, 2 * CAP * LANES), jnp.int32),
        pltpu.SemaphoreType.DMA,
    ]


def put_out(nb, acc, out_refs, first):
    for s, out in enumerate(out_refs):
        for b in range(nb):
            out[:, b * BLK : (b + 1) * BLK] = acc[(first + s) * nb + b].astype(out.dtype)


def prepare(nz, ny, nb, place_ref, geos, pays, fluxes, pairs, features, acc, slots_v, slots, sem):
    row_feat, row_area, col_feat, col_area, flux = features
    width = slots.shape[1]
    for s in range(nz):
        g = geos[s][...].astype(F32)
        slots_v[s : s + 1, :] = g[14:15, :width].astype(jnp.int32)
    for m in range(ny):
        g = pays[m][0:GEO, :].astype(F32)
        slots_v[nz + m : nz + m + 1, :] = g[14:15, :width].astype(jnp.int32)
    copy = pltpu.make_async_copy(slots_v, slots, sem)
    copy.start()
    for s in range(nz):
        forms, h = row_features(geos[s][...].astype(F32))
        for b in range(nb):
            here = slice(b * BLK, (b + 1) * BLK)
            row_area[s * nb + b] = h[:, here]
            for v in range(3):
                row_feat[s * nb + b, v] = forms[v][:, here]
    acc[...] = jnp.zeros(acc.shape, F32)
    copy.wait()
    list_pairs(nz, ny, nb, place_ref, slots, pairs)
    depth = lax.broadcasted_iota(jnp.int32, (KDIM, LANES), 0)
    pick = jnp.where((depth >= 40) & (depth < 43), 1.0, 0.0).astype(BF16)
    for m in range(ny):
        feat = column_features(pays[m][0:GEO, :].astype(F32)).astype(BF16)
        for b in range(nb):
            here = slice(b * BLK, (b + 1) * BLK)
            turned = jnp.transpose(feat[:, here])
            col_feat[m * nb + b] = turned
            col_area[m * nb + b] = jnp.dot(turned, pick, preferred_element_type=F32)
            flux[m * nb + b] = fluxes[m][:, here] if fluxes else pays[m][GEO:, here]


def tile_of(code, last, features):
    row_feat, row_area, col_feat, col_area, _ = features
    rb, cb = jnp.minimum(code // 4096, last), code % 4096
    left = col_feat[cb]
    f, s, q = (jnp.dot(left, row_feat[rb, v], preferred_element_type=F32) for v in range(3))
    area = col_area[cb]
    area = jnp.concatenate([area] * (BLK // LANES), axis=1) + row_area[rb]
    top = jnp.maximum(f, 0.0) * jnp.maximum(s, 0.0)
    return (top * pltpu.reciprocal(q * (math.pi * q - area), approx=True)).astype(BF16)


def form_tiles(unroll, first, count, last, pairs, features, tiles):
    def some(t, carry):
        for u in range(unroll):
            tiles[t * unroll + u] = tile_of(pairs[first + t * unroll + u], last, features)
        return carry

    lax.fori_loop(0, (count + unroll - 1) // unroll, some, 0)


def apply_tiles(first, count, spare, pairs, tiles, flux, acc):
    def some(t, carry):
        sums = []
        for u in range(APPLY_UNROLL):
            code = pairs[first + t * APPLY_UNROLL + u]
            tile = tiles[t * APPLY_UNROLL + u]
            sums.append((code // 4096, jnp.dot(flux[code % 4096], tile, preferred_element_type=F32)))
        for rb, total in sums:
            acc[jnp.minimum(rb, spare)] += total
        return carry

    lax.fori_loop(0, (count + APPLY_UNROLL - 1) // APPLY_UNROLL, some, 0)


def far_kernel(nz, ny, nb, place_ref, *refs):
    geos, pays, refs = refs[:nz], refs[nz : nz + ny], refs[nz + ny :]
    outs, refs = refs[: nz - 1], refs[nz - 1 :]
    tiles, pairs, features, own = refs[0], refs[1], refs[2:7], refs[7:]
    acc = own[0]
    _, numbers = sections(nz, ny)
    prepare(nz, ny, nb, place_ref, geos, pays, None, pairs, features, *own)
    count = pairs[numbers]
    form_tiles(8, 0, count, nz * nb - 1, pairs, features, tiles)
    apply_tiles(0, count, nz * nb, pairs, tiles, features[4], acc)
    put_out(nb, acc, outs, 1)


def near_kernel(nz, ny, nb, pairs, *refs):
    features, out, tiles, acc = refs[:5], refs[5], refs[6], refs[7]
    second, numbers = sections(nz, ny)
    count = pairs[numbers + 1]
    acc[...] = jnp.zeros(acc.shape, F32)
    form_tiles(4, second, count, nb - 1, pairs, features, tiles)
    apply_tiles(second, count, nb, pairs, tiles, features[4], acc)
    put_out(nb, acc, [out], 0)


def apply_kernel(nz, ny, nb, pairs, far_ref, near_ref, *refs):
    fluxes, refs = refs[:ny], refs[ny:]
    outs, refs = refs[:nz], refs[nz:]
    flux, acc = refs
    second, numbers = sections(nz, ny)
    for m in range(ny):
        for b in range(nb):
            flux[m * nb + b] = fluxes[m][:, b * BLK : (b + 1) * BLK]
    acc[...] = jnp.zeros(acc.shape, F32)
    apply_tiles(0, pairs[numbers], nz * nb, pairs, far_ref, flux, acc)
    apply_tiles(second, pairs[numbers + 1], nz * nb, pairs, near_ref, flux, acc)
    put_out(nb, acc, outs, 0)


def whole_kernel(nz, ny, nb, fresh, place_ref, *refs):
    geos, pays, refs = refs[:nz], refs[nz : nz + ny], refs[nz + ny :]
    fluxes, refs = (refs[:ny], refs[ny:]) if fresh else (None, refs)
    outs, features, own, pairs = refs[:nz], refs[nz : nz + 5], refs[nz + 5 : -1], refs[-1]
    acc, flux = own[0], features[4]
    second, numbers = sections(nz, ny)
    prepare(nz, ny, nb, place_ref, geos, pays, fluxes, pairs, features, *own)
    for section, start in enumerate((0, second)):

        def one(t, carry):
            code = pairs[start + t]
            tile = tile_of(code, nz * nb - 1, features)
            acc[code // 4096] += jnp.dot(flux[code % 4096], tile, preferred_element_type=F32)
            return carry

        lax.fori_loop(0, pairs[numbers + section], one, 0)
    put_out(nb, acc, outs, 0)


def per_device(nz, ny, positions, normals, emission, material, area_level, reflect_table, area_table, pair_slots):
    patches = positions.shape[1]
    nb = patches // BLK
    second, numbers = sections(nz, ny)
    keep = numbers * BLK * BLK * 2 <= KEEP_BYTES
    place = jnp.stack([lax.axis_index("gx"), lax.axis_index("gy")]).astype(jnp.int32)

    def call(kernel, name, megabytes, ins, outs, scratch, args):
        scalar = [getattr(x, "memory_space", None) == pltpu.SMEM for x in outs]
        spaces = [SMEM() if s else VMEM() for s in scalar]
        outs = [jax.ShapeDtypeStruct(x.shape, x.dtype) if s else x for x, s in zip(outs, scalar)]
        return pl.pallas_call(
            kernel,
            out_shape=tuple(outs),
            in_specs=ins,
            out_specs=tuple(spaces),
            scratch_shapes=scratch,
            compiler_params=megabytes and pltpu.CompilerParams(vmem_limit_bytes=megabytes * 2**20),
            name=name,
        )(*args)

    payload, geo, area = call(
        pack_kernel,
        "pack",
        None,
        [VMEM()] * 4 + [SMEM(), VMEM()],
        [
            pltpu.VMEM((GEO + BANDS, patches), BF16),
            pltpu.VMEM((GEO, patches), BF16),
            jax.ShapeDtypeStruct((1, patches), F32),
        ],
        [pltpu.VMEM((GEO, patches), F32)],
        (
            positions,
            normals,
            emission,
            area_level.reshape(1, patches),
            area_table,
            jnp.transpose(pair_slots[0], (1, 2, 0)),
        ),
    )

    def along(x):
        return [lax.ppermute(x, "gx", [(i, (i + s) % nz) for i in range(nz)]) for s in range(1, nz)]

    def plane(x):
        got = {0: x}
        for m in range(2, ny, 2):
            got[m] = lax.ppermute(x, "gy", [(i, i ^ m) for i in range(ny)])
        for m in range(0, ny, 2):
            got[m + 1] = lax.ppermute(got[m], "gy", [(i, i ^ 1) for i in range(ny)])
        return [got[m] for m in range(ny)]

    def sent(parts):
        return [
            lax.ppermute(part, "gx", [(i, (i - s) % nz) for i in range(nz)])
            for s, part in enumerate(parts, 1)
        ]

    def total(own, parts):
        for part in parts:
            own = own + part.astype(F32)
        return own

    own_part = jax.ShapeDtypeStruct((BANDS, patches), F32)
    far_parts = [jax.ShapeDtypeStruct((BANDS, patches), BF16)] * (nz - 1)
    features, own = feature_scratch(nz, ny, nb), own_scratch(nz, ny, nb)
    acc = own[0]
    pairs_list = pltpu.SMEM((numbers + 2,), jnp.int32)

    kind_hot = (
        material[None, :] == jnp.arange(reflect_table.shape[0], dtype=jnp.int32)[:, None]
    ).astype(F32)
    reflect = jnp.dot(jnp.transpose(reflect_table), kind_hot, precision=lax.Precision.HIGHEST)

    rows = [geo] + along(geo)
    cols = plane(payload)

    def whole(fluxes):
        got = call(
            functools.partial(whole_kernel, nz, ny, nb, bool(fluxes)),
            "whole",
            60,
            [SMEM()] + [VMEM()] * (nz + ny + len(fluxes)),
            [own_part] + far_parts,
            features + own + [pairs_list],
            (place, *rows, *cols, *fluxes),
        )
        return total(got[0], sent(got[1:]))

    if keep:
        got = call(
            functools.partial(far_kernel, nz, ny, nb),
            "far",
            16,
            [SMEM()] + [VMEM()] * (nz + ny),
            far_parts + [pltpu.VMEM((second, BLK, BLK), BF16), pairs_list] + features,
            own,
            (place, *rows, *cols),
        )
        returned = sent(got[: nz - 1])
        far_tiles, pairs, *kept = got[nz - 1 :]
        own_sum, near_tiles = call(
            functools.partial(near_kernel, nz, ny, nb),
            "near",
            8,
            [SMEM()] + [VMEM()] * 5,
            [own_part, pltpu.VMEM((numbers - second, BLK, BLK), BF16)],
            [pltpu.VMEM((nb + 1, BANDS, BLK), F32)],
            (pairs, *kept),
        )
        irradiation = total(own_sum, returned)
    else:
        irradiation = whole([])
    radiosity = emission + reflect * irradiation
    fluxes = plane((area * radiosity).astype(BF16))
    if keep:
        got = call(
            functools.partial(apply_kernel, nz, ny, nb),
            "apply",
            4,
            [SMEM()] + [VMEM()] * (2 + ny),
            [own_part] + far_parts,
            [features[4], acc],
            (pairs, far_tiles, near_tiles, *fluxes),
        )
        irradiation = total(got[0], sent(got[1:]))
    else:
        irradiation = whole(fluxes)
    return emission + reflect * irradiation


def solution(mesh):
    nz, ny = mesh.shape["gx"], mesh.shape["gy"]
    both = ("gx", "gy")
    placed = (
        P(None, both),
        P(None, both),
        P(None, both),
        P(both),
        P(both),
        P(),
        P(),
        P(both, None, None, None),
    )
    return jax.shard_map(
        functools.partial(per_device, nz, ny),
        mesh=mesh,
        in_specs=placed,
        out_specs=P(None, both),
        check_vma=False,
    )
```

time: 67.2 us -> 65.7 us (0.978); the launches traced: 66.4 us -> 65.8 us
  starting transfers between devices: 24.5 us -> 27.1 us
  waiting for transfers between devices: 19 us -> 17.7 us
  Pallas kernels: 20.2 us -> 19.1 us
  other arithmetic: 1.73 us -> 0.84 us
    ppermute x6, starting transfers between devices: 7.09 us -> 10.7 us  [sent(): lax.ppermute(part, 'gx', [(i, (i - s) % nz) for i in range(nz)])]
    pallas_call x3 -> x4, Pallas kernels: 20.2 us -> 19.1 us  [call(): pl.pallas_call(kernel, out_shape=tuple(outs), in_specs=ins, out_specs=tup...]
    convert_element_type x1, other arithmetic: 0.96 us -> 0.06 us  [per_device(): fluxes = plane((area * radiosity).astype(BF16))]
    ppermute x6, starting transfers between devices: 9.02 us -> 8.19 us  [plane(): got[m] = lax.ppermute(x, 'gy', [(i, i ^ m) for i in range(ny)])]
  transfers between devices with their start and end apart: 23 -> 23, of which waited for: 9 -> 9; matrix products, arithmetic and copies ran while one was open for 2% -> 2% of each run, Pallas kernels for 0% -> 4%
where the time goes in v4:
time: 65.7 us; the launch traced here: 65.8 us
  starting transfers between devices  27.1 us (41%)
  Pallas kernels  19.1 us (29%)
  waiting for transfers between devices  17.7 us (27%)
  matrix products  0.95 us (1%)
  other arithmetic  0.84 us (1%)
    pallas_call x4, Pallas kernels, call(): pl.pallas_call(kernel, out_shape=tuple(outs), in_specs=ins, out_specs=tup...  19.1 us
    ppermute x6, starting transfers between devices, sent(): lax.ppermute(part, 'gx', [(i, (i - s) % nz) for i in range(nz)])  10.7 us
    ppermute x6, waiting for transfers between devices, sent(): lax.ppermute(part, 'gx', [(i, (i - s) % nz) for i in range(nz)])  8.75 us
    ppermute x6, starting transfers between devices, plane(): got[m] = lax.ppermute(x, 'gy', [(i, i ^ m) for i in range(ny)])  8.19 us
    ppermute x3, starting transfers between devices, along(): lax.ppermute(x, 'gx', [(i, (i + s) % nz) for i in range(nz)])  7.23 us
    ppermute x3, waiting for transfers between devices, along(): lax.ppermute(x, 'gx', [(i, (i + s) % nz) for i in range(nz)])  3.94 us
    ppermute x6, waiting for transfers between devices, plane(): got[m] = lax.ppermute(x, 'gy', [(i, i ^ m) for i in range(ny)])  3.78 us
  transfers between devices with their start and end apart: 23, of which 9 were waited for; matrix products, arithmetic and copies ran while one was open for 2% of the time, Pallas kernels for 4%

profile of v4, /device:TPU:0, one launch (start us, length us, event | category | flops | bytes accessed | tf_op | source)
XLA Modules:
  0.0 65.8 jit_solution(10889634234887847649)
XLA Ops:
  0.0 1.6 %pack.1 = (bf16[32,2048]{1,0:T(8,128)(2,1)S(1)}, bf16[16,2048]{1,0:T(8,128)(2,1)S(1)}, f32[1,2048]{1,0:T(1,128)}) custom-call(f32[3,2048]{1,0:T(4,128)} %pos_ref.1, f32[3,2048]{1,0:T(4,128)} %nrm_ref.1, f32[16,2048]{1,0:T(8,128)} %emi_ref.1, s32[1,2048]{1,0:T(1,128)} %bitcast.10, f32[8]{0:T(128)} %table_ref.1, s32[2,2,32]{2,1,0:T(2,128)} %bitcast.12), custom_call_target="tpu_custom_call" | custom-call | tf_op jit(solution)/shard_map/pack/pallas_call | solution.py:309
  1.6 2.9 %collective-permute-start.4 = (bf16[32,2048]{1,0:T(8,128)(2,1)S(1)}, bf16[32,2048]{1,0:T(8,128)(2,1)S(1)}, u32[]{:S(2)}, u32[]{:S(2)}) collective-permute-start(bf16[32,2048]{1,0:T(8,128)(2,1)S(1)} %get-tuple-element.25.refs_4_), channel_id=1, source_target_pairs={{0,2},{1,3},{2,0},{3,1},{4,6},{5,7},{6,4},{7,5},{8,10},{9,11},{10,... | collective-permute-start | bytes 393224 | tf_op jit(solution)/shard_map/ppermute | solution.py:346
  4.5 1.5 %collective-permute-start.6 = (bf16[32,2048]{1,0:T(8,128)(2,1)S(1)}, bf16[32,2048]{1,0:T(8,128)(2,1)S(1)}, u32[]{:S(2)}, u32[]{:S(2)}) collective-permute-start(bf16[32,2048]{1,0:T(8,128)(2,1)S(1)} %get-tuple-element.25.refs_4_), channel_id=1, source_target_pairs={{0,4},{1,5},{2,6},{3,7},{4,0},{5,1},{6,2},{7,3},{8,12},{9,13},{10,... | collective-permute-start | bytes 393224 | tf_op jit(solution)/shard_map/ppermute | solution.py:346
  6.1 0.0 collective-permute-start.8
  6.1 2.1 %collective-permute-start = (bf16[16,2048]{1,0:T(8,128)(2,1)S(1)}, bf16[16,2048]{1,0:T(8,128)(2,1)S(1)}, u32[]{:S(2)}, u32[]{:S(2)}) collective-permute-start(bf16[16,2048]{1,0:T(8,128)(2,1)S(1)} %get-tuple-element.24.refs_0_), channel_id=1, source_target_pairs={{0,8},{8,16},{16,24},{24,0},{1,9},{9,17},{17,25},{25,1},{2,10},{10... | collective-permute-start | bytes 196616 | tf_op jit(solution)/shard_map/ppermute | solution.py:341
  8.1 2.6 %collective-permute-start.1 = (bf16[16,2048]{1,0:T(8,128)(2,1)S(1)}, bf16[16,2048]{1,0:T(8,128)(2,1)S(1)}, u32[]{:S(2)}, u32[]{:S(2)}) collective-permute-start(bf16[16,2048]{1,0:T(8,128)(2,1)S(1)} %get-tuple-element.24.refs_0_), channel_id=1, source_target_pairs={{0,16},{8,24},{16,0},{24,8},{1,17},{9,25},{17,1},{25,9},{2,18},{10... | collective-permute-start | bytes 196616 | tf_op jit(solution)/shard_map/ppermute | solution.py:341
  10.7 2.1 %collective-permute-done.refs_1_ = bf16[16,2048]{1,0:T(8,128)(2,1)S(1)} collective-permute-done((bf16[16,2048]{1,0:T(8,128)(2,1)S(1)}, bf16[16,2048]{1,0:T(8,128)(2,1)S(1)}, u32[]{:S(2)}, u32[]{:S(2)}) %collective-permute-start) | collective-permute-done | bytes 65568 | tf_op jit(solution)/shard_map/ppermute | solution.py:341
  12.8 0.0 collective-permute-start.3
  12.8 0.0 collective-permute-done.4.refs_6_
  12.8 0.5 collective-permute-start.5
  13.3 0.0 collective-permute-done.6.refs_8_
  13.3 0.1 collective-permute-start.7
  13.4 0.0 collective-permute-done.8.refs_10_
  13.4 0.4 collective-permute-start.9
  13.8 0.0 collective-permute-done.1.refs_2_
  13.8 2.6 %collective-permute-start.2 = (bf16[16,2048]{1,0:T(8,128)(2,1)S(1)}, bf16[16,2048]{1,0:T(8,128)(2,1)S(1)}, u32[]{:S(2)}, u32[]{:S(2)}) collective-permute-start(bf16[16,2048]{1,0:T(8,128)(2,1)S(1)} %get-tuple-element.24.refs_0_), channel_id=1, source_target_pairs={{0,24},{8,0},{16,8},{24,16},{1,25},{9,1},{17,9},{25,17},{2,26},{10... | collective-permute-start | bytes 196616 | tf_op jit(solution)/shard_map/ppermute | solution.py:341
  16.4 0.1 pad_add_fusion.place_ref
  16.5 1.8 %collective-permute-done.2.refs_3_ = bf16[16,2048]{1,0:T(8,128)(2,1)S(1)} collective-permute-done((bf16[16,2048]{1,0:T(8,128)(2,1)S(1)}, bf16[16,2048]{1,0:T(8,128)(2,1)S(1)}, u32[]{:S(2)}, u32[]{:S(2)}) %collective-permute-start.2) | collective-permute-done | bytes 65568 | tf_op jit(solution)/shard_map/ppermute | solution.py:341
  18.3 0.0 collective-permute-done.5.refs_7_
  18.3 0.0 collective-permute-done.7.refs_9_
  18.4 11.9 %far.1 = (bf16[16,2048]{1,0:T(8,128)(2,1)S(1)}, bf16[16,2048]{1,0:T(8,128)(2,1)S(1)}, bf16[16,2048]{1,0:T(8,128)(2,1)S(1)}, bf16[104,256,256]{2,1,0:T(8,128)(2,1...) custom-call(s32[2]{0:T(128)S(1)} %pad_add_fusion.place_ref, ...), custom_call_target="tpu_custom_call" | custom-call | tf_op jit(solution)/shard_map/far/pallas_call | solution.py:309
  30.3 5.5 %collective-permute-start.10 = (bf16[16,2048]{1,0:T(8,128)(2,1)S(1)}, bf16[16,2048]{1,0:T(8,128)(2,1)S(1)}, u32[]{:S(2)}, u32[]{:S(2)}) collective-permute-start(bf16[16,2048]{1,0:T(8,128)(2,1)S(1)} %get-tuple-element.36), channel_id=1, source_target_pairs={{0,24},{8,0},{16,8},{24,16},{1,25},{9,1},{17,9},{25,17},{2,26},{10... | collective-permute-start | bytes 196616 | tf_op jit(solution)/shard_map/ppermute | solution.py:353
  35.8 0.0 collective-permute-start.11
  35.8 0.6 collective-permute-start.12
  36.4 0.9 %convolution_bitcast_fusion = f32[16,2048]{1,0:T(8,128)S(1)} fusion(f32[8,16]{1,0:T(8,128)S(1)} %copy-done, s32[2048]{0:T(1024)} %param.11), kind=kOutput, calls=%fused_computation | convolution fusion | flops 3162112 | bytes 139776 | tf_op jit(solution)/shard_map/dot_general | solution.py:371
  37.4 0.0 copy-start.1
  37.4 0.0 copy-start.2
  37.4 2.9 %near.1 = (f32[16,2048]{1,0:T(8,128)S(1)}, bf16[40,256,256]{2,1,0:T(8,128)(2,1)S(1)}) custom-call(s32[146]{0:T(256)S(1)} %get-tuple-element.26.pairs, bf16[32,3,48,256]{3,2,1,0:T(8,128)(2,1)S(1)} %get-tuple-element.28.refs_0_, f32[32,1,256]{2,1,0:T(1,128)S(1)} %get-tuple-element.29.refs_1_, bf16[64,256,48]{2,1,0:T(8,128)(2,1)S(1)} %get-tuple-element.30.refs_2_, ...), custom_call_target="tpu_custom_call" | custom-call | tf_op jit(solution)/shard_map/near/pallas_call | solution.py:309
  40.3 2.1 %collective-permute-done.11 = bf16[16,2048]{1,0:T(8,128)(2,1)S(1)} collective-permute-done((bf16[16,2048]{1,0:T(8,128)(2,1)S(1)}, bf16[16,2048]{1,0:T(8,128)(2,1)S(1)}, u32[]{:S(2)}, u32[]{:S(2)}) %collective-permute-start.11) | collective-permute-done | bytes 65568 | tf_op jit(solution)/shard_map/ppermute | solution.py:353
  42.4 0.0 collective-permute-done.12
  42.4 0.1 multiply_convert_fusion.refs_0_
  42.5 1.5 %collective-permute-start.14 = (bf16[16,2048]{1,0:T(8,128)(2,1)S(1)}, bf16[16,2048]{1,0:T(8,128)(2,1)S(1)}, u32[]{:S(2)}, u32[]{:S(2)}) collective-permute-start(bf16[16,2048]{1,0:T(8,128)(2,1)S(1)} %multiply_convert_fusion.refs_0_), channel_id=1, source_target_pairs={{0,2},{1,3},{2,0},{3,1},{4,6},{5,7},{6,4},{7,5},{8,10},{9,11},{10,... | collective-permute-start | bytes 196616 | tf_op jit(solution)/shard_map/ppermute | solution.py:346
  44.0 0.8 %collective-permute-start.16 = (bf16[16,2048]{1,0:T(8,128)(2,1)S(1)}, bf16[16,2048]{1,0:T(8,128)(2,1)S(1)}, u32[]{:S(2)}, u32[]{:S(2)}) collective-permute-start(bf16[16,2048]{1,0:T(8,128)(2,1)S(1)} %multiply_convert_fusion.refs_0_), channel_id=1, source_target_pairs={{0,4},{1,5},{2,6},{3,7},{4,0},{5,1},{6,2},{7,3},{8,12},{9,13},{10,... | collective-permute-start | bytes 196616 | tf_op jit(solution)/shard_map/ppermute | solution.py:346
  44.8 1.4 %collective-permute-start.18 = (bf16[16,2048]{1,0:T(8,128)(2,1)S(1)}, bf16[16,2048]{1,0:T(8,128)(2,1)S(1)}, u32[]{:S(2)}, u32[]{:S(2)}) collective-permute-start(bf16[16,2048]{1,0:T(8,128)(2,1)S(1)} %multiply_convert_fusion.refs_0_), channel_id=1, source_target_pairs={{0,6},{1,7},{2,4},{3,5},{4,2},{5,3},{6,0},{7,1},{8,14},{9,15},{10,... | collective-permute-start | bytes 196616 | tf_op jit(solution)/shard_map/ppermute | solution.py:346
  46.2 0.6 collective-permute-done.14.refs_2_
  46.8 0.0 collective-permute-start.15
  46.8 1.8 %collective-permute-done.16.refs_4_ = bf16[16,2048]{1,0:T(8,128)(2,1)S(1)} collective-permute-done((bf16[16,2048]{1,0:T(8,128)(2,1)S(1)}, bf16[16,2048]{1,0:T(8,128)(2,1)S(1)}, u32[]{:S(2)}, u32[]{:S(2)}) %collective-permute-start.16) | collective-permute-done | bytes 65568 | tf_op jit(solution)/shard_map/ppermute | solution.py:346
  48.6 0.0 collective-permute-start.17
  48.6 1.4 %collective-permute-done.18.refs_6_ = bf16[16,2048]{1,0:T(8,128)(2,1)S(1)} collective-permute-done((bf16[16,2048]{1,0:T(8,128)(2,1)S(1)}, bf16[16,2048]{1,0:T(8,128)(2,1)S(1)}, u32[]{:S(2)}, u32[]{:S(2)}) %collective-permute-start.18) | collective-permute-done | bytes 65568 | tf_op jit(solution)/shard_map/ppermute | solution.py:346
  50.0 0.0 collective-permute-done.17.refs_5_
  50.0 1.2 %collective-permute-done.19.refs_7_ = bf16[16,2048]{1,0:T(8,128)(2,1)S(1)} collective-permute-done((bf16[16,2048]{1,0:T(8,128)(2,1)S(1)}, bf16[16,2048]{1,0:T(8,128)(2,1)S(1)}, u32[]{:S(2)}, u32[]{:S(2)}) %collective-permute-start.19) | collective-permute-done | bytes 65568 | tf_op jit(solution)/shard_map/ppermute | solution.py:348
  51.2 2.7 %apply.1 = (f32[16,2048]{1,0:T(8,128)S(1)}, bf16[16,2048]{1,0:T(8,128)(2,1)S(1)}, bf16[16,2048]{1,0:T(8,128)(2,1)S(1)}, bf16[16,2048]{1,0:T(8,128)(2,1)S(1)}) custom-call(s32[146]{0:T(256)S(1)} %get-tuple-element.26.pairs, bf16[104,256,256]{2,1,0:T(8,128)(2,1)S(1)} %get-tuple-element.27.far_ref, bf16[40,256,256]{2,1,0:T(8,128)(2,1)S(1)} %get-tuple-element.33.near_ref, ...), custom_call_target="tpu_custom_call" | custom-call | tf_op jit(solution)/shard_map/apply/pallas_call | solution.py:309
  53.9 3.1 %collective-permute-start.20 = (bf16[16,2048]{1,0:T(8,128)(2,1)S(1)}, bf16[16,2048]{1,0:T(8,128)(2,1)S(1)}, u32[]{:S(2)}, u32[]{:S(2)}) collective-permute-start(bf16[16,2048]{1,0:T(8,128)(2,1)S(1)} %get-tuple-element.40), channel_id=1, source_target_pairs={{0,24},{8,0},{16,8},{24,16},{1,25},{9,1},{17,9},{25,17},{2,26},{10... | collective-permute-start | bytes 196616 | tf_op jit(solution)/shard_map/ppermute | solution.py:353
  57.0 1.5 %collective-permute-start.21 = (bf16[16,2048]{1,0:T(8,128)(2,1)S(1)}, bf16[16,2048]{1,0:T(8,128)(2,1)S(1)}, u32[]{:S(2)}, u32[]{:S(2)}) collective-permute-start(bf16[16,2048]{1,0:T(8,128)(2,1)S(1)} %get-tuple-element.41), channel_id=1, source_target_pairs={{0,16},{8,24},{16,0},{24,8},{1,17},{9,25},{17,1},{25,9},{2,18},{10... | collective-permute-start | bytes 196616 | tf_op jit(solution)/shard_map/ppermute | solution.py:353
  58.5 0.0 collective-permute-start.22
  58.5 1.2 %collective-permute-done.20 = bf16[16,2048]{1,0:T(8,128)(2,1)S(1)} collective-permute-done((bf16[16,2048]{1,0:T(8,128)(2,1)S(1)}, bf16[16,2048]{1,0:T(8,128)(2,1)S(1)}, u32[]{:S(2)}, u32[]{:S(2)}) %collective-permute-start.20) | collective-permute-done | bytes 65568 | tf_op jit(solution)/shard_map/ppermute | solution.py:353
  59.7 5.4 %collective-permute-done.21 = bf16[16,2048]{1,0:T(8,128)(2,1)S(1)} collective-permute-done((bf16[16,2048]{1,0:T(8,128)(2,1)S(1)}, bf16[16,2048]{1,0:T(8,128)(2,1)S(1)}, u32[]{:S(2)}, u32[]{:S(2)}) %collective-permute-start.21) | collective-permute-done | bytes 65568 | tf_op jit(solution)/shard_map/ppermute | solution.py:353
  65.1 0.7 %multiply_add_fusion = f32[16,2048]{1,0:T(8,128)} fusion(f32[16,2048]{1,0:T(8,128)S(1)} %copy-done.1, f32[16,2048]{1,0:T(8,128)S(1)} %convolution_bitcast_fusion, bf16[16,2048]{1,0:T(8,128)(2,1)S(1)} %collective-permute-done.22, bf16[16,2048]{1,0:T(8,128)(2,1)S(1)} %collective-permute-done.21, f32[16,2048]{1,0:T(8,128)S(1)} %get-tuple-element.39, ...), kind=kLoop, calls=%fused_computation.1 | loop fusion | flops 262144 | bytes 720896 | tf_op jit(solution)/shard_map/add | solution.py:427
  (12 shorter events, 0.0 us)
Async XLA Ops:
  0.0 36.4 %copy-start = (f32[8,16]{1,0:T(8,128)S(1)}, f32[8,16]{1,0:T(8,128)}, u32[]{:S(2)}) copy-start(f32[8,16]{1,0:T(8,128)} %param.13) | copy-start | bytes 1540
  1.6 11.2 %collective-permute-start.4 = (bf16[32,2048]{1,0:T(8,128)(2,1)S(1)}, bf16[32,2048]{1,0:T(8,128)(2,1)S(1)}, u32[]{:S(2)}, u32[]{:S(2)}) collective-permute-start(bf16[32,2048]{1,0:T(8,128)(2,1)S(1)} %get-tuple-element.25.refs_4_), channel_id=1, source_target_pairs={{0,2},{1,3},{2,0},{3,1},{4,6},{5,7},{6,4},{7,5},{8,10},{9,11},{10,... | collective-permute-start | bytes 393224 | tf_op jit(solution)/shard_map/ppermute | solution.py:346
  4.5 8.8 %collective-permute-start.6 = (bf16[32,2048]{1,0:T(8,128)(2,1)S(1)}, bf16[32,2048]{1,0:T(8,128)(2,1)S(1)}, u32[]{:S(2)}, u32[]{:S(2)}) collective-permute-start(bf16[32,2048]{1,0:T(8,128)(2,1)S(1)} %get-tuple-element.25.refs_4_), channel_id=1, source_target_pairs={{0,4},{1,5},{2,6},{3,7},{4,0},{5,1},{6,2},{7,3},{8,12},{9,13},{10,... | collective-permute-start | bytes 393224 | tf_op jit(solution)/shard_map/ppermute | solution.py:346
  6.1 7.3 %collective-permute-start.8 = (bf16[32,2048]{1,0:T(8,128)(2,1)S(1)}, bf16[32,2048]{1,0:T(8,128)(2,1)S(1)}, u32[]{:S(2)}, u32[]{:S(2)}) collective-permute-start(bf16[32,2048]{1,0:T(8,128)(2,1)S(1)} %get-tuple-element.25.refs_4_), channel_id=1, source_target_pairs={{0,6},{1,7},{2,4},{3,5},{4,2},{5,3},{6,0},{7,1},{8,14},{9,15},{10,... | collective-permute-start | bytes 393224 | tf_op jit(solution)/shard_map/ppermute | solution.py:346
  6.1 6.8 %collective-permute-start = (bf16[16,2048]{1,0:T(8,128)(2,1)S(1)}, bf16[16,2048]{1,0:T(8,128)(2,1)S(1)}, u32[]{:S(2)}, u32[]{:S(2)}) collective-permute-start(bf16[16,2048]{1,0:T(8,128)(2,1)S(1)} %get-tuple-element.24.refs_0_), channel_id=1, source_target_pairs={{0,8},{8,16},{16,24},{24,0},{1,9},{9,17},{17,25},{25,1},{2,10},{10... | collective-permute-start | bytes 196616 | tf_op jit(solution)/shard_map/ppermute | solution.py:341
  8.1 5.7 %collective-permute-start.1 = (bf16[16,2048]{1,0:T(8,128)(2,1)S(1)}, bf16[16,2048]{1,0:T(8,128)(2,1)S(1)}, u32[]{:S(2)}, u32[]{:S(2)}) collective-permute-start(bf16[16,2048]{1,0:T(8,128)(2,1)S(1)} %get-tuple-element.24.refs_0_), channel_id=1, source_target_pairs={{0,16},{8,24},{16,0},{24,8},{1,17},{9,25},{17,1},{25,9},{2,18},{10... | collective-permute-start | bytes 196616 | tf_op jit(solution)/shard_map/ppermute | solution.py:341
  12.8 5.5 %collective-permute-start.3 = (bf16[32,2048]{1,0:T(8,128)(2,1)S(1)}, bf16[32,2048]{1,0:T(8,128)(2,1)S(1)}, u32[]{:S(2)}, u32[]{:S(2)}) collective-permute-start(bf16[32,2048]{1,0:T(8,128)(2,1)S(1)} %get-tuple-element.25.refs_4_), channel_id=1, source_target_pairs={{0,1},{1,0},{2,3},{3,2},{4,5},{5,4},{6,7},{7,6},{8,9},{9,8},{10,11... | collective-permute-start | bytes 393224 | tf_op jit(solution)/shard_map/ppermute | solution.py:348
  12.8 5.5 %collective-permute-start.5 = (bf16[32,2048]{1,0:T(8,128)(2,1)S(1)}, bf16[32,2048]{1,0:T(8,128)(2,1)S(1)}, u32[]{:S(2)}, u32[]{:S(2)}) collective-permute-start(bf16[32,2048]{1,0:T(8,128)(2,1)S(1)} %collective-permute-done.4.refs_6_), channel_id=1, source_target_pairs={{0,1},{1,0},{2,3},{3,2},{4,5},{5,4},{6,7},{7,6},{8,9},{9,8},{10,11... | collective-permute-start | bytes 393224 | tf_op jit(solution)/shard_map/ppermute | solution.py:348
  13.3 5.0 %collective-permute-start.7 = (bf16[32,2048]{1,0:T(8,128)(2,1)S(1)}, bf16[32,2048]{1,0:T(8,128)(2,1)S(1)}, u32[]{:S(2)}, u32[]{:S(2)}) collective-permute-start(bf16[32,2048]{1,0:T(8,128)(2,1)S(1)} %collective-permute-done.6.refs_8_), channel_id=1, source_target_pairs={{0,1},{1,0},{2,3},{3,2},{4,5},{5,4},{6,7},{7,6},{8,9},{9,8},{10,11... | collective-permute-start | bytes 393224 | tf_op jit(solution)/shard_map/ppermute | solution.py:348
  13.4 5.0 %collective-permute-start.9 = (bf16[32,2048]{1,0:T(8,128)(2,1)S(1)}, bf16[32,2048]{1,0:T(8,128)(2,1)S(1)}, u32[]{:S(2)}, u32[]{:S(2)}) collective-permute-start(bf16[32,2048]{1,0:T(8,128)(2,1)S(1)} %collective-permute-done.8.refs_10_), channel_id=1, source_target_pairs={{0,1},{1,0},{2,3},{3,2},{4,5},{5,4},{6,7},{7,6},{8,9},{9,8},{10,11... | collective-permute-start | bytes 393224 | tf_op jit(solution)/shard_map/ppermute | solution.py:348
  13.8 4.5 %collective-permute-start.2 = (bf16[16,2048]{1,0:T(8,128)(2,1)S(1)}, bf16[16,2048]{1,0:T(8,128)(2,1)S(1)}, u32[]{:S(2)}, u32[]{:S(2)}) collective-permute-start(bf16[16,2048]{1,0:T(8,128)(2,1)S(1)} %get-tuple-element.24.refs_0_), channel_id=1, source_target_pairs={{0,24},{8,0},{16,8},{24,16},{1,25},{9,1},{17,9},{25,17},{2,26},{10... | collective-permute-start | bytes 196616 | tf_op jit(solution)/shard_map/ppermute | solution.py:341
  30.3 10.0 %collective-permute-start.10 = (bf16[16,2048]{1,0:T(8,128)(2,1)S(1)}, bf16[16,2048]{1,0:T(8,128)(2,1)S(1)}, u32[]{:S(2)}, u32[]{:S(2)}) collective-permute-start(bf16[16,2048]{1,0:T(8,128)(2,1)S(1)} %get-tuple-element.36), channel_id=1, source_target_pairs={{0,24},{8,0},{16,8},{24,16},{1,25},{9,1},{17,9},{25,17},{2,26},{10... | collective-permute-start | bytes 196616 | tf_op jit(solution)/shard_map/ppermute | solution.py:353
  35.8 6.6 %collective-permute-start.11 = (bf16[16,2048]{1,0:T(8,128)(2,1)S(1)}, bf16[16,2048]{1,0:T(8,128)(2,1)S(1)}, u32[]{:S(2)}, u32[]{:S(2)}) collective-permute-start(bf16[16,2048]{1,0:T(8,128)(2,1)S(1)} %get-tuple-element.37), channel_id=1, source_target_pairs={{0,16},{8,24},{16,0},{24,8},{1,17},{9,25},{17,1},{25,9},{2,18},{10... | collective-permute-start | bytes 196616 | tf_op jit(solution)/shard_map/ppermute | solution.py:353
  35.8 6.6 %collective-permute-start.12 = (bf16[16,2048]{1,0:T(8,128)(2,1)S(1)}, bf16[16,2048]{1,0:T(8,128)(2,1)S(1)}, u32[]{:S(2)}, u32[]{:S(2)}) collective-permute-start(bf16[16,2048]{1,0:T(8,128)(2,1)S(1)} %get-tuple-element.38), channel_id=1, source_target_pairs={{0,8},{8,16},{16,24},{24,0},{1,9},{9,17},{17,25},{25,1},{2,10},{10... | collective-permute-start | bytes 196616 | tf_op jit(solution)/shard_map/ppermute | solution.py:353
  37.4 5.0 %copy-start.1 = (f32[16,2048]{1,0:T(8,128)S(1)}, f32[16,2048]{1,0:T(8,128)}, u32[]{:S(2)}) copy-start(f32[16,2048]{1,0:T(8,128)} %emi_ref.1) | copy-start | bytes 393220
  37.4 5.0 %copy-start.2 = (f32[1,2048]{1,0:T(1,128)S(1)}, f32[1,2048]{1,0:T(1,128)}, u32[]{:S(2)}) copy-start(f32[1,2048]{1,0:T(1,128)} %get-tuple-element.34) | copy-start | bytes 24580
  42.5 4.3 %collective-permute-start.14 = (bf16[16,2048]{1,0:T(8,128)(2,1)S(1)}, bf16[16,2048]{1,0:T(8,128)(2,1)S(1)}, u32[]{:S(2)}, u32[]{:S(2)}) collective-permute-start(bf16[16,2048]{1,0:T(8,128)(2,1)S(1)} %multiply_convert_fusion.refs_0_), channel_id=1, source_target_pairs={{0,2},{1,3},{2,0},{3,1},{4,6},{5,7},{6,4},{7,5},{8,10},{9,11},{10,... | collective-permute-start | bytes 196616 | tf_op jit(solution)/shard_map/ppermute | solution.py:346
  44.0 4.6 %collective-permute-start.16 = (bf16[16,2048]{1,0:T(8,128)(2,1)S(1)}, bf16[16,2048]{1,0:T(8,128)(2,1)S(1)}, u32[]{:S(2)}, u32[]{:S(2)}) collective-permute-start(bf16[16,2048]{1,0:T(8,128)(2,1)S(1)} %multiply_convert_fusion.refs_0_), channel_id=1, source_target_pairs={{0,4},{1,5},{2,6},{3,7},{4,0},{5,1},{6,2},{7,3},{8,12},{9,13},{10,... | collective-permute-start | bytes 196616 | tf_op jit(solution)/shard_map/ppermute | solution.py:346
  44.8 5.2 %collective-permute-start.18 = (bf16[16,2048]{1,0:T(8,128)(2,1)S(1)}, bf16[16,2048]{1,0:T(8,128)(2,1)S(1)}, u32[]{:S(2)}, u32[]{:S(2)}) collective-permute-start(bf16[16,2048]{1,0:T(8,128)(2,1)S(1)} %multiply_convert_fusion.refs_0_), channel_id=1, source_target_pairs={{0,6},{1,7},{2,4},{3,5},{4,2},{5,3},{6,0},{7,1},{8,14},{9,15},{10,... | collective-permute-start | bytes 196616 | tf_op jit(solution)/shard_map/ppermute | solution.py:346
  46.2 3.8 %collective-permute-start.13 = (bf16[16,2048]{1,0:T(8,128)(2,1)S(1)}, bf16[16,2048]{1,0:T(8,128)(2,1)S(1)}, u32[]{:S(2)}, u32[]{:S(2)}) collective-permute-start(bf16[16,2048]{1,0:T(8,128)(2,1)S(1)} %multiply_convert_fusion.refs_0_), channel_id=1, source_target_pairs={{0,1},{1,0},{2,3},{3,2},{4,5},{5,4},{6,7},{7,6},{8,9},{9,8},{10,11... | collective-permute-start | bytes 196616 | tf_op jit(solution)/shard_map/ppermute | solution.py:348
  46.8 3.2 %collective-permute-start.15 = (bf16[16,2048]{1,0:T(8,128)(2,1)S(1)}, bf16[16,2048]{1,0:T(8,128)(2,1)S(1)}, u32[]{:S(2)}, u32[]{:S(2)}) collective-permute-start(bf16[16,2048]{1,0:T(8,128)(2,1)S(1)} %collective-permute-done.14.refs_2_), channel_id=1, source_target_pairs={{0,1},{1,0},{2,3},{3,2},{4,5},{5,4},{6,7},{7,6},{8,9},{9,8},{10,11... | collective-permute-start | bytes 196616 | tf_op jit(solution)/shard_map/ppermute | solution.py:348
  48.6 1.4 %collective-permute-start.17 = (bf16[16,2048]{1,0:T(8,128)(2,1)S(1)}, bf16[16,2048]{1,0:T(8,128)(2,1)S(1)}, u32[]{:S(2)}, u32[]{:S(2)}) collective-permute-start(bf16[16,2048]{1,0:T(8,128)(2,1)S(1)} %collective-permute-done.16.refs_4_), channel_id=1, source_target_pairs={{0,1},{1,0},{2,3},{3,2},{4,5},{5,4},{6,7},{7,6},{8,9},{9,8},{10,11... | collective-permute-start | bytes 196616 | tf_op jit(solution)/shard_map/ppermute | solution.py:348
  50.0 1.3 %collective-permute-start.19 = (bf16[16,2048]{1,0:T(8,128)(2,1)S(1)}, bf16[16,2048]{1,0:T(8,128)(2,1)S(1)}, u32[]{:S(2)}, u32[]{:S(2)}) collective-permute-start(bf16[16,2048]{1,0:T(8,128)(2,1)S(1)} %collective-permute-done.18.refs_6_), channel_id=1, source_target_pairs={{0,1},{1,0},{2,3},{3,2},{4,5},{5,4},{6,7},{7,6},{8,9},{9,8},{10,11... | collective-permute-start | bytes 196616 | tf_op jit(solution)/shard_map/ppermute | solution.py:348
  53.9 5.7 %collective-permute-start.20 = (bf16[16,2048]{1,0:T(8,128)(2,1)S(1)}, bf16[16,2048]{1,0:T(8,128)(2,1)S(1)}, u32[]{:S(2)}, u32[]{:S(2)}) collective-permute-start(bf16[16,2048]{1,0:T(8,128)(2,1)S(1)} %get-tuple-element.40), channel_id=1, source_target_pairs={{0,24},{8,0},{16,8},{24,16},{1,25},{9,1},{17,9},{25,17},{2,26},{10... | collective-permute-start | bytes 196616 | tf_op jit(solution)/shard_map/ppermute | solution.py:353
  57.0 8.1 %collective-permute-start.21 = (bf16[16,2048]{1,0:T(8,128)(2,1)S(1)}, bf16[16,2048]{1,0:T(8,128)(2,1)S(1)}, u32[]{:S(2)}, u32[]{:S(2)}) collective-permute-start(bf16[16,2048]{1,0:T(8,128)(2,1)S(1)} %get-tuple-element.41), channel_id=1, source_target_pairs={{0,16},{8,24},{16,0},{24,8},{1,17},{9,25},{17,1},{25,9},{2,18},{10... | collective-permute-start | bytes 196616 | tf_op jit(solution)/shard_map/ppermute | solution.py:353
  58.5 6.6 %collective-permute-start.22 = (bf16[16,2048]{1,0:T(8,128)(2,1)S(1)}, bf16[16,2048]{1,0:T(8,128)(2,1)S(1)}, u32[]{:S(2)}, u32[]{:S(2)}) collective-permute-start(bf16[16,2048]{1,0:T(8,128)(2,1)S(1)} %get-tuple-element.42), channel_id=1, source_target_pairs={{0,8},{8,16},{16,24},{24,0},{1,9},{9,17},{17,25},{25,1},{2,10},{10... | collective-permute-start | bytes 196616 | tf_op jit(solution)/shard_map/ppermute | solution.py:353

commit v5 on v4

--- a/solution.py
+++ b/solution.py
@@ -36,8 +36,8 @@
 def pack_kernel(pos_ref, nrm_ref, emi_ref, level_ref, table_ref, slot_ref, pay_ref, geo_ref, area_ref, rows):
     level = level_ref[...]
     area = jnp.zeros(level.shape, F32)
-    for k in range(table_ref.shape[0]):
-        area = jnp.where(level == k, table_ref[k], area)
+    for k in range(table_ref.shape[1]):
+        area = jnp.where(level == k, table_ref[:, k : k + 1], area)
     area_ref[...] = area
     p1, p2 = split(pos_ref[...], 2)
     n1, n2 = split(nrm_ref[...], 2)
@@ -112,13 +112,13 @@
 
 def sections(nz, ny):
     one = ny * 2 * CAP
-    second = (nz - 1) * one + SPARE
-    return second, second + one + SPARE
-
-
-def list_pairs(nz, ny, nb, place_ref, slots, pairs):
-    z, k = place_ref[0], place_ref[1]
-    second, numbers = sections(nz, ny)
+    second = (nz - 1) * one + 2 * SPARE
+    return second, second + one + 2 * SPARE
+
+
+def list_pairs(nz, ny, nb, slots, pairs):
+    z, k = lax.axis_index("gx"), lax.axis_index("gy")
+    second, bounds = sections(nz, ny)
 
     def peer(s, m, count):
         zs = lax.rem(z - s + nz, nz)
@@ -133,17 +133,20 @@
             count = count + (row >= 0).astype(jnp.int32)
         return count
 
-    for section, (start, lines) in enumerate(((0, range(1, nz)), (second, range(1)))):
-        count = jnp.int32(start)
+    for start, lines in ((0, range(1, nz)), (second, range(1))):
+        for t in range(SPARE):
+            pairs[start + t] = nz * nb * 4096
+        count = jnp.int32(start + SPARE)
         for s in lines:
+            pairs[bounds + 2 * s] = count
             if ny <= 8:
                 for m in range(ny):
                     count = peer(s, m, count)
             else:
                 count = lax.fori_loop(0, ny, functools.partial(peer, s), count)
+            pairs[bounds + 2 * s + 1] = count
         for t in range(SPARE):
             pairs[count + t] = nz * nb * 4096
-        pairs[numbers + section] = count - start
 
 
 def feature_scratch(nz, ny, nb):
@@ -172,7 +175,7 @@
             out[:, b * BLK : (b + 1) * BLK] = acc[(first + s) * nb + b].astype(out.dtype)
 
 
-def prepare(nz, ny, nb, place_ref, geos, pays, fluxes, pairs, features, acc, slots_v, slots, sem):
+def prepare(nz, ny, nb, geos, pays, fluxes, pairs, features, acc, slots_v, slots, sem):
     row_feat, row_area, col_feat, col_area, flux = features
     width = slots.shape[1]
     for s in range(nz):
@@ -192,7 +195,7 @@
                 row_feat[s * nb + b, v] = forms[v][:, here]
     acc[...] = jnp.zeros(acc.shape, F32)
     copy.wait()
-    list_pairs(nz, ny, nb, place_ref, slots, pairs)
+    list_pairs(nz, ny, nb, slots, pairs)
     depth = lax.broadcasted_iota(jnp.int32, (KDIM, LANES), 0)
     pick = jnp.where((depth >= 40) & (depth < 43), 1.0, 0.0).astype(BF16)
     for m in range(ny):
@@ -216,96 +219,107 @@
     return (top * pltpu.reciprocal(q * (math.pi * q - area), approx=True)).astype(BF16)
 
 
-def form_tiles(unroll, first, count, last, pairs, features, tiles):
-    def some(t, carry):
+def form_and_apply(start, end, unroll, last, pairs, features, tiles, acc):
+    flux = features[4]
+
+    def add(step):
+        sums = []
         for u in range(unroll):
-            tiles[t * unroll + u] = tile_of(pairs[first + t * unroll + u], last, features)
+            t = step * unroll + u
+            code = pairs[start + t]
+            total = jnp.dot(flux[code % 4096], tiles[t], preferred_element_type=F32)
+            sums.append((jnp.minimum(code // 4096, last + 1), total))
+        return sums
+
+    def some(step, carry):
+        sums = add(step - 1)
+        for u in range(unroll):
+            t = step * unroll + u
+            tiles[t] = tile_of(pairs[start + t], last, features)
+        for rb, total in sums:
+            acc[rb] += total
         return carry
 
-    lax.fori_loop(0, (count + unroll - 1) // unroll, some, 0)
-
-
-def apply_tiles(first, count, spare, pairs, tiles, flux, acc):
-    def some(t, carry):
+    first = SPARE // unroll
+    steps = (end - start + unroll - 1) // unroll
+    lax.fori_loop(first, steps, some, 0)
+    for rb, total in add(steps - 1):
+        acc[rb] += total
+
+
+def apply_tiles(start, begin, end, spare, pairs, tiles, flux, acc):
+    def some(step, carry):
         sums = []
         for u in range(APPLY_UNROLL):
-            code = pairs[first + t * APPLY_UNROLL + u]
-            tile = tiles[t * APPLY_UNROLL + u]
-            sums.append((code // 4096, jnp.dot(flux[code % 4096], tile, preferred_element_type=F32)))
+            t = begin + step * APPLY_UNROLL + u
+            code = pairs[t]
+            total = jnp.dot(flux[code % 4096], tiles[t - start], preferred_element_type=F32)
+            sums.append((jnp.where(t < end, (code // 4096) % spare, spare), total))
         for rb, total in sums:
-            acc[jnp.minimum(rb, spare)] += total
+            acc[rb] += total
         return carry
 
-    lax.fori_loop(0, (count + APPLY_UNROLL - 1) // APPLY_UNROLL, some, 0)
-
-
-def far_kernel(nz, ny, nb, place_ref, *refs):
+    lax.fori_loop(0, (end - begin + APPLY_UNROLL - 1) // APPLY_UNROLL, some, 0)
+
+
+def far_kernel(nz, ny, nb, *refs):
     geos, pays, refs = refs[:nz], refs[nz : nz + ny], refs[nz + ny :]
     outs, refs = refs[: nz - 1], refs[nz - 1 :]
     tiles, pairs, features, own = refs[0], refs[1], refs[2:7], refs[7:]
     acc = own[0]
-    _, numbers = sections(nz, ny)
-    prepare(nz, ny, nb, place_ref, geos, pays, None, pairs, features, *own)
-    count = pairs[numbers]
-    form_tiles(8, 0, count, nz * nb - 1, pairs, features, tiles)
-    apply_tiles(0, count, nz * nb, pairs, tiles, features[4], acc)
+    _, bounds = sections(nz, ny)
+    prepare(nz, ny, nb, geos, pays, None, pairs, features, *own)
+    form_and_apply(0, pairs[bounds + 2 * nz - 1], 8, nz * nb - 1, pairs, features, tiles, acc)
     put_out(nb, acc, outs, 1)
 
 
 def near_kernel(nz, ny, nb, pairs, *refs):
     features, out, tiles, acc = refs[:5], refs[5], refs[6], refs[7]
-    second, numbers = sections(nz, ny)
-    count = pairs[numbers + 1]
+    second, bounds = sections(nz, ny)
     acc[...] = jnp.zeros(acc.shape, F32)
-    form_tiles(4, second, count, nb - 1, pairs, features, tiles)
-    apply_tiles(second, count, nb, pairs, tiles, features[4], acc)
+    form_and_apply(second, pairs[bounds + 1], 4, nb - 1, pairs, features, tiles, acc)
     put_out(nb, acc, [out], 0)
 
 
-def apply_kernel(nz, ny, nb, pairs, far_ref, near_ref, *refs):
-    fluxes, refs = refs[:ny], refs[ny:]
-    outs, refs = refs[:nz], refs[nz:]
-    flux, acc = refs
-    second, numbers = sections(nz, ny)
+def apply_kernel(nz, ny, nb, s, pairs, tiles, *refs):
+    fluxes, out, flux, acc = refs[:ny], *refs[ny:]
+    second, bounds = sections(nz, ny)
     for m in range(ny):
         for b in range(nb):
             flux[m * nb + b] = fluxes[m][:, b * BLK : (b + 1) * BLK]
     acc[...] = jnp.zeros(acc.shape, F32)
-    apply_tiles(0, pairs[numbers], nz * nb, pairs, far_ref, flux, acc)
-    apply_tiles(second, pairs[numbers + 1], nz * nb, pairs, near_ref, flux, acc)
-    put_out(nb, acc, outs, 0)
-
-
-def whole_kernel(nz, ny, nb, fresh, place_ref, *refs):
+    start = 0 if s else second
+    apply_tiles(start, pairs[bounds + 2 * s], pairs[bounds + 2 * s + 1], nb, pairs, tiles, flux, acc)
+    put_out(nb, acc, [out], 0)
+
+
+def whole_kernel(nz, ny, nb, fresh, *refs):
     geos, pays, refs = refs[:nz], refs[nz : nz + ny], refs[nz + ny :]
     fluxes, refs = (refs[:ny], refs[ny:]) if fresh else (None, refs)
     outs, features, own, pairs = refs[:nz], refs[nz : nz + 5], refs[nz + 5 : -1], refs[-1]
     acc, flux = own[0], features[4]
-    second, numbers = sections(nz, ny)
-    prepare(nz, ny, nb, place_ref, geos, pays, fluxes, pairs, features, *own)
-    for section, start in enumerate((0, second)):
+    _, bounds = sections(nz, ny)
+    prepare(nz, ny, nb, geos, pays, fluxes, pairs, features, *own)
+    for s in range(nz):
 
         def one(t, carry):
-            code = pairs[start + t]
+            code = pairs[t]
             tile = tile_of(code, nz * nb - 1, features)
             acc[code // 4096] += jnp.dot(flux[code % 4096], tile, preferred_element_type=F32)
             return carry
 
-        lax.fori_loop(0, pairs[numbers + section], one, 0)
+        lax.fori_loop(pairs[bounds + 2 * s], pairs[bounds + 2 * s + 1], one, 0)
     put_out(nb, acc, outs, 0)
 
 
 def per_device(nz, ny, positions, normals, emission, material, area_level, reflect_table, area_table, pair_slots):
     patches = positions.shape[1]
     nb = patches // BLK
-    second, numbers = sections(nz, ny)
-    keep = numbers * BLK * BLK * 2 <= KEEP_BYTES
-    place = jnp.stack([lax.axis_index("gx"), lax.axis_index("gy")]).astype(jnp.int32)
+    second, bounds = sections(nz, ny)
+    keep = bounds * BLK * BLK * 2 <= KEEP_BYTES
 
     def call(kernel, name, megabytes, ins, outs, scratch, args):
-        scalar = [getattr(x, "memory_space", None) == pltpu.SMEM for x in outs]
-        spaces = [SMEM() if s else VMEM() for s in scalar]
-        outs = [jax.ShapeDtypeStruct(x.shape, x.dtype) if s else x for x, s in zip(outs, scalar)]
+        spaces = [SMEM() if getattr(x, "memory_space", None) == pltpu.SMEM else VMEM() for x in outs]
         return pl.pallas_call(
             kernel,
             out_shape=tuple(outs),
@@ -320,7 +334,7 @@
         pack_kernel,
         "pack",
         None,
-        [VMEM()] * 4 + [SMEM(), VMEM()],
+        [VMEM()] * 6,
         [
             pltpu.VMEM((GEO + BANDS, patches), BF16),
             pltpu.VMEM((GEO, patches), BF16),
@@ -332,7 +346,7 @@
             normals,
             emission,
             area_level.reshape(1, patches),
-            area_table,
+            area_table.reshape(1, -1),
             jnp.transpose(pair_slots[0], (1, 2, 0)),
         ),
     )
@@ -340,12 +354,15 @@
     def along(x):
         return [lax.ppermute(x, "gx", [(i, (i + s) % nz) for i in range(nz)]) for s in range(1, nz)]
 
-    def plane(x):
+    def plane(x, after=None):
         got = {0: x}
         for m in range(2, ny, 2):
             got[m] = lax.ppermute(x, "gy", [(i, i ^ m) for i in range(ny)])
         for m in range(0, ny, 2):
-            got[m + 1] = lax.ppermute(got[m], "gy", [(i, i ^ 1) for i in range(ny)])
+            held = got[m]
+            if after is not None and m == 0:
+                held, _ = lax.optimization_barrier((held, after))
+            got[m + 1] = lax.ppermute(held, "gy", [(i, i ^ 1) for i in range(ny)])
         return [got[m] for m in range(ny)]
 
     def sent(parts):
@@ -363,7 +380,7 @@
     far_parts = [jax.ShapeDtypeStruct((BANDS, patches), BF16)] * (nz - 1)
     features, own = feature_scratch(nz, ny, nb), own_scratch(nz, ny, nb)
     acc = own[0]
-    pairs_list = pltpu.SMEM((numbers + 2,), jnp.int32)
+    pairs_list = pltpu.SMEM((bounds + 2 * nz,), jnp.int32)
 
     kind_hot = (
         material[None, :] == jnp.arange(reflect_table.shape[0], dtype=jnp.int32)[:, None]
@@ -371,17 +388,17 @@
     reflect = jnp.dot(jnp.transpose(reflect_table), kind_hot, precision=lax.Precision.HIGHEST)
 
     rows = [geo] + along(geo)
-    cols = plane(payload)
+    cols = plane(payload, rows[1])
 
     def whole(fluxes):
         got = call(
             functools.partial(whole_kernel, nz, ny, nb, bool(fluxes)),
             "whole",
             60,
-            [SMEM()] + [VMEM()] * (nz + ny + len(fluxes)),
+            [VMEM()] * (nz + ny + len(fluxes)),
             [own_part] + far_parts,
             features + own + [pairs_list],
-            (place, *rows, *cols, *fluxes),
+            (*rows, *cols, *fluxes),
         )
         return total(got[0], sent(got[1:]))
 
@@ -390,10 +407,10 @@
             functools.partial(far_kernel, nz, ny, nb),
             "far",
             16,
-            [SMEM()] + [VMEM()] * (nz + ny),
+            [VMEM()] * (nz + ny),
             far_parts + [pltpu.VMEM((second, BLK, BLK), BF16), pairs_list] + features,
             own,
-            (place, *rows, *cols),
+            (*rows, *cols),
         )
         returned = sent(got[: nz - 1])
         far_tiles, pairs, *kept = got[nz - 1 :]
@@ -402,7 +419,7 @@
             "near",
             8,
             [SMEM()] + [VMEM()] * 5,
-            [own_part, pltpu.VMEM((numbers - second, BLK, BLK), BF16)],
+            [own_part, pltpu.VMEM((bounds - second, BLK, BLK), BF16)],
             [pltpu.VMEM((nb + 1, BANDS, BLK), F32)],
             (pairs, *kept),
         )
@@ -412,16 +429,19 @@
     radiosity = emission + reflect * irradiation
     fluxes = plane((area * radiosity).astype(BF16))
     if keep:
-        got = call(
-            functools.partial(apply_kernel, nz, ny, nb),
-            "apply",
-            4,
-            [SMEM()] + [VMEM()] * (2 + ny),
-            [own_part] + far_parts,
-            [features[4], acc],
-            (pairs, far_tiles, near_tiles, *fluxes),
-        )
-        irradiation = total(got[0], sent(got[1:]))
+        parts = [
+            call(
+                functools.partial(apply_kernel, nz, ny, nb, s),
+                "apply",
+                4,
+                [SMEM()] + [VMEM()] * (1 + ny),
+                [far_parts[0] if s else own_part],
+                [features[4], pltpu.VMEM((nb + 1, BANDS, BLK), F32)],
+                (pairs, far_tiles if s else near_tiles, *fluxes),
+            )[0]
+            for s in range(nz)
+        ]
+        irradiation = total(parts[0], sent(parts[1:]))
     else:
         irradiation = whole(fluxes)
     return emission + reflect * irradiation

time: 65.7 us -> 60.8 us (0.925)
  Pallas kernels: 19.1 us -> 15.7 us
  waiting for transfers between devices: 17.7 us -> 15.7 us
    pallas_call x4 -> x7, Pallas kernels: 19.1 us -> 15.7 us  [call(): pl.pallas_call(kernel, out_shape=tuple(outs), in_specs=ins, out_specs=tup...]
    ppermute x6, waiting for transfers between devices: 8.75 us -> 7.08 us  [sent(): lax.ppermute(part, 'gx', [(i, (i - s) % nz) for i in range(nz)])]
  transfers between devices with their start and end apart: 23 -> 23, of which waited for: 9 -> 10; matrix products, arithmetic and copies ran while one was open for 2% -> 2% of each run, Pallas kernels for 4% -> 7%
where the time goes in v5:
time: 60.8 us; the launch traced here: 60.4 us
  starting transfers between devices  27.2 us (45%)
  Pallas kernels  15.7 us (26%)
  waiting for transfers between devices  15.7 us (26%)
  matrix products  0.95 us (2%)
  other arithmetic  0.74 us (1%)
    pallas_call x7, Pallas kernels, call(): pl.pallas_call(kernel, out_shape=tuple(outs), in_specs=ins, out_specs=tup...  15.7 us
    ppermute x6, starting transfers between devices, sent(): lax.ppermute(part, 'gx', [(i, (i - s) % nz) for i in range(nz)])  10.9 us
    ppermute x6, starting transfers between devices, plane(): got[m] = lax.ppermute(x, 'gy', [(i, i ^ m) for i in range(ny)])  8.01 us
    ppermute x3, starting transfers between devices, along(): lax.ppermute(x, 'gx', [(i, (i + s) % nz) for i in range(nz)])  7.23 us
    ppermute x6, waiting for transfers between devices, sent(): lax.ppermute(part, 'gx', [(i, (i - s) % nz) for i in range(nz)])  7.08 us
    ppermute x3, waiting for transfers between devices, along(): lax.ppermute(x, 'gx', [(i, (i + s) % nz) for i in range(nz)])  4.02 us
    ppermute x6, waiting for transfers between devices, plane(): got[m] = lax.ppermute(x, 'gy', [(i, i ^ m) for i in range(ny)])  3.31 us
    ppermute x8, waiting for transfers between devices, plane(): got[m + 1] = lax.ppermute(held, 'gy', [(i, i ^ 1) for i in range(ny)])  1.25 us
  transfers between devices with their start and end apart: 23, of which 10 were waited for; matrix products, arithmetic and copies ran while one was open for 2% of the time, Pallas kernels for 7%

profile of v5, /device:TPU:0, one launch (start us, length us, event | category | flops | bytes accessed | tf_op | source)
XLA Modules:
  0.0 60.4 jit_solution(7190076950152061602)
XLA Ops:
  0.0 1.7 %pack.1 = (bf16[32,2048]{1,0:T(8,128)(2,1)S(1)}, bf16[16,2048]{1,0:T(8,128)(2,1)S(1)}, f32[1,2048]{1,0:T(1,128)}) custom-call(f32[3,2048]{1,0:T(4,128)} %pos_ref.1, f32[3,2048]{1,0:T(4,128)} %nrm_ref.1, f32[16,2048]{1,0:T(8,128)} %emi_ref.1, s32[1,2048]{1,0:T(1,128)} %bitcast.9, f32[1,8]{1,0:T(1,128)} %bitcast.12, s32[2,2,32]{2,1,0:T(2,128)} %bitcast.11), custom_call_target="tpu_custom_call" | custom-call | tf_op jit(solution)/shard_map/pack/pallas_call | solution.py:323
  1.7 2.9 %collective-permute-start.4 = (bf16[32,2048]{1,0:T(8,128)(2,1)S(1)}, bf16[32,2048]{1,0:T(8,128)(2,1)S(1)}, u32[]{:S(2)}, u32[]{:S(2)}) collective-permute-start(bf16[32,2048]{1,0:T(8,128)(2,1)S(1)} %get-tuple-element.23.refs_4_), channel_id=1, source_target_pairs={{0,2},{1,3},{2,0},{3,1},{4,6},{5,7},{6,4},{7,5},{8,10},{9,11},{10,... | collective-permute-start | bytes 393224 | tf_op jit(solution)/shard_map/ppermute | solution.py:360
  4.6 1.5 %collective-permute-start.6 = (bf16[32,2048]{1,0:T(8,128)(2,1)S(1)}, bf16[32,2048]{1,0:T(8,128)(2,1)S(1)}, u32[]{:S(2)}, u32[]{:S(2)}) collective-permute-start(bf16[32,2048]{1,0:T(8,128)(2,1)S(1)} %get-tuple-element.23.refs_4_), channel_id=1, source_target_pairs={{0,4},{1,5},{2,6},{3,7},{4,0},{5,1},{6,2},{7,3},{8,12},{9,13},{10,... | collective-permute-start | bytes 393224 | tf_op jit(solution)/shard_map/ppermute | solution.py:360
  6.1 0.0 collective-permute-start.8
  6.1 2.1 %collective-permute-start = (bf16[16,2048]{1,0:T(8,128)(2,1)S(1)}, bf16[16,2048]{1,0:T(8,128)(2,1)S(1)}, u32[]{:S(2)}, u32[]{:S(2)}) collective-permute-start(bf16[16,2048]{1,0:T(8,128)(2,1)S(1)} %get-tuple-element.21.refs_0_), channel_id=1, source_target_pairs={{0,8},{8,16},{16,24},{24,0},{1,9},{9,17},{17,25},{25,1},{2,10},{10... | collective-permute-start | bytes 196616 | tf_op jit(solution)/shard_map/ppermute | solution.py:355
  8.2 2.6 %collective-permute-start.1 = (bf16[16,2048]{1,0:T(8,128)(2,1)S(1)}, bf16[16,2048]{1,0:T(8,128)(2,1)S(1)}, u32[]{:S(2)}, u32[]{:S(2)}) collective-permute-start(bf16[16,2048]{1,0:T(8,128)(2,1)S(1)} %get-tuple-element.21.refs_0_), channel_id=1, source_target_pairs={{0,16},{8,24},{16,0},{24,8},{1,17},{9,25},{17,1},{25,9},{2,18},{10... | collective-permute-start | bytes 196616 | tf_op jit(solution)/shard_map/ppermute | solution.py:355
  10.8 2.1 %collective-permute-done.refs_1_ = bf16[16,2048]{1,0:T(8,128)(2,1)S(1)} collective-permute-done((bf16[16,2048]{1,0:T(8,128)(2,1)S(1)}, bf16[16,2048]{1,0:T(8,128)(2,1)S(1)}, u32[]{:S(2)}, u32[]{:S(2)}) %collective-permute-start) | collective-permute-done | bytes 65568 | tf_op jit(solution)/shard_map/ppermute | solution.py:355
  12.9 0.0 collective-permute-done.4.refs_6_
  12.9 0.5 collective-permute-start.5
  13.4 0.0 collective-permute-done.6.refs_8_
  13.4 0.1 collective-permute-start.7
  13.5 0.4 collective-permute-start.9
  13.9 0.0 collective-permute-done.1.refs_2_
  13.9 2.6 %collective-permute-start.2 = (bf16[16,2048]{1,0:T(8,128)(2,1)S(1)}, bf16[16,2048]{1,0:T(8,128)(2,1)S(1)}, u32[]{:S(2)}, u32[]{:S(2)}) collective-permute-start(bf16[16,2048]{1,0:T(8,128)(2,1)S(1)} %get-tuple-element.21.refs_0_), channel_id=1, source_target_pairs={{0,24},{8,0},{16,8},{24,16},{1,25},{9,1},{17,9},{25,17},{2,26},{10... | collective-permute-start | bytes 196616 | tf_op jit(solution)/shard_map/ppermute | solution.py:355
  16.5 1.9 %collective-permute-done.2.refs_3_ = bf16[16,2048]{1,0:T(8,128)(2,1)S(1)} collective-permute-done((bf16[16,2048]{1,0:T(8,128)(2,1)S(1)}, bf16[16,2048]{1,0:T(8,128)(2,1)S(1)}, u32[]{:S(2)}, u32[]{:S(2)}) %collective-permute-start.2) | collective-permute-done | bytes 65568 | tf_op jit(solution)/shard_map/ppermute | solution.py:355
  18.4 0.0 collective-permute-done.7.refs_9_
  18.4 9.1 %far.1 = (bf16[16,2048]{1,0:T(8,128)(2,1)S(1)}, bf16[16,2048]{1,0:T(8,128)(2,1)S(1)}, bf16[16,2048]{1,0:T(8,128)(2,1)S(1)}, bf16[112,256,256]{2,1,0:T(8,128)(2,1...) custom-call(bf16[16,2048]{1,0:T(8,128)(2,1)S(1)} %get-tuple-element., ...), custom_call_target="tpu_custom_call" | custom-call | tf_op jit(solution)/shard_map/far/pallas_call | solution.py:323
  27.5 6.5 %collective-permute-start.10 = (bf16[16,2048]{1,0:T(8,128)(2,1)S(1)}, bf16[16,2048]{1,0:T(8,128)(2,1)S(1)}, u32[]{:S(2)}, u32[]{:S(2)}) collective-permute-start(bf16[16,2048]{1,0:T(8,128)(2,1)S(1)} %get-tuple-element.33), channel_id=1, source_target_pairs={{0,24},{8,0},{16,8},{24,16},{1,25},{9,1},{17,9},{25,17},{2,26},{10... | collective-permute-start | bytes 196616 | tf_op jit(solution)/shard_map/ppermute | solution.py:370
  34.0 0.6 %collective-permute-start.12 = (bf16[16,2048]{1,0:T(8,128)(2,1)S(1)}, bf16[16,2048]{1,0:T(8,128)(2,1)S(1)}, u32[]{:S(2)}, u32[]{:S(2)}) collective-permute-start(bf16[16,2048]{1,0:T(8,128)(2,1)S(1)} %get-tuple-element.35), channel_id=1, source_target_pairs={{0,8},{8,16},{16,24},{24,0},{1,9},{9,17},{17,25},{25,1},{2,10},{10... | collective-permute-start | bytes 196616 | tf_op jit(solution)/shard_map/ppermute | solution.py:370
  34.6 0.9 %convolution_bitcast_fusion = f32[16,2048]{1,0:T(8,128)S(1)} fusion(f32[8,16]{1,0:T(8,128)S(1)} %copy-done, s32[2048]{0:T(1024)} %param.11), kind=kOutput, calls=%fused_computation | convolution fusion | flops 3162112 | bytes 139776 | tf_op jit(solution)/shard_map/dot_general | solution.py:388
  35.6 0.0 copy-start.1
  35.6 0.0 copy-start.2
  35.6 2.7 %near.1 = (f32[16,2048]{1,0:T(8,128)S(1)}, bf16[48,256,256]{2,1,0:T(8,128)(2,1)S(1)}) custom-call(s32[168]{0:T(256)S(4)} %get-tuple-element.24.pairs, bf16[32,3,48,256]{3,2,1,0:T(8,128)(2,1)S(1)} %get-tuple-element.25.refs_0_, f32[32,1,256]{2,1,0:T(1,128)S(1)} %get-tuple-element.26.refs_1_, bf16[64,256,48]{2,1,0:T(8,128)(2,1)S(1)} %get-tuple-element.27.refs_2_, ...), custom_call_target="tpu_custom_call" | custom-call | tf_op jit(solution)/shard_map/near/pallas_call | solution.py:323
  38.4 0.0 collective-permute-done.10
  38.4 0.8 %collective-permute-done.11 = bf16[16,2048]{1,0:T(8,128)(2,1)S(1)} collective-permute-done((bf16[16,2048]{1,0:T(8,128)(2,1)S(1)}, bf16[16,2048]{1,0:T(8,128)(2,1)S(1)}, u32[]{:S(2)}, u32[]{:S(2)}) %collective-permute-start.11) | collective-permute-done | bytes 65568 | tf_op jit(solution)/shard_map/ppermute | solution.py:370
  39.2 0.9 %collective-permute-done.12 = bf16[16,2048]{1,0:T(8,128)(2,1)S(1)} collective-permute-done((bf16[16,2048]{1,0:T(8,128)(2,1)S(1)}, bf16[16,2048]{1,0:T(8,128)(2,1)S(1)}, u32[]{:S(2)}, u32[]{:S(2)}) %collective-permute-start.12) | collective-permute-done | bytes 65568 | tf_op jit(solution)/shard_map/ppermute | solution.py:370
  40.1 1.0 %collective-permute-start.14 = (bf16[16,2048]{1,0:T(8,128)(2,1)S(1)}, bf16[16,2048]{1,0:T(8,128)(2,1)S(1)}, u32[]{:S(2)}, u32[]{:S(2)}) collective-permute-start(bf16[16,2048]{1,0:T(8,128)(2,1)S(1)} %multiply_convert_fusion.refs_0_), channel_id=1, source_target_pairs={{0,2},{1,3},{2,0},{3,1},{4,6},{5,7},{6,4},{7,5},{8,10},{9,11},{10,... | collective-permute-start | bytes 196616 | tf_op jit(solution)/shard_map/ppermute | solution.py:360
  41.1 0.7 %collective-permute-start.16 = (bf16[16,2048]{1,0:T(8,128)(2,1)S(1)}, bf16[16,2048]{1,0:T(8,128)(2,1)S(1)}, u32[]{:S(2)}, u32[]{:S(2)}) collective-permute-start(bf16[16,2048]{1,0:T(8,128)(2,1)S(1)} %multiply_convert_fusion.refs_0_), channel_id=1, source_target_pairs={{0,4},{1,5},{2,6},{3,7},{4,0},{5,1},{6,2},{7,3},{8,12},{9,13},{10,... | collective-permute-start | bytes 196616 | tf_op jit(solution)/shard_map/ppermute | solution.py:360
  41.8 1.9 %collective-permute-start.18 = (bf16[16,2048]{1,0:T(8,128)(2,1)S(1)}, bf16[16,2048]{1,0:T(8,128)(2,1)S(1)}, u32[]{:S(2)}, u32[]{:S(2)}) collective-permute-start(bf16[16,2048]{1,0:T(8,128)(2,1)S(1)} %multiply_convert_fusion.refs_0_), channel_id=1, source_target_pairs={{0,6},{1,7},{2,4},{3,5},{4,2},{5,3},{6,0},{7,1},{8,14},{9,15},{10,... | collective-permute-start | bytes 196616 | tf_op jit(solution)/shard_map/ppermute | solution.py:360
  43.7 0.8 %collective-permute-done.14.refs_2_ = bf16[16,2048]{1,0:T(8,128)(2,1)S(1)} collective-permute-done((bf16[16,2048]{1,0:T(8,128)(2,1)S(1)}, bf16[16,2048]{1,0:T(8,128)(2,1)S(1)}, u32[]{:S(2)}, u32[]{:S(2)}) %collective-permute-start.14) | collective-permute-done | bytes 65568 | tf_op jit(solution)/shard_map/ppermute | solution.py:360
  44.5 0.0 collective-permute-start.15
  44.5 0.9 %collective-permute-done.16.refs_4_ = bf16[16,2048]{1,0:T(8,128)(2,1)S(1)} collective-permute-done((bf16[16,2048]{1,0:T(8,128)(2,1)S(1)}, bf16[16,2048]{1,0:T(8,128)(2,1)S(1)}, u32[]{:S(2)}, u32[]{:S(2)}) %collective-permute-start.16) | collective-permute-done | bytes 65568 | tf_op jit(solution)/shard_map/ppermute | solution.py:360
  45.4 1.6 %collective-permute-done.18.refs_6_ = bf16[16,2048]{1,0:T(8,128)(2,1)S(1)} collective-permute-done((bf16[16,2048]{1,0:T(8,128)(2,1)S(1)}, bf16[16,2048]{1,0:T(8,128)(2,1)S(1)}, u32[]{:S(2)}, u32[]{:S(2)}) %collective-permute-start.18) | collective-permute-done | bytes 65568 | tf_op jit(solution)/shard_map/ppermute | solution.py:360
  47.0 0.0 collective-permute-start.19
  47.0 0.0 collective-permute-done.13.refs_1_
  47.0 0.0 collective-permute-done.15.refs_3_
  47.0 0.0 collective-permute-done.17.refs_5_
  47.0 1.2 %collective-permute-done.19.refs_7_ = bf16[16,2048]{1,0:T(8,128)(2,1)S(1)} collective-permute-done((bf16[16,2048]{1,0:T(8,128)(2,1)S(1)}, bf16[16,2048]{1,0:T(8,128)(2,1)S(1)}, u32[]{:S(2)}, u32[]{:S(2)}) %collective-permute-start.19) | collective-permute-done | bytes 65568 | tf_op jit(solution)/shard_map/ppermute | solution.py:365
  48.2 0.6 apply.5
  48.8 2.8 %collective-permute-start.20 = (bf16[16,2048]{1,0:T(8,128)(2,1)S(1)}, bf16[16,2048]{1,0:T(8,128)(2,1)S(1)}, u32[]{:S(2)}, u32[]{:S(2)}) collective-permute-start(bf16[16,2048]{1,0:T(8,128)(2,1)S(1)} %apply.5), channel_id=1, source_target_pairs={{0,24},{8,0},{16,8},{24,16},{1,25},{9,1},{17,9},{25,17},{2,26},{10... | collective-permute-start | bytes 196616 | tf_op jit(solution)/shard_map/ppermute | solution.py:370
  51.6 0.6 apply.6
  52.2 0.8 %collective-permute-start.21 = (bf16[16,2048]{1,0:T(8,128)(2,1)S(1)}, bf16[16,2048]{1,0:T(8,128)(2,1)S(1)}, u32[]{:S(2)}, u32[]{:S(2)}) collective-permute-start(bf16[16,2048]{1,0:T(8,128)(2,1)S(1)} %apply.6), channel_id=1, source_target_pairs={{0,16},{8,24},{16,0},{24,8},{1,17},{9,25},{17,1},{25,9},{2,18},{10... | collective-permute-start | bytes 196616 | tf_op jit(solution)/shard_map/ppermute | solution.py:370
  53.0 0.6 apply.7
  53.6 0.1 collective-permute-start.22
  53.7 0.6 apply.4
  54.3 3.5 %collective-permute-done.21 = bf16[16,2048]{1,0:T(8,128)(2,1)S(1)} collective-permute-done((bf16[16,2048]{1,0:T(8,128)(2,1)S(1)}, bf16[16,2048]{1,0:T(8,128)(2,1)S(1)}, u32[]{:S(2)}, u32[]{:S(2)}) %collective-permute-start.21) | collective-permute-done | bytes 65568 | tf_op jit(solution)/shard_map/ppermute | solution.py:370
  57.8 1.9 %collective-permute-done.22 = bf16[16,2048]{1,0:T(8,128)(2,1)S(1)} collective-permute-done((bf16[16,2048]{1,0:T(8,128)(2,1)S(1)}, bf16[16,2048]{1,0:T(8,128)(2,1)S(1)}, u32[]{:S(2)}, u32[]{:S(2)}) %collective-permute-start.22) | collective-permute-done | bytes 65568 | tf_op jit(solution)/shard_map/ppermute | solution.py:370
  59.7 0.7 %multiply_add_fusion = f32[16,2048]{1,0:T(8,128)} fusion(f32[16,2048]{1,0:T(8,128)S(1)} %copy-done.1, f32[16,2048]{1,0:T(8,128)S(1)} %convolution_bitcast_fusion, bf16[16,2048]{1,0:T(8,128)(2,1)S(1)} %collective-permute-done.22, bf16[16,2048]{1,0:T(8,128)(2,1)S(1)} %collective-permute-done.21, f32[16,2048]{1,0:T(8,128)S(1)} %apply.4, ...), kind=kLoop, calls=%fused_computation.1 | loop fusion | flops 262144 | bytes 720896 | tf_op jit(solution)/shard_map/add | solution.py:447
  (14 shorter events, 0.1 us)
Async XLA Ops:
  0.0 34.6 %copy-start = (f32[8,16]{1,0:T(8,128)S(1)}, f32[8,16]{1,0:T(8,128)}, u32[]{:S(2)}) copy-start(f32[8,16]{1,0:T(8,128)} %param.13) | copy-start | bytes 1540
  1.7 11.2 %collective-permute-start.4 = (bf16[32,2048]{1,0:T(8,128)(2,1)S(1)}, bf16[32,2048]{1,0:T(8,128)(2,1)S(1)}, u32[]{:S(2)}, u32[]{:S(2)}) collective-permute-start(bf16[32,2048]{1,0:T(8,128)(2,1)S(1)} %get-tuple-element.23.refs_4_), channel_id=1, source_target_pairs={{0,2},{1,3},{2,0},{3,1},{4,6},{5,7},{6,4},{7,5},{8,10},{9,11},{10,... | collective-permute-start | bytes 393224 | tf_op jit(solution)/shard_map/ppermute | solution.py:360
  4.6 8.8 %collective-permute-start.6 = (bf16[32,2048]{1,0:T(8,128)(2,1)S(1)}, bf16[32,2048]{1,0:T(8,128)(2,1)S(1)}, u32[]{:S(2)}, u32[]{:S(2)}) collective-permute-start(bf16[32,2048]{1,0:T(8,128)(2,1)S(1)} %get-tuple-element.23.refs_4_), channel_id=1, source_target_pairs={{0,4},{1,5},{2,6},{3,7},{4,0},{5,1},{6,2},{7,3},{8,12},{9,13},{10,... | collective-permute-start | bytes 393224 | tf_op jit(solution)/shard_map/ppermute | solution.py:360
  6.1 7.3 %collective-permute-start.8 = (bf16[32,2048]{1,0:T(8,128)(2,1)S(1)}, bf16[32,2048]{1,0:T(8,128)(2,1)S(1)}, u32[]{:S(2)}, u32[]{:S(2)}) collective-permute-start(bf16[32,2048]{1,0:T(8,128)(2,1)S(1)} %get-tuple-element.23.refs_4_), channel_id=1, source_target_pairs={{0,6},{1,7},{2,4},{3,5},{4,2},{5,3},{6,0},{7,1},{8,14},{9,15},{10,... | collective-permute-start | bytes 393224 | tf_op jit(solution)/shard_map/ppermute | solution.py:360
  6.1 6.8 %collective-permute-start = (bf16[16,2048]{1,0:T(8,128)(2,1)S(1)}, bf16[16,2048]{1,0:T(8,128)(2,1)S(1)}, u32[]{:S(2)}, u32[]{:S(2)}) collective-permute-start(bf16[16,2048]{1,0:T(8,128)(2,1)S(1)} %get-tuple-element.21.refs_0_), channel_id=1, source_target_pairs={{0,8},{8,16},{16,24},{24,0},{1,9},{9,17},{17,25},{25,1},{2,10},{10... | collective-permute-start | bytes 196616 | tf_op jit(solution)/shard_map/ppermute | solution.py:355
  8.2 5.7 %collective-permute-start.1 = (bf16[16,2048]{1,0:T(8,128)(2,1)S(1)}, bf16[16,2048]{1,0:T(8,128)(2,1)S(1)}, u32[]{:S(2)}, u32[]{:S(2)}) collective-permute-start(bf16[16,2048]{1,0:T(8,128)(2,1)S(1)} %get-tuple-element.21.refs_0_), channel_id=1, source_target_pairs={{0,16},{8,24},{16,0},{24,8},{1,17},{9,25},{17,1},{25,9},{2,18},{10... | collective-permute-start | bytes 196616 | tf_op jit(solution)/shard_map/ppermute | solution.py:355
  12.9 5.5 %collective-permute-start.3 = (bf16[32,2048]{1,0:T(8,128)(2,1)S(1)}, bf16[32,2048]{1,0:T(8,128)(2,1)S(1)}, u32[]{:S(2)}, u32[]{:S(2)}) collective-permute-start(bf16[32,2048]{1,0:T(8,128)(2,1)S(1)} %get-tuple-element.23.refs_4_), channel_id=1, source_target_pairs={{0,1},{1,0},{2,3},{3,2},{4,5},{5,4},{6,7},{7,6},{8,9},{9,8},{10,11... | collective-permute-start | bytes 393224 | tf_op jit(solution)/shard_map/ppermute | solution.py:365
  12.9 5.5 %collective-permute-start.5 = (bf16[32,2048]{1,0:T(8,128)(2,1)S(1)}, bf16[32,2048]{1,0:T(8,128)(2,1)S(1)}, u32[]{:S(2)}, u32[]{:S(2)}) collective-permute-start(bf16[32,2048]{1,0:T(8,128)(2,1)S(1)} %collective-permute-done.4.refs_6_), channel_id=1, source_target_pairs={{0,1},{1,0},{2,3},{3,2},{4,5},{5,4},{6,7},{7,6},{8,9},{9,8},{10,11... | collective-permute-start | bytes 393224 | tf_op jit(solution)/shard_map/ppermute | solution.py:365
  13.4 5.0 %collective-permute-start.7 = (bf16[32,2048]{1,0:T(8,128)(2,1)S(1)}, bf16[32,2048]{1,0:T(8,128)(2,1)S(1)}, u32[]{:S(2)}, u32[]{:S(2)}) collective-permute-start(bf16[32,2048]{1,0:T(8,128)(2,1)S(1)} %collective-permute-done.6.refs_8_), channel_id=1, source_target_pairs={{0,1},{1,0},{2,3},{3,2},{4,5},{5,4},{6,7},{7,6},{8,9},{9,8},{10,11... | collective-permute-start | bytes 393224 | tf_op jit(solution)/shard_map/ppermute | solution.py:365
  13.5 5.0 %collective-permute-start.9 = (bf16[32,2048]{1,0:T(8,128)(2,1)S(1)}, bf16[32,2048]{1,0:T(8,128)(2,1)S(1)}, u32[]{:S(2)}, u32[]{:S(2)}) collective-permute-start(bf16[32,2048]{1,0:T(8,128)(2,1)S(1)} %collective-permute-done.8.refs_10_), channel_id=1, source_target_pairs={{0,1},{1,0},{2,3},{3,2},{4,5},{5,4},{6,7},{7,6},{8,9},{9,8},{10,11... | collective-permute-start | bytes 393224 | tf_op jit(solution)/shard_map/ppermute | solution.py:365
  13.9 4.5 %collective-permute-start.2 = (bf16[16,2048]{1,0:T(8,128)(2,1)S(1)}, bf16[16,2048]{1,0:T(8,128)(2,1)S(1)}, u32[]{:S(2)}, u32[]{:S(2)}) collective-permute-start(bf16[16,2048]{1,0:T(8,128)(2,1)S(1)} %get-tuple-element.21.refs_0_), channel_id=1, source_target_pairs={{0,24},{8,0},{16,8},{24,16},{1,25},{9,1},{17,9},{25,17},{2,26},{10... | collective-permute-start | bytes 196616 | tf_op jit(solution)/shard_map/ppermute | solution.py:355
  27.5 10.9 %collective-permute-start.10 = (bf16[16,2048]{1,0:T(8,128)(2,1)S(1)}, bf16[16,2048]{1,0:T(8,128)(2,1)S(1)}, u32[]{:S(2)}, u32[]{:S(2)}) collective-permute-start(bf16[16,2048]{1,0:T(8,128)(2,1)S(1)} %get-tuple-element.33), channel_id=1, source_target_pairs={{0,24},{8,0},{16,8},{24,16},{1,25},{9,1},{17,9},{25,17},{2,26},{10... | collective-permute-start | bytes 196616 | tf_op jit(solution)/shard_map/ppermute | solution.py:370
  34.0 5.2 %collective-permute-start.11 = (bf16[16,2048]{1,0:T(8,128)(2,1)S(1)}, bf16[16,2048]{1,0:T(8,128)(2,1)S(1)}, u32[]{:S(2)}, u32[]{:S(2)}) collective-permute-start(bf16[16,2048]{1,0:T(8,128)(2,1)S(1)} %get-tuple-element.34), channel_id=1, source_target_pairs={{0,16},{8,24},{16,0},{24,8},{1,17},{9,25},{17,1},{25,9},{2,18},{10... | collective-permute-start | bytes 196616 | tf_op jit(solution)/shard_map/ppermute | solution.py:370
  34.0 6.1 %collective-permute-start.12 = (bf16[16,2048]{1,0:T(8,128)(2,1)S(1)}, bf16[16,2048]{1,0:T(8,128)(2,1)S(1)}, u32[]{:S(2)}, u32[]{:S(2)}) collective-permute-start(bf16[16,2048]{1,0:T(8,128)(2,1)S(1)} %get-tuple-element.35), channel_id=1, source_target_pairs={{0,8},{8,16},{16,24},{24,0},{1,9},{9,17},{17,25},{25,1},{2,10},{10... | collective-permute-start | bytes 196616 | tf_op jit(solution)/shard_map/ppermute | solution.py:370
  35.6 4.5 %copy-start.1 = (f32[16,2048]{1,0:T(8,128)S(1)}, f32[16,2048]{1,0:T(8,128)}, u32[]{:S(2)}) copy-start(f32[16,2048]{1,0:T(8,128)} %emi_ref.1) | copy-start | bytes 393220
  35.6 4.5 %copy-start.2 = (f32[1,2048]{1,0:T(1,128)S(1)}, f32[1,2048]{1,0:T(1,128)}, u32[]{:S(2)}) copy-start(f32[1,2048]{1,0:T(1,128)} %get-tuple-element.31) | copy-start | bytes 24580
  40.1 4.3 %collective-permute-start.14 = (bf16[16,2048]{1,0:T(8,128)(2,1)S(1)}, bf16[16,2048]{1,0:T(8,128)(2,1)S(1)}, u32[]{:S(2)}, u32[]{:S(2)}) collective-permute-start(bf16[16,2048]{1,0:T(8,128)(2,1)S(1)} %multiply_convert_fusion.refs_0_), channel_id=1, source_target_pairs={{0,2},{1,3},{2,0},{3,1},{4,6},{5,7},{6,4},{7,5},{8,10},{9,11},{10,... | collective-permute-start | bytes 196616 | tf_op jit(solution)/shard_map/ppermute | solution.py:360
  41.1 4.3 %collective-permute-start.16 = (bf16[16,2048]{1,0:T(8,128)(2,1)S(1)}, bf16[16,2048]{1,0:T(8,128)(2,1)S(1)}, u32[]{:S(2)}, u32[]{:S(2)}) collective-permute-start(bf16[16,2048]{1,0:T(8,128)(2,1)S(1)} %multiply_convert_fusion.refs_0_), channel_id=1, source_target_pairs={{0,4},{1,5},{2,6},{3,7},{4,0},{5,1},{6,2},{7,3},{8,12},{9,13},{10,... | collective-permute-start | bytes 196616 | tf_op jit(solution)/shard_map/ppermute | solution.py:360
  41.8 5.2 %collective-permute-start.18 = (bf16[16,2048]{1,0:T(8,128)(2,1)S(1)}, bf16[16,2048]{1,0:T(8,128)(2,1)S(1)}, u32[]{:S(2)}, u32[]{:S(2)}) collective-permute-start(bf16[16,2048]{1,0:T(8,128)(2,1)S(1)} %multiply_convert_fusion.refs_0_), channel_id=1, source_target_pairs={{0,6},{1,7},{2,4},{3,5},{4,2},{5,3},{6,0},{7,1},{8,14},{9,15},{10,... | collective-permute-start | bytes 196616 | tf_op jit(solution)/shard_map/ppermute | solution.py:360
  43.7 3.3 %collective-permute-start.13 = (bf16[16,2048]{1,0:T(8,128)(2,1)S(1)}, bf16[16,2048]{1,0:T(8,128)(2,1)S(1)}, u32[]{:S(2)}, u32[]{:S(2)}) collective-permute-start(bf16[16,2048]{1,0:T(8,128)(2,1)S(1)} %multiply_convert_fusion.refs_0_), channel_id=1, source_target_pairs={{0,1},{1,0},{2,3},{3,2},{4,5},{5,4},{6,7},{7,6},{8,9},{9,8},{10,11... | collective-permute-start | bytes 196616 | tf_op jit(solution)/shard_map/ppermute | solution.py:365
  44.5 2.5 %collective-permute-start.15 = (bf16[16,2048]{1,0:T(8,128)(2,1)S(1)}, bf16[16,2048]{1,0:T(8,128)(2,1)S(1)}, u32[]{:S(2)}, u32[]{:S(2)}) collective-permute-start(bf16[16,2048]{1,0:T(8,128)(2,1)S(1)} %collective-permute-done.14.refs_2_), channel_id=1, source_target_pairs={{0,1},{1,0},{2,3},{3,2},{4,5},{5,4},{6,7},{7,6},{8,9},{9,8},{10,11... | collective-permute-start | bytes 196616 | tf_op jit(solution)/shard_map/ppermute | solution.py:365
  45.4 1.6 %collective-permute-start.17 = (bf16[16,2048]{1,0:T(8,128)(2,1)S(1)}, bf16[16,2048]{1,0:T(8,128)(2,1)S(1)}, u32[]{:S(2)}, u32[]{:S(2)}) collective-permute-start(bf16[16,2048]{1,0:T(8,128)(2,1)S(1)} %collective-permute-done.16.refs_4_), channel_id=1, source_target_pairs={{0,1},{1,0},{2,3},{3,2},{4,5},{5,4},{6,7},{7,6},{8,9},{9,8},{10,11... | collective-permute-start | bytes 196616 | tf_op jit(solution)/shard_map/ppermute | solution.py:365
  47.0 1.3 %collective-permute-start.19 = (bf16[16,2048]{1,0:T(8,128)(2,1)S(1)}, bf16[16,2048]{1,0:T(8,128)(2,1)S(1)}, u32[]{:S(2)}, u32[]{:S(2)}) collective-permute-start(bf16[16,2048]{1,0:T(8,128)(2,1)S(1)} %collective-permute-done.18.refs_6_), channel_id=1, source_target_pairs={{0,1},{1,0},{2,3},{3,2},{4,5},{5,4},{6,7},{7,6},{8,9},{9,8},{10,11... | collective-permute-start | bytes 196616 | tf_op jit(solution)/shard_map/ppermute | solution.py:365
  48.8 5.5 %collective-permute-start.20 = (bf16[16,2048]{1,0:T(8,128)(2,1)S(1)}, bf16[16,2048]{1,0:T(8,128)(2,1)S(1)}, u32[]{:S(2)}, u32[]{:S(2)}) collective-permute-start(bf16[16,2048]{1,0:T(8,128)(2,1)S(1)} %apply.5), channel_id=1, source_target_pairs={{0,24},{8,0},{16,8},{24,16},{1,25},{9,1},{17,9},{25,17},{2,26},{10... | collective-permute-start | bytes 196616 | tf_op jit(solution)/shard_map/ppermute | solution.py:370
  52.2 5.6 %collective-permute-start.21 = (bf16[16,2048]{1,0:T(8,128)(2,1)S(1)}, bf16[16,2048]{1,0:T(8,128)(2,1)S(1)}, u32[]{:S(2)}, u32[]{:S(2)}) collective-permute-start(bf16[16,2048]{1,0:T(8,128)(2,1)S(1)} %apply.6), channel_id=1, source_target_pairs={{0,16},{8,24},{16,0},{24,8},{1,17},{9,25},{17,1},{25,9},{2,18},{10... | collective-permute-start | bytes 196616 | tf_op jit(solution)/shard_map/ppermute | solution.py:370
  53.6 6.1 %collective-permute-start.22 = (bf16[16,2048]{1,0:T(8,128)(2,1)S(1)}, bf16[16,2048]{1,0:T(8,128)(2,1)S(1)}, u32[]{:S(2)}, u32[]{:S(2)}) collective-permute-start(bf16[16,2048]{1,0:T(8,128)(2,1)S(1)} %apply.7), channel_id=1, source_target_pairs={{0,8},{8,16},{16,24},{24,0},{1,9},{9,17},{17,25},{25,1},{2,10},{10... | collective-permute-start | bytes 196616 | tf_op jit(solution)/shard_map/ppermute | solution.py:370

commit v6 on v5

--- a/solution.py
+++ b/solution.py
@@ -16,6 +16,8 @@
 KDIM = 48
 APPLY_UNROLL = 8
 SPARE = 8
+FIRST_ORDER = {"m1": "z3", "m3": "z2", "m5": "z1"}
+LATER_ORDER = {}
 KEEP_BYTES = 24 * 2**20
 BF16 = jnp.bfloat16
 F32 = jnp.float32
@@ -66,25 +68,24 @@
     half = 0.5 * (pos[6:7] + pos[7:8])
     pp = jnp.sum(jnp.where(row < 3, p * p, 0.0), axis=0, keepdims=True)
     dot = jnp.sum(jnp.where(row < 3, n * p, 0.0), axis=0, keepdims=True)
-    return pos, nrm, row, split(pp + half, 3), split(-dot, 3), (math.pi - 1.0) * half
+    area = (1.0 - 1.0 / math.pi) * half
+    terms = split(jnp.where(row == 0, pp + half, jnp.where(row == 1, -dot, area)), 3)
+    return pos, nrm, row, terms, area
 
 
 def column_features(g):
-    pos, nrm, row, q, c, h = terms_of(g)
+    pos, nrm, row, terms, _ = terms_of(g)
     zero = jnp.zeros(pos.shape, F32)
     one = jnp.where(row == 6, 1.0, zero)
     pos = jnp.where(row < 6, pos, one)
     nrm = jnp.where(row < 6, nrm, one)
-    consts, areas = zero, zero
-    for t, value in enumerate(q + c):
-        consts = jnp.where(row == t, value, consts)
-    for t, value in enumerate(split(h, 3)):
-        areas = jnp.where(row == t, value, areas)
-    return jnp.concatenate([pos, nrm, pos, nrm, consts, areas], axis=0)
+    later = jnp.where(row < 6, pltpu.roll(terms[1], 3, 0), pltpu.roll(terms[2], 6, 0))
+    consts = jnp.where(row < 3, terms[0], later)
+    return jnp.concatenate([pos, nrm, pos, nrm, consts, zero], axis=0)
 
 
 def row_features(g):
-    pos, nrm, row, q, c, h = terms_of(g)
+    pos, nrm, row, terms, area = terms_of(g)
     zero = jnp.zeros(pos.shape, F32)
 
     def both(x):
@@ -92,22 +93,25 @@
         low = jnp.where(row < 3, pltpu.roll(x, 5, 0), x)
         return jnp.where(row < 6, high, 0.0), jnp.where(row < 6, low, 0.0)
 
-    def with_last(x, value):
-        return jnp.where(row == 6, value, x)
+    def with_last(x, t, which):
+        return jnp.where(row == 6, terms[t][which : which + 1], x)
+
+    def ones(first):
+        return jnp.where(row % 3 == first, 1.0, zero)
 
     p_hi, p_lo = both(pos)
     n_hi, n_lo = both(nrm)
-    facing = [with_last(n_hi, c[0]), with_last(zero, c[1]), with_last(n_lo, c[2]), zero, zero, zero]
-    seen = [zero, p_hi, zero, p_lo, jnp.where((row >= 3) & (row < 6), 1.0, zero), zero]
+    facing = [with_last(n_hi, 0, 1), with_last(zero, 1, 1), with_last(n_lo, 2, 1), zero, zero, zero]
+    seen = [zero, p_hi, zero, p_lo, ones(1), zero]
     near = [
-        with_last(-2.0 * p_hi, q[0]),
-        with_last(zero, q[1]),
-        with_last(-2.0 * p_lo, q[2]),
+        with_last(-2.0 * p_hi, 0, 0),
+        with_last(zero, 1, 0),
+        with_last(-2.0 * p_lo, 2, 0),
         zero,
-        jnp.where(row < 3, 1.0, zero),
+        ones(0),
         zero,
     ]
-    return [jnp.concatenate(parts, axis=0).astype(BF16) for parts in (facing, seen, near)], h
+    return [jnp.concatenate(parts, axis=0).astype(BF16) for parts in (facing, seen, near)], area
 
 
 def sections(nz, ny):
@@ -172,7 +176,7 @@
 def put_out(nb, acc, out_refs, first):
     for s, out in enumerate(out_refs):
         for b in range(nb):
-            out[:, b * BLK : (b + 1) * BLK] = acc[(first + s) * nb + b].astype(out.dtype)
+            out[:, b * BLK : (b + 1) * BLK] = (acc[(first + s) * nb + b] * (1.0 / math.pi)).astype(out.dtype)
 
 
 def prepare(nz, ny, nb, geos, pays, fluxes, pairs, features, acc, slots_v, slots, sem):
@@ -197,7 +201,7 @@
     copy.wait()
     list_pairs(nz, ny, nb, slots, pairs)
     depth = lax.broadcasted_iota(jnp.int32, (KDIM, LANES), 0)
-    pick = jnp.where((depth >= 40) & (depth < 43), 1.0, 0.0).astype(BF16)
+    pick = jnp.where((depth == 34) | (depth == 37), 1.0, 0.0).astype(BF16)
     for m in range(ny):
         feat = column_features(pays[m][0:GEO, :].astype(F32)).astype(BF16)
         for b in range(nb):
@@ -216,7 +220,7 @@
     area = col_area[cb]
     area = jnp.concatenate([area] * (BLK // LANES), axis=1) + row_area[rb]
     top = jnp.maximum(f, 0.0) * jnp.maximum(s, 0.0)
-    return (top * pltpu.reciprocal(q * (math.pi * q - area), approx=True)).astype(BF16)
+    return (top * pltpu.reciprocal(q * (q - area), approx=True)).astype(BF16)
 
 
 def form_and_apply(start, end, unroll, last, pairs, features, tiles, acc):
@@ -351,19 +355,26 @@
         ),
     )
 
-    def along(x):
-        return [lax.ppermute(x, "gx", [(i, (i + s) % nz) for i in range(nz)]) for s in range(1, nz)]
-
-    def plane(x, after=None):
-        got = {0: x}
-        for m in range(2, ny, 2):
-            got[m] = lax.ppermute(x, "gy", [(i, i ^ m) for i in range(ny)])
-        for m in range(0, ny, 2):
-            held = got[m]
-            if after is not None and m == 0:
-                held, _ = lax.optimization_barrier((held, after))
-            got[m + 1] = lax.ppermute(held, "gy", [(i, i ^ 1) for i in range(ny)])
-        return [got[m] for m in range(ny)]
+    def exchange(row_source, column_source, after):
+        got = {"z0": row_source, "m0": column_source}
+        todo = [] if row_source is None else [f"z{s}" for s in range(1, nz)]
+        todo += [f"m{m}" for m in range(2, ny, 2)] + [f"m{m}" for m in range(1, ny, 2)]
+        while todo:
+            for name in list(todo):
+                far, step = name[0] == "z", int(name[1:])
+                source = "z0" if far else f"m{step - 1}" if step % 2 else "m0"
+                if source not in got or after.get(name, source) not in got:
+                    continue
+                held = got[source]
+                if name in after:
+                    held, _ = lax.optimization_barrier((held, got[after[name]]))
+                if far:
+                    got[name] = lax.ppermute(held, "gx", [(i, (i + step) % nz) for i in range(nz)])
+                else:
+                    turn = 1 if step % 2 else step
+                    got[name] = lax.ppermute(held, "gy", [(i, i ^ turn) for i in range(ny)])
+                todo.remove(name)
+        return got
 
     def sent(parts):
         return [
@@ -382,13 +393,53 @@
     acc = own[0]
     pairs_list = pltpu.SMEM((bounds + 2 * nz,), jnp.int32)
 
+    def exchange(row_source, column_source, after):
+        got = {"z0": row_source, "m0": column_source}
+        todo = [] if row_source is None else [f"z{s}" for s in range(1, nz)]
+        todo += [f"m{m}" for m in range(2, ny, 2)] + [f"m{m}" for m in range(1, ny, 2)]
+        while todo:
+            for name in list(todo):
+                far, step = name[0] == "z", int(name[1:])
+                source = "z0" if far else f"m{step - 1}" if step % 2 else "m0"
+                if source not in got or after.get(name, source) not in got:
+                    continue
+                held = got[source]
+                if name in after:
+                    held, _ = lax.optimization_barrier((held, got[after[name]]))
+                if far:
+                    got[name] = lax.ppermute(held, "gx", [(i, (i + step) % nz) for i in range(nz)])
+                else:
+                    turn = 1 if step % 2 else step
+                    got[name] = lax.ppermute(held, "gy", [(i, i ^ turn) for i in range(ny)])
+                todo.remove(name)
+        return got
+
+    def sent(parts):
+        return [
+            lax.ppermute(part, "gx", [(i, (i - s) % nz) for i in range(nz)])
+            for s, part in enumerate(parts, 1)
+        ]
+
+    def total(own, parts):
+        for part in parts:
+            own = own + part.astype(F32)
+        return own
+
+    own_part = jax.ShapeDtypeStruct((BANDS, patches), F32)
+    far_parts = [jax.ShapeDtypeStruct((BANDS, patches), BF16)] * (nz - 1)
+    features, own = feature_scratch(nz, ny, nb), own_scratch(nz, ny, nb)
+    acc = own[0]
+    pairs_list = pltpu.SMEM((bounds + 2 * nz,), jnp.int32)
+
     kind_hot = (
         material[None, :] == jnp.arange(reflect_table.shape[0], dtype=jnp.int32)[:, None]
     ).astype(F32)
     reflect = jnp.dot(jnp.transpose(reflect_table), kind_hot, precision=lax.Precision.HIGHEST)
 
-    rows = [geo] + along(geo)
-    cols = plane(payload, rows[1])
+    ordered = nz == 4 and ny == 8
+    got = exchange(geo, payload, FIRST_ORDER if ordered else {})
+    rows, cols = [got[f"z{s}"] for s in range(nz)], [got[f"m{m}"] for m in range(ny)]
+
 
     def whole(fluxes):
         got = call(
@@ -427,7 +478,8 @@
     else:
         irradiation = whole([])
     radiosity = emission + reflect * irradiation
-    fluxes = plane((area * radiosity).astype(BF16))
+    got = exchange(None, (area * radiosity).astype(BF16), LATER_ORDER if ordered else {})
+    fluxes = [got[f"m{m}"] for m in range(ny)]
     if keep:
         parts = [
             call(

time: 60.8 us -> 58.2 us (0.957)
  starting transfers between devices: 27.2 us -> 21.1 us
  Pallas kernels: 15.7 us -> 17.7 us
  waiting for transfers between devices: 15.7 us -> 17.4 us
    ppermute x6, starting transfers between devices: 10.9 us -> 7.1 us  [sent(): lax.ppermute(part, 'gx', [(i, (i - s) % nz) for i in range(nz)])]
    ppermute x17, waiting for transfers between devices: 8.58 us -> 10.9 us  [the longest x3 5.91 us: exchange(): lax.ppermute(held, 'gx', [(i, (i + step) % nz) for i in range(nz)])]
    ppermute x17, starting transfers between devices: 16.3 us -> 14 us  [the longest x14 9.83 us: exchange(): got[name] = lax.ppermute(held, 'gy', [(i, i ^ turn) for i in range(ny)])]
    pallas_call x7, Pallas kernels: 15.7 us -> 17.7 us  [call(): pl.pallas_call(kernel, out_shape=tuple(outs), in_specs=ins, out_specs=tup...]
    ppermute x6, waiting for transfers between devices: 7.08 us -> 6.45 us  [sent(): lax.ppermute(part, 'gx', [(i, (i - s) % nz) for i in range(nz)])]
  transfers between devices with their start and end apart: 23 -> 23, of which waited for: 10 -> 11; matrix products, arithmetic and copies ran while one was open for 2% -> 2% of each run, Pallas kernels for 7% -> 8%
where the time goes in v6:
time: 58.2 us; the launch traced here: 58 us
  starting transfers between devices  21.1 us (36%)
  Pallas kernels  17.7 us (30%)
  waiting for transfers between devices  17.4 us (30%)
  matrix products  0.95 us (2%)
  other arithmetic  0.75 us (1%)
    pallas_call x7, Pallas kernels, call(): pl.pallas_call(kernel, out_shape=tuple(outs), in_specs=ins, out_specs=tup...  17.7 us
    ppermute x14, starting transfers between devices, exchange(): got[name] = lax.ppermute(held, 'gy', [(i, i ^ turn) for i in range(ny)])  9.83 us
    ppermute x6, starting transfers between devices, sent(): lax.ppermute(part, 'gx', [(i, (i - s) % nz) for i in range(nz)])  7.1 us
    ppermute x6, waiting for transfers between devices, sent(): lax.ppermute(part, 'gx', [(i, (i - s) % nz) for i in range(nz)])  6.45 us
    ppermute x3, waiting for transfers between devices, exchange(): lax.ppermute(held, 'gx', [(i, (i + step) % nz) for i in range(nz)])  5.91 us
    ppermute x14, waiting for transfers between devices, exchange(): got[name] = lax.ppermute(held, 'gy', [(i, i ^ turn) for i in range(ny)])  5 us
    ppermute x3, starting transfers between devices, exchange(): lax.ppermute(held, 'gx', [(i, (i + step) % nz) for i in range(nz)])  4.16 us
  transfers between devices with their start and end apart: 23, of which 11 were waited for; matrix products, arithmetic and copies ran while one was open for 2% of the time, Pallas kernels for 8%

profile of v6, /device:TPU:0, one launch (start us, length us, event | category | flops | bytes accessed | tf_op | source)
XLA Modules:
  0.0 58.0 jit_solution(15917751667785759640)
XLA Ops:
  0.0 1.7 %pack.1 = (bf16[32,2048]{1,0:T(8,128)(2,1)S(1)}, bf16[16,2048]{1,0:T(8,128)(2,1)S(1)}, f32[1,2048]{1,0:T(1,128)}) custom-call(f32[3,2048]{1,0:T(4,128)} %pos_ref.1, f32[3,2048]{1,0:T(4,128)} %nrm_ref.1, f32[16,2048]{1,0:T(8,128)} %emi_ref.1, s32[1,2048]{1,0:T(1,128)} %bitcast.9, f32[1,8]{1,0:T(1,128)} %bitcast.12, s32[2,2,32]{2,1,0:T(2,128)} %bitcast.11), custom_call_target="tpu_custom_call" | custom-call | tf_op jit(solution)/shard_map/pack/pallas_call | solution.py:327
  1.7 2.9 %collective-permute-start.4 = (bf16[32,2048]{1,0:T(8,128)(2,1)S(1)}, bf16[32,2048]{1,0:T(8,128)(2,1)S(1)}, u32[]{:S(2)}, u32[]{:S(2)}) collective-permute-start(bf16[32,2048]{1,0:T(8,128)(2,1)S(1)} %get-tuple-element.25.refs_4_), channel_id=1, source_target_pairs={{0,2},{1,3},{2,0},{3,1},{4,6},{5,7},{6,4},{7,5},{8,10},{9,11},{10,... | collective-permute-start | bytes 393224 | tf_op jit(solution)/shard_map/ppermute | solution.py:413
  4.6 3.6 %collective-permute-start.2 = (bf16[16,2048]{1,0:T(8,128)(2,1)S(1)}, bf16[16,2048]{1,0:T(8,128)(2,1)S(1)}, u32[]{:S(2)}, u32[]{:S(2)}) collective-permute-start(bf16[16,2048]{1,0:T(8,128)(2,1)S(1)} %get-tuple-element.23.refs_0_), channel_id=1, source_target_pairs={{0,24},{8,0},{16,8},{24,16},{1,25},{9,1},{17,9},{25,17},{2,26},{10... | collective-permute-start | bytes 196616 | tf_op jit(solution)/shard_map/ppermute | solution.py:410
  8.2 1.5 %collective-permute-start.6 = (bf16[32,2048]{1,0:T(8,128)(2,1)S(1)}, bf16[32,2048]{1,0:T(8,128)(2,1)S(1)}, u32[]{:S(2)}, u32[]{:S(2)}) collective-permute-start(bf16[32,2048]{1,0:T(8,128)(2,1)S(1)} %get-tuple-element.25.refs_4_), channel_id=1, source_target_pairs={{0,4},{1,5},{2,6},{3,7},{4,0},{5,1},{6,2},{7,3},{8,12},{9,13},{10,... | collective-permute-start | bytes 393224 | tf_op jit(solution)/shard_map/ppermute | solution.py:413
  9.7 0.5 collective-permute-start.8
  10.2 0.5 collective-permute-done.2.refs_3_
  10.7 0.6 collective-permute-start
  11.2 4.1 %collective-permute-done.1.refs_2_ = bf16[16,2048]{1,0:T(8,128)(2,1)S(1)} collective-permute-done((bf16[16,2048]{1,0:T(8,128)(2,1)S(1)}, bf16[16,2048]{1,0:T(8,128)(2,1)S(1)}, u32[]{:S(2)}, u32[]{:S(2)}) %collective-permute-start.1) | collective-permute-done | bytes 65568 | tf_op jit(solution)/shard_map/ppermute | solution.py:410
  15.4 0.5 collective-permute-start.5
  15.9 1.3 %collective-permute-done.refs_1_ = bf16[16,2048]{1,0:T(8,128)(2,1)S(1)} collective-permute-done((bf16[16,2048]{1,0:T(8,128)(2,1)S(1)}, bf16[16,2048]{1,0:T(8,128)(2,1)S(1)}, u32[]{:S(2)}, u32[]{:S(2)}) %collective-permute-start) | collective-permute-done | bytes 65568 | tf_op jit(solution)/shard_map/ppermute | solution.py:410
  17.2 0.0 collective-permute-done.6.refs_8_
  17.2 0.0 collective-permute-start.7
  17.2 0.5 collective-permute-start.9
  17.7 0.0 collective-permute-done.3.refs_5_
  17.7 0.0 collective-permute-done.5.refs_7_
  17.7 0.8 %collective-permute-done.7.refs_9_ = bf16[32,2048]{1,0:T(8,128)(2,1)S(1)} collective-permute-done((bf16[32,2048]{1,0:T(8,128)(2,1)S(1)}, bf16[32,2048]{1,0:T(8,128)(2,1)S(1)}, u32[]{:S(2)}, u32[]{:S(2)}) %collective-permute-start.7) | collective-permute-done | bytes 131104 | tf_op jit(solution)/shard_map/ppermute | solution.py:413
  18.5 0.2 collective-permute-done.9.refs_11_
  18.7 10.8 %far.1 = (bf16[16,2048]{1,0:T(8,128)(2,1)S(1)}, bf16[16,2048]{1,0:T(8,128)(2,1)S(1)}, bf16[16,2048]{1,0:T(8,128)(2,1)S(1)}, bf16[112,256,256]{2,1,0:T(8,128)(2,1...) custom-call(bf16[16,2048]{1,0:T(8,128)(2,1)S(1)} %get-tuple-element., ...), custom_call_target="tpu_custom_call" | custom-call | tf_op jit(solution)/shard_map/far/pallas_call | solution.py:327
  29.6 3.2 %collective-permute-start.10 = (bf16[16,2048]{1,0:T(8,128)(2,1)S(1)}, bf16[16,2048]{1,0:T(8,128)(2,1)S(1)}, u32[]{:S(2)}, u32[]{:S(2)}) collective-permute-start(bf16[16,2048]{1,0:T(8,128)(2,1)S(1)} %get-tuple-element.37), channel_id=1, source_target_pairs={{0,24},{8,0},{16,8},{24,16},{1,25},{9,1},{17,9},{25,17},{2,26},{10... | collective-permute-start | bytes 196616 | tf_op jit(solution)/shard_map/ppermute | solution.py:419
  32.7 0.0 collective-permute-start.11
  32.7 0.6 %collective-permute-start.12 = (bf16[16,2048]{1,0:T(8,128)(2,1)S(1)}, bf16[16,2048]{1,0:T(8,128)(2,1)S(1)}, u32[]{:S(2)}, u32[]{:S(2)}) collective-permute-start(bf16[16,2048]{1,0:T(8,128)(2,1)S(1)} %get-tuple-element.39), channel_id=1, source_target_pairs={{0,8},{8,16},{16,24},{24,0},{1,9},{9,17},{17,25},{25,1},{2,10},{10... | collective-permute-start | bytes 196616 | tf_op jit(solution)/shard_map/ppermute | solution.py:419
  33.4 0.9 %convolution_bitcast_fusion = f32[16,2048]{1,0:T(8,128)S(1)} fusion(f32[8,16]{1,0:T(8,128)S(1)} %copy-done, s32[2048]{0:T(1024)} %param.11), kind=kOutput, calls=%fused_computation | convolution fusion | flops 3162112 | bytes 139776 | tf_op jit(solution)/shard_map/dot_general | solution.py:437
  34.3 0.0 copy-start.1
  34.3 0.0 copy-start.2
  34.4 2.7 %near.1 = (f32[16,2048]{1,0:T(8,128)S(1)}, bf16[48,256,256]{2,1,0:T(8,128)(2,1)S(1)}) custom-call(s32[168]{0:T(256)S(4)} %get-tuple-element.28.pairs, bf16[32,3,48,256]{3,2,1,0:T(8,128)(2,1)S(1)} %get-tuple-element.29.refs_0_, f32[32,1,256]{2,1,0:T(1,128)S(1)} %get-tuple-element.30.refs_1_, bf16[64,256,48]{2,1,0:T(8,128)(2,1)S(1)} %get-tuple-element.31.refs_2_, ...), custom_call_target="tpu_custom_call" | custom-call | tf_op jit(solution)/shard_map/near/pallas_call | solution.py:327
  37.1 0.0 collective-permute-done.10
  37.1 2.0 %collective-permute-done.11 = bf16[16,2048]{1,0:T(8,128)(2,1)S(1)} collective-permute-done((bf16[16,2048]{1,0:T(8,128)(2,1)S(1)}, bf16[16,2048]{1,0:T(8,128)(2,1)S(1)}, u32[]{:S(2)}, u32[]{:S(2)}) %collective-permute-start.11) | collective-permute-done | bytes 65568 | tf_op jit(solution)/shard_map/ppermute | solution.py:419
  39.0 0.0 collective-permute-done.12
  39.1 0.1 multiply_convert_fusion.refs_0_
  39.1 0.1 collective-permute-start.14
  39.2 1.4 %collective-permute-start.16 = (bf16[16,2048]{1,0:T(8,128)(2,1)S(1)}, bf16[16,2048]{1,0:T(8,128)(2,1)S(1)}, u32[]{:S(2)}, u32[]{:S(2)}) collective-permute-start(bf16[16,2048]{1,0:T(8,128)(2,1)S(1)} %multiply_convert_fusion.refs_0_), channel_id=1, source_target_pairs={{0,4},{1,5},{2,6},{3,7},{4,0},{5,1},{6,2},{7,3},{8,12},{9,13},{10,... | collective-permute-start | bytes 196616 | tf_op jit(solution)/shard_map/ppermute | solution.py:413
  40.6 2.1 %collective-permute-start.18 = (bf16[16,2048]{1,0:T(8,128)(2,1)S(1)}, bf16[16,2048]{1,0:T(8,128)(2,1)S(1)}, u32[]{:S(2)}, u32[]{:S(2)}) collective-permute-start(bf16[16,2048]{1,0:T(8,128)(2,1)S(1)} %multiply_convert_fusion.refs_0_), channel_id=1, source_target_pairs={{0,6},{1,7},{2,4},{3,5},{4,2},{5,3},{6,0},{7,1},{8,14},{9,15},{10,... | collective-permute-start | bytes 196616 | tf_op jit(solution)/shard_map/ppermute | solution.py:413
  42.7 0.0 collective-permute-start.13
  42.7 1.2 %collective-permute-done.14.refs_2_ = bf16[16,2048]{1,0:T(8,128)(2,1)S(1)} collective-permute-done((bf16[16,2048]{1,0:T(8,128)(2,1)S(1)}, bf16[16,2048]{1,0:T(8,128)(2,1)S(1)}, u32[]{:S(2)}, u32[]{:S(2)}) %collective-permute-start.14) | collective-permute-done | bytes 65568 | tf_op jit(solution)/shard_map/ppermute | solution.py:413
  43.9 0.0 collective-permute-start.15
  43.9 0.2 collective-permute-done.16.refs_4_
  44.1 0.3 collective-permute-start.17
  44.4 1.3 %collective-permute-done.18.refs_6_ = bf16[16,2048]{1,0:T(8,128)(2,1)S(1)} collective-permute-done((bf16[16,2048]{1,0:T(8,128)(2,1)S(1)}, bf16[16,2048]{1,0:T(8,128)(2,1)S(1)}, u32[]{:S(2)}, u32[]{:S(2)}) %collective-permute-start.18) | collective-permute-done | bytes 65568 | tf_op jit(solution)/shard_map/ppermute | solution.py:413
  45.8 1.2 %collective-permute-done.19.refs_7_ = bf16[16,2048]{1,0:T(8,128)(2,1)S(1)} collective-permute-done((bf16[16,2048]{1,0:T(8,128)(2,1)S(1)}, bf16[16,2048]{1,0:T(8,128)(2,1)S(1)}, u32[]{:S(2)}, u32[]{:S(2)}) %collective-permute-start.19) | collective-permute-done | bytes 65568 | tf_op jit(solution)/shard_map/ppermute | solution.py:413
  47.0 0.6 apply.5
  47.6 1.0 %collective-permute-start.20 = (bf16[16,2048]{1,0:T(8,128)(2,1)S(1)}, bf16[16,2048]{1,0:T(8,128)(2,1)S(1)}, u32[]{:S(2)}, u32[]{:S(2)}) collective-permute-start(bf16[16,2048]{1,0:T(8,128)(2,1)S(1)} %apply.5), channel_id=1, source_target_pairs={{0,24},{8,0},{16,8},{24,16},{1,25},{9,1},{17,9},{25,17},{2,26},{10... | collective-permute-start | bytes 196616 | tf_op jit(solution)/shard_map/ppermute | solution.py:419
  48.5 0.6 apply.6
  49.1 1.0 %collective-permute-start.21 = (bf16[16,2048]{1,0:T(8,128)(2,1)S(1)}, bf16[16,2048]{1,0:T(8,128)(2,1)S(1)}, u32[]{:S(2)}, u32[]{:S(2)}) collective-permute-start(bf16[16,2048]{1,0:T(8,128)(2,1)S(1)} %apply.6), channel_id=1, source_target_pairs={{0,16},{8,24},{16,0},{24,8},{1,17},{9,25},{17,1},{25,9},{2,18},{10... | collective-permute-start | bytes 196616 | tf_op jit(solution)/shard_map/ppermute | solution.py:419
  50.1 0.8 %apply.7 = bf16[16,2048]{1,0:T(8,128)(2,1)S(1)} custom-call(s32[168]{0:T(256)S(4)} %get-tuple-element.28.pairs, bf16[112,256,256]{2,1,0:T(8,128)(2,1)S(1)} %get-tuple-element.40.tiles, bf16[16,2048]{1,0:T(8,128)(2,1)S(1)} %multiply_convert_fusion.refs_0_, bf16[16,2048]{1,0:T(8,128)(2,1)S(1)} %collective-permute-done.13.refs_1_, ...), custom_call_target="tpu_custom_call" | custom-call | tf_op jit(solution)/shard_map/apply/pallas_call | solution.py:327
  50.9 1.3 %collective-permute-start.22 = (bf16[16,2048]{1,0:T(8,128)(2,1)S(1)}, bf16[16,2048]{1,0:T(8,128)(2,1)S(1)}, u32[]{:S(2)}, u32[]{:S(2)}) collective-permute-start(bf16[16,2048]{1,0:T(8,128)(2,1)S(1)} %apply.7), channel_id=1, source_target_pairs={{0,8},{8,16},{16,24},{24,0},{1,9},{9,17},{17,25},{25,1},{2,10},{10... | collective-permute-start | bytes 196616 | tf_op jit(solution)/shard_map/ppermute | solution.py:419
  52.3 0.6 apply.4
  52.8 4.5 %collective-permute-done.21 = bf16[16,2048]{1,0:T(8,128)(2,1)S(1)} collective-permute-done((bf16[16,2048]{1,0:T(8,128)(2,1)S(1)}, bf16[16,2048]{1,0:T(8,128)(2,1)S(1)}, u32[]{:S(2)}, u32[]{:S(2)}) %collective-permute-start.21) | collective-permute-done | bytes 65568 | tf_op jit(solution)/shard_map/ppermute | solution.py:419
  57.3 0.7 %multiply_add_fusion = f32[16,2048]{1,0:T(8,128)} fusion(f32[16,2048]{1,0:T(8,128)S(1)} %copy-done.1, f32[16,2048]{1,0:T(8,128)S(1)} %convolution_bitcast_fusion, bf16[16,2048]{1,0:T(8,128)(2,1)S(1)} %collective-permute-done.22, bf16[16,2048]{1,0:T(8,128)(2,1)S(1)} %collective-permute-done.21, f32[16,2048]{1,0:T(8,128)S(1)} %apply.4, ...), kind=kLoop, calls=%fused_computation.1 | loop fusion | flops 262144 | bytes 720896 | tf_op jit(solution)/shard_map/add | solution.py:499
  (14 shorter events, 0.0 us)
Async XLA Ops:
  0.0 33.4 %copy-start = (f32[8,16]{1,0:T(8,128)S(1)}, f32[8,16]{1,0:T(8,128)}, u32[]{:S(2)}) copy-start(f32[8,16]{1,0:T(8,128)} %param.13) | copy-start | bytes 1540
  1.7 13.7 %collective-permute-start.4 = (bf16[32,2048]{1,0:T(8,128)(2,1)S(1)}, bf16[32,2048]{1,0:T(8,128)(2,1)S(1)}, u32[]{:S(2)}, u32[]{:S(2)}) collective-permute-start(bf16[32,2048]{1,0:T(8,128)(2,1)S(1)} %get-tuple-element.25.refs_4_), channel_id=1, source_target_pairs={{0,2},{1,3},{2,0},{3,1},{4,6},{5,7},{6,4},{7,5},{8,10},{9,11},{10,... | collective-permute-start | bytes 393224 | tf_op jit(solution)/shard_map/ppermute | solution.py:413
  4.6 6.1 %collective-permute-start.2 = (bf16[16,2048]{1,0:T(8,128)(2,1)S(1)}, bf16[16,2048]{1,0:T(8,128)(2,1)S(1)}, u32[]{:S(2)}, u32[]{:S(2)}) collective-permute-start(bf16[16,2048]{1,0:T(8,128)(2,1)S(1)} %get-tuple-element.23.refs_0_), channel_id=1, source_target_pairs={{0,24},{8,0},{16,8},{24,16},{1,25},{9,1},{17,9},{25,17},{2,26},{10... | collective-permute-start | bytes 196616 | tf_op jit(solution)/shard_map/ppermute | solution.py:410
  8.2 9.0 %collective-permute-start.6 = (bf16[32,2048]{1,0:T(8,128)(2,1)S(1)}, bf16[32,2048]{1,0:T(8,128)(2,1)S(1)}, u32[]{:S(2)}, u32[]{:S(2)}) collective-permute-start(bf16[32,2048]{1,0:T(8,128)(2,1)S(1)} %get-tuple-element.25.refs_4_), channel_id=1, source_target_pairs={{0,4},{1,5},{2,6},{3,7},{4,0},{5,1},{6,2},{7,3},{8,12},{9,13},{10,... | collective-permute-start | bytes 393224 | tf_op jit(solution)/shard_map/ppermute | solution.py:413
  9.7 7.5 %collective-permute-start.8 = (bf16[32,2048]{1,0:T(8,128)(2,1)S(1)}, bf16[32,2048]{1,0:T(8,128)(2,1)S(1)}, u32[]{:S(2)}, u32[]{:S(2)}) collective-permute-start(bf16[32,2048]{1,0:T(8,128)(2,1)S(1)} %get-tuple-element.25.refs_4_), channel_id=1, source_target_pairs={{0,6},{1,7},{2,4},{3,5},{4,2},{5,3},{6,0},{7,1},{8,14},{9,15},{10,... | collective-permute-start | bytes 393224 | tf_op jit(solution)/shard_map/ppermute | solution.py:413
  10.2 5.2 %collective-permute-start.1 = (bf16[16,2048]{1,0:T(8,128)(2,1)S(1)}, bf16[16,2048]{1,0:T(8,128)(2,1)S(1)}, u32[]{:S(2)}, u32[]{:S(2)}) collective-permute-start(bf16[16,2048]{1,0:T(8,128)(2,1)S(1)} %get-tuple-element.23.refs_0_), channel_id=1, source_target_pairs={{0,16},{8,24},{16,0},{24,8},{1,17},{9,25},{17,1},{25,9},{2,18},{10... | collective-permute-start | bytes 196616 | tf_op jit(solution)/shard_map/ppermute | solution.py:410
  10.7 6.5 %collective-permute-start = (bf16[16,2048]{1,0:T(8,128)(2,1)S(1)}, bf16[16,2048]{1,0:T(8,128)(2,1)S(1)}, u32[]{:S(2)}, u32[]{:S(2)}) collective-permute-start(bf16[16,2048]{1,0:T(8,128)(2,1)S(1)} %get-tuple-element.23.refs_0_), channel_id=1, source_target_pairs={{0,8},{8,16},{16,24},{24,0},{1,9},{9,17},{17,25},{25,1},{2,10},{10... | collective-permute-start | bytes 196616 | tf_op jit(solution)/shard_map/ppermute | solution.py:410
  15.4 2.3 %collective-permute-start.3 = (bf16[32,2048]{1,0:T(8,128)(2,1)S(1)}, bf16[32,2048]{1,0:T(8,128)(2,1)S(1)}, u32[]{:S(2)}, u32[]{:S(2)}) collective-permute-start(bf16[32,2048]{1,0:T(8,128)(2,1)S(1)} %get-tuple-element.25.refs_4_), channel_id=1, source_target_pairs={{0,1},{1,0},{2,3},{3,2},{4,5},{5,4},{6,7},{7,6},{8,9},{9,8},{10,11... | collective-permute-start | bytes 393224 | tf_op jit(solution)/shard_map/ppermute | solution.py:413
  15.4 2.3 %collective-permute-start.5 = (bf16[32,2048]{1,0:T(8,128)(2,1)S(1)}, bf16[32,2048]{1,0:T(8,128)(2,1)S(1)}, u32[]{:S(2)}, u32[]{:S(2)}) collective-permute-start(bf16[32,2048]{1,0:T(8,128)(2,1)S(1)} %collective-permute-done.4.refs_6_), channel_id=1, source_target_pairs={{0,1},{1,0},{2,3},{3,2},{4,5},{5,4},{6,7},{7,6},{8,9},{9,8},{10,11... | collective-permute-start | bytes 393224 | tf_op jit(solution)/shard_map/ppermute | solution.py:413
  17.2 1.3 %collective-permute-start.7 = (bf16[32,2048]{1,0:T(8,128)(2,1)S(1)}, bf16[32,2048]{1,0:T(8,128)(2,1)S(1)}, u32[]{:S(2)}, u32[]{:S(2)}) collective-permute-start(bf16[32,2048]{1,0:T(8,128)(2,1)S(1)} %collective-permute-done.6.refs_8_), channel_id=1, source_target_pairs={{0,1},{1,0},{2,3},{3,2},{4,5},{5,4},{6,7},{7,6},{8,9},{9,8},{10,11... | collective-permute-start | bytes 393224 | tf_op jit(solution)/shard_map/ppermute | solution.py:413
  17.2 1.5 %collective-permute-start.9 = (bf16[32,2048]{1,0:T(8,128)(2,1)S(1)}, bf16[32,2048]{1,0:T(8,128)(2,1)S(1)}, u32[]{:S(2)}, u32[]{:S(2)}) collective-permute-start(bf16[32,2048]{1,0:T(8,128)(2,1)S(1)} %collective-permute-done.8.refs_10_), channel_id=1, source_target_pairs={{0,1},{1,0},{2,3},{3,2},{4,5},{5,4},{6,7},{7,6},{8,9},{9,8},{10,11... | collective-permute-start | bytes 393224 | tf_op jit(solution)/shard_map/ppermute | solution.py:413
  29.6 7.5 %collective-permute-start.10 = (bf16[16,2048]{1,0:T(8,128)(2,1)S(1)}, bf16[16,2048]{1,0:T(8,128)(2,1)S(1)}, u32[]{:S(2)}, u32[]{:S(2)}) collective-permute-start(bf16[16,2048]{1,0:T(8,128)(2,1)S(1)} %get-tuple-element.37), channel_id=1, source_target_pairs={{0,24},{8,0},{16,8},{24,16},{1,25},{9,1},{17,9},{25,17},{2,26},{10... | collective-permute-start | bytes 196616 | tf_op jit(solution)/shard_map/ppermute | solution.py:419
  32.7 6.3 %collective-permute-start.11 = (bf16[16,2048]{1,0:T(8,128)(2,1)S(1)}, bf16[16,2048]{1,0:T(8,128)(2,1)S(1)}, u32[]{:S(2)}, u32[]{:S(2)}) collective-permute-start(bf16[16,2048]{1,0:T(8,128)(2,1)S(1)} %get-tuple-element.38), channel_id=1, source_target_pairs={{0,16},{8,24},{16,0},{24,8},{1,17},{9,25},{17,1},{25,9},{2,18},{10... | collective-permute-start | bytes 196616 | tf_op jit(solution)/shard_map/ppermute | solution.py:419
  32.7 6.3 %collective-permute-start.12 = (bf16[16,2048]{1,0:T(8,128)(2,1)S(1)}, bf16[16,2048]{1,0:T(8,128)(2,1)S(1)}, u32[]{:S(2)}, u32[]{:S(2)}) collective-permute-start(bf16[16,2048]{1,0:T(8,128)(2,1)S(1)} %get-tuple-element.39), channel_id=1, source_target_pairs={{0,8},{8,16},{16,24},{24,0},{1,9},{9,17},{17,25},{25,1},{2,10},{10... | collective-permute-start | bytes 196616 | tf_op jit(solution)/shard_map/ppermute | solution.py:419
  34.3 4.7 %copy-start.1 = (f32[16,2048]{1,0:T(8,128)S(1)}, f32[16,2048]{1,0:T(8,128)}, u32[]{:S(2)}) copy-start(f32[16,2048]{1,0:T(8,128)} %emi_ref.1) | copy-start | bytes 393220
  34.3 4.7 %copy-start.2 = (f32[1,2048]{1,0:T(1,128)S(1)}, f32[1,2048]{1,0:T(1,128)}, u32[]{:S(2)}) copy-start(f32[1,2048]{1,0:T(1,128)} %get-tuple-element.35) | copy-start | bytes 24580
  39.1 4.8 %collective-permute-start.14 = (bf16[16,2048]{1,0:T(8,128)(2,1)S(1)}, bf16[16,2048]{1,0:T(8,128)(2,1)S(1)}, u32[]{:S(2)}, u32[]{:S(2)}) collective-permute-start(bf16[16,2048]{1,0:T(8,128)(2,1)S(1)} %multiply_convert_fusion.refs_0_), channel_id=1, source_target_pairs={{0,2},{1,3},{2,0},{3,1},{4,6},{5,7},{6,4},{7,5},{8,10},{9,11},{10,... | collective-permute-start | bytes 196616 | tf_op jit(solution)/shard_map/ppermute | solution.py:413
  39.2 4.9 %collective-permute-start.16 = (bf16[16,2048]{1,0:T(8,128)(2,1)S(1)}, bf16[16,2048]{1,0:T(8,128)(2,1)S(1)}, u32[]{:S(2)}, u32[]{:S(2)}) collective-permute-start(bf16[16,2048]{1,0:T(8,128)(2,1)S(1)} %multiply_convert_fusion.refs_0_), channel_id=1, source_target_pairs={{0,4},{1,5},{2,6},{3,7},{4,0},{5,1},{6,2},{7,3},{8,12},{9,13},{10,... | collective-permute-start | bytes 196616 | tf_op jit(solution)/shard_map/ppermute | solution.py:413
  40.6 5.2 %collective-permute-start.18 = (bf16[16,2048]{1,0:T(8,128)(2,1)S(1)}, bf16[16,2048]{1,0:T(8,128)(2,1)S(1)}, u32[]{:S(2)}, u32[]{:S(2)}) collective-permute-start(bf16[16,2048]{1,0:T(8,128)(2,1)S(1)} %multiply_convert_fusion.refs_0_), channel_id=1, source_target_pairs={{0,6},{1,7},{2,4},{3,5},{4,2},{5,3},{6,0},{7,1},{8,14},{9,15},{10,... | collective-permute-start | bytes 196616 | tf_op jit(solution)/shard_map/ppermute | solution.py:413
  42.7 3.1 %collective-permute-start.13 = (bf16[16,2048]{1,0:T(8,128)(2,1)S(1)}, bf16[16,2048]{1,0:T(8,128)(2,1)S(1)}, u32[]{:S(2)}, u32[]{:S(2)}) collective-permute-start(bf16[16,2048]{1,0:T(8,128)(2,1)S(1)} %multiply_convert_fusion.refs_0_), channel_id=1, source_target_pairs={{0,1},{1,0},{2,3},{3,2},{4,5},{5,4},{6,7},{7,6},{8,9},{9,8},{10,11... | collective-permute-start | bytes 196616 | tf_op jit(solution)/shard_map/ppermute | solution.py:413
  43.9 1.8 %collective-permute-start.15 = (bf16[16,2048]{1,0:T(8,128)(2,1)S(1)}, bf16[16,2048]{1,0:T(8,128)(2,1)S(1)}, u32[]{:S(2)}, u32[]{:S(2)}) collective-permute-start(bf16[16,2048]{1,0:T(8,128)(2,1)S(1)} %collective-permute-done.14.refs_2_), channel_id=1, source_target_pairs={{0,1},{1,0},{2,3},{3,2},{4,5},{5,4},{6,7},{7,6},{8,9},{9,8},{10,11... | collective-permute-start | bytes 196616 | tf_op jit(solution)/shard_map/ppermute | solution.py:413
  44.1 1.6 %collective-permute-start.17 = (bf16[16,2048]{1,0:T(8,128)(2,1)S(1)}, bf16[16,2048]{1,0:T(8,128)(2,1)S(1)}, u32[]{:S(2)}, u32[]{:S(2)}) collective-permute-start(bf16[16,2048]{1,0:T(8,128)(2,1)S(1)} %collective-permute-done.16.refs_4_), channel_id=1, source_target_pairs={{0,1},{1,0},{2,3},{3,2},{4,5},{5,4},{6,7},{7,6},{8,9},{9,8},{10,11... | collective-permute-start | bytes 196616 | tf_op jit(solution)/shard_map/ppermute | solution.py:413
  45.7 1.3 %collective-permute-start.19 = (bf16[16,2048]{1,0:T(8,128)(2,1)S(1)}, bf16[16,2048]{1,0:T(8,128)(2,1)S(1)}, u32[]{:S(2)}, u32[]{:S(2)}) collective-permute-start(bf16[16,2048]{1,0:T(8,128)(2,1)S(1)} %collective-permute-done.18.refs_6_), channel_id=1, source_target_pairs={{0,1},{1,0},{2,3},{3,2},{4,5},{5,4},{6,7},{7,6},{8,9},{9,8},{10,11... | collective-permute-start | bytes 196616 | tf_op jit(solution)/shard_map/ppermute | solution.py:413
  47.6 5.3 %collective-permute-start.20 = (bf16[16,2048]{1,0:T(8,128)(2,1)S(1)}, bf16[16,2048]{1,0:T(8,128)(2,1)S(1)}, u32[]{:S(2)}, u32[]{:S(2)}) collective-permute-start(bf16[16,2048]{1,0:T(8,128)(2,1)S(1)} %apply.5), channel_id=1, source_target_pairs={{0,24},{8,0},{16,8},{24,16},{1,25},{9,1},{17,9},{25,17},{2,26},{10... | collective-permute-start | bytes 196616 | tf_op jit(solution)/shard_map/ppermute | solution.py:419
  49.1 8.2 %collective-permute-start.21 = (bf16[16,2048]{1,0:T(8,128)(2,1)S(1)}, bf16[16,2048]{1,0:T(8,128)(2,1)S(1)}, u32[]{:S(2)}, u32[]{:S(2)}) collective-permute-start(bf16[16,2048]{1,0:T(8,128)(2,1)S(1)} %apply.6), channel_id=1, source_target_pairs={{0,16},{8,24},{16,0},{24,8},{1,17},{9,25},{17,1},{25,9},{2,18},{10... | collective-permute-start | bytes 196616 | tf_op jit(solution)/shard_map/ppermute | solution.py:419
  50.9 6.4 %collective-permute-start.22 = (bf16[16,2048]{1,0:T(8,128)(2,1)S(1)}, bf16[16,2048]{1,0:T(8,128)(2,1)S(1)}, u32[]{:S(2)}, u32[]{:S(2)}) collective-permute-start(bf16[16,2048]{1,0:T(8,128)(2,1)S(1)} %apply.7), channel_id=1, source_target_pairs={{0,8},{8,16},{16,24},{24,0},{1,9},{9,17},{17,25},{25,1},{2,10},{10... | collective-permute-start | bytes 196616 | tf_op jit(solution)/shard_map/ppermute | solution.py:419

commit v7 on v6

--- a/solution.py
+++ b/solution.py
@@ -16,8 +16,9 @@
 KDIM = 48
 APPLY_UNROLL = 8
 SPARE = 8
-FIRST_ORDER = {"m1": "z3", "m3": "z2", "m5": "z1"}
+FIRST_ORDER = {"m1": "z1", "m3": "z2", "m5": "z3"}
 LATER_ORDER = {}
+TOGETHER = [(1,), (2,), (3,), (0,)]
 KEEP_BYTES = 24 * 2**20
 BF16 = jnp.bfloat16
 F32 = jnp.float32
@@ -35,7 +36,9 @@
     return out
 
 
-def pack_kernel(pos_ref, nrm_ref, emi_ref, level_ref, table_ref, slot_ref, pay_ref, geo_ref, area_ref, rows):
+def pack_kernel(
+    pos_ref, nrm_ref, emi_ref, level_ref, table_ref, kind_ref, share_ref, slot_ref, pay_ref, geo_ref, area_ref, reflect_ref, rows
+):
     level = level_ref[...]
     area = jnp.zeros(level.shape, F32)
     for k in range(table_ref.shape[1]):
@@ -58,6 +61,12 @@
     geo_ref[...] = geo
     pay_ref[0:GEO, :] = geo
     pay_ref[GEO:, :] = (area * emi_ref[...]).astype(BF16)
+    kind = jnp.broadcast_to(kind_ref[...], reflect_ref.shape)
+    share = jnp.transpose(share_ref[...])
+    reflect = jnp.zeros(reflect_ref.shape, F32)
+    for k in range(share.shape[1]):
+        reflect = jnp.where(kind == k, share[:, k : k + 1], reflect)
+    reflect_ref[...] = reflect
 
 
 def terms_of(g):
@@ -285,16 +294,18 @@
     put_out(nb, acc, [out], 0)
 
 
-def apply_kernel(nz, ny, nb, s, pairs, tiles, *refs):
-    fluxes, out, flux, acc = refs[:ny], *refs[ny:]
+def apply_kernel(nz, ny, nb, lines, pairs, *refs):
+    tiles, refs = refs[: len(lines)], refs[len(lines) :]
+    fluxes, outs, flux, acc = refs[:ny], refs[ny:-2], *refs[-2:]
     second, bounds = sections(nz, ny)
     for m in range(ny):
         for b in range(nb):
             flux[m * nb + b] = fluxes[m][:, b * BLK : (b + 1) * BLK]
-    acc[...] = jnp.zeros(acc.shape, F32)
-    start = 0 if s else second
-    apply_tiles(start, pairs[bounds + 2 * s], pairs[bounds + 2 * s + 1], nb, pairs, tiles, flux, acc)
-    put_out(nb, acc, [out], 0)
+    for s, tile, out in zip(lines, tiles, outs):
+        acc[...] = jnp.zeros(acc.shape, F32)
+        start = 0 if s else second
+        apply_tiles(start, pairs[bounds + 2 * s], pairs[bounds + 2 * s + 1], nb, pairs, tile, flux, acc)
+        put_out(nb, acc, [out], 0)
 
 
 def whole_kernel(nz, ny, nb, fresh, *refs):
@@ -334,15 +345,16 @@
             name=name,
         )(*args)
 
-    payload, geo, area = call(
+    payload, geo, area, reflect = call(
         pack_kernel,
         "pack",
         None,
-        [VMEM()] * 6,
+        [VMEM()] * 8,
         [
             pltpu.VMEM((GEO + BANDS, patches), BF16),
             pltpu.VMEM((GEO, patches), BF16),
-            jax.ShapeDtypeStruct((1, patches), F32),
+            pltpu.VMEM((1, patches), F32),
+            pltpu.VMEM((BANDS, patches), F32),
         ],
         [pltpu.VMEM((GEO, patches), F32)],
         (
@@ -351,6 +363,8 @@
             emission,
             area_level.reshape(1, patches),
             area_table.reshape(1, -1),
+            material.reshape(1, patches),
+            reflect_table,
             jnp.transpose(pair_slots[0], (1, 2, 0)),
         ),
     )
@@ -393,53 +407,9 @@
     acc = own[0]
     pairs_list = pltpu.SMEM((bounds + 2 * nz,), jnp.int32)
 
-    def exchange(row_source, column_source, after):
-        got = {"z0": row_source, "m0": column_source}
-        todo = [] if row_source is None else [f"z{s}" for s in range(1, nz)]
-        todo += [f"m{m}" for m in range(2, ny, 2)] + [f"m{m}" for m in range(1, ny, 2)]
-        while todo:
-            for name in list(todo):
-                far, step = name[0] == "z", int(name[1:])
-                source = "z0" if far else f"m{step - 1}" if step % 2 else "m0"
-                if source not in got or after.get(name, source) not in got:
-                    continue
-                held = got[source]
-                if name in after:
-                    held, _ = lax.optimization_barrier((held, got[after[name]]))
-                if far:
-                    got[name] = lax.ppermute(held, "gx", [(i, (i + step) % nz) for i in range(nz)])
-                else:
-                    turn = 1 if step % 2 else step
-                    got[name] = lax.ppermute(held, "gy", [(i, i ^ turn) for i in range(ny)])
-                todo.remove(name)
-        return got
-
-    def sent(parts):
-        return [
-            lax.ppermute(part, "gx", [(i, (i - s) % nz) for i in range(nz)])
-            for s, part in enumerate(parts, 1)
-        ]
-
-    def total(own, parts):
-        for part in parts:
-            own = own + part.astype(F32)
-        return own
-
-    own_part = jax.ShapeDtypeStruct((BANDS, patches), F32)
-    far_parts = [jax.ShapeDtypeStruct((BANDS, patches), BF16)] * (nz - 1)
-    features, own = feature_scratch(nz, ny, nb), own_scratch(nz, ny, nb)
-    acc = own[0]
-    pairs_list = pltpu.SMEM((bounds + 2 * nz,), jnp.int32)
-
-    kind_hot = (
-        material[None, :] == jnp.arange(reflect_table.shape[0], dtype=jnp.int32)[:, None]
-    ).astype(F32)
-    reflect = jnp.dot(jnp.transpose(reflect_table), kind_hot, precision=lax.Precision.HIGHEST)
-
     ordered = nz == 4 and ny == 8
     got = exchange(geo, payload, FIRST_ORDER if ordered else {})
     rows, cols = [got[f"z{s}"] for s in range(nz)], [got[f"m{m}"] for m in range(ny)]
-
 
     def whole(fluxes):
         got = call(
@@ -481,19 +451,19 @@
     got = exchange(None, (area * radiosity).astype(BF16), LATER_ORDER if ordered else {})
     fluxes = [got[f"m{m}"] for m in range(ny)]
     if keep:
-        parts = [
-            call(
-                functools.partial(apply_kernel, nz, ny, nb, s),
+        parts = {}
+        for lines in TOGETHER if ordered else [range(1, nz), [0]]:
+            got = call(
+                functools.partial(apply_kernel, nz, ny, nb, lines),
                 "apply",
                 4,
-                [SMEM()] + [VMEM()] * (1 + ny),
-                [far_parts[0] if s else own_part],
+                [SMEM()] + [VMEM()] * (len(lines) + ny),
+                [far_parts[0] if s else own_part for s in lines],
                 [features[4], pltpu.VMEM((nb + 1, BANDS, BLK), F32)],
-                (pairs, far_tiles if s else near_tiles, *fluxes),
-            )[0]
-            for s in range(nz)
-        ]
-        irradiation = total(parts[0], sent(parts[1:]))
+                (pairs, *[far_tiles if s else near_tiles for s in lines], *fluxes),
+            )
+            parts.update(zip(lines, got))
+        irradiation = total(parts[0], sent([parts[s] for s in range(1, nz)]))
     else:
         irradiation = whole(fluxes)
     return emission + reflect * irradiation

time: 58.2 us -> 56.7 us (0.974)
  starting transfers between devices: 21.1 us -> 24 us
  waiting for transfers between devices: 17.4 us -> 15.5 us
  Pallas kernels: 17.7 us -> 16.2 us
  matrix products: 0.95 us -> 0 us
    ppermute x6, starting transfers between devices: 7.1 us -> 10.1 us  [sent(): lax.ppermute(part, 'gx', [(i, (i - s) % nz) for i in range(nz)])]
    pallas_call x7, Pallas kernels: 17.7 us -> 16.2 us  [call(): pl.pallas_call(kernel, out_shape=tuple(outs), in_specs=ins, out_specs=tup...]
    ppermute x6, waiting for transfers between devices: 6.45 us -> 5.1 us  [sent(): lax.ppermute(part, 'gx', [(i, (i - s) % nz) for i in range(nz)])]
    ppermute x3, waiting for transfers between devices: 5.91 us -> 4.56 us  [exchange(): lax.ppermute(held, 'gx', [(i, (i + step) % nz) for i in range(nz)])]
    dot_general x1 -> x0, matrix products: 0.95 us -> none  [per_device(): jnp.dot(jnp.transpose(reflect_table), kind_hot, precision=lax.Precision.H...]
    ppermute x14, waiting for transfers between devices: 5 us -> 5.81 us  [exchange(): got[name] = lax.ppermute(held, 'gy', [(i, i ^ turn) for i in range(ny)])]
  transfers between devices with their start and end apart: 23 -> 23, of which waited for: 11 -> 12; matrix products, arithmetic and copies ran while one was open for 2% -> 0% of each run, Pallas kernels for 8% -> 10%
where the time goes in v7:
time: 56.7 us; the launch traced here: 56.6 us
  starting transfers between devices  24 us (42%)
  Pallas kernels  16.2 us (29%)
  waiting for transfers between devices  15.5 us (27%)
  other arithmetic  0.76 us (1%)
    pallas_call x7, Pallas kernels, call(): pl.pallas_call(kernel, out_shape=tuple(outs), in_specs=ins, out_specs=tup...  16.2 us
    ppermute x6, starting transfers between devices, sent(): lax.ppermute(part, 'gx', [(i, (i - s) % nz) for i in range(nz)])  10.1 us
    ppermute x14, starting transfers between devices, exchange(): got[name] = lax.ppermute(held, 'gy', [(i, i ^ turn) for i in range(ny)])  9.62 us
    ppermute x14, waiting for transfers between devices, exchange(): got[name] = lax.ppermute(held, 'gy', [(i, i ^ turn) for i in range(ny)])  5.81 us
    ppermute x6, waiting for transfers between devices, sent(): lax.ppermute(part, 'gx', [(i, (i - s) % nz) for i in range(nz)])  5.1 us
    ppermute x3, waiting for transfers between devices, exchange(): lax.ppermute(held, 'gx', [(i, (i + step) % nz) for i in range(nz)])  4.56 us
    ppermute x3, starting transfers between devices, exchange(): lax.ppermute(held, 'gx', [(i, (i + step) % nz) for i in range(nz)])  4.29 us
  transfers between devices with their start and end apart: 23, of which 12 were waited for; matrix products, arithmetic and copies ran while one was open for 0% of the time, Pallas kernels for 10%

profile of v7, /device:TPU:0, one launch (start us, length us, event | category | flops | bytes accessed | tf_op | source)
XLA Modules:
  0.0 56.6 jit_solution(16656839649446479617)
XLA Ops:
  0.0 1.2 %pack.1 = (bf16[32,2048]{1,0:T(8,128)(2,1)S(1)}, bf16[16,2048]{1,0:T(8,128)(2,1)S(1)}, f32[1,2048]{1,0:T(1,128)S(1)}, f32[16,2048]{1,0:T(8,128)S(1)}) custom-call(f32[3,2048]{1,0:T(4,128)} %pos_ref.1, f32[3,2048]{1,0:T(4,128)} %nrm_ref.1, f32[16,2048]{1,0:T(8,128)} %emi_ref.1, s32[1,2048]{1,0:T(1,128)} %bitcast.8, f32[1,8]{1,0:T(1,128)} %bitcast.11, ...), custom_call_target="tpu_custom_call" | custom-call | tf_op jit(solution)/shard_map/pack/pallas_call | solution.py:338
  1.2 3.0 %collective-permute-start.6 = (bf16[32,2048]{1,0:T(8,128)(2,1)S(1)}, bf16[32,2048]{1,0:T(8,128)(2,1)S(1)}, u32[]{:S(2)}, u32[]{:S(2)}) collective-permute-start(bf16[32,2048]{1,0:T(8,128)(2,1)S(1)} %get-tuple-element.27.refs_4_), channel_id=1, source_target_pairs={{0,4},{1,5},{2,6},{3,7},{4,0},{5,1},{6,2},{7,3},{8,12},{9,13},{10,... | collective-permute-start | bytes 393224 | tf_op jit(solution)/shard_map/ppermute | solution.py:389
  4.3 1.6 %collective-permute-start = (bf16[16,2048]{1,0:T(8,128)(2,1)S(1)}, bf16[16,2048]{1,0:T(8,128)(2,1)S(1)}, u32[]{:S(2)}, u32[]{:S(2)}) collective-permute-start(bf16[16,2048]{1,0:T(8,128)(2,1)S(1)} %get-tuple-element.25.refs_0_), channel_id=1, source_target_pairs={{0,8},{8,16},{16,24},{24,0},{1,9},{9,17},{17,25},{25,1},{2,10},{10... | collective-permute-start | bytes 196616 | tf_op jit(solution)/shard_map/ppermute | solution.py:386
  5.8 1.5 %collective-permute-start.4 = (bf16[32,2048]{1,0:T(8,128)(2,1)S(1)}, bf16[32,2048]{1,0:T(8,128)(2,1)S(1)}, u32[]{:S(2)}, u32[]{:S(2)}) collective-permute-start(bf16[32,2048]{1,0:T(8,128)(2,1)S(1)} %get-tuple-element.27.refs_4_), channel_id=1, source_target_pairs={{0,2},{1,3},{2,0},{3,1},{4,6},{5,7},{6,4},{7,5},{8,10},{9,11},{10,... | collective-permute-start | bytes 393224 | tf_op jit(solution)/shard_map/ppermute | solution.py:389
  7.3 0.5 collective-permute-start.8
  7.8 2.0 %collective-permute-start.2 = (bf16[16,2048]{1,0:T(8,128)(2,1)S(1)}, bf16[16,2048]{1,0:T(8,128)(2,1)S(1)}, u32[]{:S(2)}, u32[]{:S(2)}) collective-permute-start(bf16[16,2048]{1,0:T(8,128)(2,1)S(1)} %get-tuple-element.25.refs_0_), channel_id=1, source_target_pairs={{0,24},{8,0},{16,8},{24,16},{1,25},{9,1},{17,9},{25,17},{2,26},{10... | collective-permute-start | bytes 196616 | tf_op jit(solution)/shard_map/ppermute | solution.py:386
  9.8 0.6 %collective-permute-done.refs_1_ = bf16[16,2048]{1,0:T(8,128)(2,1)S(1)} collective-permute-done((bf16[16,2048]{1,0:T(8,128)(2,1)S(1)}, bf16[16,2048]{1,0:T(8,128)(2,1)S(1)}, u32[]{:S(2)}, u32[]{:S(2)}) %collective-permute-start) | collective-permute-done | bytes 65568 | tf_op jit(solution)/shard_map/ppermute | solution.py:386
  10.4 0.7 %collective-permute-start.1 = (bf16[16,2048]{1,0:T(8,128)(2,1)S(1)}, bf16[16,2048]{1,0:T(8,128)(2,1)S(1)}, u32[]{:S(2)}, u32[]{:S(2)}) collective-permute-start(bf16[16,2048]{1,0:T(8,128)(2,1)S(1)} %get-tuple-element.25.refs_0_), channel_id=1, source_target_pairs={{0,16},{8,24},{16,0},{24,8},{1,17},{9,25},{17,1},{25,9},{2,18},{10... | collective-permute-start | bytes 196616 | tf_op jit(solution)/shard_map/ppermute | solution.py:386
  11.1 1.0 %collective-permute-done.2.refs_3_ = bf16[16,2048]{1,0:T(8,128)(2,1)S(1)} collective-permute-done((bf16[16,2048]{1,0:T(8,128)(2,1)S(1)}, bf16[16,2048]{1,0:T(8,128)(2,1)S(1)}, u32[]{:S(2)}, u32[]{:S(2)}) %collective-permute-start.2) | collective-permute-done | bytes 65568 | tf_op jit(solution)/shard_map/ppermute | solution.py:386
  12.1 0.0 collective-permute-start.3
  12.1 0.0 collective-permute-done.6.refs_8_
  12.1 0.5 collective-permute-start.7
  12.6 3.0 %collective-permute-done.1.refs_2_ = bf16[16,2048]{1,0:T(8,128)(2,1)S(1)} collective-permute-done((bf16[16,2048]{1,0:T(8,128)(2,1)S(1)}, bf16[16,2048]{1,0:T(8,128)(2,1)S(1)}, u32[]{:S(2)}, u32[]{:S(2)}) %collective-permute-start.1) | collective-permute-done | bytes 65568 | tf_op jit(solution)/shard_map/ppermute | solution.py:386
  15.6 0.0 collective-permute-done.8.refs_10_
  15.6 0.0 collective-permute-start.9
  15.6 0.5 collective-permute-start.5
  16.1 0.0 collective-permute-done.3.refs_5_
  16.1 0.8 %collective-permute-done.9.refs_11_ = bf16[32,2048]{1,0:T(8,128)(2,1)S(1)} collective-permute-done((bf16[32,2048]{1,0:T(8,128)(2,1)S(1)}, bf16[32,2048]{1,0:T(8,128)(2,1)S(1)}, u32[]{:S(2)}, u32[]{:S(2)}) %collective-permute-start.9) | collective-permute-done | bytes 131104 | tf_op jit(solution)/shard_map/ppermute | solution.py:389
  16.9 0.0 collective-permute-done.7.refs_9_
  16.9 0.2 collective-permute-done.5.refs_7_
  17.1 8.6 %far.1 = (bf16[16,2048]{1,0:T(8,128)(2,1)S(1)}, bf16[16,2048]{1,0:T(8,128)(2,1)S(1)}, bf16[16,2048]{1,0:T(8,128)(2,1)S(1)}, bf16[112,256,256]{2,1,0:T(8,128)(2,1...) custom-call(bf16[16,2048]{1,0:T(8,128)(2,1)S(1)} %get-tuple-element., ...), custom_call_target="tpu_custom_call" | custom-call | tf_op jit(solution)/shard_map/far/pallas_call | solution.py:338
  25.7 4.6 %collective-permute-start.10 = (bf16[16,2048]{1,0:T(8,128)(2,1)S(1)}, bf16[16,2048]{1,0:T(8,128)(2,1)S(1)}, u32[]{:S(2)}, u32[]{:S(2)}) collective-permute-start(bf16[16,2048]{1,0:T(8,128)(2,1)S(1)} %get-tuple-element.39), channel_id=1, source_target_pairs={{0,24},{8,0},{16,8},{24,16},{1,25},{9,1},{17,9},{25,17},{2,26},{10... | collective-permute-start | bytes 196616 | tf_op jit(solution)/shard_map/ppermute | solution.py:395
  30.3 0.1 collective-permute-start.11
  30.3 1.5 %collective-permute-start.12 = (bf16[16,2048]{1,0:T(8,128)(2,1)S(1)}, bf16[16,2048]{1,0:T(8,128)(2,1)S(1)}, u32[]{:S(2)}, u32[]{:S(2)}) collective-permute-start(bf16[16,2048]{1,0:T(8,128)(2,1)S(1)} %get-tuple-element.41), channel_id=1, source_target_pairs={{0,8},{8,16},{16,24},{24,0},{1,9},{9,17},{17,25},{25,1},{2,10},{10... | collective-permute-start | bytes 196616 | tf_op jit(solution)/shard_map/ppermute | solution.py:395
  31.9 3.9 %near.1 = (f32[16,2048]{1,0:T(8,128)S(1)}, bf16[48,256,256]{2,1,0:T(8,128)(2,1)S(1)}) custom-call(s32[168]{0:T(256)S(4)} %get-tuple-element.30.pairs, bf16[32,3,48,256]{3,2,1,0:T(8,128)(2,1)S(1)} %get-tuple-element.31.refs_0_, f32[32,1,256]{2,1,0:T(1,128)S(1)} %get-tuple-element.32.refs_1_, bf16[64,256,48]{2,1,0:T(8,128)(2,1)S(1)} %get-tuple-element.33.refs_2_, ...), custom_call_target="tpu_custom_call" | custom-call | tf_op jit(solution)/shard_map/near/pallas_call | solution.py:338
  35.8 0.0 collective-permute-done.10
  35.8 1.2 %collective-permute-done.11 = bf16[16,2048]{1,0:T(8,128)(2,1)S(1)} collective-permute-done((bf16[16,2048]{1,0:T(8,128)(2,1)S(1)}, bf16[16,2048]{1,0:T(8,128)(2,1)S(1)}, u32[]{:S(2)}, u32[]{:S(2)}) %collective-permute-start.11) | collective-permute-done | bytes 65568 | tf_op jit(solution)/shard_map/ppermute | solution.py:395
  37.1 0.0 collective-permute-done.12
  37.1 0.1 multiply_convert_fusion.refs_1_
  37.1 1.9 %collective-permute-start.18 = (bf16[16,2048]{1,0:T(8,128)(2,1)S(1)}, bf16[16,2048]{1,0:T(8,128)(2,1)S(1)}, u32[]{:S(2)}, u32[]{:S(2)}) collective-permute-start(bf16[16,2048]{1,0:T(8,128)(2,1)S(1)} %multiply_convert_fusion.refs_1_), channel_id=1, source_target_pairs={{0,6},{1,7},{2,4},{3,5},{4,2},{5,3},{6,0},{7,1},{8,14},{9,15},{10,... | collective-permute-start | bytes 196616 | tf_op jit(solution)/shard_map/ppermute | solution.py:389
  39.0 1.0 %collective-permute-start.16 = (bf16[16,2048]{1,0:T(8,128)(2,1)S(1)}, bf16[16,2048]{1,0:T(8,128)(2,1)S(1)}, u32[]{:S(2)}, u32[]{:S(2)}) collective-permute-start(bf16[16,2048]{1,0:T(8,128)(2,1)S(1)} %multiply_convert_fusion.refs_1_), channel_id=1, source_target_pairs={{0,4},{1,5},{2,6},{3,7},{4,0},{5,1},{6,2},{7,3},{8,12},{9,13},{10,... | collective-permute-start | bytes 196616 | tf_op jit(solution)/shard_map/ppermute | solution.py:389
  40.0 0.7 %collective-permute-start.14 = (bf16[16,2048]{1,0:T(8,128)(2,1)S(1)}, bf16[16,2048]{1,0:T(8,128)(2,1)S(1)}, u32[]{:S(2)}, u32[]{:S(2)}) collective-permute-start(bf16[16,2048]{1,0:T(8,128)(2,1)S(1)} %multiply_convert_fusion.refs_1_), channel_id=1, source_target_pairs={{0,2},{1,3},{2,0},{3,1},{4,6},{5,7},{6,4},{7,5},{8,10},{9,11},{10,... | collective-permute-start | bytes 196616 | tf_op jit(solution)/shard_map/ppermute | solution.py:389
  40.7 2.3 %collective-permute-done.18.refs_7_ = bf16[16,2048]{1,0:T(8,128)(2,1)S(1)} collective-permute-done((bf16[16,2048]{1,0:T(8,128)(2,1)S(1)}, bf16[16,2048]{1,0:T(8,128)(2,1)S(1)}, u32[]{:S(2)}, u32[]{:S(2)}) %collective-permute-start.18) | collective-permute-done | bytes 65568 | tf_op jit(solution)/shard_map/ppermute | solution.py:389
  43.1 0.5 collective-permute-done.16.refs_5_
  43.5 0.0 collective-permute-start.17
  43.6 0.7 %collective-permute-done.14.refs_3_ = bf16[16,2048]{1,0:T(8,128)(2,1)S(1)} collective-permute-done((bf16[16,2048]{1,0:T(8,128)(2,1)S(1)}, bf16[16,2048]{1,0:T(8,128)(2,1)S(1)}, u32[]{:S(2)}, u32[]{:S(2)}) %collective-permute-start.14) | collective-permute-done | bytes 65568 | tf_op jit(solution)/shard_map/ppermute | solution.py:389
  44.3 0.0 collective-permute-done.19.refs_8_
  44.3 0.5 collective-permute-done.17.refs_6_
  44.8 0.8 %collective-permute-done.15.refs_4_ = bf16[16,2048]{1,0:T(8,128)(2,1)S(1)} collective-permute-done((bf16[16,2048]{1,0:T(8,128)(2,1)S(1)}, bf16[16,2048]{1,0:T(8,128)(2,1)S(1)}, u32[]{:S(2)}, u32[]{:S(2)}) %collective-permute-start.15) | collective-permute-done | bytes 65568 | tf_op jit(solution)/shard_map/ppermute | solution.py:389
  45.5 0.6 %apply.5 = bf16[16,2048]{1,0:T(8,128)(2,1)S(1)} custom-call(s32[168]{0:T(256)S(4)} %get-tuple-element.30.pairs, bf16[112,256,256]{2,1,0:T(8,128)(2,1)S(1)} %get-tuple-element.42.refs_0_, bf16[16,2048]{1,0:T(8,128)(2,1)S(1)} %multiply_convert_fusion.refs_1_, bf16[16,2048]{1,0:T(8,128)(2,1)S(1)} %collective-permute-done.13.refs_2_, ...), custom_call_target="tpu_custom_call" | custom-call | tf_op jit(solution)/shard_map/apply/pallas_call | solution.py:338
  46.1 1.5 %collective-permute-start.20 = (bf16[16,2048]{1,0:T(8,128)(2,1)S(1)}, bf16[16,2048]{1,0:T(8,128)(2,1)S(1)}, u32[]{:S(2)}, u32[]{:S(2)}) collective-permute-start(bf16[16,2048]{1,0:T(8,128)(2,1)S(1)} %apply.5), channel_id=1, source_target_pairs={{0,24},{8,0},{16,8},{24,16},{1,25},{9,1},{17,9},{25,17},{2,26},{10... | collective-permute-start | bytes 196616 | tf_op jit(solution)/shard_map/ppermute | solution.py:395
  47.6 0.6 %apply.6 = bf16[16,2048]{1,0:T(8,128)(2,1)S(1)} custom-call(s32[168]{0:T(256)S(4)} %get-tuple-element.30.pairs, bf16[112,256,256]{2,1,0:T(8,128)(2,1)S(1)} %get-tuple-element.42.refs_0_, bf16[16,2048]{1,0:T(8,128)(2,1)S(1)} %multiply_convert_fusion.refs_1_, bf16[16,2048]{1,0:T(8,128)(2,1)S(1)} %collective-permute-done.13.refs_2_, ...), custom_call_target="tpu_custom_call" | custom-call | tf_op jit(solution)/shard_map/apply/pallas_call | solution.py:338
  48.1 0.4 collective-permute-start.21
  48.5 0.6 %apply.7 = bf16[16,2048]{1,0:T(8,128)(2,1)S(1)} custom-call(s32[168]{0:T(256)S(4)} %get-tuple-element.30.pairs, bf16[112,256,256]{2,1,0:T(8,128)(2,1)S(1)} %get-tuple-element.42.refs_0_, bf16[16,2048]{1,0:T(8,128)(2,1)S(1)} %multiply_convert_fusion.refs_1_, bf16[16,2048]{1,0:T(8,128)(2,1)S(1)} %collective-permute-done.13.refs_2_, ...), custom_call_target="tpu_custom_call" | custom-call | tf_op jit(solution)/shard_map/apply/pallas_call | solution.py:338
  49.1 2.1 %collective-permute-start.22 = (bf16[16,2048]{1,0:T(8,128)(2,1)S(1)}, bf16[16,2048]{1,0:T(8,128)(2,1)S(1)}, u32[]{:S(2)}, u32[]{:S(2)}) collective-permute-start(bf16[16,2048]{1,0:T(8,128)(2,1)S(1)} %apply.7), channel_id=1, source_target_pairs={{0,8},{8,16},{16,24},{24,0},{1,9},{9,17},{17,25},{25,1},{2,10},{10... | collective-permute-start | bytes 196616 | tf_op jit(solution)/shard_map/ppermute | solution.py:395
  51.2 0.8 %apply.4 = f32[16,2048]{1,0:T(8,128)S(1)} custom-call(s32[168]{0:T(256)S(4)} %get-tuple-element.30.pairs, bf16[48,256,256]{2,1,0:T(8,128)(2,1)S(1)} %get-tuple-element.36.refs_0_, bf16[16,2048]{1,0:T(8,128)(2,1)S(1)} %multiply_convert_fusion.refs_1_, bf16[16,2048]{1,0:T(8,128)(2,1)S(1)} %collective-permute-done.13.refs_2_, ...), custom_call_target="tpu_custom_call" | custom-call | tf_op jit(solution)/shard_map/apply/pallas_call | solution.py:338
  52.0 3.8 %collective-permute-done.21 = bf16[16,2048]{1,0:T(8,128)(2,1)S(1)} collective-permute-done((bf16[16,2048]{1,0:T(8,128)(2,1)S(1)}, bf16[16,2048]{1,0:T(8,128)(2,1)S(1)}, u32[]{:S(2)}, u32[]{:S(2)}) %collective-permute-start.21) | collective-permute-done | bytes 65568 | tf_op jit(solution)/shard_map/ppermute | solution.py:395
  55.9 0.7 %multiply_add_fusion = f32[16,2048]{1,0:T(8,128)} fusion(f32[16,2048]{1,0:T(8,128)S(1)} %copy-done, f32[16,2048]{1,0:T(8,128)S(1)} %get-tuple-element.24, bf16[16,2048]{1,0:T(8,128)(2,1)S(1)} %collective-permute-done.22, bf16[16,2048]{1,0:T(8,128)(2,1)S(1)} %collective-permute-done.21, f32[16,2048]{1,0:T(8,128)S(1)} %apply.4, ...), kind=kLoop, calls=%fused_computation | loop fusion | flops 262144 | bytes 720896 | tf_op jit(solution)/shard_map/add | solution.py:469
  (9 shorter events, 0.0 us)
Async XLA Ops:
  1.2 10.9 %collective-permute-start.6 = (bf16[32,2048]{1,0:T(8,128)(2,1)S(1)}, bf16[32,2048]{1,0:T(8,128)(2,1)S(1)}, u32[]{:S(2)}, u32[]{:S(2)}) collective-permute-start(bf16[32,2048]{1,0:T(8,128)(2,1)S(1)} %get-tuple-element.27.refs_4_), channel_id=1, source_target_pairs={{0,4},{1,5},{2,6},{3,7},{4,0},{5,1},{6,2},{7,3},{8,12},{9,13},{10,... | collective-permute-start | bytes 393224 | tf_op jit(solution)/shard_map/ppermute | solution.py:389
  4.3 6.2 %collective-permute-start = (bf16[16,2048]{1,0:T(8,128)(2,1)S(1)}, bf16[16,2048]{1,0:T(8,128)(2,1)S(1)}, u32[]{:S(2)}, u32[]{:S(2)}) collective-permute-start(bf16[16,2048]{1,0:T(8,128)(2,1)S(1)} %get-tuple-element.25.refs_0_), channel_id=1, source_target_pairs={{0,8},{8,16},{16,24},{24,0},{1,9},{9,17},{17,25},{25,1},{2,10},{10... | collective-permute-start | bytes 196616 | tf_op jit(solution)/shard_map/ppermute | solution.py:386
  5.8 9.8 %collective-permute-start.4 = (bf16[32,2048]{1,0:T(8,128)(2,1)S(1)}, bf16[32,2048]{1,0:T(8,128)(2,1)S(1)}, u32[]{:S(2)}, u32[]{:S(2)}) collective-permute-start(bf16[32,2048]{1,0:T(8,128)(2,1)S(1)} %get-tuple-element.27.refs_4_), channel_id=1, source_target_pairs={{0,2},{1,3},{2,0},{3,1},{4,6},{5,7},{6,4},{7,5},{8,10},{9,11},{10,... | collective-permute-start | bytes 393224 | tf_op jit(solution)/shard_map/ppermute | solution.py:389
  7.3 8.3 %collective-permute-start.8 = (bf16[32,2048]{1,0:T(8,128)(2,1)S(1)}, bf16[32,2048]{1,0:T(8,128)(2,1)S(1)}, u32[]{:S(2)}, u32[]{:S(2)}) collective-permute-start(bf16[32,2048]{1,0:T(8,128)(2,1)S(1)} %get-tuple-element.27.refs_4_), channel_id=1, source_target_pairs={{0,6},{1,7},{2,4},{3,5},{4,2},{5,3},{6,0},{7,1},{8,14},{9,15},{10,... | collective-permute-start | bytes 393224 | tf_op jit(solution)/shard_map/ppermute | solution.py:389
  7.8 4.3 %collective-permute-start.2 = (bf16[16,2048]{1,0:T(8,128)(2,1)S(1)}, bf16[16,2048]{1,0:T(8,128)(2,1)S(1)}, u32[]{:S(2)}, u32[]{:S(2)}) collective-permute-start(bf16[16,2048]{1,0:T(8,128)(2,1)S(1)} %get-tuple-element.25.refs_0_), channel_id=1, source_target_pairs={{0,24},{8,0},{16,8},{24,16},{1,25},{9,1},{17,9},{25,17},{2,26},{10... | collective-permute-start | bytes 196616 | tf_op jit(solution)/shard_map/ppermute | solution.py:386
  10.4 5.2 %collective-permute-start.1 = (bf16[16,2048]{1,0:T(8,128)(2,1)S(1)}, bf16[16,2048]{1,0:T(8,128)(2,1)S(1)}, u32[]{:S(2)}, u32[]{:S(2)}) collective-permute-start(bf16[16,2048]{1,0:T(8,128)(2,1)S(1)} %get-tuple-element.25.refs_0_), channel_id=1, source_target_pairs={{0,16},{8,24},{16,0},{24,8},{1,17},{9,25},{17,1},{25,9},{2,18},{10... | collective-permute-start | bytes 196616 | tf_op jit(solution)/shard_map/ppermute | solution.py:386
  12.1 4.0 %collective-permute-start.3 = (bf16[32,2048]{1,0:T(8,128)(2,1)S(1)}, bf16[32,2048]{1,0:T(8,128)(2,1)S(1)}, u32[]{:S(2)}, u32[]{:S(2)}) collective-permute-start(bf16[32,2048]{1,0:T(8,128)(2,1)S(1)} %get-tuple-element.27.refs_4_), channel_id=1, source_target_pairs={{0,1},{1,0},{2,3},{3,2},{4,5},{5,4},{6,7},{7,6},{8,9},{9,8},{10,11... | collective-permute-start | bytes 393224 | tf_op jit(solution)/shard_map/ppermute | solution.py:389
  12.1 4.9 %collective-permute-start.7 = (bf16[32,2048]{1,0:T(8,128)(2,1)S(1)}, bf16[32,2048]{1,0:T(8,128)(2,1)S(1)}, u32[]{:S(2)}, u32[]{:S(2)}) collective-permute-start(bf16[32,2048]{1,0:T(8,128)(2,1)S(1)} %collective-permute-done.6.refs_8_), channel_id=1, source_target_pairs={{0,1},{1,0},{2,3},{3,2},{4,5},{5,4},{6,7},{7,6},{8,9},{9,8},{10,11... | collective-permute-start | bytes 393224 | tf_op jit(solution)/shard_map/ppermute | solution.py:389
  15.6 1.4 %collective-permute-start.9 = (bf16[32,2048]{1,0:T(8,128)(2,1)S(1)}, bf16[32,2048]{1,0:T(8,128)(2,1)S(1)}, u32[]{:S(2)}, u32[]{:S(2)}) collective-permute-start(bf16[32,2048]{1,0:T(8,128)(2,1)S(1)} %collective-permute-done.8.refs_10_), channel_id=1, source_target_pairs={{0,1},{1,0},{2,3},{3,2},{4,5},{5,4},{6,7},{7,6},{8,9},{9,8},{10,11... | collective-permute-start | bytes 393224 | tf_op jit(solution)/shard_map/ppermute | solution.py:389
  15.6 1.5 %collective-permute-start.5 = (bf16[32,2048]{1,0:T(8,128)(2,1)S(1)}, bf16[32,2048]{1,0:T(8,128)(2,1)S(1)}, u32[]{:S(2)}, u32[]{:S(2)}) collective-permute-start(bf16[32,2048]{1,0:T(8,128)(2,1)S(1)} %collective-permute-done.4.refs_6_), channel_id=1, source_target_pairs={{0,1},{1,0},{2,3},{3,2},{4,5},{5,4},{6,7},{7,6},{8,9},{9,8},{10,11... | collective-permute-start | bytes 393224 | tf_op jit(solution)/shard_map/ppermute | solution.py:389
  25.7 10.1 %collective-permute-start.10 = (bf16[16,2048]{1,0:T(8,128)(2,1)S(1)}, bf16[16,2048]{1,0:T(8,128)(2,1)S(1)}, u32[]{:S(2)}, u32[]{:S(2)}) collective-permute-start(bf16[16,2048]{1,0:T(8,128)(2,1)S(1)} %get-tuple-element.39), channel_id=1, source_target_pairs={{0,24},{8,0},{16,8},{24,16},{1,25},{9,1},{17,9},{25,17},{2,26},{10... | collective-permute-start | bytes 196616 | tf_op jit(solution)/shard_map/ppermute | solution.py:395
  30.3 6.8 %collective-permute-start.11 = (bf16[16,2048]{1,0:T(8,128)(2,1)S(1)}, bf16[16,2048]{1,0:T(8,128)(2,1)S(1)}, u32[]{:S(2)}, u32[]{:S(2)}) collective-permute-start(bf16[16,2048]{1,0:T(8,128)(2,1)S(1)} %get-tuple-element.40), channel_id=1, source_target_pairs={{0,16},{8,24},{16,0},{24,8},{1,17},{9,25},{17,1},{25,9},{2,18},{10... | collective-permute-start | bytes 196616 | tf_op jit(solution)/shard_map/ppermute | solution.py:395
  30.3 6.7 %collective-permute-start.12 = (bf16[16,2048]{1,0:T(8,128)(2,1)S(1)}, bf16[16,2048]{1,0:T(8,128)(2,1)S(1)}, u32[]{:S(2)}, u32[]{:S(2)}) collective-permute-start(bf16[16,2048]{1,0:T(8,128)(2,1)S(1)} %get-tuple-element.41), channel_id=1, source_target_pairs={{0,8},{8,16},{16,24},{24,0},{1,9},{9,17},{17,25},{25,1},{2,10},{10... | collective-permute-start | bytes 196616 | tf_op jit(solution)/shard_map/ppermute | solution.py:395
  31.9 5.2 %copy-start = (f32[16,2048]{1,0:T(8,128)S(1)}, f32[16,2048]{1,0:T(8,128)}, u32[]{:S(2)}) copy-start(f32[16,2048]{1,0:T(8,128)} %emi_ref.1) | copy-start | bytes 393220
  37.1 5.9 %collective-permute-start.18 = (bf16[16,2048]{1,0:T(8,128)(2,1)S(1)}, bf16[16,2048]{1,0:T(8,128)(2,1)S(1)}, u32[]{:S(2)}, u32[]{:S(2)}) collective-permute-start(bf16[16,2048]{1,0:T(8,128)(2,1)S(1)} %multiply_convert_fusion.refs_1_), channel_id=1, source_target_pairs={{0,6},{1,7},{2,4},{3,5},{4,2},{5,3},{6,0},{7,1},{8,14},{9,15},{10,... | collective-permute-start | bytes 196616 | tf_op jit(solution)/shard_map/ppermute | solution.py:389
  39.0 4.5 %collective-permute-start.16 = (bf16[16,2048]{1,0:T(8,128)(2,1)S(1)}, bf16[16,2048]{1,0:T(8,128)(2,1)S(1)}, u32[]{:S(2)}, u32[]{:S(2)}) collective-permute-start(bf16[16,2048]{1,0:T(8,128)(2,1)S(1)} %multiply_convert_fusion.refs_1_), channel_id=1, source_target_pairs={{0,4},{1,5},{2,6},{3,7},{4,0},{5,1},{6,2},{7,3},{8,12},{9,13},{10,... | collective-permute-start | bytes 196616 | tf_op jit(solution)/shard_map/ppermute | solution.py:389
  40.0 4.3 %collective-permute-start.14 = (bf16[16,2048]{1,0:T(8,128)(2,1)S(1)}, bf16[16,2048]{1,0:T(8,128)(2,1)S(1)}, u32[]{:S(2)}, u32[]{:S(2)}) collective-permute-start(bf16[16,2048]{1,0:T(8,128)(2,1)S(1)} %multiply_convert_fusion.refs_1_), channel_id=1, source_target_pairs={{0,2},{1,3},{2,0},{3,1},{4,6},{5,7},{6,4},{7,5},{8,10},{9,11},{10,... | collective-permute-start | bytes 196616 | tf_op jit(solution)/shard_map/ppermute | solution.py:389
  40.7 3.6 %collective-permute-start.13 = (bf16[16,2048]{1,0:T(8,128)(2,1)S(1)}, bf16[16,2048]{1,0:T(8,128)(2,1)S(1)}, u32[]{:S(2)}, u32[]{:S(2)}) collective-permute-start(bf16[16,2048]{1,0:T(8,128)(2,1)S(1)} %multiply_convert_fusion.refs_1_), channel_id=1, source_target_pairs={{0,1},{1,0},{2,3},{3,2},{4,5},{5,4},{6,7},{7,6},{8,9},{9,8},{10,11... | collective-permute-start | bytes 196616 | tf_op jit(solution)/shard_map/ppermute | solution.py:389
  43.1 1.3 %collective-permute-start.19 = (bf16[16,2048]{1,0:T(8,128)(2,1)S(1)}, bf16[16,2048]{1,0:T(8,128)(2,1)S(1)}, u32[]{:S(2)}, u32[]{:S(2)}) collective-permute-start(bf16[16,2048]{1,0:T(8,128)(2,1)S(1)} %collective-permute-done.18.refs_7_), channel_id=1, source_target_pairs={{0,1},{1,0},{2,3},{3,2},{4,5},{5,4},{6,7},{7,6},{8,9},{9,8},{10,11... | collective-permute-start | bytes 196616 | tf_op jit(solution)/shard_map/ppermute | solution.py:389
  43.5 1.3 %collective-permute-start.17 = (bf16[16,2048]{1,0:T(8,128)(2,1)S(1)}, bf16[16,2048]{1,0:T(8,128)(2,1)S(1)}, u32[]{:S(2)}, u32[]{:S(2)}) collective-permute-start(bf16[16,2048]{1,0:T(8,128)(2,1)S(1)} %collective-permute-done.16.refs_5_), channel_id=1, source_target_pairs={{0,1},{1,0},{2,3},{3,2},{4,5},{5,4},{6,7},{7,6},{8,9},{9,8},{10,11... | collective-permute-start | bytes 196616 | tf_op jit(solution)/shard_map/ppermute | solution.py:389
  44.3 1.3 %collective-permute-start.15 = (bf16[16,2048]{1,0:T(8,128)(2,1)S(1)}, bf16[16,2048]{1,0:T(8,128)(2,1)S(1)}, u32[]{:S(2)}, u32[]{:S(2)}) collective-permute-start(bf16[16,2048]{1,0:T(8,128)(2,1)S(1)} %collective-permute-done.14.refs_3_), channel_id=1, source_target_pairs={{0,1},{1,0},{2,3},{3,2},{4,5},{5,4},{6,7},{7,6},{8,9},{9,8},{10,11... | collective-permute-start | bytes 196616 | tf_op jit(solution)/shard_map/ppermute | solution.py:389
  46.1 5.9 %collective-permute-start.20 = (bf16[16,2048]{1,0:T(8,128)(2,1)S(1)}, bf16[16,2048]{1,0:T(8,128)(2,1)S(1)}, u32[]{:S(2)}, u32[]{:S(2)}) collective-permute-start(bf16[16,2048]{1,0:T(8,128)(2,1)S(1)} %apply.5), channel_id=1, source_target_pairs={{0,24},{8,0},{16,8},{24,16},{1,25},{9,1},{17,9},{25,17},{2,26},{10... | collective-permute-start | bytes 196616 | tf_op jit(solution)/shard_map/ppermute | solution.py:395
  48.1 7.7 %collective-permute-start.21 = (bf16[16,2048]{1,0:T(8,128)(2,1)S(1)}, bf16[16,2048]{1,0:T(8,128)(2,1)S(1)}, u32[]{:S(2)}, u32[]{:S(2)}) collective-permute-start(bf16[16,2048]{1,0:T(8,128)(2,1)S(1)} %apply.6), channel_id=1, source_target_pairs={{0,16},{8,24},{16,0},{24,8},{1,17},{9,25},{17,1},{25,9},{2,18},{10... | collective-permute-start | bytes 196616 | tf_op jit(solution)/shard_map/ppermute | solution.py:395
  49.1 6.7 %collective-permute-start.22 = (bf16[16,2048]{1,0:T(8,128)(2,1)S(1)}, bf16[16,2048]{1,0:T(8,128)(2,1)S(1)}, u32[]{:S(2)}, u32[]{:S(2)}) collective-permute-start(bf16[16,2048]{1,0:T(8,128)(2,1)S(1)} %apply.7), channel_id=1, source_target_pairs={{0,8},{8,16},{16,24},{24,0},{1,9},{9,17},{17,25},{25,1},{2,10},{10... | collective-permute-start | bytes 196616 | tf_op jit(solution)/shard_map/ppermute | solution.py:395

commit v8 on v7

--- a/solution.py
+++ b/solution.py
@@ -37,7 +37,7 @@
 
 
 def pack_kernel(
-    pos_ref, nrm_ref, emi_ref, level_ref, table_ref, kind_ref, share_ref, slot_ref, pay_ref, geo_ref, area_ref, reflect_ref, rows
+    pos_ref, nrm_ref, emi_ref, level_ref, table_ref, kind_ref, share_ref, slot_ref, pay_ref, geo_ref, area_ref, reflect_ref, kept_ref, rows
 ):
     level = level_ref[...]
     area = jnp.zeros(level.shape, F32)
@@ -67,6 +67,7 @@
     for k in range(share.shape[1]):
         reflect = jnp.where(kind == k, share[:, k : k + 1], reflect)
     reflect_ref[...] = reflect
+    kept_ref[...] = emi_ref[...]
 
 
 def terms_of(g):
@@ -345,7 +346,7 @@
             name=name,
         )(*args)
 
-    payload, geo, area, reflect = call(
+    payload, geo, area, reflect, emission = call(
         pack_kernel,
         "pack",
         None,
@@ -354,6 +355,7 @@
             pltpu.VMEM((GEO + BANDS, patches), BF16),
             pltpu.VMEM((GEO, patches), BF16),
             pltpu.VMEM((1, patches), F32),
+            pltpu.VMEM((BANDS, patches), F32),
             pltpu.VMEM((BANDS, patches), F32),
         ],
         [pltpu.VMEM((GEO, patches), F32)],

time: 56.7 us -> 57.4 us (1.012)
  starting transfers between devices: 24 us -> 22.1 us
  waiting for transfers between devices: 15.5 us -> 16.8 us
  Pallas kernels: 16.2 us -> 17 us
    ppermute x6, starting transfers between devices: 10.1 us -> 7.67 us  [sent(): lax.ppermute(part, 'gx', [(i, (i - s) % nz) for i in range(nz)])]
    pallas_call x7, Pallas kernels: 16.2 us -> 17 us  [call(): pl.pallas_call(kernel, out_shape=tuple(outs), in_specs=ins, out_specs=tup...]
    ppermute x14, waiting for transfers between devices: 5.81 us -> 6.53 us  [exchange(): got[name] = lax.ppermute(held, 'gy', [(i, i ^ turn) for i in range(ny)])]
    ppermute x6, waiting for transfers between devices: 5.1 us -> 5.69 us  [sent(): lax.ppermute(part, 'gx', [(i, (i - s) % nz) for i in range(nz)])]
  transfers between devices with their start and end apart: 23 -> 23, of which waited for: 12 -> 13; matrix products, arithmetic and copies ran while one was open for 0% -> 0% of each run, Pallas kernels for 10% -> 10%
where the time goes in v8:
time: 57.4 us; the launch traced here: 56.8 us
  starting transfers between devices  22.1 us (39%)
  Pallas kernels  17 us (30%)
  waiting for transfers between devices  16.8 us (29%)
  other arithmetic  0.77 us (1%)
    pallas_call x7, Pallas kernels, call(): pl.pallas_call(kernel, out_shape=tuple(outs), in_specs=ins, out_specs=tup...  17 us
    ppermute x14, starting transfers between devices, exchange(): got[name] = lax.ppermute(held, 'gy', [(i, i ^ turn) for i in range(ny)])  10.2 us
    ppermute x6, starting transfers between devices, sent(): lax.ppermute(part, 'gx', [(i, (i - s) % nz) for i in range(nz)])  7.67 us
    ppermute x14, waiting for transfers between devices, exchange(): got[name] = lax.ppermute(held, 'gy', [(i, i ^ turn) for i in range(ny)])  6.53 us
    ppermute x6, waiting for transfers between devices, sent(): lax.ppermute(part, 'gx', [(i, (i - s) % nz) for i in range(nz)])  5.69 us
    ppermute x3, waiting for transfers between devices, exchange(): lax.ppermute(held, 'gx', [(i, (i + step) % nz) for i in range(nz)])  4.56 us
    ppermute x3, starting transfers between devices, exchange(): lax.ppermute(held, 'gx', [(i, (i + step) % nz) for i in range(nz)])  4.29 us
  transfers between devices with their start and end apart: 23, of which 13 were waited for; matrix products, arithmetic and copies ran while one was open for 0% of the time, Pallas kernels for 10%

profile of v8, /device:TPU:0, one launch (start us, length us, event | category | flops | bytes accessed | tf_op | source)
XLA Modules:
  0.0 56.8 jit_solution(539610850654550498)
XLA Ops:
  0.0 1.2 %pack.1 = (bf16[32,2048]{1,0:T(8,128)(2,1)S(1)}, bf16[16,2048]{1,0:T(8,128)(2,1)S(1)}, f32[1,2048]{1,0:T(1,128)S(1)}, f32[16,2048]{1,0:T(8,128)S(1)}, f32[16,2048]{1,0:T(8,128)S(1)}) custom-call(f32[3,2048]{1,0:T(4,128)} %pos_ref.1, f32[3,2048]{1,0:T(4,128)} %nrm_ref.1, f32[16,2048]{1,0:T(8,128)} %emi_ref.1, s32[1,2048]{1,0:T(1,128)} %bitcast.8, ...), custom_call_target="tpu_custom_call" | custom-call | tf_op jit(solution)/shard_map/pack/pallas_call | solution.py:339
  1.2 3.0 %collective-permute-start.6 = (bf16[32,2048]{1,0:T(8,128)(2,1)S(1)}, bf16[32,2048]{1,0:T(8,128)(2,1)S(1)}, u32[]{:S(2)}, u32[]{:S(2)}) collective-permute-start(bf16[32,2048]{1,0:T(8,128)(2,1)S(1)} %get-tuple-element.29.refs_4_), channel_id=1, source_target_pairs={{0,4},{1,5},{2,6},{3,7},{4,0},{5,1},{6,2},{7,3},{8,12},{9,13},{10,... | collective-permute-start | bytes 393224 | tf_op jit(solution)/shard_map/ppermute | solution.py:391
  4.3 1.6 %collective-permute-start = (bf16[16,2048]{1,0:T(8,128)(2,1)S(1)}, bf16[16,2048]{1,0:T(8,128)(2,1)S(1)}, u32[]{:S(2)}, u32[]{:S(2)}) collective-permute-start(bf16[16,2048]{1,0:T(8,128)(2,1)S(1)} %get-tuple-element.27.refs_0_), channel_id=1, source_target_pairs={{0,8},{8,16},{16,24},{24,0},{1,9},{9,17},{17,25},{25,1},{2,10},{10... | collective-permute-start | bytes 196616 | tf_op jit(solution)/shard_map/ppermute | solution.py:388
  5.8 1.5 %collective-permute-start.4 = (bf16[32,2048]{1,0:T(8,128)(2,1)S(1)}, bf16[32,2048]{1,0:T(8,128)(2,1)S(1)}, u32[]{:S(2)}, u32[]{:S(2)}) collective-permute-start(bf16[32,2048]{1,0:T(8,128)(2,1)S(1)} %get-tuple-element.29.refs_4_), channel_id=1, source_target_pairs={{0,2},{1,3},{2,0},{3,1},{4,6},{5,7},{6,4},{7,5},{8,10},{9,11},{10,... | collective-permute-start | bytes 393224 | tf_op jit(solution)/shard_map/ppermute | solution.py:391
  7.3 0.5 collective-permute-start.8
  7.8 2.0 %collective-permute-start.2 = (bf16[16,2048]{1,0:T(8,128)(2,1)S(1)}, bf16[16,2048]{1,0:T(8,128)(2,1)S(1)}, u32[]{:S(2)}, u32[]{:S(2)}) collective-permute-start(bf16[16,2048]{1,0:T(8,128)(2,1)S(1)} %get-tuple-element.27.refs_0_), channel_id=1, source_target_pairs={{0,24},{8,0},{16,8},{24,16},{1,25},{9,1},{17,9},{25,17},{2,26},{10... | collective-permute-start | bytes 196616 | tf_op jit(solution)/shard_map/ppermute | solution.py:388
  9.8 0.6 %collective-permute-done.refs_1_ = bf16[16,2048]{1,0:T(8,128)(2,1)S(1)} collective-permute-done((bf16[16,2048]{1,0:T(8,128)(2,1)S(1)}, bf16[16,2048]{1,0:T(8,128)(2,1)S(1)}, u32[]{:S(2)}, u32[]{:S(2)}) %collective-permute-start) | collective-permute-done | bytes 65568 | tf_op jit(solution)/shard_map/ppermute | solution.py:388
  10.4 0.7 %collective-permute-start.1 = (bf16[16,2048]{1,0:T(8,128)(2,1)S(1)}, bf16[16,2048]{1,0:T(8,128)(2,1)S(1)}, u32[]{:S(2)}, u32[]{:S(2)}) collective-permute-start(bf16[16,2048]{1,0:T(8,128)(2,1)S(1)} %get-tuple-element.27.refs_0_), channel_id=1, source_target_pairs={{0,16},{8,24},{16,0},{24,8},{1,17},{9,25},{17,1},{25,9},{2,18},{10... | collective-permute-start | bytes 196616 | tf_op jit(solution)/shard_map/ppermute | solution.py:388
  11.1 1.0 %collective-permute-done.2.refs_3_ = bf16[16,2048]{1,0:T(8,128)(2,1)S(1)} collective-permute-done((bf16[16,2048]{1,0:T(8,128)(2,1)S(1)}, bf16[16,2048]{1,0:T(8,128)(2,1)S(1)}, u32[]{:S(2)}, u32[]{:S(2)}) %collective-permute-start.2) | collective-permute-done | bytes 65568 | tf_op jit(solution)/shard_map/ppermute | solution.py:388
  12.1 0.0 collective-permute-start.3
  12.1 0.0 collective-permute-done.6.refs_8_
  12.1 0.5 collective-permute-start.7
  12.6 3.0 %collective-permute-done.1.refs_2_ = bf16[16,2048]{1,0:T(8,128)(2,1)S(1)} collective-permute-done((bf16[16,2048]{1,0:T(8,128)(2,1)S(1)}, bf16[16,2048]{1,0:T(8,128)(2,1)S(1)}, u32[]{:S(2)}, u32[]{:S(2)}) %collective-permute-start.1) | collective-permute-done | bytes 65568 | tf_op jit(solution)/shard_map/ppermute | solution.py:388
  15.6 0.0 collective-permute-done.4.refs_6_
  15.6 0.5 collective-permute-start.5
  16.1 0.8 %collective-permute-done.9.refs_11_ = bf16[32,2048]{1,0:T(8,128)(2,1)S(1)} collective-permute-done((bf16[32,2048]{1,0:T(8,128)(2,1)S(1)}, bf16[32,2048]{1,0:T(8,128)(2,1)S(1)}, u32[]{:S(2)}, u32[]{:S(2)}) %collective-permute-start.9) | collective-permute-done | bytes 131104 | tf_op jit(solution)/shard_map/ppermute | solution.py:391
  17.0 0.0 collective-permute-done.7.refs_9_
  17.0 0.2 collective-permute-done.5.refs_7_
  17.1 9.7 %far.1 = (bf16[16,2048]{1,0:T(8,128)(2,1)S(1)}, bf16[16,2048]{1,0:T(8,128)(2,1)S(1)}, bf16[16,2048]{1,0:T(8,128)(2,1)S(1)}, bf16[112,256,256]{2,1,0:T(8,128)(2,1...) custom-call(bf16[16,2048]{1,0:T(8,128)(2,1)S(1)} %get-tuple-element., ...), custom_call_target="tpu_custom_call" | custom-call | tf_op jit(solution)/shard_map/far/pallas_call | solution.py:339
  26.9 3.5 %collective-permute-start.10 = (bf16[16,2048]{1,0:T(8,128)(2,1)S(1)}, bf16[16,2048]{1,0:T(8,128)(2,1)S(1)}, u32[]{:S(2)}, u32[]{:S(2)}) collective-permute-start(bf16[16,2048]{1,0:T(8,128)(2,1)S(1)} %get-tuple-element.41), channel_id=1, source_target_pairs={{0,24},{8,0},{16,8},{24,16},{1,25},{9,1},{17,9},{25,17},{2,26},{10... | collective-permute-start | bytes 196616 | tf_op jit(solution)/shard_map/ppermute | solution.py:397
  30.3 0.6 %collective-permute-start.12 = (bf16[16,2048]{1,0:T(8,128)(2,1)S(1)}, bf16[16,2048]{1,0:T(8,128)(2,1)S(1)}, u32[]{:S(2)}, u32[]{:S(2)}) collective-permute-start(bf16[16,2048]{1,0:T(8,128)(2,1)S(1)} %get-tuple-element.43), channel_id=1, source_target_pairs={{0,8},{8,16},{16,24},{24,0},{1,9},{9,17},{17,25},{25,1},{2,10},{10... | collective-permute-start | bytes 196616 | tf_op jit(solution)/shard_map/ppermute | solution.py:397
  31.0 3.3 %near.1 = (f32[16,2048]{1,0:T(8,128)S(1)}, bf16[48,256,256]{2,1,0:T(8,128)(2,1)S(1)}) custom-call(s32[168]{0:T(256)S(4)} %get-tuple-element.32.pairs, bf16[32,3,48,256]{3,2,1,0:T(8,128)(2,1)S(1)} %get-tuple-element.33.refs_0_, f32[32,1,256]{2,1,0:T(1,128)S(1)} %get-tuple-element.34.refs_1_, bf16[64,256,48]{2,1,0:T(8,128)(2,1)S(1)} %get-tuple-element.35.refs_2_, ...), custom_call_target="tpu_custom_call" | custom-call | tf_op jit(solution)/shard_map/near/pallas_call | solution.py:339
  34.3 1.2 %collective-permute-done.11 = bf16[16,2048]{1,0:T(8,128)(2,1)S(1)} collective-permute-done((bf16[16,2048]{1,0:T(8,128)(2,1)S(1)}, bf16[16,2048]{1,0:T(8,128)(2,1)S(1)}, u32[]{:S(2)}, u32[]{:S(2)}) %collective-permute-start.11) | collective-permute-done | bytes 65568 | tf_op jit(solution)/shard_map/ppermute | solution.py:397
  35.5 0.8 %collective-permute-done.12 = bf16[16,2048]{1,0:T(8,128)(2,1)S(1)} collective-permute-done((bf16[16,2048]{1,0:T(8,128)(2,1)S(1)}, bf16[16,2048]{1,0:T(8,128)(2,1)S(1)}, u32[]{:S(2)}, u32[]{:S(2)}) %collective-permute-start.12) | collective-permute-done | bytes 65568 | tf_op jit(solution)/shard_map/ppermute | solution.py:397
  36.4 0.1 multiply_convert_fusion.refs_1_
  36.4 3.3 %collective-permute-start.18 = (bf16[16,2048]{1,0:T(8,128)(2,1)S(1)}, bf16[16,2048]{1,0:T(8,128)(2,1)S(1)}, u32[]{:S(2)}, u32[]{:S(2)}) collective-permute-start(bf16[16,2048]{1,0:T(8,128)(2,1)S(1)} %multiply_convert_fusion.refs_1_), channel_id=1, source_target_pairs={{0,6},{1,7},{2,4},{3,5},{4,2},{5,3},{6,0},{7,1},{8,14},{9,15},{10,... | collective-permute-start | bytes 196616 | tf_op jit(solution)/shard_map/ppermute | solution.py:391
  39.7 0.9 %collective-permute-start.16 = (bf16[16,2048]{1,0:T(8,128)(2,1)S(1)}, bf16[16,2048]{1,0:T(8,128)(2,1)S(1)}, u32[]{:S(2)}, u32[]{:S(2)}) collective-permute-start(bf16[16,2048]{1,0:T(8,128)(2,1)S(1)} %multiply_convert_fusion.refs_1_), channel_id=1, source_target_pairs={{0,4},{1,5},{2,6},{3,7},{4,0},{5,1},{6,2},{7,3},{8,12},{9,13},{10,... | collective-permute-start | bytes 196616 | tf_op jit(solution)/shard_map/ppermute | solution.py:391
  40.6 0.0 collective-permute-start.14
  40.6 0.0 collective-permute-start.13
  40.6 1.5 %collective-permute-done.18.refs_7_ = bf16[16,2048]{1,0:T(8,128)(2,1)S(1)} collective-permute-done((bf16[16,2048]{1,0:T(8,128)(2,1)S(1)}, bf16[16,2048]{1,0:T(8,128)(2,1)S(1)}, u32[]{:S(2)}, u32[]{:S(2)}) %collective-permute-start.18) | collective-permute-done | bytes 65568 | tf_op jit(solution)/shard_map/ppermute | solution.py:391
  42.1 0.0 collective-permute-start.19
  42.1 1.9 %collective-permute-done.16.refs_5_ = bf16[16,2048]{1,0:T(8,128)(2,1)S(1)} collective-permute-done((bf16[16,2048]{1,0:T(8,128)(2,1)S(1)}, bf16[16,2048]{1,0:T(8,128)(2,1)S(1)}, u32[]{:S(2)}, u32[]{:S(2)}) %collective-permute-start.16) | collective-permute-done | bytes 65568 | tf_op jit(solution)/shard_map/ppermute | solution.py:391
  44.0 0.0 collective-permute-start.17
  44.0 0.9 %collective-permute-done.14.refs_3_ = bf16[16,2048]{1,0:T(8,128)(2,1)S(1)} collective-permute-done((bf16[16,2048]{1,0:T(8,128)(2,1)S(1)}, bf16[16,2048]{1,0:T(8,128)(2,1)S(1)}, u32[]{:S(2)}, u32[]{:S(2)}) %collective-permute-start.14) | collective-permute-done | bytes 65568 | tf_op jit(solution)/shard_map/ppermute | solution.py:391
  44.8 0.0 collective-permute-start.15
  44.8 0.0 collective-permute-done.13.refs_2_
  44.8 0.0 collective-permute-done.19.refs_8_
  44.8 0.4 collective-permute-done.17.refs_6_
  45.2 0.9 %collective-permute-done.15.refs_4_ = bf16[16,2048]{1,0:T(8,128)(2,1)S(1)} collective-permute-done((bf16[16,2048]{1,0:T(8,128)(2,1)S(1)}, bf16[16,2048]{1,0:T(8,128)(2,1)S(1)}, u32[]{:S(2)}, u32[]{:S(2)}) %collective-permute-start.15) | collective-permute-done | bytes 65568 | tf_op jit(solution)/shard_map/ppermute | solution.py:391
  46.1 0.6 apply.5
  46.7 1.2 %collective-permute-start.20 = (bf16[16,2048]{1,0:T(8,128)(2,1)S(1)}, bf16[16,2048]{1,0:T(8,128)(2,1)S(1)}, u32[]{:S(2)}, u32[]{:S(2)}) collective-permute-start(bf16[16,2048]{1,0:T(8,128)(2,1)S(1)} %apply.5), channel_id=1, source_target_pairs={{0,24},{8,0},{16,8},{24,16},{1,25},{9,1},{17,9},{25,17},{2,26},{10... | collective-permute-start | bytes 196616 | tf_op jit(solution)/shard_map/ppermute | solution.py:397
  47.9 0.8 %apply.6 = bf16[16,2048]{1,0:T(8,128)(2,1)S(1)} custom-call(s32[168]{0:T(256)S(4)} %get-tuple-element.32.pairs, bf16[112,256,256]{2,1,0:T(8,128)(2,1)S(1)} %get-tuple-element.44.refs_0_, bf16[16,2048]{1,0:T(8,128)(2,1)S(1)} %multiply_convert_fusion.refs_1_, bf16[16,2048]{1,0:T(8,128)(2,1)S(1)} %collective-permute-done.13.refs_2_, ...), custom_call_target="tpu_custom_call" | custom-call | tf_op jit(solution)/shard_map/apply/pallas_call | solution.py:339
  48.7 0.5 collective-permute-start.21
  49.2 0.6 apply.7
  49.8 1.8 %collective-permute-start.22 = (bf16[16,2048]{1,0:T(8,128)(2,1)S(1)}, bf16[16,2048]{1,0:T(8,128)(2,1)S(1)}, u32[]{:S(2)}, u32[]{:S(2)}) collective-permute-start(bf16[16,2048]{1,0:T(8,128)(2,1)S(1)} %apply.7), channel_id=1, source_target_pairs={{0,8},{8,16},{16,24},{24,0},{1,9},{9,17},{17,25},{25,1},{2,10},{10... | collective-permute-start | bytes 196616 | tf_op jit(solution)/shard_map/ppermute | solution.py:397
  51.6 0.8 %apply.4 = f32[16,2048]{1,0:T(8,128)S(1)} custom-call(s32[168]{0:T(256)S(4)} %get-tuple-element.32.pairs, bf16[48,256,256]{2,1,0:T(8,128)(2,1)S(1)} %get-tuple-element.38.refs_0_, bf16[16,2048]{1,0:T(8,128)(2,1)S(1)} %multiply_convert_fusion.refs_1_, bf16[16,2048]{1,0:T(8,128)(2,1)S(1)} %collective-permute-done.13.refs_2_, ...), custom_call_target="tpu_custom_call" | custom-call | tf_op jit(solution)/shard_map/apply/pallas_call | solution.py:339
  52.5 3.6 %collective-permute-done.21 = bf16[16,2048]{1,0:T(8,128)(2,1)S(1)} collective-permute-done((bf16[16,2048]{1,0:T(8,128)(2,1)S(1)}, bf16[16,2048]{1,0:T(8,128)(2,1)S(1)}, u32[]{:S(2)}, u32[]{:S(2)}) %collective-permute-start.21) | collective-permute-done | bytes 65568 | tf_op jit(solution)/shard_map/ppermute | solution.py:397
  56.1 0.7 %multiply_add_fusion = f32[16,2048]{1,0:T(8,128)} fusion(f32[16,2048]{1,0:T(8,128)S(1)} %get-tuple-element.25, f32[16,2048]{1,0:T(8,128)S(1)} %get-tuple-element.26, bf16[16,2048]{1,0:T(8,128)(2,1)S(1)} %collective-permute-done.22, bf16[16,2048]{1,0:T(8,128)(2,1)S(1)} %collective-permute-done.21, f32[16,2048]{1,0:T(8,128)S(1)} %apply.4, ...), kind=kLoop, calls=%fused_computation | loop fusion | flops 262144 | bytes 720896 | tf_op jit(solution)/shard_map/add | solution.py:471
  (7 shorter events, 0.0 us)
Async XLA Ops:
  1.2 10.9 %collective-permute-start.6 = (bf16[32,2048]{1,0:T(8,128)(2,1)S(1)}, bf16[32,2048]{1,0:T(8,128)(2,1)S(1)}, u32[]{:S(2)}, u32[]{:S(2)}) collective-permute-start(bf16[32,2048]{1,0:T(8,128)(2,1)S(1)} %get-tuple-element.29.refs_4_), channel_id=1, source_target_pairs={{0,4},{1,5},{2,6},{3,7},{4,0},{5,1},{6,2},{7,3},{8,12},{9,13},{10,... | collective-permute-start | bytes 393224 | tf_op jit(solution)/shard_map/ppermute | solution.py:391
  4.3 6.2 %collective-permute-start = (bf16[16,2048]{1,0:T(8,128)(2,1)S(1)}, bf16[16,2048]{1,0:T(8,128)(2,1)S(1)}, u32[]{:S(2)}, u32[]{:S(2)}) collective-permute-start(bf16[16,2048]{1,0:T(8,128)(2,1)S(1)} %get-tuple-element.27.refs_0_), channel_id=1, source_target_pairs={{0,8},{8,16},{16,24},{24,0},{1,9},{9,17},{17,25},{25,1},{2,10},{10... | collective-permute-start | bytes 196616 | tf_op jit(solution)/shard_map/ppermute | solution.py:388
  5.8 9.8 %collective-permute-start.4 = (bf16[32,2048]{1,0:T(8,128)(2,1)S(1)}, bf16[32,2048]{1,0:T(8,128)(2,1)S(1)}, u32[]{:S(2)}, u32[]{:S(2)}) collective-permute-start(bf16[32,2048]{1,0:T(8,128)(2,1)S(1)} %get-tuple-element.29.refs_4_), channel_id=1, source_target_pairs={{0,2},{1,3},{2,0},{3,1},{4,6},{5,7},{6,4},{7,5},{8,10},{9,11},{10,... | collective-permute-start | bytes 393224 | tf_op jit(solution)/shard_map/ppermute | solution.py:391
  7.3 8.3 %collective-permute-start.8 = (bf16[32,2048]{1,0:T(8,128)(2,1)S(1)}, bf16[32,2048]{1,0:T(8,128)(2,1)S(1)}, u32[]{:S(2)}, u32[]{:S(2)}) collective-permute-start(bf16[32,2048]{1,0:T(8,128)(2,1)S(1)} %get-tuple-element.29.refs_4_), channel_id=1, source_target_pairs={{0,6},{1,7},{2,4},{3,5},{4,2},{5,3},{6,0},{7,1},{8,14},{9,15},{10,... | collective-permute-start | bytes 393224 | tf_op jit(solution)/shard_map/ppermute | solution.py:391
  7.8 4.3 %collective-permute-start.2 = (bf16[16,2048]{1,0:T(8,128)(2,1)S(1)}, bf16[16,2048]{1,0:T(8,128)(2,1)S(1)}, u32[]{:S(2)}, u32[]{:S(2)}) collective-permute-start(bf16[16,2048]{1,0:T(8,128)(2,1)S(1)} %get-tuple-element.27.refs_0_), channel_id=1, source_target_pairs={{0,24},{8,0},{16,8},{24,16},{1,25},{9,1},{17,9},{25,17},{2,26},{10... | collective-permute-start | bytes 196616 | tf_op jit(solution)/shard_map/ppermute | solution.py:388
  10.4 5.2 %collective-permute-start.1 = (bf16[16,2048]{1,0:T(8,128)(2,1)S(1)}, bf16[16,2048]{1,0:T(8,128)(2,1)S(1)}, u32[]{:S(2)}, u32[]{:S(2)}) collective-permute-start(bf16[16,2048]{1,0:T(8,128)(2,1)S(1)} %get-tuple-element.27.refs_0_), channel_id=1, source_target_pairs={{0,16},{8,24},{16,0},{24,8},{1,17},{9,25},{17,1},{25,9},{2,18},{10... | collective-permute-start | bytes 196616 | tf_op jit(solution)/shard_map/ppermute | solution.py:388
  12.1 4.0 %collective-permute-start.3 = (bf16[32,2048]{1,0:T(8,128)(2,1)S(1)}, bf16[32,2048]{1,0:T(8,128)(2,1)S(1)}, u32[]{:S(2)}, u32[]{:S(2)}) collective-permute-start(bf16[32,2048]{1,0:T(8,128)(2,1)S(1)} %get-tuple-element.29.refs_4_), channel_id=1, source_target_pairs={{0,1},{1,0},{2,3},{3,2},{4,5},{5,4},{6,7},{7,6},{8,9},{9,8},{10,11... | collective-permute-start | bytes 393224 | tf_op jit(solution)/shard_map/ppermute | solution.py:391
  12.1 4.9 %collective-permute-start.7 = (bf16[32,2048]{1,0:T(8,128)(2,1)S(1)}, bf16[32,2048]{1,0:T(8,128)(2,1)S(1)}, u32[]{:S(2)}, u32[]{:S(2)}) collective-permute-start(bf16[32,2048]{1,0:T(8,128)(2,1)S(1)} %collective-permute-done.6.refs_8_), channel_id=1, source_target_pairs={{0,1},{1,0},{2,3},{3,2},{4,5},{5,4},{6,7},{7,6},{8,9},{9,8},{10,11... | collective-permute-start | bytes 393224 | tf_op jit(solution)/shard_map/ppermute | solution.py:391
  15.6 1.4 %collective-permute-start.9 = (bf16[32,2048]{1,0:T(8,128)(2,1)S(1)}, bf16[32,2048]{1,0:T(8,128)(2,1)S(1)}, u32[]{:S(2)}, u32[]{:S(2)}) collective-permute-start(bf16[32,2048]{1,0:T(8,128)(2,1)S(1)} %collective-permute-done.8.refs_10_), channel_id=1, source_target_pairs={{0,1},{1,0},{2,3},{3,2},{4,5},{5,4},{6,7},{7,6},{8,9},{9,8},{10,11... | collective-permute-start | bytes 393224 | tf_op jit(solution)/shard_map/ppermute | solution.py:391
  15.6 1.5 %collective-permute-start.5 = (bf16[32,2048]{1,0:T(8,128)(2,1)S(1)}, bf16[32,2048]{1,0:T(8,128)(2,1)S(1)}, u32[]{:S(2)}, u32[]{:S(2)}) collective-permute-start(bf16[32,2048]{1,0:T(8,128)(2,1)S(1)} %collective-permute-done.4.refs_6_), channel_id=1, source_target_pairs={{0,1},{1,0},{2,3},{3,2},{4,5},{5,4},{6,7},{7,6},{8,9},{9,8},{10,11... | collective-permute-start | bytes 393224 | tf_op jit(solution)/shard_map/ppermute | solution.py:391
  26.9 7.4 %collective-permute-start.10 = (bf16[16,2048]{1,0:T(8,128)(2,1)S(1)}, bf16[16,2048]{1,0:T(8,128)(2,1)S(1)}, u32[]{:S(2)}, u32[]{:S(2)}) collective-permute-start(bf16[16,2048]{1,0:T(8,128)(2,1)S(1)} %get-tuple-element.41), channel_id=1, source_target_pairs={{0,24},{8,0},{16,8},{24,16},{1,25},{9,1},{17,9},{25,17},{2,26},{10... | collective-permute-start | bytes 196616 | tf_op jit(solution)/shard_map/ppermute | solution.py:397
  30.3 5.2 %collective-permute-start.11 = (bf16[16,2048]{1,0:T(8,128)(2,1)S(1)}, bf16[16,2048]{1,0:T(8,128)(2,1)S(1)}, u32[]{:S(2)}, u32[]{:S(2)}) collective-permute-start(bf16[16,2048]{1,0:T(8,128)(2,1)S(1)} %get-tuple-element.42), channel_id=1, source_target_pairs={{0,16},{8,24},{16,0},{24,8},{1,17},{9,25},{17,1},{25,9},{2,18},{10... | collective-permute-start | bytes 196616 | tf_op jit(solution)/shard_map/ppermute | solution.py:397
  30.3 6.1 %collective-permute-start.12 = (bf16[16,2048]{1,0:T(8,128)(2,1)S(1)}, bf16[16,2048]{1,0:T(8,128)(2,1)S(1)}, u32[]{:S(2)}, u32[]{:S(2)}) collective-permute-start(bf16[16,2048]{1,0:T(8,128)(2,1)S(1)} %get-tuple-element.43), channel_id=1, source_target_pairs={{0,8},{8,16},{16,24},{24,0},{1,9},{9,17},{17,25},{25,1},{2,10},{10... | collective-permute-start | bytes 196616 | tf_op jit(solution)/shard_map/ppermute | solution.py:397
  36.4 5.6 %collective-permute-start.18 = (bf16[16,2048]{1,0:T(8,128)(2,1)S(1)}, bf16[16,2048]{1,0:T(8,128)(2,1)S(1)}, u32[]{:S(2)}, u32[]{:S(2)}) collective-permute-start(bf16[16,2048]{1,0:T(8,128)(2,1)S(1)} %multiply_convert_fusion.refs_1_), channel_id=1, source_target_pairs={{0,6},{1,7},{2,4},{3,5},{4,2},{5,3},{6,0},{7,1},{8,14},{9,15},{10,... | collective-permute-start | bytes 196616 | tf_op jit(solution)/shard_map/ppermute | solution.py:391
  39.7 4.3 %collective-permute-start.16 = (bf16[16,2048]{1,0:T(8,128)(2,1)S(1)}, bf16[16,2048]{1,0:T(8,128)(2,1)S(1)}, u32[]{:S(2)}, u32[]{:S(2)}) collective-permute-start(bf16[16,2048]{1,0:T(8,128)(2,1)S(1)} %multiply_convert_fusion.refs_1_), channel_id=1, source_target_pairs={{0,4},{1,5},{2,6},{3,7},{4,0},{5,1},{6,2},{7,3},{8,12},{9,13},{10,... | collective-permute-start | bytes 196616 | tf_op jit(solution)/shard_map/ppermute | solution.py:391
  40.6 4.3 %collective-permute-start.14 = (bf16[16,2048]{1,0:T(8,128)(2,1)S(1)}, bf16[16,2048]{1,0:T(8,128)(2,1)S(1)}, u32[]{:S(2)}, u32[]{:S(2)}) collective-permute-start(bf16[16,2048]{1,0:T(8,128)(2,1)S(1)} %multiply_convert_fusion.refs_1_), channel_id=1, source_target_pairs={{0,2},{1,3},{2,0},{3,1},{4,6},{5,7},{6,4},{7,5},{8,10},{9,11},{10,... | collective-permute-start | bytes 196616 | tf_op jit(solution)/shard_map/ppermute | solution.py:391
  40.6 4.3 %collective-permute-start.13 = (bf16[16,2048]{1,0:T(8,128)(2,1)S(1)}, bf16[16,2048]{1,0:T(8,128)(2,1)S(1)}, u32[]{:S(2)}, u32[]{:S(2)}) collective-permute-start(bf16[16,2048]{1,0:T(8,128)(2,1)S(1)} %multiply_convert_fusion.refs_1_), channel_id=1, source_target_pairs={{0,1},{1,0},{2,3},{3,2},{4,5},{5,4},{6,7},{7,6},{8,9},{9,8},{10,11... | collective-permute-start | bytes 196616 | tf_op jit(solution)/shard_map/ppermute | solution.py:391
  42.1 2.8 %collective-permute-start.19 = (bf16[16,2048]{1,0:T(8,128)(2,1)S(1)}, bf16[16,2048]{1,0:T(8,128)(2,1)S(1)}, u32[]{:S(2)}, u32[]{:S(2)}) collective-permute-start(bf16[16,2048]{1,0:T(8,128)(2,1)S(1)} %collective-permute-done.18.refs_7_), channel_id=1, source_target_pairs={{0,1},{1,0},{2,3},{3,2},{4,5},{5,4},{6,7},{7,6},{8,9},{9,8},{10,11... | collective-permute-start | bytes 196616 | tf_op jit(solution)/shard_map/ppermute | solution.py:391
  44.0 1.3 %collective-permute-start.17 = (bf16[16,2048]{1,0:T(8,128)(2,1)S(1)}, bf16[16,2048]{1,0:T(8,128)(2,1)S(1)}, u32[]{:S(2)}, u32[]{:S(2)}) collective-permute-start(bf16[16,2048]{1,0:T(8,128)(2,1)S(1)} %collective-permute-done.16.refs_5_), channel_id=1, source_target_pairs={{0,1},{1,0},{2,3},{3,2},{4,5},{5,4},{6,7},{7,6},{8,9},{9,8},{10,11... | collective-permute-start | bytes 196616 | tf_op jit(solution)/shard_map/ppermute | solution.py:391
  44.8 1.3 %collective-permute-start.15 = (bf16[16,2048]{1,0:T(8,128)(2,1)S(1)}, bf16[16,2048]{1,0:T(8,128)(2,1)S(1)}, u32[]{:S(2)}, u32[]{:S(2)}) collective-permute-start(bf16[16,2048]{1,0:T(8,128)(2,1)S(1)} %collective-permute-done.14.refs_3_), channel_id=1, source_target_pairs={{0,1},{1,0},{2,3},{3,2},{4,5},{5,4},{6,7},{7,6},{8,9},{9,8},{10,11... | collective-permute-start | bytes 196616 | tf_op jit(solution)/shard_map/ppermute | solution.py:391
  46.7 5.8 %collective-permute-start.20 = (bf16[16,2048]{1,0:T(8,128)(2,1)S(1)}, bf16[16,2048]{1,0:T(8,128)(2,1)S(1)}, u32[]{:S(2)}, u32[]{:S(2)}) collective-permute-start(bf16[16,2048]{1,0:T(8,128)(2,1)S(1)} %apply.5), channel_id=1, source_target_pairs={{0,24},{8,0},{16,8},{24,16},{1,25},{9,1},{17,9},{25,17},{2,26},{10... | collective-permute-start | bytes 196616 | tf_op jit(solution)/shard_map/ppermute | solution.py:397
  48.7 7.4 %collective-permute-start.21 = (bf16[16,2048]{1,0:T(8,128)(2,1)S(1)}, bf16[16,2048]{1,0:T(8,128)(2,1)S(1)}, u32[]{:S(2)}, u32[]{:S(2)}) collective-permute-start(bf16[16,2048]{1,0:T(8,128)(2,1)S(1)} %apply.6), channel_id=1, source_target_pairs={{0,16},{8,24},{16,0},{24,8},{1,17},{9,25},{17,1},{25,9},{2,18},{10... | collective-permute-start | bytes 196616 | tf_op jit(solution)/shard_map/ppermute | solution.py:397
  49.8 6.3 %collective-permute-start.22 = (bf16[16,2048]{1,0:T(8,128)(2,1)S(1)}, bf16[16,2048]{1,0:T(8,128)(2,1)S(1)}, u32[]{:S(2)}, u32[]{:S(2)}) collective-permute-start(bf16[16,2048]{1,0:T(8,128)(2,1)S(1)} %apply.7), channel_id=1, source_target_pairs={{0,8},{8,16},{16,24},{24,0},{1,9},{9,17},{17,25},{25,1},{2,10},{10... | collective-permute-start | bytes 196616 | tf_op jit(solution)/shard_map/ppermute | solution.py:397

commit v9 on v8

--- a/solution.py
+++ b/solution.py
@@ -295,13 +295,17 @@
     put_out(nb, acc, [out], 0)
 
 
-def apply_kernel(nz, ny, nb, lines, pairs, *refs):
+def apply_kernel(nz, ny, nb, lines, laid, pairs, *refs):
     tiles, refs = refs[: len(lines)], refs[len(lines) :]
-    fluxes, outs, flux, acc = refs[:ny], refs[ny:-2], *refs[-2:]
+    acc = refs[-1]
     second, bounds = sections(nz, ny)
-    for m in range(ny):
-        for b in range(nb):
-            flux[m * nb + b] = fluxes[m][:, b * BLK : (b + 1) * BLK]
+    if laid:
+        flux, outs = refs[0], refs[1:-1]
+    else:
+        fluxes, outs, flux = refs[:ny], refs[ny:-2], refs[-2]
+        for m in range(ny):
+            for b in range(nb):
+                flux[m * nb + b] = fluxes[m][:, b * BLK : (b + 1) * BLK]
     for s, tile, out in zip(lines, tiles, outs):
         acc[...] = jnp.zeros(acc.shape, F32)
         start = 0 if s else second
@@ -453,17 +457,18 @@
     got = exchange(None, (area * radiosity).astype(BF16), LATER_ORDER if ordered else {})
     fluxes = [got[f"m{m}"] for m in range(ny)]
     if keep:
-        parts = {}
+        parts, flux = {}, None
         for lines in TOGETHER if ordered else [range(1, nz), [0]]:
             got = call(
-                functools.partial(apply_kernel, nz, ny, nb, lines),
+                functools.partial(apply_kernel, nz, ny, nb, lines, flux is not None),
                 "apply",
                 4,
-                [SMEM()] + [VMEM()] * (len(lines) + ny),
-                [far_parts[0] if s else own_part for s in lines],
-                [features[4], pltpu.VMEM((nb + 1, BANDS, BLK), F32)],
-                (pairs, *[far_tiles if s else near_tiles for s in lines], *fluxes),
+                [SMEM()] + [VMEM()] * (len(lines) + (ny if flux is None else 1)),
+                [far_parts[0] if s else own_part for s in lines] + ([features[4]] if flux is None else []),
+                [pltpu.VMEM((nb + 1, BANDS, BLK), F32)],
+                (pairs, *[far_tiles if s else near_tiles for s in lines], *(fluxes if flux is None else [flux])),
             )
+            flux = got[-1] if flux is None else flux
             parts.update(zip(lines, got))
         irradiation = total(parts[0], sent([parts[s] for s in range(1, nz)]))
     else:

time: 57.4 us -> 57.1 us (level)
  starting transfers between devices: 22.1 us -> 23.8 us
  Pallas kernels: 17 us -> 16.1 us
  waiting for transfers between devices: 16.8 us -> 16.1 us
    ppermute x6, starting transfers between devices: 7.67 us -> 9.45 us  [sent(): lax.ppermute(part, 'gx', [(i, (i - s) % nz) for i in range(nz)])]
    ppermute x14, waiting for transfers between devices: 6.53 us -> 5.01 us  [exchange(): got[name] = lax.ppermute(held, 'gy', [(i, i ^ turn) for i in range(ny)])]
    pallas_call x7, Pallas kernels: 17 us -> 16.1 us  [call(): pl.pallas_call(kernel, out_shape=tuple(outs), in_specs=ins, out_specs=tup...]
    ppermute x6, waiting for transfers between devices: 5.69 us -> 6.55 us  [sent(): lax.ppermute(part, 'gx', [(i, (i - s) % nz) for i in range(nz)])]
  transfers between devices with their start and end apart: 23 -> 23, of which waited for: 13 -> 12; matrix products, arithmetic and copies ran while one was open for 0% -> 0% of each run, Pallas kernels for 10% -> 6%
where the time goes in v9:
time: 57.1 us; the launch traced here: 56.9 us
  starting transfers between devices  23.8 us (42%)
  Pallas kernels  16.1 us (28%)
  waiting for transfers between devices  16.1 us (28%)
  other arithmetic  0.77 us (1%)
    pallas_call x7, Pallas kernels, call(): pl.pallas_call(kernel, out_shape=tuple(outs), in_specs=ins, out_specs=tup...  16.1 us
    ppermute x14, starting transfers between devices, exchange(): got[name] = lax.ppermute(held, 'gy', [(i, i ^ turn) for i in range(ny)])  10.1 us
    ppermute x6, starting transfers between devices, sent(): lax.ppermute(part, 'gx', [(i, (i - s) % nz) for i in range(nz)])  9.45 us
    ppermute x6, waiting for transfers between devices, sent(): lax.ppermute(part, 'gx', [(i, (i - s) % nz) for i in range(nz)])  6.55 us
    ppermute x14, waiting for transfers between devices, exchange(): got[name] = lax.ppermute(held, 'gy', [(i, i ^ turn) for i in range(ny)])  5.01 us
    ppermute x3, waiting for transfers between devices, exchange(): lax.ppermute(held, 'gx', [(i, (i + step) % nz) for i in range(nz)])  4.56 us
    ppermute x3, starting transfers between devices, exchange(): lax.ppermute(held, 'gx', [(i, (i + step) % nz) for i in range(nz)])  4.29 us
  transfers between devices with their start and end apart: 23, of which 12 were waited for; matrix products, arithmetic and copies ran while one was open for 0% of the time, Pallas kernels for 6%

profile of v9, /device:TPU:0, one launch (start us, length us, event | category | flops | bytes accessed | tf_op | source)
XLA Modules:
  0.0 56.9 jit_solution(4612017718302893421)
XLA Ops:
  0.0 1.2 %pack.1 = (bf16[32,2048]{1,0:T(8,128)(2,1)S(1)}, bf16[16,2048]{1,0:T(8,128)(2,1)S(1)}, f32[1,2048]{1,0:T(1,128)S(1)}, f32[16,2048]{1,0:T(8,128)S(1)}, f32[16,2048]{1,0:T(8,128)S(1)}) custom-call(f32[3,2048]{1,0:T(4,128)} %pos_ref.1, f32[3,2048]{1,0:T(4,128)} %nrm_ref.1, f32[16,2048]{1,0:T(8,128)} %emi_ref.1, s32[1,2048]{1,0:T(1,128)} %bitcast.8, ...), custom_call_target="tpu_custom_call" | custom-call | tf_op jit(solution)/shard_map/pack/pallas_call | solution.py:343
  1.2 3.0 %collective-permute-start.6 = (bf16[32,2048]{1,0:T(8,128)(2,1)S(1)}, bf16[32,2048]{1,0:T(8,128)(2,1)S(1)}, u32[]{:S(2)}, u32[]{:S(2)}) collective-permute-start(bf16[32,2048]{1,0:T(8,128)(2,1)S(1)} %get-tuple-element.31.refs_4_), channel_id=1, source_target_pairs={{0,4},{1,5},{2,6},{3,7},{4,0},{5,1},{6,2},{7,3},{8,12},{9,13},{10,... | collective-permute-start | bytes 393224 | tf_op jit(solution)/shard_map/ppermute | solution.py:395
  4.3 1.6 %collective-permute-start = (bf16[16,2048]{1,0:T(8,128)(2,1)S(1)}, bf16[16,2048]{1,0:T(8,128)(2,1)S(1)}, u32[]{:S(2)}, u32[]{:S(2)}) collective-permute-start(bf16[16,2048]{1,0:T(8,128)(2,1)S(1)} %get-tuple-element.29.refs_0_), channel_id=1, source_target_pairs={{0,8},{8,16},{16,24},{24,0},{1,9},{9,17},{17,25},{25,1},{2,10},{10... | collective-permute-start | bytes 196616 | tf_op jit(solution)/shard_map/ppermute | solution.py:392
  5.8 1.5 %collective-permute-start.4 = (bf16[32,2048]{1,0:T(8,128)(2,1)S(1)}, bf16[32,2048]{1,0:T(8,128)(2,1)S(1)}, u32[]{:S(2)}, u32[]{:S(2)}) collective-permute-start(bf16[32,2048]{1,0:T(8,128)(2,1)S(1)} %get-tuple-element.31.refs_4_), channel_id=1, source_target_pairs={{0,2},{1,3},{2,0},{3,1},{4,6},{5,7},{6,4},{7,5},{8,10},{9,11},{10,... | collective-permute-start | bytes 393224 | tf_op jit(solution)/shard_map/ppermute | solution.py:395
  7.3 0.5 collective-permute-start.8
  7.8 2.0 %collective-permute-start.2 = (bf16[16,2048]{1,0:T(8,128)(2,1)S(1)}, bf16[16,2048]{1,0:T(8,128)(2,1)S(1)}, u32[]{:S(2)}, u32[]{:S(2)}) collective-permute-start(bf16[16,2048]{1,0:T(8,128)(2,1)S(1)} %get-tuple-element.29.refs_0_), channel_id=1, source_target_pairs={{0,24},{8,0},{16,8},{24,16},{1,25},{9,1},{17,9},{25,17},{2,26},{10... | collective-permute-start | bytes 196616 | tf_op jit(solution)/shard_map/ppermute | solution.py:392
  9.8 0.6 %collective-permute-done.refs_1_ = bf16[16,2048]{1,0:T(8,128)(2,1)S(1)} collective-permute-done((bf16[16,2048]{1,0:T(8,128)(2,1)S(1)}, bf16[16,2048]{1,0:T(8,128)(2,1)S(1)}, u32[]{:S(2)}, u32[]{:S(2)}) %collective-permute-start) | collective-permute-done | bytes 65568 | tf_op jit(solution)/shard_map/ppermute | solution.py:392
  10.4 0.7 %collective-permute-start.1 = (bf16[16,2048]{1,0:T(8,128)(2,1)S(1)}, bf16[16,2048]{1,0:T(8,128)(2,1)S(1)}, u32[]{:S(2)}, u32[]{:S(2)}) collective-permute-start(bf16[16,2048]{1,0:T(8,128)(2,1)S(1)} %get-tuple-element.29.refs_0_), channel_id=1, source_target_pairs={{0,16},{8,24},{16,0},{24,8},{1,17},{9,25},{17,1},{25,9},{2,18},{10... | collective-permute-start | bytes 196616 | tf_op jit(solution)/shard_map/ppermute | solution.py:392
  11.1 1.0 %collective-permute-done.2.refs_3_ = bf16[16,2048]{1,0:T(8,128)(2,1)S(1)} collective-permute-done((bf16[16,2048]{1,0:T(8,128)(2,1)S(1)}, bf16[16,2048]{1,0:T(8,128)(2,1)S(1)}, u32[]{:S(2)}, u32[]{:S(2)}) %collective-permute-start.2) | collective-permute-done | bytes 65568 | tf_op jit(solution)/shard_map/ppermute | solution.py:392
  12.1 0.0 collective-permute-start.3
  12.1 0.0 collective-permute-done.6.refs_8_
  12.1 0.5 collective-permute-start.7
  12.6 3.0 %collective-permute-done.1.refs_2_ = bf16[16,2048]{1,0:T(8,128)(2,1)S(1)} collective-permute-done((bf16[16,2048]{1,0:T(8,128)(2,1)S(1)}, bf16[16,2048]{1,0:T(8,128)(2,1)S(1)}, u32[]{:S(2)}, u32[]{:S(2)}) %collective-permute-start.1) | collective-permute-done | bytes 65568 | tf_op jit(solution)/shard_map/ppermute | solution.py:392
  15.6 0.0 collective-permute-done.4.refs_6_
  15.6 0.5 collective-permute-start.5
  16.1 0.8 %collective-permute-done.9.refs_11_ = bf16[32,2048]{1,0:T(8,128)(2,1)S(1)} collective-permute-done((bf16[32,2048]{1,0:T(8,128)(2,1)S(1)}, bf16[32,2048]{1,0:T(8,128)(2,1)S(1)}, u32[]{:S(2)}, u32[]{:S(2)}) %collective-permute-start.9) | collective-permute-done | bytes 131104 | tf_op jit(solution)/shard_map/ppermute | solution.py:395
  17.0 0.0 collective-permute-done.7.refs_9_
  17.0 0.2 collective-permute-done.5.refs_7_
  17.1 9.7 %far.1 = (bf16[16,2048]{1,0:T(8,128)(2,1)S(1)}, bf16[16,2048]{1,0:T(8,128)(2,1)S(1)}, bf16[16,2048]{1,0:T(8,128)(2,1)S(1)}, bf16[112,256,256]{2,1,0:T(8,128)(2,1...) custom-call(bf16[16,2048]{1,0:T(8,128)(2,1)S(1)} %get-tuple-element., ...), custom_call_target="tpu_custom_call" | custom-call | tf_op jit(solution)/shard_map/far/pallas_call | solution.py:343
  26.9 3.5 %collective-permute-start.10 = (bf16[16,2048]{1,0:T(8,128)(2,1)S(1)}, bf16[16,2048]{1,0:T(8,128)(2,1)S(1)}, u32[]{:S(2)}, u32[]{:S(2)}) collective-permute-start(bf16[16,2048]{1,0:T(8,128)(2,1)S(1)} %get-tuple-element.44), channel_id=1, source_target_pairs={{0,24},{8,0},{16,8},{24,16},{1,25},{9,1},{17,9},{25,17},{2,26},{10... | collective-permute-start | bytes 196616 | tf_op jit(solution)/shard_map/ppermute | solution.py:401
  30.3 0.0 collective-permute-start.11
  30.3 0.6 %collective-permute-start.12 = (bf16[16,2048]{1,0:T(8,128)(2,1)S(1)}, bf16[16,2048]{1,0:T(8,128)(2,1)S(1)}, u32[]{:S(2)}, u32[]{:S(2)}) collective-permute-start(bf16[16,2048]{1,0:T(8,128)(2,1)S(1)} %get-tuple-element.46), channel_id=1, source_target_pairs={{0,8},{8,16},{16,24},{24,0},{1,9},{9,17},{17,25},{25,1},{2,10},{10... | collective-permute-start | bytes 196616 | tf_op jit(solution)/shard_map/ppermute | solution.py:401
  30.9 2.7 %near.1 = (f32[16,2048]{1,0:T(8,128)S(1)}, bf16[48,256,256]{2,1,0:T(8,128)(2,1)S(1)}) custom-call(s32[168]{0:T(256)S(4)} %get-tuple-element.34.pairs, bf16[32,3,48,256]{3,2,1,0:T(8,128)(2,1)S(1)} %get-tuple-element.35.refs_0_, f32[32,1,256]{2,1,0:T(1,128)S(1)} %get-tuple-element.36.refs_1_, bf16[64,256,48]{2,1,0:T(8,128)(2,1)S(1)} %get-tuple-element.37.refs_2_, ...), custom_call_target="tpu_custom_call" | custom-call | tf_op jit(solution)/shard_map/near/pallas_call | solution.py:343
  33.6 0.0 collective-permute-done.10
  33.7 3.7 %collective-permute-done.11 = bf16[16,2048]{1,0:T(8,128)(2,1)S(1)} collective-permute-done((bf16[16,2048]{1,0:T(8,128)(2,1)S(1)}, bf16[16,2048]{1,0:T(8,128)(2,1)S(1)}, u32[]{:S(2)}, u32[]{:S(2)}) %collective-permute-start.11) | collective-permute-done | bytes 65568 | tf_op jit(solution)/shard_map/ppermute | solution.py:401
  37.4 0.1 multiply_convert_fusion.refs_1_
  37.5 2.2 %collective-permute-start.18 = (bf16[16,2048]{1,0:T(8,128)(2,1)S(1)}, bf16[16,2048]{1,0:T(8,128)(2,1)S(1)}, u32[]{:S(2)}, u32[]{:S(2)}) collective-permute-start(bf16[16,2048]{1,0:T(8,128)(2,1)S(1)} %multiply_convert_fusion.refs_1_), channel_id=1, source_target_pairs={{0,6},{1,7},{2,4},{3,5},{4,2},{5,3},{6,0},{7,1},{8,14},{9,15},{10,... | collective-permute-start | bytes 196616 | tf_op jit(solution)/shard_map/ppermute | solution.py:395
  39.7 1.3 %collective-permute-start.14 = (bf16[16,2048]{1,0:T(8,128)(2,1)S(1)}, bf16[16,2048]{1,0:T(8,128)(2,1)S(1)}, u32[]{:S(2)}, u32[]{:S(2)}) collective-permute-start(bf16[16,2048]{1,0:T(8,128)(2,1)S(1)} %multiply_convert_fusion.refs_1_), channel_id=1, source_target_pairs={{0,2},{1,3},{2,0},{3,1},{4,6},{5,7},{6,4},{7,5},{8,10},{9,11},{10,... | collective-permute-start | bytes 196616 | tf_op jit(solution)/shard_map/ppermute | solution.py:395
  41.0 1.7 %collective-permute-done.18.refs_7_ = bf16[16,2048]{1,0:T(8,128)(2,1)S(1)} collective-permute-done((bf16[16,2048]{1,0:T(8,128)(2,1)S(1)}, bf16[16,2048]{1,0:T(8,128)(2,1)S(1)}, u32[]{:S(2)}, u32[]{:S(2)}) %collective-permute-start.18) | collective-permute-done | bytes 65568 | tf_op jit(solution)/shard_map/ppermute | solution.py:395
  42.8 1.3 %collective-permute-done.16.refs_5_ = bf16[16,2048]{1,0:T(8,128)(2,1)S(1)} collective-permute-done((bf16[16,2048]{1,0:T(8,128)(2,1)S(1)}, bf16[16,2048]{1,0:T(8,128)(2,1)S(1)}, u32[]{:S(2)}, u32[]{:S(2)}) %collective-permute-start.16) | collective-permute-done | bytes 65568 | tf_op jit(solution)/shard_map/ppermute | solution.py:395
  44.1 0.0 collective-permute-start.17
  44.1 0.0 collective-permute-done.14.refs_3_
  44.1 0.5 collective-permute-start.15
  44.6 0.0 collective-permute-done.13.refs_2_
  44.6 0.0 collective-permute-done.19.refs_8_
  44.6 0.7 %collective-permute-done.17.refs_6_ = bf16[16,2048]{1,0:T(8,128)(2,1)S(1)} collective-permute-done((bf16[16,2048]{1,0:T(8,128)(2,1)S(1)}, bf16[16,2048]{1,0:T(8,128)(2,1)S(1)}, u32[]{:S(2)}, u32[]{:S(2)}) %collective-permute-start.17) | collective-permute-done | bytes 65568 | tf_op jit(solution)/shard_map/ppermute | solution.py:395
  45.4 0.2 collective-permute-done.15.refs_4_
  45.5 0.6 apply.4
  46.1 0.8 %apply.7 = bf16[16,2048]{1,0:T(8,128)(2,1)S(1)} custom-call(s32[168]{0:T(256)S(4)} %get-tuple-element.34.pairs, bf16[112,256,256]{2,1,0:T(8,128)(2,1)S(1)} %get-tuple-element.41.refs_0_, bf16[64,16,256]{2,1,0:T(8,128)(2,1)S(1)} %get-tuple-element.47.refs_1_), custom_call_target="tpu_custom_call" | custom-call | tf_op jit(solution)/shard_map/apply/pallas_call | solution.py:343
  46.9 0.5 apply.6
  47.4 1.5 %collective-permute-start.21 = (bf16[16,2048]{1,0:T(8,128)(2,1)S(1)}, bf16[16,2048]{1,0:T(8,128)(2,1)S(1)}, u32[]{:S(2)}, u32[]{:S(2)}) collective-permute-start(bf16[16,2048]{1,0:T(8,128)(2,1)S(1)} %apply.6), channel_id=1, source_target_pairs={{0,16},{8,24},{16,0},{24,8},{1,17},{9,25},{17,1},{25,9},{2,18},{10... | collective-permute-start | bytes 196616 | tf_op jit(solution)/shard_map/ppermute | solution.py:401
  49.0 0.9 %collective-permute-start.22 = (bf16[16,2048]{1,0:T(8,128)(2,1)S(1)}, bf16[16,2048]{1,0:T(8,128)(2,1)S(1)}, u32[]{:S(2)}, u32[]{:S(2)}) collective-permute-start(bf16[16,2048]{1,0:T(8,128)(2,1)S(1)} %apply.7), channel_id=1, source_target_pairs={{0,8},{8,16},{16,24},{24,0},{1,9},{9,17},{17,25},{25,1},{2,10},{10... | collective-permute-start | bytes 196616 | tf_op jit(solution)/shard_map/ppermute | solution.py:401
  49.8 3.0 %collective-permute-start.20 = (bf16[16,2048]{1,0:T(8,128)(2,1)S(1)}, bf16[16,2048]{1,0:T(8,128)(2,1)S(1)}, u32[]{:S(2)}, u32[]{:S(2)}) collective-permute-start(bf16[16,2048]{1,0:T(8,128)(2,1)S(1)} %get-tuple-element.48), channel_id=1, source_target_pairs={{0,24},{8,0},{16,8},{24,16},{1,25},{9,1},{17,9},{25,17},{2,26},{10... | collective-permute-start | bytes 196616 | tf_op jit(solution)/shard_map/ppermute | solution.py:401
  52.8 0.5 apply.5
  53.3 2.5 %collective-permute-done.21 = bf16[16,2048]{1,0:T(8,128)(2,1)S(1)} collective-permute-done((bf16[16,2048]{1,0:T(8,128)(2,1)S(1)}, bf16[16,2048]{1,0:T(8,128)(2,1)S(1)}, u32[]{:S(2)}, u32[]{:S(2)}) %collective-permute-start.21) | collective-permute-done | bytes 65568 | tf_op jit(solution)/shard_map/ppermute | solution.py:401
  55.8 0.0 collective-permute-done.22
  55.8 0.3 collective-permute-done.20
  56.2 0.7 %multiply_add_fusion = f32[16,2048]{1,0:T(8,128)} fusion(f32[16,2048]{1,0:T(8,128)S(1)} %get-tuple-element.27, f32[16,2048]{1,0:T(8,128)S(1)} %get-tuple-element.28, bf16[16,2048]{1,0:T(8,128)(2,1)S(1)} %collective-permute-done.22, bf16[16,2048]{1,0:T(8,128)(2,1)S(1)} %collective-permute-done.21, f32[16,2048]{1,0:T(8,128)S(1)} %apply.5, ...), kind=kLoop, calls=%fused_computation | loop fusion | flops 262144 | bytes 720896 | tf_op jit(solution)/shard_map/add | solution.py:476
  (7 shorter events, 0.0 us)
Async XLA Ops:
  1.2 10.9 %collective-permute-start.6 = (bf16[32,2048]{1,0:T(8,128)(2,1)S(1)}, bf16[32,2048]{1,0:T(8,128)(2,1)S(1)}, u32[]{:S(2)}, u32[]{:S(2)}) collective-permute-start(bf16[32,2048]{1,0:T(8,128)(2,1)S(1)} %get-tuple-element.31.refs_4_), channel_id=1, source_target_pairs={{0,4},{1,5},{2,6},{3,7},{4,0},{5,1},{6,2},{7,3},{8,12},{9,13},{10,... | collective-permute-start | bytes 393224 | tf_op jit(solution)/shard_map/ppermute | solution.py:395
  4.3 6.2 %collective-permute-start = (bf16[16,2048]{1,0:T(8,128)(2,1)S(1)}, bf16[16,2048]{1,0:T(8,128)(2,1)S(1)}, u32[]{:S(2)}, u32[]{:S(2)}) collective-permute-start(bf16[16,2048]{1,0:T(8,128)(2,1)S(1)} %get-tuple-element.29.refs_0_), channel_id=1, source_target_pairs={{0,8},{8,16},{16,24},{24,0},{1,9},{9,17},{17,25},{25,1},{2,10},{10... | collective-permute-start | bytes 196616 | tf_op jit(solution)/shard_map/ppermute | solution.py:392
  5.8 9.8 %collective-permute-start.4 = (bf16[32,2048]{1,0:T(8,128)(2,1)S(1)}, bf16[32,2048]{1,0:T(8,128)(2,1)S(1)}, u32[]{:S(2)}, u32[]{:S(2)}) collective-permute-start(bf16[32,2048]{1,0:T(8,128)(2,1)S(1)} %get-tuple-element.31.refs_4_), channel_id=1, source_target_pairs={{0,2},{1,3},{2,0},{3,1},{4,6},{5,7},{6,4},{7,5},{8,10},{9,11},{10,... | collective-permute-start | bytes 393224 | tf_op jit(solution)/shard_map/ppermute | solution.py:395
  7.3 8.3 %collective-permute-start.8 = (bf16[32,2048]{1,0:T(8,128)(2,1)S(1)}, bf16[32,2048]{1,0:T(8,128)(2,1)S(1)}, u32[]{:S(2)}, u32[]{:S(2)}) collective-permute-start(bf16[32,2048]{1,0:T(8,128)(2,1)S(1)} %get-tuple-element.31.refs_4_), channel_id=1, source_target_pairs={{0,6},{1,7},{2,4},{3,5},{4,2},{5,3},{6,0},{7,1},{8,14},{9,15},{10,... | collective-permute-start | bytes 393224 | tf_op jit(solution)/shard_map/ppermute | solution.py:395
  7.8 4.3 %collective-permute-start.2 = (bf16[16,2048]{1,0:T(8,128)(2,1)S(1)}, bf16[16,2048]{1,0:T(8,128)(2,1)S(1)}, u32[]{:S(2)}, u32[]{:S(2)}) collective-permute-start(bf16[16,2048]{1,0:T(8,128)(2,1)S(1)} %get-tuple-element.29.refs_0_), channel_id=1, source_target_pairs={{0,24},{8,0},{16,8},{24,16},{1,25},{9,1},{17,9},{25,17},{2,26},{10... | collective-permute-start | bytes 196616 | tf_op jit(solution)/shard_map/ppermute | solution.py:392
  10.4 5.2 %collective-permute-start.1 = (bf16[16,2048]{1,0:T(8,128)(2,1)S(1)}, bf16[16,2048]{1,0:T(8,128)(2,1)S(1)}, u32[]{:S(2)}, u32[]{:S(2)}) collective-permute-start(bf16[16,2048]{1,0:T(8,128)(2,1)S(1)} %get-tuple-element.29.refs_0_), channel_id=1, source_target_pairs={{0,16},{8,24},{16,0},{24,8},{1,17},{9,25},{17,1},{25,9},{2,18},{10... | collective-permute-start | bytes 196616 | tf_op jit(solution)/shard_map/ppermute | solution.py:392
  12.1 4.0 %collective-permute-start.3 = (bf16[32,2048]{1,0:T(8,128)(2,1)S(1)}, bf16[32,2048]{1,0:T(8,128)(2,1)S(1)}, u32[]{:S(2)}, u32[]{:S(2)}) collective-permute-start(bf16[32,2048]{1,0:T(8,128)(2,1)S(1)} %get-tuple-element.31.refs_4_), channel_id=1, source_target_pairs={{0,1},{1,0},{2,3},{3,2},{4,5},{5,4},{6,7},{7,6},{8,9},{9,8},{10,11... | collective-permute-start | bytes 393224 | tf_op jit(solution)/shard_map/ppermute | solution.py:395
  12.1 4.9 %collective-permute-start.7 = (bf16[32,2048]{1,0:T(8,128)(2,1)S(1)}, bf16[32,2048]{1,0:T(8,128)(2,1)S(1)}, u32[]{:S(2)}, u32[]{:S(2)}) collective-permute-start(bf16[32,2048]{1,0:T(8,128)(2,1)S(1)} %collective-permute-done.6.refs_8_), channel_id=1, source_target_pairs={{0,1},{1,0},{2,3},{3,2},{4,5},{5,4},{6,7},{7,6},{8,9},{9,8},{10,11... | collective-permute-start | bytes 393224 | tf_op jit(solution)/shard_map/ppermute | solution.py:395
  15.6 1.4 %collective-permute-start.9 = (bf16[32,2048]{1,0:T(8,128)(2,1)S(1)}, bf16[32,2048]{1,0:T(8,128)(2,1)S(1)}, u32[]{:S(2)}, u32[]{:S(2)}) collective-permute-start(bf16[32,2048]{1,0:T(8,128)(2,1)S(1)} %collective-permute-done.8.refs_10_), channel_id=1, source_target_pairs={{0,1},{1,0},{2,3},{3,2},{4,5},{5,4},{6,7},{7,6},{8,9},{9,8},{10,11... | collective-permute-start | bytes 393224 | tf_op jit(solution)/shard_map/ppermute | solution.py:395
  15.6 1.5 %collective-permute-start.5 = (bf16[32,2048]{1,0:T(8,128)(2,1)S(1)}, bf16[32,2048]{1,0:T(8,128)(2,1)S(1)}, u32[]{:S(2)}, u32[]{:S(2)}) collective-permute-start(bf16[32,2048]{1,0:T(8,128)(2,1)S(1)} %collective-permute-done.4.refs_6_), channel_id=1, source_target_pairs={{0,1},{1,0},{2,3},{3,2},{4,5},{5,4},{6,7},{7,6},{8,9},{9,8},{10,11... | collective-permute-start | bytes 393224 | tf_op jit(solution)/shard_map/ppermute | solution.py:395
  26.9 6.8 %collective-permute-start.10 = (bf16[16,2048]{1,0:T(8,128)(2,1)S(1)}, bf16[16,2048]{1,0:T(8,128)(2,1)S(1)}, u32[]{:S(2)}, u32[]{:S(2)}) collective-permute-start(bf16[16,2048]{1,0:T(8,128)(2,1)S(1)} %get-tuple-element.44), channel_id=1, source_target_pairs={{0,24},{8,0},{16,8},{24,16},{1,25},{9,1},{17,9},{25,17},{2,26},{10... | collective-permute-start | bytes 196616 | tf_op jit(solution)/shard_map/ppermute | solution.py:401
  30.3 7.1 %collective-permute-start.11 = (bf16[16,2048]{1,0:T(8,128)(2,1)S(1)}, bf16[16,2048]{1,0:T(8,128)(2,1)S(1)}, u32[]{:S(2)}, u32[]{:S(2)}) collective-permute-start(bf16[16,2048]{1,0:T(8,128)(2,1)S(1)} %get-tuple-element.45), channel_id=1, source_target_pairs={{0,16},{8,24},{16,0},{24,8},{1,17},{9,25},{17,1},{25,9},{2,18},{10... | collective-permute-start | bytes 196616 | tf_op jit(solution)/shard_map/ppermute | solution.py:401
  30.3 7.1 %collective-permute-start.12 = (bf16[16,2048]{1,0:T(8,128)(2,1)S(1)}, bf16[16,2048]{1,0:T(8,128)(2,1)S(1)}, u32[]{:S(2)}, u32[]{:S(2)}) collective-permute-start(bf16[16,2048]{1,0:T(8,128)(2,1)S(1)} %get-tuple-element.46), channel_id=1, source_target_pairs={{0,8},{8,16},{16,24},{24,0},{1,9},{9,17},{17,25},{25,1},{2,10},{10... | collective-permute-start | bytes 196616 | tf_op jit(solution)/shard_map/ppermute | solution.py:401
  37.5 5.3 %collective-permute-start.18 = (bf16[16,2048]{1,0:T(8,128)(2,1)S(1)}, bf16[16,2048]{1,0:T(8,128)(2,1)S(1)}, u32[]{:S(2)}, u32[]{:S(2)}) collective-permute-start(bf16[16,2048]{1,0:T(8,128)(2,1)S(1)} %multiply_convert_fusion.refs_1_), channel_id=1, source_target_pairs={{0,6},{1,7},{2,4},{3,5},{4,2},{5,3},{6,0},{7,1},{8,14},{9,15},{10,... | collective-permute-start | bytes 196616 | tf_op jit(solution)/shard_map/ppermute | solution.py:395
  39.7 4.4 %collective-permute-start.16 = (bf16[16,2048]{1,0:T(8,128)(2,1)S(1)}, bf16[16,2048]{1,0:T(8,128)(2,1)S(1)}, u32[]{:S(2)}, u32[]{:S(2)}) collective-permute-start(bf16[16,2048]{1,0:T(8,128)(2,1)S(1)} %multiply_convert_fusion.refs_1_), channel_id=1, source_target_pairs={{0,4},{1,5},{2,6},{3,7},{4,0},{5,1},{6,2},{7,3},{8,12},{9,13},{10,... | collective-permute-start | bytes 196616 | tf_op jit(solution)/shard_map/ppermute | solution.py:395
  39.7 4.4 %collective-permute-start.14 = (bf16[16,2048]{1,0:T(8,128)(2,1)S(1)}, bf16[16,2048]{1,0:T(8,128)(2,1)S(1)}, u32[]{:S(2)}, u32[]{:S(2)}) collective-permute-start(bf16[16,2048]{1,0:T(8,128)(2,1)S(1)} %multiply_convert_fusion.refs_1_), channel_id=1, source_target_pairs={{0,2},{1,3},{2,0},{3,1},{4,6},{5,7},{6,4},{7,5},{8,10},{9,11},{10,... | collective-permute-start | bytes 196616 | tf_op jit(solution)/shard_map/ppermute | solution.py:395
  41.0 3.6 %collective-permute-start.13 = (bf16[16,2048]{1,0:T(8,128)(2,1)S(1)}, bf16[16,2048]{1,0:T(8,128)(2,1)S(1)}, u32[]{:S(2)}, u32[]{:S(2)}) collective-permute-start(bf16[16,2048]{1,0:T(8,128)(2,1)S(1)} %multiply_convert_fusion.refs_1_), channel_id=1, source_target_pairs={{0,1},{1,0},{2,3},{3,2},{4,5},{5,4},{6,7},{7,6},{8,9},{9,8},{10,11... | collective-permute-start | bytes 196616 | tf_op jit(solution)/shard_map/ppermute | solution.py:395
  42.8 1.9 %collective-permute-start.19 = (bf16[16,2048]{1,0:T(8,128)(2,1)S(1)}, bf16[16,2048]{1,0:T(8,128)(2,1)S(1)}, u32[]{:S(2)}, u32[]{:S(2)}) collective-permute-start(bf16[16,2048]{1,0:T(8,128)(2,1)S(1)} %collective-permute-done.18.refs_7_), channel_id=1, source_target_pairs={{0,1},{1,0},{2,3},{3,2},{4,5},{5,4},{6,7},{7,6},{8,9},{9,8},{10,11... | collective-permute-start | bytes 196616 | tf_op jit(solution)/shard_map/ppermute | solution.py:395
  44.1 1.3 %collective-permute-start.17 = (bf16[16,2048]{1,0:T(8,128)(2,1)S(1)}, bf16[16,2048]{1,0:T(8,128)(2,1)S(1)}, u32[]{:S(2)}, u32[]{:S(2)}) collective-permute-start(bf16[16,2048]{1,0:T(8,128)(2,1)S(1)} %collective-permute-done.16.refs_5_), channel_id=1, source_target_pairs={{0,1},{1,0},{2,3},{3,2},{4,5},{5,4},{6,7},{7,6},{8,9},{9,8},{10,11... | collective-permute-start | bytes 196616 | tf_op jit(solution)/shard_map/ppermute | solution.py:395
  44.1 1.4 %collective-permute-start.15 = (bf16[16,2048]{1,0:T(8,128)(2,1)S(1)}, bf16[16,2048]{1,0:T(8,128)(2,1)S(1)}, u32[]{:S(2)}, u32[]{:S(2)}) collective-permute-start(bf16[16,2048]{1,0:T(8,128)(2,1)S(1)} %collective-permute-done.14.refs_3_), channel_id=1, source_target_pairs={{0,1},{1,0},{2,3},{3,2},{4,5},{5,4},{6,7},{7,6},{8,9},{9,8},{10,11... | collective-permute-start | bytes 196616 | tf_op jit(solution)/shard_map/ppermute | solution.py:395
  47.4 8.4 %collective-permute-start.21 = (bf16[16,2048]{1,0:T(8,128)(2,1)S(1)}, bf16[16,2048]{1,0:T(8,128)(2,1)S(1)}, u32[]{:S(2)}, u32[]{:S(2)}) collective-permute-start(bf16[16,2048]{1,0:T(8,128)(2,1)S(1)} %apply.6), channel_id=1, source_target_pairs={{0,16},{8,24},{16,0},{24,8},{1,17},{9,25},{17,1},{25,9},{2,18},{10... | collective-permute-start | bytes 196616 | tf_op jit(solution)/shard_map/ppermute | solution.py:401
  49.0 6.9 %collective-permute-start.22 = (bf16[16,2048]{1,0:T(8,128)(2,1)S(1)}, bf16[16,2048]{1,0:T(8,128)(2,1)S(1)}, u32[]{:S(2)}, u32[]{:S(2)}) collective-permute-start(bf16[16,2048]{1,0:T(8,128)(2,1)S(1)} %apply.7), channel_id=1, source_target_pairs={{0,8},{8,16},{16,24},{24,0},{1,9},{9,17},{17,25},{25,1},{2,10},{10... | collective-permute-start | bytes 196616 | tf_op jit(solution)/shard_map/ppermute | solution.py:401
  49.8 6.3 %collective-permute-start.20 = (bf16[16,2048]{1,0:T(8,128)(2,1)S(1)}, bf16[16,2048]{1,0:T(8,128)(2,1)S(1)}, u32[]{:S(2)}, u32[]{:S(2)}) collective-permute-start(bf16[16,2048]{1,0:T(8,128)(2,1)S(1)} %get-tuple-element.48), channel_id=1, source_target_pairs={{0,24},{8,0},{16,8},{24,16},{1,25},{9,1},{17,9},{25,17},{2,26},{10... | collective-permute-start | bytes 196616 | tf_op jit(solution)/shard_map/ppermute | solution.py:401
